TPU v7x, 512 devices: a whole 4x8x8 slice. The times are simulated.
512 devices in a mesh: gx: 32 (over z, x), gy: 16 (over y, core).
Axes of the slice: x: 4, y: 8, z: 8, core: 2. Of those that a mesh axis runs over, the one named last changes fastest.
Arguments:
- mentions: bfloat16 [131072, 768], P(('gx', 'gy')), may hold values from -64 to 64
- type_table: float32 [65536, 768], P(('gx', 'gy')), may hold values from -1.25 to 1.25
- adam_m: float32 [65536, 768], P(('gx', 'gy')), may hold values from -6 to 6
- adam_v: float32 [65536, 768], P(('gx', 'gy')), may hold values from 0.01 to 10
- logit_scale: float32 [1], replicated, may hold values from 3 to 6
- block_lists: int32 [1024, 16], P(('gx', 'gy')), may hold values from 0 to 511, as said below
- list_lengths: int32 [1024], P(('gx', 'gy')), may hold values from 4 to 16
- gold_slot: int32 [131072], P(('gx', 'gy')), may hold values from 0 to 15, as said below
- gold_row: int32 [131072], P(('gx', 'gy')), may hold values from 0 to 127
Outputs:
- new_table: float32 [65536, 768], P(('gx', 'gy'))
- new_first: float32 [65536, 768], P(('gx', 'gy'))
- new_second: float32 [65536, 768], P(('gx', 'gy'))
- mention_grad: bfloat16 [131072, 768], P(('gx', 'gy'))
- scale_grad: float32 [1], replicated
Inputs may be any that keep to these rules, and one draw needn't show every extreme that they name: `block_lists`: row g names 16 distinct type blocks, all owned by devices with the same gy index as the device holding mention block g; only the first list_lengths[g] entries are used. `gold_slot`: below the list length of the mention's block.
All inputs are finite; a program needn't handle non-finite values.
Results may differ from a plain program's by a relative error of at most 0.0069.
Values may be sent and summed in bfloat16 or wider, within the bound.
No kernel may reach another device: no remote copies, remote signals or barrier semaphores. Data moves between devices by JAX's collectives and lax.ppermute only.
A program may use at most 128 MiB of HBM per device.

v0:
```python
import jax
import jax.numpy as jnp
from jax import lax
from jax.sharding import PartitionSpec as P

beta_one = 0.9
beta_two = 0.999
learn_rate = 0.02
adam_eps = 1e-08
first_fix = 0.9999734386011124
second_fix = 0.09520785288629038


def adam_rows(type_table, adam_m, adam_v, type_grad):
    moment_one = beta_one * adam_m + (1.0 - beta_one) * type_grad
    moment_two = beta_two * adam_v + (1.0 - beta_two) * type_grad * type_grad
    updated = type_table - learn_rate * (moment_one / first_fix) / (
        jnp.sqrt(moment_two / second_fix) + adam_eps
    )
    return (updated, moment_one, moment_two)


def per_device(
    mentions,
    type_table,
    adam_m,
    adam_v,
    logit_scale,
    block_lists,
    list_lengths,
    gold_slot,
    gold_row,
):
    row_count = lax.axis_size("gx")
    col_count = lax.axis_size("gy")
    block_rows, width = type_table.shape
    groups, slot_max = block_lists.shape
    factor = logit_scale[0]
    mention_rows = mentions.reshape(groups, block_rows, width)
    slot_live = jnp.arange(slot_max, dtype=jnp.int32)[None, :] < list_lengths[:, None]
    owner_row = block_lists // col_count
    row_ids = jnp.arange(row_count, dtype=jnp.int32)
    listed_rows = jnp.any(
        slot_live[:, :, None] & (owner_row[:, :, None] == row_ids[None, None, :]), axis=1
    )
    slot_ids = gold_slot.reshape(groups, block_rows)
    gold_rows = gold_row.reshape(groups, block_rows)
    gold_blocks = jnp.take_along_axis(block_lists, slot_ids, axis=1)
    gold_column = gold_blocks // col_count * block_rows + gold_rows
    local_bf = type_table.astype(jnp.bfloat16)

    def column_live(row_span):
        owner_idx = jnp.arange(row_span, dtype=jnp.int32) // block_rows
        return jnp.any(
            listed_rows[:, None, :] & (owner_idx[None, :, None] == row_ids[None, None, :]), axis=-1
        )

    gathered = lax.all_gather(local_bf, "gx", axis=0, tiled=True)
    row_max = jnp.full((groups, block_rows), -1e30, jnp.float32)
    raw_dot = jnp.einsum("gbd,nd->gbn", mention_rows, gathered, preferred_element_type=jnp.float32)
    scores = factor * raw_dot
    usable = column_live(gathered.shape[0])[:, None, :]
    shard_max = jnp.max(jnp.where(usable, scores, -jnp.inf), axis=-1)
    merged_max = jnp.maximum(row_max, shard_max)
    shard_total = jnp.sum(jnp.where(usable, jnp.exp(scores - merged_max[..., None]), 0.0), axis=-1)
    log_total = merged_max + jnp.log(shard_total)
    raw_dot = jnp.einsum("gbd,nd->gbn", mention_rows, gathered, preferred_element_type=jnp.float32)
    scores = factor * raw_dot
    usable = column_live(gathered.shape[0])[:, None, :]
    weights = jnp.where(usable, jnp.exp(scores - log_total[..., None]), 0.0)
    columns = jnp.arange(gathered.shape[0], dtype=jnp.int32)
    target = (columns[None, None, :] == gold_column[:, :, None]).astype(jnp.float32)
    grad_scores = weights - target
    scale_part = jnp.sum(grad_scores * raw_dot)
    grad_bf = grad_scores.astype(jnp.bfloat16)
    mention_part = jnp.einsum("gbn,nd->gbd", grad_bf, gathered, preferred_element_type=jnp.float32)
    type_part = jnp.einsum("gbn,gbd->nd", grad_bf, mention_rows, preferred_element_type=jnp.float32)
    outgoing = (factor * type_part).astype(jnp.bfloat16).reshape(row_count, block_rows, width)
    received = lax.all_to_all(outgoing, "gx", split_axis=0, concat_axis=0, tiled=True)
    type_grad = jnp.sum(received, axis=0, dtype=jnp.float32)
    new_table, new_first, new_second = adam_rows(type_table, adam_m, adam_v, type_grad)
    mention_grad = (factor * mention_part).astype(jnp.bfloat16).reshape(groups * block_rows, width)
    grand_total = lax.psum(scale_part, ("gx", "gy"))
    scale_grad = (grand_total / (groups * block_rows * row_count * col_count)).reshape(1)
    return (new_table, new_first, new_second, mention_grad, scale_grad)


def solution(mesh):
    return jax.shard_map(
        per_device,
        mesh=mesh,
        in_specs=(
            P(("gx", "gy"), None),
            P(("gx", "gy"), None),
            P(("gx", "gy"), None),
            P(("gx", "gy"), None),
            P(),
            P(("gx", "gy"), None),
            P(("gx", "gy")),
            P(("gx", "gy")),
            P(("gx", "gy")),
        ),
        out_specs=(
            P(("gx", "gy"), None),
            P(("gx", "gy"), None),
            P(("gx", "gy"), None),
            P(("gx", "gy"), None),
            P(),
        ),
        check_vma=False,
    )
```

profile of v0, /device:TPU:1, one launch (start us, length us, event | category | flops | bytes accessed | tf_op | source)
XLA Modules:
  0.0 381.4 jit_solution(327549213349755757)
XLA Ops:
  7.2 0.0 copy-start
  7.2 0.0 all-gather.2.cloned.1.call-start
  7.2 1.7 convert_element_type.18
  9.0 0.0 all-gather.2.cloned.1.call-update
  9.6 0.7 fusion.21
  10.3 2.3 gather_fusion
  12.7 0.7 iota_compare_fusion.3
  13.4 0.7 and_select_fusion.2
  14.1 0.1 fusion.16
  14.2 0.1 iota_compare_fusion.1
  14.2 0.2 and_reduce_fusion
  14.5 0.7 bitcast_add_fusion
  15.2 96.5 %all-gather.2.cloned.1.call-done = bf16[4096,768]{1,0:T(8,128)(2,1)} async-done(((bf16[128,768]{1,0:T(8,128)(2,1)}), bf16[4096,768]{1,0:T(8,128)(2,1)}) %all-gather.2.cloned.1.call-update) | async-done | bytes 6291472 | tf_op jit(solution)/shard_map/all_gather | solution.py:58
  111.7 0.0 copy-done
  111.7 4.7 %select_reduce_fusion.1 = (f32[2,128]{1,0:T(2,128)S(1)}, f32[2,128,4096]{2,1,0:T(8,128)S(1)}) fusion(f32[]{:T(128)} %bitcast.39, pred[2,4096]{1,0:T(4,128)(4,1)S(1)} %and_reduce_fusion, bf16[2,128,768]{2,1,0:T(8,128)(2,1)S(1)} %bitcast.43, bf16[4096,768]{1,0:T(8,128)(2,1)} %all-gather.2.cloned.1.call-done), kind=kOutput, calls=%fused_computation.12 | convolution fusion | flops 1613758208 | bytes 10888196 | tf_op jit(solution)/shard_map/gbd,nd->gbn/dot_general | solution.py:67
  116.4 0.0 copy-start.1
  116.4 1.1 select_reduce_fusion
  117.5 5.8 %fusion = bf16[4096,768]{1,0:T(8,128)(2,1)} fusion(bf16[2,128,768]{2,1,0:T(8,128)(2,1)S(1)} %bitcast.44, f32[]{:T(128)} %bitcast.38, f32[2,128,4096]{2,1,0:T(8,128)S(1)} %get-tuple-element.9, s32[2,128]{1,0:T(2,128)S(1)} %bitcast_add_fusion, f32[2,128]{1,0:T(2,128)S(1)} %log_add_fusion, pred[2,4096]{1,0:T(4,128)(4,1)S(1)} %and_reduce_fusion), kind=kOutput, calls=%fused_computation.2 | convolution fusion | flops 1624244224 | bytes 10889220 | tf_op jit(solution)/shard_map/gbn,gbd->nd/dot_general | solution.py:77
  123.3 0.0 copy-done.1
  123.3 5.3 %all-to-all-start = ((bf16[32,128,768]{2,1,0:T(8,128)(2,1)}), bf16[32,128,768]{2,1,0:T(8,128)(2,1)}, u32[]{:S(2)}, u32[]{:S(2)}) async-start(bf16[32,128,768]{2,1,0:T(8,128)(2,1)} %bitcast.45), calls=%async_computation | async-start | bytes 12582912 | tf_op jit(solution)/shard_map/all_to_all | solution.py:79
  128.6 4.4 %multiply_reduce_fusion = f32[]{:T(128)} fusion(f32[2,128,4096]{2,1,0:T(8,128)} %copy-done.1, s32[2,128]{1,0:T(2,128)S(1)} %bitcast_add_fusion, f32[2,128]{1,0:T(2,128)S(1)} %log_add_fusion, f32[]{:T(128)} %bitcast.41, pred[2,4096]{1,0:T(4,128)(4,1)S(1)} %and_reduce_fusion), kind=kLoop, calls=%fused_computation.8 | loop fusion | flops 8388607 | bytes 4204552 | tf_op jit(solution)/shard_map/reduce_sum | solution.py:74
  133.0 227.4 %psum.7 = f32[]{:T(128)} all-reduce(f32[]{:T(128)} %multiply_reduce_fusion), channel_id=1, replica_groups=mesh['gx'=32,'gy'=16] {'gx','gy'}, use_global_device_ids=true, to_apply=%region_6.7 | all-reduce | flops 1 | bytes 8 | tf_op jit(solution)/shard_map/psum | solution.py:83
  361.1 7.4 %fusion.9 = bf16[2,128,768]{2,1,0:T(8,128)(2,1)} fusion(bf16[4096,768]{1,0:T(8,128)(2,1)} %all-gather.2.cloned.1.call-done, f32[]{:T(128)} %bitcast.40, f32[2,128,4096]{2,1,0:T(8,128)} %copy-done.1, s32[2,128]{1,0:T(2,128)S(1)} %bitcast_add_fusion, f32[2,128]{1,0:T(2,128)S(1)} %log_add_fusion, pred[2,4096]{1,0:T(4,128)(4,1)S(1)} %and_reduce_fusion), kind=kOutput, calls=%fused_computation.15 | convolution fusion | flops 1618345984 | bytes 10889220 | tf_op jit(solution)/shard_map/gbn,nd->gbd/dot_general | solution.py:76
  368.4 0.0 copy-start.2
  368.4 0.0 copy-start.3
  368.4 0.0 copy-start.4
  368.4 0.0 all-to-all-done
  368.4 3.8 convert_reduce_fusion
  372.3 0.0 copy-done.2
  372.3 0.0 copy-done.3
  372.3 0.0 copy-done.4
  372.3 1.2 divide_subtract_fusion
  (3 shorter events, 0.0 us)
Async XLA Ops:
  7.2 104.5 %copy-start = (bf16[256,768]{1,0:T(8,128)(2,1)S(1)}, bf16[256,768]{1,0:T(8,128)(2,1)}, u32[]{:S(2)}) copy-start(bf16[256,768]{1,0:T(8,128)(2,1)} %param.9) | copy-start | bytes 1179652
  7.2 104.5 %all-gather.2.cloned.1.call-start = ((), (), s32[]{:S(2)}) async-start(), calls=%async_computation.1 | async-start | bytes 6488064 | tf_op jit(solution)/shard_map/all_gather | solution.py:58
  116.4 6.9 %copy-start.1 = (f32[2,128,4096]{2,1,0:T(8,128)}, f32[2,128,4096]{2,1,0:T(8,128)S(1)}, u32[]{:S(2)}) copy-start(f32[2,128,4096]{2,1,0:T(8,128)S(1)} %get-tuple-element.9) | copy-start | bytes 12582916
  123.3 245.2 %all-to-all-start = ((bf16[32,128,768]{2,1,0:T(8,128)(2,1)}), bf16[32,128,768]{2,1,0:T(8,128)(2,1)}, u32[]{:S(2)}, u32[]{:S(2)}) async-start(bf16[32,128,768]{2,1,0:T(8,128)(2,1)} %bitcast.45), calls=%async_computation | async-start | bytes 12582912 | tf_op jit(solution)/shard_map/all_to_all | solution.py:79
  368.4 3.8 %copy-start.2 = (f32[128,768]{1,0:T(8,128)S(1)}, f32[128,768]{1,0:T(8,128)}, u32[]{:S(2)}) copy-start(f32[128,768]{1,0:T(8,128)} %param.10) | copy-start | bytes 1179652
  368.4 3.8 %copy-start.3 = (f32[128,768]{1,0:T(8,128)S(1)}, f32[128,768]{1,0:T(8,128)}, u32[]{:S(2)}) copy-start(f32[128,768]{1,0:T(8,128)} %param.11) | copy-start | bytes 1179652
  368.4 3.8 %copy-start.4 = (f32[128,768]{1,0:T(8,128)S(1)}, f32[128,768]{1,0:T(8,128)}, u32[]{:S(2)}) copy-start(f32[128,768]{1,0:T(8,128)} %param.12) | copy-start | bytes 1179652
Sparse Core Ops, SparseCore 0:
  11.7 99.8 all-gather.1
where the time goes:
time: 382 us; the launch traced here: 381 us
  blocking collectives  227 us (59%)
  waiting for transfers between devices  96.5 us (25%)
  matrix products  17.8 us (5%)
  between operations  16.5 us (4%)
  other arithmetic  15.5 us (4%)
  starting transfers between devices  5.33 us (1%)
    psum x1, blocking collectives, per_device(): grand_total = lax.psum(scale_part, ('gx', 'gy'))  227 us
    all_gather x1, waiting for transfers between devices, per_device(): gathered = lax.all_gather(local_bf, 'gx', axis=0, tiled=True)  96.5 us
  transfers between devices with their start and end apart: 2, of which 1 were waited for; matrix products, arithmetic and copies ran while one was open for 5% of the time, Pallas kernels for 0%

commit v1 on v0

v1 whole, which is shorter than its diff:
```python
import jax
import jax.numpy as jnp
from jax import lax
from jax.experimental import pallas as pl
from jax.experimental.pallas import tpu as pltpu
from jax.sharding import Mesh, PartitionSpec as P

beta_one = 0.9
beta_two = 0.999
learn_rate = 0.02
adam_eps = 1e-08
first_fix = 0.9999734386011124
second_fix = 0.09520785288629038

X_SIZE = 4
LOW = -1e30
META_ROWS = 16
STAT_ROWS = 8
f32 = jnp.float32
bf16 = jnp.bfloat16


def adam_rows(type_table, adam_m, adam_v, type_grad):
    moment_one = beta_one * adam_m + (1.0 - beta_one) * type_grad
    moment_two = beta_two * adam_v + (1.0 - beta_two) * type_grad * type_grad
    updated = type_table - learn_rate * (moment_one / first_fix) / (
        jnp.sqrt(moment_two / second_fix) + adam_eps
    )
    return (updated, moment_one, moment_two)


def scores_kernel(factor_ref, m_ref, t_ref, meta_ref, raw_ref, stat_ref):
    step = pl.program_id(0)
    factor = factor_ref[0]
    rows = m_ref.shape[1]
    chunks = t_ref.shape[0] // 128
    raw_ref[0] = lax.dot_general(
        t_ref[...], m_ref[0], (((1,), (1,)), ((), ())), preferred_element_type=f32
    )
    top = jnp.full((1, rows), LOW, f32)
    for c in range(chunks):
        live = meta_ref[0, c : c + 1, :] > 0.0
        part = jnp.max(factor * raw_ref[0, c * 128 : (c + 1) * 128, :], axis=0, keepdims=True)
        top = jnp.maximum(top, jnp.where(live, part, LOW))
    total = jnp.zeros((1, rows), f32)
    for c in range(chunks):
        live = meta_ref[0, c : c + 1, :] > 0.0
        scores = factor * raw_ref[0, c * 128 : (c + 1) * 128, :]
        part = jnp.sum(jnp.exp(scores - top), axis=0, keepdims=True)
        total = total + jnp.where(live, part, 0.0)
    stat = jnp.concatenate([top, total, jnp.zeros((STAT_ROWS - 2, rows), f32)], axis=0)
    for d in range(stat_ref.shape[0]):
        stat_ref[d, :, pl.ds(pl.multiple_of(step * rows, 128), rows)] = stat


def grads_kernel(factor_ref, raw_ref, meta_ref, stat_ref, m_ref, g_ref, type_ref, scale_ref, acc_ref, sum_ref):
    step = pl.program_id(0)
    factor = factor_ref[0]
    rows = m_ref.shape[1]
    chunks = raw_ref.shape[1] // 128
    tops = stat_ref[:, 0, :]
    sums = stat_ref[:, 1, :]
    top = jnp.max(tops, axis=0, keepdims=True)
    log_total = top + jnp.log(jnp.sum(sums * jnp.exp(tops - top), axis=0, keepdims=True))
    gold = meta_ref[0, chunks : chunks + 1, :].astype(jnp.int32)
    ids = lax.broadcasted_iota(jnp.int32, (128, rows), 0)
    scale = jnp.zeros((1, rows), f32)
    for c in range(chunks):
        live = meta_ref[0, c : c + 1, :] > 0.0
        raw = raw_ref[0, c * 128 : (c + 1) * 128, :]
        weights = jnp.where(live, jnp.exp(factor * raw - log_total), 0.0)
        grad = weights - jnp.where(ids + c * 128 == gold, 1.0, 0.0)
        scale = scale + jnp.sum(grad * raw, axis=0, keepdims=True)
        g_ref[0, c * 128 : (c + 1) * 128, :] = grad.astype(bf16)
    part = jnp.dot(g_ref[0], m_ref[0], preferred_element_type=f32)

    @pl.when(step == 0)
    def _():
        acc_ref[...] = part
        sum_ref[...] = scale

    @pl.when(step > 0)
    def _():
        acc_ref[...] += part
        sum_ref[...] += scale

    @pl.when(step == pl.num_programs(0) - 1)
    def _():
        type_ref[...] = (factor * acc_ref[...]).astype(bf16)
        scale_ref[...] = jnp.broadcast_to(jnp.sum(sum_ref[...], axis=1, keepdims=True), scale_ref.shape)


def mention_kernel(factor_ref, g_ref, t_ref, out_ref):
    part = lax.dot_general(
        g_ref[0], t_ref[...], (((0,), (0,)), ((), ())), preferred_element_type=f32
    )
    out_ref[0] = (factor_ref[0] * part).astype(bf16)


def params():
    return pltpu.CompilerParams(
        dimension_semantics=("arbitrary",), vmem_limit_bytes=40 * 1024 * 1024
    )


def per_device(
    mentions,
    type_table,
    adam_m,
    adam_v,
    logit_scale,
    block_lists,
    list_lengths,
    gold_slot,
    gold_row,
):
    z_size = lax.axis_size("gz")
    x_size = lax.axis_size("gx")
    col_count = lax.axis_size("gy")
    devices = z_size * x_size * col_count
    block_rows, width = type_table.shape
    groups, slot_max = block_lists.shape
    rows = groups * block_rows
    types = z_size * block_rows
    smem = pl.BlockSpec(memory_space=pltpu.SMEM)

    table = lax.all_gather(type_table.astype(bf16), "gz", axis=0, tiled=True)
    gathered = lax.all_to_all(
        jnp.broadcast_to(mentions[None], (x_size, rows, width)), "gx", 0, 0, tiled=True
    )

    slot_live = jnp.arange(slot_max, dtype=jnp.int32)[None, :] < list_lengths[:, None]
    owner = block_lists // col_count
    owner_ids = jnp.arange(z_size * x_size, dtype=jnp.int32)
    listed = jnp.any(
        slot_live[:, :, None] & (owner[:, :, None] == owner_ids[None, None, :]), axis=1
    )
    listed = listed.reshape(groups, z_size, x_size).transpose(2, 1, 0).astype(f32)
    listed = jnp.repeat(listed, block_rows, axis=2)
    slots = gold_slot.reshape(groups, block_rows)
    slot_ids = jnp.arange(slot_max, dtype=jnp.int32)
    gold_owner = jnp.sum(
        jnp.where(slots[:, :, None] == slot_ids[None, None, :], owner[:, None, :], 0), axis=2
    ).reshape(1, rows)
    x_ids = jnp.arange(x_size, dtype=jnp.int32)[:, None]
    gold = jnp.where(
        gold_owner % x_size == x_ids,
        gold_owner // x_size * block_rows + gold_row.reshape(1, rows),
        -1,
    ).astype(f32)
    meta = jnp.concatenate(
        [listed, gold[:, None, :], jnp.zeros((x_size, META_ROWS - z_size - 1, rows), f32)], axis=1
    )
    meta = lax.all_to_all(meta, "gx", 0, 0, tiled=True)

    tile = lambda *shape: pl.BlockSpec((1,) + shape, lambda j: (j, 0, 0))
    whole = pl.BlockSpec((types, width), lambda j: (0, 0))
    raw_dot, stats = pl.pallas_call(
        scores_kernel,
        grid=(x_size,),
        in_specs=[smem, tile(rows, width), whole, tile(META_ROWS, rows)],
        out_specs=[
            tile(types, rows),
            pl.BlockSpec((x_size, STAT_ROWS, x_size * rows), lambda j: (0, 0, 0)),
        ],
        out_shape=[
            jax.ShapeDtypeStruct((x_size, types, rows), f32),
            jax.ShapeDtypeStruct((x_size, STAT_ROWS, x_size * rows), f32),
        ],
        compiler_params=params(),
        name="scores",
    )(logit_scale, gathered, table, meta)
    stats = lax.all_to_all(stats, "gx", 0, 0, tiled=True)
    grads, type_part, scale_part = pl.pallas_call(
        grads_kernel,
        grid=(x_size,),
        in_specs=[
            smem,
            tile(types, rows),
            tile(META_ROWS, rows),
            pl.BlockSpec((x_size, STAT_ROWS, rows), lambda j: (0, 0, j)),
            tile(rows, width),
        ],
        out_specs=[
            tile(types, rows),
            whole,
            pl.BlockSpec((1, 128), lambda j: (0, 0)),
        ],
        out_shape=[
            jax.ShapeDtypeStruct((x_size, types, rows), bf16),
            jax.ShapeDtypeStruct((types, width), bf16),
            jax.ShapeDtypeStruct((1, 128), f32),
        ],
        scratch_shapes=[pltpu.VMEM((types, width), f32), pltpu.VMEM((1, rows), f32)],
        compiler_params=params(),
        name="grads",
    )(logit_scale, raw_dot, meta, stats, gathered)
    type_grad = lax.psum_scatter(type_part, "gz", scatter_dimension=0, tiled=True)
    mention_part = pl.pallas_call(
        mention_kernel,
        grid=(x_size,),
        in_specs=[smem, tile(types, rows), whole],
        out_specs=tile(rows, width),
        out_shape=jax.ShapeDtypeStruct((x_size, rows, width), bf16),
        compiler_params=params(),
        name="mention_part",
    )(logit_scale, grads, table)
    mention_grad = lax.all_to_all(mention_part, "gx", 0, 0, tiled=True)
    mention_grad = jnp.sum(mention_grad, axis=0, dtype=f32).astype(bf16)
    scale_parts = lax.all_to_all(
        jnp.broadcast_to(scale_part[None], (devices, 1, 128)), ("gz", "gx", "gy"), 0, 0, tiled=True
    )
    scale_grad = (jnp.sum(scale_parts[:, 0, 0]) / (rows * devices)).reshape(1)
    new_table, new_first, new_second = adam_rows(
        type_table, adam_m, adam_v, type_grad.astype(f32)
    )
    return (new_table, new_first, new_second, mention_grad, scale_grad)


def solution(mesh):
    gx, gy = mesh.devices.shape
    split = Mesh(mesh.devices.reshape(gx // X_SIZE, X_SIZE, gy), ("gz", "gx", "gy"))
    axes = ("gz", "gx", "gy")
    rows = P(axes, None)
    return jax.shard_map(
        per_device,
        mesh=split,
        in_specs=(rows, rows, rows, rows, P(), rows, P(axes), P(axes), P(axes)),
        out_specs=(rows, rows, rows, rows, P()),
        check_vma=False,
    )
```

time: 382 us -> 149 us (0.39)
  blocking collectives: 227 us -> 17.7 us
  waiting for transfers between devices: 96.5 us -> 59.2 us
  starting transfers between devices: 5.33 us -> 25.5 us
  matrix products: 17.8 us -> 0 us
  Pallas kernels: 0 us -> 12.7 us
  other arithmetic: 15.5 us -> 9.05 us
  local copies, waits for them, and re-layouts: 2.35 us -> 7.76 us
    psum x1 -> x0, blocking collectives: 227 us -> none  [per_device(): grand_total = lax.psum(scale_part, ('gx', 'gy'))]
    all_gather x1, waiting for transfers between devices: 96.5 us -> 13.9 us  [per_device(): table = lax.all_gather(type_table.astype(bf16), 'gz', axis=0, tiled=True)]
    all_to_all x1 -> x3, waiting for transfers between devices: 0.01 us -> 45.3 us  [the longest x1 19 us: per_device(): mention_grad = lax.all_to_all(mention_part, 'gx', 0, 0, tiled=True)]
    all_to_all x1 -> x3, starting transfers between devices: 5.29 us -> 25.4 us  [the longest x1 18.3 us: per_device(): lax.all_to_all(jnp.broadcast_to(scale_part[None], (devices, 1, 128)), ('g...]
    dot_general x3 -> x0, matrix products: 17.8 us -> none  [the longest x1 7.38 us: per_device(): jnp.einsum('gbn,nd->gbd', grad_bf, gathered, preferred_element_type=jnp.f...]
    all_to_all x0 -> x2, blocking collectives: none -> 17.7 us  [the longest x1 9.11 us: per_device(): meta = lax.all_to_all(meta, 'gx', 0, 0, tiled=True)]
    pallas_call x0 -> x3, Pallas kernels: none -> 12.7 us  [the longest x1 6.1 us: per_device(): pl.pallas_call(grads_kernel, grid=(x_size,), in_specs=[smem, tile(types,...]
    reduce_sum x3, other arithmetic: 9.33 us -> 2.98 us  [the longest x1 1.14 us: per_device(): scale_grad = (jnp.sum(scale_parts[:, 0, 0]) / (rows * devices)).reshape(1)]
  transfers between devices with their start and end apart: 2 -> 5, of which waited for: 1 -> 4; matrix products, arithmetic and copies ran while one was open for 5% -> 6% of each run, Pallas kernels for 0% -> 2%
where the time goes in v1:
time: 149 us; the launch traced here: 148 us
  waiting for transfers between devices  59.2 us (40%)
  starting transfers between devices  25.5 us (17%)
  blocking collectives  17.7 us (12%)
  between operations  16.6 us (11%)
  Pallas kernels  12.7 us (9%)
  other arithmetic  9.05 us (6%)
  local copies, waits for them, and re-layouts  7.76 us (5%)
    all_to_all x1, waiting for transfers between devices, per_device(): mention_grad = lax.all_to_all(mention_part, 'gx', 0, 0, tiled=True)  19 us
    all_to_all x1, starting transfers between devices, per_device(): lax.all_to_all(jnp.broadcast_to(scale_part[None], (devices, 1, 128)), ('g...  18.3 us
    all_to_all x1, waiting for transfers between devices, per_device(): lax.all_to_all(jnp.broadcast_to(mentions[None], (x_size, rows, width)), '...  13.9 us
    all_gather x1, waiting for transfers between devices, per_device(): table = lax.all_gather(type_table.astype(bf16), 'gz', axis=0, tiled=True)  13.9 us
    all_to_all x1, waiting for transfers between devices, per_device(): lax.all_to_all(jnp.broadcast_to(scale_part[None], (devices, 1, 128)), ('g...  12.3 us
    all_to_all x1, blocking collectives, per_device(): meta = lax.all_to_all(meta, 'gx', 0, 0, tiled=True)  9.11 us
    all_to_all x1, blocking collectives, per_device(): stats = lax.all_to_all(stats, 'gx', 0, 0, tiled=True)  8.6 us
    pallas_call x1, Pallas kernels, per_device(): pl.pallas_call(grads_kernel, grid=(x_size,), in_specs=[smem, tile(types,...  6.1 us
  transfers between devices with their start and end apart: 5, of which 4 were waited for; matrix products, arithmetic and copies ran while one was open for 6% of the time, Pallas kernels for 2%

profile of v1, /device:TPU:1, one launch (start us, length us, event | category | flops | bytes accessed | tf_op | source)
XLA Modules:
  0.0 148.5 jit_solution(12896663711421079100)
XLA Ops:
  7.2 1.7 %convert_element_type.27 = bf16[128,768]{1,0:T(8,128)(2,1)} convert(f32[128,768]{1,0:T(8,128)} %param.10) | non-fusion elementwise | flops 98304 | bytes 589824 | tf_op jit(solution)/shard_map/convert_element_type | solution.py:127
  8.9 0.7 iota_compare_fusion.2
  9.7 0.7 and_select_fusion.2
  10.3 0.1 fusion.3
  10.5 0.1 reshape.160
  10.5 0.1 copy.17
  10.6 0.1 pad.2.clone
  10.7 0.8 select_reduce_fusion
  11.5 0.7 and_select_fusion.1
  12.2 0.1 broadcast_bitcast_fusion
  12.2 0.1 maximum_maximum_fusion
  12.3 9.1 %all_to_all.25.meta_ref = f32[4,16,256]{2,1,0:T(8,128)S(1)} all-to-all(f32[4,16,256]{2,1,0:T(8,128)S(1)} %maximum_maximum_fusion), channel_id=1, replica_groups=mesh['gz'=8,'gx'=4,'gy'=16] {'gx'}, dimensions={0} | all-to-all | bytes 131072 | tf_op jit(solution)/shard_map/all_to_all | solution.py:154
  21.4 2.2 %broadcast_in_dim.34 = bf16[4,256,768]{2,1,0:T(8,128)(2,1)} broadcast(bf16[256,768]{1,0:T(8,128)(2,1)} %param.9), dimensions={1,2} | broadcast | bytes 1966080 | tf_op jit(solution)/shard_map/broadcast_in_dim | solution.py:129
  23.7 3.6 %all-to-all-start = ((bf16[4,256,768]{2,1,0:T(8,128)(2,1)}), bf16[4,256,768]{2,1,0:T(8,128)(2,1)S(1)}, u32[]{:S(2)}, u32[]{:S(2)}) async-start(bf16[4,256,768]{2,1,0:T(8,128)(2,1)} %broadcast_in_dim.34), calls=%async_computation | async-start | bytes 3145728 | tf_op jit(solution)/shard_map/all_to_all | solution.py:128
  27.2 0.0 reduce-scatter.2.cloned.1.call-start
  27.9 13.9 %all-to-all-done.m_ref = bf16[4,256,768]{2,1,0:T(8,128)(2,1)S(1)} async-done(((bf16[4,256,768]{2,1,0:T(8,128)(2,1)}), bf16[4,256,768]{2,1,0:T(8,128)(2,1)S(1)}, u32[]{:S(2)}, u32[]{:S(2)}) %all-to-all-start) | async-done | bytes 1572896 | tf_op jit(solution)/shard_map/all_to_all | solution.py:128
  41.9 13.9 %all-gather.2.cloned.1.call-done.t_ref = bf16[1024,768]{1,0:T(8,128)(2,1)} async-done(((bf16[128,768]{1,0:T(8,128)(2,1)}), bf16[1024,768]{1,0:T(8,128)(2,1)}) %all-gather.2.cloned.1.call-update) | async-done | bytes 1572880 | tf_op jit(solution)/shard_map/all_gather | solution.py:127
  55.7 1.4 copy-done
  57.1 3.2 %scores.1 = (f32[4,1024,256]{2,1,0:T(8,128)S(1)}, f32[4,8,1024]{2,1,0:T(8,128)S(1)}) custom-call(f32[1]{0:T(128)S(6)} %copy.20.factor_ref, bf16[4,256,768]{2,1,0:T(8,128)(2,1)S(1)} %all-to-all-done.m_ref, bf16[1024,768]{1,0:T(8,128)(2,1)S(1)} %copy-done, f32[4,16,256]{2,1,0:T(8,128)S(1)} %all_to_all.25.meta_ref), custom_call_target="tpu_custom_call" | custom-call | tf_op jit(solution)/shard_map/scores/pallas_call | solution.py:158
  60.3 8.6 %all_to_all.26.stat_ref = f32[4,8,1024]{2,1,0:T(8,128)S(1)} all-to-all(f32[4,8,1024]{2,1,0:T(8,128)S(1)} %get-tuple-element.11), channel_id=1, replica_groups=mesh['gz'=8,'gx'=4,'gy'=16] {'gx'}, dimensions={0} | all-to-all | bytes 262144 | tf_op jit(solution)/shard_map/all_to_all | solution.py:173
  68.9 6.1 %grads.1 = (bf16[4,1024,256]{2,1,0:T(8,128)(2,1)S(1)}, bf16[1024,768]{1,0:T(8,128)(2,1)}, f32[1,128]{1,0:T(1,128)S(1)}) custom-call(f32[1]{0:T(128)S(6)} %copy.20.factor_ref, f32[4,1024,256]{2,1,0:T(8,128)S(1)} %get-tuple-element.10.raw_ref, f32[4,16,256]{2,1,0:T(8,128)S(1)} %all_to_all.25.meta_ref, f32[4,8,1024]{2,1,0:T(8,128)S(1)} %all_to_all.26.stat_ref, ...), custom_call_target="tpu_custom_call" | custom-call | tf_op jit(solution)/shard_map/grads/pallas_call | solution.py:174
  75.1 1.3 copy-done.2
  76.4 0.8 broadcast_in_dim.61
  77.3 18.3 %all-to-all-start.4 = ((f32[512,1,128]{2,1,0:T(1,128)}), f32[512,1,128]{2,1,0:T(1,128)S(1)}, u32[]{:S(2)}, u32[]{:S(2)}) async-start(f32[512,1,128]{2,1,0:T(1,128)} %broadcast_in_dim.61), calls=%async_computation.5 | async-start | bytes 524288 | tf_op jit(solution)/shard_map/all_to_all | solution.py:210
  95.6 1.6 %copy-done.3 = bf16[4,1024,256]{2,1,0:T(8,128)(2,1)S(1)} copy-done((bf16[4,1024,256]{2,1,0:T(8,128)(2,1)S(1)}, bf16[4,1024,256]{2,1,0:T(8,128)(2,1)}, u32[]{:S(2)}) %copy-start.3) | copy-done | bytes 2097176
  97.2 3.4 %mention_part.1 = bf16[4,256,768]{2,1,0:T(8,128)(2,1)} custom-call(f32[1]{0:T(128)S(6)} %copy.20.factor_ref, bf16[4,1024,256]{2,1,0:T(8,128)(2,1)S(1)} %copy-done.3, bf16[1024,768]{1,0:T(8,128)(2,1)S(1)} %copy-done.1), custom_call_target="tpu_custom_call" | custom-call | tf_op jit(solution)/shard_map/mention_part/pallas_call | solution.py:199
  100.6 12.3 %all-to-all-done.4 = f32[512,1,128]{2,1,0:T(1,128)S(1)} async-done(((f32[512,1,128]{2,1,0:T(1,128)}), f32[512,1,128]{2,1,0:T(1,128)S(1)}, u32[]{:S(2)}, u32[]{:S(2)}) %all-to-all-start.4) | async-done | bytes 262176 | tf_op jit(solution)/shard_map/all_to_all | solution.py:210
  112.9 3.6 %all-to-all-start.3 = ((bf16[4,256,768]{2,1,0:T(8,128)(2,1)}), bf16[4,256,768]{2,1,0:T(8,128)(2,1)S(1)}, u32[]{:S(2)}, u32[]{:S(2)}) async-start(bf16[4,256,768]{2,1,0:T(8,128)(2,1)} %mention_part.1), calls=%async_computation.4 | async-start | bytes 3145728 | tf_op jit(solution)/shard_map/all_to_all | solution.py:208
  116.5 1.1 slice_reduce_fusion
  118.3 19.0 %all-to-all-done.3 = bf16[4,256,768]{2,1,0:T(8,128)(2,1)S(1)} async-done(((bf16[4,256,768]{2,1,0:T(8,128)(2,1)}), bf16[4,256,768]{2,1,0:T(8,128)(2,1)S(1)}, u32[]{:S(2)}, u32[]{:S(2)}) %all-to-all-start.3) | async-done | bytes 1572896 | tf_op jit(solution)/shard_map/all_to_all | solution.py:208
  137.3 1.1 reduce_sum.31
  138.4 2.1 %divide_subtract_fusion = (f32[128,768]{1,0:T(8,128)}, f32[128,768]{1,0:T(8,128)}, f32[128,768]{1,0:T(8,128)}) fusion(f32[128,768]{1,0:T(8,128)S(1)} %copy-done.4, bf16[128,768]{1,0:T(8,128)(2,1)} %reduce-scatter.2.cloned.1.call-done, f32[128,768]{1,0:T(8,128)S(1)} %copy-done.5, f32[128,768]{1,0:T(8,128)S(1)} %copy-done.6), kind=kLoop, calls=%fused_computation.4 | loop fusion | flops 1277952 | bytes 2555904 | tf_op jit(solution)/shard_map/sub | solution.py:26
  (18 shorter events, 0.1 us)
Async XLA Ops:
  7.2 48.6 %all-gather.2.cloned.1.call-start = ((), (), s32[]{:S(2)}) async-start(), calls=%async_computation.6 | async-start | bytes 1769472 | tf_op jit(solution)/shard_map/all_gather | solution.py:127
  23.7 18.2 %all-to-all-start = ((bf16[4,256,768]{2,1,0:T(8,128)(2,1)}), bf16[4,256,768]{2,1,0:T(8,128)(2,1)S(1)}, u32[]{:S(2)}, u32[]{:S(2)}) async-start(bf16[4,256,768]{2,1,0:T(8,128)(2,1)} %broadcast_in_dim.34), calls=%async_computation | async-start | bytes 3145728 | tf_op jit(solution)/shard_map/all_to_all | solution.py:128
  27.2 111.2 %reduce-scatter.2.cloned.1.call-start = ((), (), s32[]{:S(2)}) async-start(), calls=%async_computation.7 | async-start | bytes 1769472 | tf_op jit(solution)/shard_map/reduce_scatter | solution.py:198
  55.7 1.4 copy-start
  75.0 1.3 copy-start.2
  76.4 19.2 %copy-start.1 = (bf16[1024,768]{1,0:T(8,128)(2,1)S(1)}, bf16[1024,768]{1,0:T(8,128)(2,1)}, u32[]{:S(2)}) copy-start(bf16[1024,768]{1,0:T(8,128)(2,1)} %all-gather.2.cloned.1.call-done.t_ref) | copy-start | bytes 4718596
  77.3 35.6 %all-to-all-start.4 = ((f32[512,1,128]{2,1,0:T(1,128)}), f32[512,1,128]{2,1,0:T(1,128)S(1)}, u32[]{:S(2)}, u32[]{:S(2)}) async-start(f32[512,1,128]{2,1,0:T(1,128)} %broadcast_in_dim.61), calls=%async_computation.5 | async-start | bytes 524288 | tf_op jit(solution)/shard_map/all_to_all | solution.py:210
  95.6 1.6 %copy-start.3 = (bf16[4,1024,256]{2,1,0:T(8,128)(2,1)S(1)}, bf16[4,1024,256]{2,1,0:T(8,128)(2,1)}, u32[]{:S(2)}) copy-start(bf16[4,1024,256]{2,1,0:T(8,128)(2,1)} %copy-done.2) | copy-start | bytes 6291460
  112.9 24.4 %all-to-all-start.3 = ((bf16[4,256,768]{2,1,0:T(8,128)(2,1)}), bf16[4,256,768]{2,1,0:T(8,128)(2,1)S(1)}, u32[]{:S(2)}, u32[]{:S(2)}) async-start(bf16[4,256,768]{2,1,0:T(8,128)(2,1)} %mention_part.1), calls=%async_computation.4 | async-start | bytes 3145728 | tf_op jit(solution)/shard_map/all_to_all | solution.py:208
  116.5 21.9 %copy-start.4 = (f32[128,768]{1,0:T(8,128)S(1)}, f32[128,768]{1,0:T(8,128)}, u32[]{:S(2)}) copy-start(f32[128,768]{1,0:T(8,128)} %param.10) | copy-start | bytes 1179652
  116.5 21.9 %copy-start.5 = (f32[128,768]{1,0:T(8,128)S(1)}, f32[128,768]{1,0:T(8,128)}, u32[]{:S(2)}) copy-start(f32[128,768]{1,0:T(8,128)} %param.11) | copy-start | bytes 1179652
  116.5 21.9 %copy-start.6 = (f32[128,768]{1,0:T(8,128)S(1)}, f32[128,768]{1,0:T(8,128)}, u32[]{:S(2)}) copy-start(f32[128,768]{1,0:T(8,128)} %param.12) | copy-start | bytes 1179652
Sparse Core Ops, SparseCore 0:
  10.7 45.0 all-gather.1
  76.5 45.2 reduce-scatter.1

commit v2 on v1

v2 whole, which is shorter than its diff:
```python
import jax
import jax.numpy as jnp
from jax import lax
from jax.experimental import pallas as pl
from jax.experimental.pallas import tpu as pltpu
from jax.sharding import Mesh, PartitionSpec as P

beta_one = 0.9
beta_two = 0.999
learn_rate = 0.02
adam_eps = 1e-08
first_fix = 0.9999734386011124
second_fix = 0.09520785288629038

X_SIZE = 4
Z_SIZE = 8
BLOCK = 128
LOW = -1e30
META_ROWS = 16
SLOTS = 16
STAT_ROWS = 8
OFFSETS = (0, -1, 1, -2, 2, -3, 3, 4)
f32 = jnp.float32
bf16 = jnp.bfloat16


def pack_kernel(cols, list_ref, len_ref, slot_ref, row_ref, m_ref, out_ref):
    rows, width = m_ref.shape
    out_ref[0, 0:rows, :] = m_ref[...]
    first = lax.broadcasted_iota(jnp.int32, (1, rows), 1) < BLOCK
    slot = slot_ref[...]
    gold = jnp.zeros((1, rows), f32)
    parts = []
    for k in range(SLOTS):
        ids = [
            jnp.where(k < len_ref[g], lax.div(list_ref[g, k], cols), -1).astype(f32)
            for g in range(2)
        ]
        part = jnp.where(first, ids[0], ids[1])
        gold = gold + jnp.where(slot == k, part, 0.0)
        parts.append(part)
    parts += [gold, row_ref[...].astype(f32)]
    per_row = width // rows
    lines = [
        jnp.concatenate(parts[i : i + per_row], axis=1) for i in range(0, len(parts), per_row)
    ]
    lines.append(jnp.zeros((META_ROWS - len(lines), width), f32))
    out_ref[0, rows : rows + META_ROWS, :] = jnp.concatenate(lines, axis=0).astype(bf16)


def read_meta(m_ref, rows):
    meta = m_ref[0, rows : rows + META_ROWS, :].astype(f32)
    per_row = meta.shape[1] // rows
    parts = [
        meta[i // per_row : i // per_row + 1, (i % per_row) * rows : (i % per_row + 1) * rows]
        for i in range(SLOTS + 2)
    ]
    owners = jnp.concatenate(parts[:SLOTS], axis=0)
    return owners, parts[SLOTS], parts[SLOTS + 1].astype(jnp.int32)


def owner_of(place_ref, offset):
    line = lax.rem(place_ref[0] + (offset + Z_SIZE), Z_SIZE)
    return line, (line * X_SIZE + place_ref[1]).astype(f32)


def listed_in(owners, owner):
    return jnp.max(jnp.where(owners == owner, 1.0, 0.0), axis=0, keepdims=True) > 0.0


def gather_tile(t_refs, tile_ref):
    at = 0
    for ref in t_refs:
        n = ref.shape[0]
        tile_ref[at : at + n, :] = ref[...]
        at += n


def scores_kernel(factor_ref, place_ref, m_ref, *refs):
    t_refs, (raw_ref, stat_ref, tile_ref) = refs[:-3], refs[-3:]
    step = pl.program_id(0)
    factor = factor_ref[0]
    rows = m_ref.shape[1] - META_ROWS
    pl.when(step == 0)(lambda: gather_tile(t_refs, tile_ref))
    raw_ref[0] = lax.dot_general(
        tile_ref[...], m_ref[0, 0:rows, :], (((1,), (1,)), ((), ())), preferred_element_type=f32
    )
    owners, gold_owner, gold_row = read_meta(m_ref, rows)
    ids = lax.broadcasted_iota(jnp.int32, (BLOCK, rows), 0)
    top = jnp.full((1, rows), LOW, f32)
    gold_raw = jnp.zeros((1, rows), f32)
    lives = []
    for c, offset in enumerate(OFFSETS):
        _, owner = owner_of(place_ref, offset)
        lives.append(listed_in(owners, owner))
        raw = raw_ref[0, c * BLOCK : (c + 1) * BLOCK, :]
        part = jnp.max(factor * raw, axis=0, keepdims=True)
        top = jnp.maximum(top, jnp.where(lives[c], part, LOW))
        gold = jnp.where(gold_owner == owner, gold_row, -1)
        gold_raw = gold_raw + jnp.sum(jnp.where(ids == gold, raw, 0.0), axis=0, keepdims=True)
    total = jnp.zeros((1, rows), f32)
    mass = jnp.zeros((1, rows), f32)
    for c in range(len(OFFSETS)):
        raw = raw_ref[0, c * BLOCK : (c + 1) * BLOCK, :]
        weights = jnp.where(lives[c], jnp.exp(factor * raw - top), 0.0)
        total = total + jnp.sum(weights, axis=0, keepdims=True)
        mass = mass + jnp.sum(weights * raw, axis=0, keepdims=True)
    stat = jnp.concatenate(
        [top, total, mass, gold_raw, jnp.zeros((STAT_ROWS - 4, rows), f32)], axis=0
    )
    for d in range(stat_ref.shape[0]):
        stat_ref[d, :, pl.ds(pl.multiple_of(step * rows, BLOCK), rows)] = stat


def grads_kernel(
    factor_ref, place_ref, raw_ref, stat_ref, m_ref, g_ref, type_ref, scale_ref, acc_ref, sum_ref
):
    step = pl.program_id(0)
    factor = factor_ref[0]
    rows = m_ref.shape[1] - META_ROWS
    tops = stat_ref[:, 0, :]
    top = jnp.max(tops, axis=0, keepdims=True)
    share = jnp.exp(tops - top)
    total = jnp.sum(stat_ref[:, 1, :] * share, axis=0, keepdims=True)
    log_total = top + jnp.log(total)
    mass = jnp.sum(stat_ref[:, 2, :] * share, axis=0, keepdims=True)
    scale = mass / total - jnp.sum(stat_ref[:, 3, :], axis=0, keepdims=True)
    owners, gold_owner, gold_row = read_meta(m_ref, rows)
    ids = lax.broadcasted_iota(jnp.int32, (BLOCK, rows), 0)
    for c, offset in enumerate(OFFSETS):
        _, owner = owner_of(place_ref, offset)
        live = listed_in(owners, owner)
        raw = raw_ref[0, c * BLOCK : (c + 1) * BLOCK, :]
        weights = jnp.where(live, jnp.exp(factor * raw - log_total), 0.0)
        gold = jnp.where(gold_owner == owner, gold_row, -1)
        grad = weights - jnp.where(ids == gold, 1.0, 0.0)
        g_ref[0, c * BLOCK : (c + 1) * BLOCK, :] = grad.astype(bf16)
    part = jnp.dot(g_ref[0], m_ref[0, 0:rows, :], preferred_element_type=f32)

    @pl.when(step == 0)
    def _():
        acc_ref[...] = part
        sum_ref[...] = scale

    @pl.when(step > 0)
    def _():
        acc_ref[...] += part
        sum_ref[...] += scale

    @pl.when(step == pl.num_programs(0) - 1)
    def _():
        for c, offset in enumerate(OFFSETS):
            line, _ = owner_of(place_ref, offset)
            type_ref[line] = (factor * acc_ref[c * BLOCK : (c + 1) * BLOCK, :]).astype(bf16)
        scale_ref[...] = jnp.broadcast_to(
            jnp.sum(sum_ref[...], axis=1, keepdims=True), scale_ref.shape
        )


def mention_kernel(factor_ref, scale_ref, g_ref, *refs):
    t_refs, (out_ref, scale_out_ref, tile_ref) = refs[:-3], refs[-3:]

    @pl.when(pl.program_id(0) == 0)
    def _():
        gather_tile(t_refs, tile_ref)
        scale_out_ref[...] = scale_ref[...]

    part = lax.dot_general(
        g_ref[0], tile_ref[...], (((0,), (0,)), ((), ())), preferred_element_type=f32
    )
    out_ref[0] = (factor_ref[0] * part).astype(bf16)


def adam_kernel(part_ref, table_ref, m_ref, v_ref, table_out, m_out, v_out):
    grad = part_ref[0].astype(f32)
    for z in range(1, part_ref.shape[0]):
        grad = grad + part_ref[z].astype(f32)
    moment_one = beta_one * m_ref[...] + (1.0 - beta_one) * grad
    moment_two = beta_two * v_ref[...] + (1.0 - beta_two) * grad * grad
    table_out[...] = table_ref[...] - learn_rate * (moment_one / first_fix) / (
        jnp.sqrt(moment_two / second_fix) + adam_eps
    )
    m_out[...] = moment_one
    v_out[...] = moment_two


def params():
    return pltpu.CompilerParams(
        dimension_semantics=("arbitrary",), vmem_limit_bytes=40 * 1024 * 1024
    )


def shifted(array, axis, size, by):
    return lax.ppermute(array, axis, [(i, (i + by) % size) for i in range(size)])


def ring_gather(block):
    half = block.shape[0] // 2
    ups, downs = [block], [block]
    for _ in range(3):
        ups.append(shifted(ups[-1], "gz", Z_SIZE, 1))
        downs.append(shifted(downs[-1], "gz", Z_SIZE, -1))
    far = [
        shifted(ups[-1][:half], "gz", Z_SIZE, 1),
        shifted(downs[-1][half:], "gz", Z_SIZE, -1),
    ]
    return [block, ups[1], downs[1], ups[2], downs[2], ups[3], downs[3]] + far


def doubled(value, axis, size):
    by = 1
    while by < size:
        value = value + lax.ppermute(value, axis, [(i, i ^ by) for i in range(size)])
        by *= 2
    return value


def per_device(
    mentions,
    type_table,
    adam_m,
    adam_v,
    logit_scale,
    block_lists,
    list_lengths,
    gold_slot,
    gold_row,
):
    cols = lax.axis_size("gy")
    devices = Z_SIZE * X_SIZE * cols
    block_rows, width = type_table.shape
    rows = mentions.shape[0]
    sent_rows = rows + META_ROWS
    types = Z_SIZE * block_rows
    smem = pl.BlockSpec(memory_space=pltpu.SMEM)
    place = jnp.stack([lax.axis_index("gz"), lax.axis_index("gx")]).astype(jnp.int32)

    def tile(*shape):
        return pl.BlockSpec((1,) + shape, lambda j: (j, 0, 0))

    def whole(*shape):
        return pl.BlockSpec(shape, lambda j: (0,) * len(shape))

    blocks = ring_gather(type_table.astype(bf16))
    block_specs = [whole(b.shape[0], width) for b in blocks]
    packed = pl.pallas_call(
        lambda *refs: pack_kernel(cols, *refs),
        grid=(X_SIZE,),
        in_specs=[smem, smem, whole(1, rows), whole(1, rows), whole(rows, width)],
        out_specs=tile(sent_rows, width),
        out_shape=jax.ShapeDtypeStruct((X_SIZE, sent_rows, width), bf16),
        compiler_params=params(),
        name="pack",
    )(block_lists, list_lengths, gold_slot.reshape(1, rows), gold_row.reshape(1, rows), mentions)
    gathered = lax.all_to_all(packed, "gx", 0, 0, tiled=True)

    raw_dot, stats = pl.pallas_call(
        scores_kernel,
        grid=(X_SIZE,),
        in_specs=[smem, smem, tile(sent_rows, width)] + block_specs,
        out_specs=[tile(types, rows), whole(X_SIZE, STAT_ROWS, X_SIZE * rows)],
        out_shape=[
            jax.ShapeDtypeStruct((X_SIZE, types, rows), f32),
            jax.ShapeDtypeStruct((X_SIZE, STAT_ROWS, X_SIZE * rows), f32),
        ],
        scratch_shapes=[pltpu.VMEM((types, width), bf16)],
        compiler_params=params(),
        name="scores",
    )(logit_scale, place, gathered, *blocks)
    stats = lax.all_to_all(stats, "gx", 0, 0, tiled=True)
    grads, type_part, scale_part = pl.pallas_call(
        grads_kernel,
        grid=(X_SIZE,),
        in_specs=[
            smem,
            smem,
            tile(types, rows),
            pl.BlockSpec((X_SIZE, STAT_ROWS, rows), lambda j: (0, 0, j)),
            tile(sent_rows, width),
        ],
        out_specs=[tile(types, rows), whole(Z_SIZE, block_rows, width), whole(1, 128)],
        out_shape=[
            jax.ShapeDtypeStruct((X_SIZE, types, rows), bf16),
            jax.ShapeDtypeStruct((Z_SIZE, block_rows, width), bf16),
            jax.ShapeDtypeStruct((1, 128), f32),
        ],
        scratch_shapes=[pltpu.VMEM((types, width), f32), pltpu.VMEM((1, rows), f32)],
        compiler_params=params(),
        name="grads",
    )(logit_scale, place, raw_dot, stats, gathered)
    type_parts = lax.all_to_all(type_part, "gz", 0, 0, tiled=True)
    mention_part, scale_part = pl.pallas_call(
        mention_kernel,
        grid=(X_SIZE,),
        in_specs=[smem, whole(1, 128), tile(types, rows)] + block_specs,
        out_specs=[tile(rows, width), whole(1, 128)],
        out_shape=[
            jax.ShapeDtypeStruct((X_SIZE, rows, width), bf16),
            jax.ShapeDtypeStruct((1, 128), f32),
        ],
        scratch_shapes=[pltpu.VMEM((types, width), bf16)],
        compiler_params=params(),
        name="mention_part",
    )(logit_scale, scale_part, grads, *blocks)
    mention_grad = lax.psum_scatter(
        mention_part.reshape(X_SIZE * rows, width), "gx", scatter_dimension=0, tiled=True
    )
    scale_sum = doubled(doubled(scale_part, "gz", Z_SIZE), "gy", cols)
    scale_grad = (scale_sum[0, 0] / (rows * devices)).reshape(1)
    slab = block_rows // 4
    row_tile = pl.BlockSpec((slab, width), lambda j: (j, 0))
    new_table, new_first, new_second = pl.pallas_call(
        adam_kernel,
        grid=(block_rows // slab,),
        in_specs=[pl.BlockSpec((Z_SIZE, slab, width), lambda j: (0, j, 0))] + [row_tile] * 3,
        out_specs=[row_tile] * 3,
        out_shape=[jax.ShapeDtypeStruct((block_rows, width), f32)] * 3,
        compiler_params=params(),
        name="adam",
    )(type_parts, type_table, adam_m, adam_v)
    return (new_table, new_first, new_second, mention_grad, scale_grad)


def solution(mesh):
    gx, gy = mesh.devices.shape
    split = Mesh(mesh.devices.reshape(gx // X_SIZE, X_SIZE, gy), ("gz", "gx", "gy"))
    axes = ("gz", "gx", "gy")
    rows = P(axes, None)
    return jax.shard_map(
        per_device,
        mesh=split,
        in_specs=(rows, rows, rows, rows, P(), rows, P(axes), P(axes), P(axes)),
        out_specs=(rows, rows, rows, rows, P()),
        check_vma=False,
    )
```

time: 149 us -> 174 us (1.17); the launches traced: 148 us -> 171 us
  starting transfers between devices: 25.5 us -> 83.9 us
  waiting for transfers between devices: 59.2 us -> 38.3 us
  blocking collectives: 17.7 us -> 8.41 us
  other arithmetic: 9.05 us -> 0.12 us
  Pallas kernels: 12.7 us -> 18.7 us
  local copies, waits for them, and re-layouts: 7.76 us -> 5.25 us
    ppermute x0 -> x15, starting transfers between devices: none -> 75.2 us  [the longest x7 41.2 us: doubled(): lax.ppermute(value, axis, [(i, i ^ by) for i in range(size)])]
    all_to_all x3 -> x2, waiting for transfers between devices: 45.3 us -> 0.01 us  [the longest x1 0.01 us: per_device(): gathered = lax.all_to_all(packed, 'gx', 0, 0, tiled=True)]
    ppermute x0 -> x15, waiting for transfers between devices: none -> 38.3 us  [the longest x7 31.8 us: doubled(): lax.ppermute(value, axis, [(i, i ^ by) for i in range(size)])]
    all_to_all x3 -> x2, starting transfers between devices: 25.4 us -> 8.7 us  [the longest x1 4.97 us: per_device(): gathered = lax.all_to_all(packed, 'gx', 0, 0, tiled=True)]
    all_gather x1 -> x0, waiting for transfers between devices: 13.9 us -> none  [per_device(): table = lax.all_gather(type_table.astype(bf16), 'gz', axis=0, tiled=True)]
    all_to_all x1 -> x0, blocking collectives: 9.11 us -> none  [per_device(): meta = lax.all_to_all(meta, 'gx', 0, 0, tiled=True)]
    pallas_call x3 -> x5, Pallas kernels: 12.7 us -> 18.7 us  [the longest x1 6.38 us: per_device(): pl.pallas_call(grads_kernel, grid=(X_SIZE,), in_specs=[smem, smem, tile(t...]
    broadcast_in_dim x3 -> x0, local copies, waits for them, and re-layouts: 3.09 us -> none  [the longest x1 2.25 us: per_device(): jnp.broadcast_to(mentions[None], (x_size, rows, width))]
  transfers between devices with their start and end apart: 5 -> 18, of which waited for: 4 -> 10; matrix products, arithmetic and copies ran while one was open for 6% -> 0% of each run, Pallas kernels for 2% -> 1%
where the time goes in v2:
time: 174 us; the launch traced here: 171 us
  starting transfers between devices  83.9 us (48%)
  waiting for transfers between devices  38.3 us (22%)
  Pallas kernels  18.7 us (11%)
  between operations  16.1 us (9%)
  blocking collectives  8.41 us (5%)
  local copies, waits for them, and re-layouts  5.25 us (3%)
    ppermute x7, starting transfers between devices, doubled(): lax.ppermute(value, axis, [(i, i ^ by) for i in range(size)])  41.2 us
    ppermute x8, starting transfers between devices, shifted(): lax.ppermute(array, axis, [(i, (i + by) % size) for i in range(size)])  34 us
    ppermute x7, waiting for transfers between devices, doubled(): lax.ppermute(value, axis, [(i, i ^ by) for i in range(size)])  31.8 us
    all_to_all x1, blocking collectives, per_device(): stats = lax.all_to_all(stats, 'gx', 0, 0, tiled=True)  8.41 us
    ppermute x8, waiting for transfers between devices, shifted(): lax.ppermute(array, axis, [(i, (i + by) % size) for i in range(size)])  6.53 us
    pallas_call x1, Pallas kernels, per_device(): pl.pallas_call(grads_kernel, grid=(X_SIZE,), in_specs=[smem, smem, tile(t...  6.38 us
    unnamed x20, local copies, waits for them, and re-layouts  5.23 us
    all_to_all x1, starting transfers between devices, per_device(): gathered = lax.all_to_all(packed, 'gx', 0, 0, tiled=True)  4.97 us
  transfers between devices with their start and end apart: 18, of which 10 were waited for; matrix products, arithmetic and copies ran while one was open for 0% of the time, Pallas kernels for 1%

profile of v2, /device:TPU:1, one launch (start us, length us, event | category | flops | bytes accessed | tf_op | source)
XLA Modules:
  0.0 170.8 jit_solution(6372348947633091912)
XLA Ops:
  7.2 1.0 copy-done.1
  10.9 2.4 %pack.1 = bf16[4,272,768]{2,1,0:T(8,128)(2,1)} custom-call(s32[2,16]{1,0:T(2,128)S(1)} %copy-done.6, s32[2]{0:T(128)S(1)} %copy-done.9, s32[1,256]{1,0:T(1,128)S(1)} %bitcast.7, s32[1,256]{1,0:T(1,128)S(1)} %bitcast.8, bf16[256,768]{1,0:T(8,128)(2,1)S(1)} %copy-done.1), custom_call_target="tpu_custom_call" | custom-call | tf_op jit(solution)/shard_map/pack/pallas_call | solution.py:246
  13.3 5.0 %all-to-all-start = ((bf16[4,272,768]{2,1,0:T(8,128)(2,1)}), bf16[4,272,768]{2,1,0:T(8,128)(2,1)S(1)}, u32[]{:S(2)}, u32[]{:S(2)}) async-start(bf16[4,272,768]{2,1,0:T(8,128)(2,1)} %pack.1), calls=%async_computation | async-start | bytes 3342336 | tf_op jit(solution)/shard_map/all_to_all | solution.py:255
  18.3 10.7 %collective-permute-start.1 = (bf16[128,768]{1,0:T(8,128)(2,1)S(1)}, bf16[128,768]{1,0:T(8,128)(2,1)S(1)}, u32[]{:S(2)}, u32[]{:S(2)}) collective-permute-start(bf16[128,768]{1,0:T(8,128)(2,1)S(1)} %convert_element_type.3.refs_0_), channel_id=1, source_target_pairs={{0,448},{64,0},{128,64},{192,128},{256,192},{320,256},{384,320},{4... | collective-permute-start | bytes 589832 | tf_op jit(solution)/shard_map/ppermute | solution.py:194
  29.0 1.9 %collective-permute-start = (bf16[128,768]{1,0:T(8,128)(2,1)S(1)}, bf16[128,768]{1,0:T(8,128)(2,1)S(1)}, u32[]{:S(2)}, u32[]{:S(2)}) collective-permute-start(bf16[128,768]{1,0:T(8,128)(2,1)S(1)} %convert_element_type.3.refs_0_), channel_id=1, source_target_pairs={{0,64},{64,128},{128,192},{192,256},{256,320},{320,384},{384,448},... | collective-permute-start | bytes 589832 | tf_op jit(solution)/shard_map/ppermute | solution.py:194
  30.9 1.3 collective-permute-done.1.refs_2_
  32.2 5.3 %collective-permute-start.3 = (bf16[128,768]{1,0:T(8,128)(2,1)S(1)}, bf16[128,768]{1,0:T(8,128)(2,1)S(1)}, u32[]{:S(2)}, u32[]{:S(2)}) collective-permute-start(bf16[128,768]{1,0:T(8,128)(2,1)S(1)} %collective-permute-done.1.refs_2_), channel_id=1, source_target_pairs={{0,448},{64,0},{128,64},{192,128},{256,192},{320,256},{384,320},{4... | collective-permute-start | bytes 589832 | tf_op jit(solution)/shard_map/ppermute | solution.py:194
  37.5 1.9 %collective-permute-start.2 = (bf16[128,768]{1,0:T(8,128)(2,1)S(1)}, bf16[128,768]{1,0:T(8,128)(2,1)S(1)}, u32[]{:S(2)}, u32[]{:S(2)}) collective-permute-start(bf16[128,768]{1,0:T(8,128)(2,1)S(1)} %collective-permute-done.refs_1_), channel_id=1, source_target_pairs={{0,64},{64,128},{128,192},{192,256},{256,320},{320,384},{384,448},... | collective-permute-start | bytes 589832 | tf_op jit(solution)/shard_map/ppermute | solution.py:194
  40.1 5.3 %collective-permute-start.5 = (bf16[128,768]{1,0:T(8,128)(2,1)S(1)}, bf16[128,768]{1,0:T(8,128)(2,1)S(1)}, u32[]{:S(2)}, u32[]{:S(2)}) collective-permute-start(bf16[128,768]{1,0:T(8,128)(2,1)S(1)} %collective-permute-done.3.refs_4_), channel_id=1, source_target_pairs={{0,448},{64,0},{128,64},{192,128},{256,192},{320,256},{384,320},{4... | collective-permute-start | bytes 589832 | tf_op jit(solution)/shard_map/ppermute | solution.py:194
  45.4 1.9 %collective-permute-start.4 = (bf16[128,768]{1,0:T(8,128)(2,1)S(1)}, bf16[128,768]{1,0:T(8,128)(2,1)S(1)}, u32[]{:S(2)}, u32[]{:S(2)}) collective-permute-start(bf16[128,768]{1,0:T(8,128)(2,1)S(1)} %collective-permute-done.2.refs_3_), channel_id=1, source_target_pairs={{0,64},{64,128},{128,192},{192,256},{256,320},{320,384},{384,448},... | collective-permute-start | bytes 589832 | tf_op jit(solution)/shard_map/ppermute | solution.py:194
  48.1 5.0 %collective-permute-start.7 = (bf16[64,768]{1,0:T(8,128)(2,1)S(1)}, bf16[64,768]{1,0:T(8,128)(2,1)S(1)}, u32[]{:S(2)}, u32[]{:S(2)}) collective-permute-start(bf16[64,768]{1,0:T(8,128)(2,1)S(1)} %slice.13), channel_id=1, source_target_pairs={{0,448},{64,0},{128,64},{192,128},{256,192},{320,256},{384,320},{4... | collective-permute-start | bytes 294920 | tf_op jit(solution)/shard_map/ppermute | solution.py:194
  53.1 1.9 %collective-permute-start.6 = (bf16[64,768]{1,0:T(8,128)(2,1)S(1)}, bf16[64,768]{1,0:T(8,128)(2,1)S(1)}, u32[]{:S(2)}, u32[]{:S(2)}) collective-permute-start(bf16[64,768]{1,0:T(8,128)(2,1)S(1)} %slice.12), channel_id=1, source_target_pairs={{0,64},{64,128},{128,192},{192,256},{256,320},{320,384},{384,448},... | collective-permute-start | bytes 294920 | tf_op jit(solution)/shard_map/ppermute | solution.py:194
  55.1 4.6 %collective-permute-done.6.refs_7_ = bf16[64,768]{1,0:T(8,128)(2,1)S(1)} collective-permute-done((bf16[64,768]{1,0:T(8,128)(2,1)S(1)}, bf16[64,768]{1,0:T(8,128)(2,1)S(1)}, u32[]{:S(2)}, u32[]{:S(2)}) %collective-permute-start.6) | collective-permute-done | bytes 98336 | tf_op jit(solution)/shard_map/ppermute | solution.py:194
  61.2 4.6 %scores.1 = (f32[4,1024,256]{2,1,0:T(8,128)S(1)}, f32[4,8,1024]{2,1,0:T(8,128)S(1)}) custom-call(f32[1]{0:T(128)S(6)} %copy.14.factor_ref, s32[2]{0:T(128)S(1)} %pad_add_fusion.place_ref, bf16[4,272,768]{2,1,0:T(8,128)(2,1)S(1)} %all-to-all-done.m_ref, bf16[128,768]{1,0:T(8,128)(2,1)S(1)} %convert_element_type.3.refs_0_, ...), custom_call_target="tpu_custom_call" | custom-call | tf_op jit(solution)/shard_map/scores/pallas_call | solution.py:257
  65.8 8.4 %all_to_all.15.stat_ref = f32[4,8,1024]{2,1,0:T(8,128)S(1)} all-to-all(f32[4,8,1024]{2,1,0:T(8,128)S(1)} %get-tuple-element.16), channel_id=1, replica_groups=mesh['gz'=8,'gx'=4,'gy'=16] {'gx'}, dimensions={0} | all-to-all | bytes 262144 | tf_op jit(solution)/shard_map/all_to_all | solution.py:270
  74.2 6.4 %grads.1 = (bf16[4,1024,256]{2,1,0:T(8,128)(2,1)S(1)}, bf16[8,128,768]{2,1,0:T(8,128)(2,1)}, f32[1,128]{1,0:T(1,128)S(1)}) custom-call(f32[1]{0:T(128)S(6)} %copy.14.factor_ref, s32[2]{0:T(128)S(1)} %pad_add_fusion.place_ref, f32[4,1024,256]{2,1,0:T(8,128)S(1)} %get-tuple-element.15.raw_ref, f32[4,8,1024]{2,1,0:T(8,128)S(1)} %all_to_all.15.stat_ref, ...), custom_call_target="tpu_custom_call" | custom-call | tf_op jit(solution)/shard_map/grads/pallas_call | solution.py:271
  80.6 3.5 %mention_part.1 = (bf16[4,256,768]{2,1,0:T(8,128)(2,1)}, f32[1,128]{1,0:T(1,128)S(1)}) custom-call(f32[1]{0:T(128)S(6)} %copy.14.factor_ref, f32[1,128]{1,0:T(1,128)S(1)} %get-tuple-element.21.scale_ref, bf16[4,1024,256]{2,1,0:T(8,128)(2,1)S(1)} %get-tuple-element.22.g_ref, bf16[128,768]{1,0:T(8,128)(2,1)S(1)} %convert_element_type.3.refs_0_, ...), custom_call_target="tpu_custom_call" | custom-call | tf_op jit(solution)/shard_map/mention_part/pallas_call | solution.py:292
  84.1 3.7 %all-to-all-start.2 = ((bf16[8,128,768]{2,1,0:T(8,128)(2,1)}), bf16[8,128,768]{2,1,0:T(8,128)(2,1)S(1)}, u32[]{:S(2)}, u32[]{:S(2)}) async-start(bf16[8,128,768]{2,1,0:T(8,128)(2,1)} %get-tuple-element.17), calls=%async_computation.2 | async-start | bytes 3145728 | tf_op jit(solution)/shard_map/all_to_all | solution.py:291
  87.8 3.3 %collective-permute-start.8 = (f32[1,128]{1,0:T(1,128)S(1)}, f32[1,128]{1,0:T(1,128)S(1)}, u32[]{:S(2)}, u32[]{:S(2)}) collective-permute-start(f32[1,128]{1,0:T(1,128)S(1)} %get-tuple-element.24), channel_id=1, source_target_pairs={{0,64},{64,0},{128,192},{192,128},{256,320},{320,256},{384,448},{4... | collective-permute-start | bytes 1544 | tf_op jit(solution)/shard_map/ppermute | solution.py:213
  91.1 22.8 %collective-permute-done.8 = f32[1,128]{1,0:T(1,128)S(1)} collective-permute-done((f32[1,128]{1,0:T(1,128)S(1)}, f32[1,128]{1,0:T(1,128)S(1)}, u32[]{:S(2)}, u32[]{:S(2)}) %collective-permute-start.8) | collective-permute-done | bytes 544 | tf_op jit(solution)/shard_map/ppermute | solution.py:213
  113.9 7.0 %collective-permute-start.9 = (f32[1,128]{1,0:T(1,128)S(1)}, f32[1,128]{1,0:T(1,128)S(1)}, u32[]{:S(2)}, u32[]{:S(2)}) collective-permute-start(f32[1,128]{1,0:T(1,128)S(1)} %add.23), channel_id=1, source_target_pairs={{0,128},{64,192},{128,0},{192,64},{256,384},{320,448},{384,256},{4... | collective-permute-start | bytes 1544 | tf_op jit(solution)/shard_map/ppermute | solution.py:213
  120.8 3.3 %collective-permute-done.9 = f32[1,128]{1,0:T(1,128)S(1)} collective-permute-done((f32[1,128]{1,0:T(1,128)S(1)}, f32[1,128]{1,0:T(1,128)S(1)}, u32[]{:S(2)}, u32[]{:S(2)}) %collective-permute-start.9) | collective-permute-done | bytes 544 | tf_op jit(solution)/shard_map/ppermute | solution.py:213
  124.2 6.2 %collective-permute-start.10 = (f32[1,128]{1,0:T(1,128)S(1)}, f32[1,128]{1,0:T(1,128)S(1)}, u32[]{:S(2)}, u32[]{:S(2)}) collective-permute-start(f32[1,128]{1,0:T(1,128)S(1)} %add.24), channel_id=1, source_target_pairs={{0,256},{64,320},{128,384},{192,448},{256,0},{320,64},{384,128},{4... | collective-permute-start | bytes 1544 | tf_op jit(solution)/shard_map/ppermute | solution.py:213
  130.4 1.9 %collective-permute-done.10 = f32[1,128]{1,0:T(1,128)S(1)} collective-permute-done((f32[1,128]{1,0:T(1,128)S(1)}, f32[1,128]{1,0:T(1,128)S(1)}, u32[]{:S(2)}, u32[]{:S(2)}) %collective-permute-start.10) | collective-permute-done | bytes 544 | tf_op jit(solution)/shard_map/ppermute | solution.py:213
  132.4 9.9 %collective-permute-start.11 = (f32[1,128]{1,0:T(1,128)S(1)}, f32[1,128]{1,0:T(1,128)S(1)}, u32[]{:S(2)}, u32[]{:S(2)}) collective-permute-start(f32[1,128]{1,0:T(1,128)S(1)} %add.25), channel_id=1, source_target_pairs={{0,1},{1,0},{2,3},{3,2},{4,5},{5,4},{6,7},{7,6},{8,9},{9,8},{10,11... | collective-permute-start | bytes 1544 | tf_op jit(solution)/shard_map/ppermute | solution.py:213
  143.1 3.2 %collective-permute-start.12 = (f32[1,128]{1,0:T(1,128)S(1)}, f32[1,128]{1,0:T(1,128)S(1)}, u32[]{:S(2)}, u32[]{:S(2)}) collective-permute-start(f32[1,128]{1,0:T(1,128)S(1)} %add.26), channel_id=1, source_target_pairs={{0,2},{1,3},{2,0},{3,1},{4,6},{5,7},{6,4},{7,5},{8,10},{9,11},{10,... | collective-permute-start | bytes 1544 | tf_op jit(solution)/shard_map/ppermute | solution.py:213
  146.3 1.1 collective-permute-done.12
  147.4 4.2 %collective-permute-start.13 = (f32[1,128]{1,0:T(1,128)S(1)}, f32[1,128]{1,0:T(1,128)S(1)}, u32[]{:S(2)}, u32[]{:S(2)}) collective-permute-start(f32[1,128]{1,0:T(1,128)S(1)} %add.27), channel_id=1, source_target_pairs={{0,4},{1,5},{2,6},{3,7},{4,0},{5,1},{6,2},{7,3},{8,12},{9,13},{10,... | collective-permute-start | bytes 1544 | tf_op jit(solution)/shard_map/ppermute | solution.py:213
  151.6 1.0 collective-permute-done.13
  152.6 7.4 %collective-permute-start.14 = (f32[1,128]{1,0:T(1,128)S(1)}, f32[1,128]{1,0:T(1,128)S(1)}, u32[]{:S(2)}, u32[]{:S(2)}) collective-permute-start(f32[1,128]{1,0:T(1,128)S(1)} %add.28), channel_id=1, source_target_pairs={{0,8},{1,9},{2,10},{3,11},{4,12},{5,13},{6,14},{7,15},{8,0},{9,1},... | collective-permute-start | bytes 1544 | tf_op jit(solution)/shard_map/ppermute | solution.py:213
  160.0 0.9 collective-permute-done.14
  161.0 1.8 %adam.1 = (f32[128,768]{1,0:T(8,128)}, f32[128,768]{1,0:T(8,128)}, f32[128,768]{1,0:T(8,128)}) custom-call(bf16[8,128,768]{2,1,0:T(8,128)(2,1)S(1)} %all-to-all-done.2.part_ref, f32[128,768]{1,0:T(8,128)S(1)} %copy-done, f32[128,768]{1,0:T(8,128)S(1)} %copy-done.4, f32[128,768]{1,0:T(8,128)S(1)} %copy-done.5), custom_call_target="tpu_custom_call" | custom-call | tf_op jit(solution)/shard_map/adam/pallas_call | solution.py:312
  (42 shorter events, 5.9 us)
Async XLA Ops:
  7.2 1.0 copy-start.1
  8.2 0.7 copy-start.6
  8.8 0.7 copy-start.7
  9.5 0.7 copy-start.8
  10.2 0.7 copy-start.9
  13.3 5.0 %copy-start = (f32[128,768]{1,0:T(8,128)S(1)}, f32[128,768]{1,0:T(8,128)}, u32[]{:S(2)}) copy-start(f32[128,768]{1,0:T(8,128)} %table_ref.1) | copy-start | bytes 1179652
  13.3 47.0 %all-to-all-start = ((bf16[4,272,768]{2,1,0:T(8,128)(2,1)}), bf16[4,272,768]{2,1,0:T(8,128)(2,1)S(1)}, u32[]{:S(2)}, u32[]{:S(2)}) async-start(bf16[4,272,768]{2,1,0:T(8,128)(2,1)} %pack.1), calls=%async_computation | async-start | bytes 3342336 | tf_op jit(solution)/shard_map/all_to_all | solution.py:255
  18.3 144.6 %reduce-scatter.2.cloned.1.call-start = ((), (), s32[]{:S(2)}) async-start(), calls=%async_computation.4 | async-start | bytes 1966080 | tf_op jit(solution)/shard_map/reduce_scatter | solution.py:305
  18.3 13.9 %collective-permute-start.1 = (bf16[128,768]{1,0:T(8,128)(2,1)S(1)}, bf16[128,768]{1,0:T(8,128)(2,1)S(1)}, u32[]{:S(2)}, u32[]{:S(2)}) collective-permute-start(bf16[128,768]{1,0:T(8,128)(2,1)S(1)} %convert_element_type.3.refs_0_), channel_id=1, source_target_pairs={{0,448},{64,0},{128,64},{192,128},{256,192},{320,256},{384,320},{4... | collective-permute-start | bytes 589832 | tf_op jit(solution)/shard_map/ppermute | solution.py:194
  29.0 8.5 %collective-permute-start = (bf16[128,768]{1,0:T(8,128)(2,1)S(1)}, bf16[128,768]{1,0:T(8,128)(2,1)S(1)}, u32[]{:S(2)}, u32[]{:S(2)}) collective-permute-start(bf16[128,768]{1,0:T(8,128)(2,1)S(1)} %convert_element_type.3.refs_0_), channel_id=1, source_target_pairs={{0,64},{64,128},{128,192},{192,256},{256,320},{320,384},{384,448},... | collective-permute-start | bytes 589832 | tf_op jit(solution)/shard_map/ppermute | solution.py:194
  32.2 7.9 %collective-permute-start.3 = (bf16[128,768]{1,0:T(8,128)(2,1)S(1)}, bf16[128,768]{1,0:T(8,128)(2,1)S(1)}, u32[]{:S(2)}, u32[]{:S(2)}) collective-permute-start(bf16[128,768]{1,0:T(8,128)(2,1)S(1)} %collective-permute-done.1.refs_2_), channel_id=1, source_target_pairs={{0,448},{64,0},{128,64},{192,128},{256,192},{320,256},{384,320},{4... | collective-permute-start | bytes 589832 | tf_op jit(solution)/shard_map/ppermute | solution.py:194
  37.5 7.9 %collective-permute-start.2 = (bf16[128,768]{1,0:T(8,128)(2,1)S(1)}, bf16[128,768]{1,0:T(8,128)(2,1)S(1)}, u32[]{:S(2)}, u32[]{:S(2)}) collective-permute-start(bf16[128,768]{1,0:T(8,128)(2,1)S(1)} %collective-permute-done.refs_1_), channel_id=1, source_target_pairs={{0,64},{64,128},{128,192},{192,256},{256,320},{320,384},{384,448},... | collective-permute-start | bytes 589832 | tf_op jit(solution)/shard_map/ppermute | solution.py:194
  40.1 7.9 %collective-permute-start.5 = (bf16[128,768]{1,0:T(8,128)(2,1)S(1)}, bf16[128,768]{1,0:T(8,128)(2,1)S(1)}, u32[]{:S(2)}, u32[]{:S(2)}) collective-permute-start(bf16[128,768]{1,0:T(8,128)(2,1)S(1)} %collective-permute-done.3.refs_4_), channel_id=1, source_target_pairs={{0,448},{64,0},{128,64},{192,128},{256,192},{320,256},{384,320},{4... | collective-permute-start | bytes 589832 | tf_op jit(solution)/shard_map/ppermute | solution.py:194
  45.4 7.6 %collective-permute-start.4 = (bf16[128,768]{1,0:T(8,128)(2,1)S(1)}, bf16[128,768]{1,0:T(8,128)(2,1)S(1)}, u32[]{:S(2)}, u32[]{:S(2)}) collective-permute-start(bf16[128,768]{1,0:T(8,128)(2,1)S(1)} %collective-permute-done.2.refs_3_), channel_id=1, source_target_pairs={{0,64},{64,128},{128,192},{192,256},{256,320},{320,384},{384,448},... | collective-permute-start | bytes 589832 | tf_op jit(solution)/shard_map/ppermute | solution.py:194
  48.1 7.1 %collective-permute-start.7 = (bf16[64,768]{1,0:T(8,128)(2,1)S(1)}, bf16[64,768]{1,0:T(8,128)(2,1)S(1)}, u32[]{:S(2)}, u32[]{:S(2)}) collective-permute-start(bf16[64,768]{1,0:T(8,128)(2,1)S(1)} %slice.13), channel_id=1, source_target_pairs={{0,448},{64,0},{128,64},{192,128},{256,192},{320,256},{384,320},{4... | collective-permute-start | bytes 294920 | tf_op jit(solution)/shard_map/ppermute | solution.py:194
  53.1 6.6 %collective-permute-start.6 = (bf16[64,768]{1,0:T(8,128)(2,1)S(1)}, bf16[64,768]{1,0:T(8,128)(2,1)S(1)}, u32[]{:S(2)}, u32[]{:S(2)}) collective-permute-start(bf16[64,768]{1,0:T(8,128)(2,1)S(1)} %slice.12), channel_id=1, source_target_pairs={{0,64},{64,128},{128,192},{192,256},{256,320},{320,384},{384,448},... | collective-permute-start | bytes 294920 | tf_op jit(solution)/shard_map/ppermute | solution.py:194
  59.7 0.6 copy-start.2
  60.3 0.9 copy-start.3
  84.1 76.9 %copy-start.4 = (f32[128,768]{1,0:T(8,128)S(1)}, f32[128,768]{1,0:T(8,128)}, u32[]{:S(2)}) copy-start(f32[128,768]{1,0:T(8,128)} %m_ref.1) | copy-start | bytes 1179652
  84.1 76.9 %copy-start.5 = (f32[128,768]{1,0:T(8,128)S(1)}, f32[128,768]{1,0:T(8,128)}, u32[]{:S(2)}) copy-start(f32[128,768]{1,0:T(8,128)} %v_ref.1) | copy-start | bytes 1179652
  84.1 76.9 %all-to-all-start.2 = ((bf16[8,128,768]{2,1,0:T(8,128)(2,1)}), bf16[8,128,768]{2,1,0:T(8,128)(2,1)S(1)}, u32[]{:S(2)}, u32[]{:S(2)}) async-start(bf16[8,128,768]{2,1,0:T(8,128)(2,1)} %get-tuple-element.17), calls=%async_computation.2 | async-start | bytes 3145728 | tf_op jit(solution)/shard_map/all_to_all | solution.py:291
  87.8 26.0 %collective-permute-start.8 = (f32[1,128]{1,0:T(1,128)S(1)}, f32[1,128]{1,0:T(1,128)S(1)}, u32[]{:S(2)}, u32[]{:S(2)}) collective-permute-start(f32[1,128]{1,0:T(1,128)S(1)} %get-tuple-element.24), channel_id=1, source_target_pairs={{0,64},{64,0},{128,192},{192,128},{256,320},{320,256},{384,448},{4... | collective-permute-start | bytes 1544 | tf_op jit(solution)/shard_map/ppermute | solution.py:213
  113.9 10.3 %collective-permute-start.9 = (f32[1,128]{1,0:T(1,128)S(1)}, f32[1,128]{1,0:T(1,128)S(1)}, u32[]{:S(2)}, u32[]{:S(2)}) collective-permute-start(f32[1,128]{1,0:T(1,128)S(1)} %add.23), channel_id=1, source_target_pairs={{0,128},{64,192},{128,0},{192,64},{256,384},{320,448},{384,256},{4... | collective-permute-start | bytes 1544 | tf_op jit(solution)/shard_map/ppermute | solution.py:213
  124.2 8.2 %collective-permute-start.10 = (f32[1,128]{1,0:T(1,128)S(1)}, f32[1,128]{1,0:T(1,128)S(1)}, u32[]{:S(2)}, u32[]{:S(2)}) collective-permute-start(f32[1,128]{1,0:T(1,128)S(1)} %add.24), channel_id=1, source_target_pairs={{0,256},{64,320},{128,384},{192,448},{256,0},{320,64},{384,128},{4... | collective-permute-start | bytes 1544 | tf_op jit(solution)/shard_map/ppermute | solution.py:213
  132.4 10.7 %collective-permute-start.11 = (f32[1,128]{1,0:T(1,128)S(1)}, f32[1,128]{1,0:T(1,128)S(1)}, u32[]{:S(2)}, u32[]{:S(2)}) collective-permute-start(f32[1,128]{1,0:T(1,128)S(1)} %add.25), channel_id=1, source_target_pairs={{0,1},{1,0},{2,3},{3,2},{4,5},{5,4},{6,7},{7,6},{8,9},{9,8},{10,11... | collective-permute-start | bytes 1544 | tf_op jit(solution)/shard_map/ppermute | solution.py:213
  143.1 4.3 %collective-permute-start.12 = (f32[1,128]{1,0:T(1,128)S(1)}, f32[1,128]{1,0:T(1,128)S(1)}, u32[]{:S(2)}, u32[]{:S(2)}) collective-permute-start(f32[1,128]{1,0:T(1,128)S(1)} %add.26), channel_id=1, source_target_pairs={{0,2},{1,3},{2,0},{3,1},{4,6},{5,7},{6,4},{7,5},{8,10},{9,11},{10,... | collective-permute-start | bytes 1544 | tf_op jit(solution)/shard_map/ppermute | solution.py:213
  147.4 5.2 %collective-permute-start.13 = (f32[1,128]{1,0:T(1,128)S(1)}, f32[1,128]{1,0:T(1,128)S(1)}, u32[]{:S(2)}, u32[]{:S(2)}) collective-permute-start(f32[1,128]{1,0:T(1,128)S(1)} %add.27), channel_id=1, source_target_pairs={{0,4},{1,5},{2,6},{3,7},{4,0},{5,1},{6,2},{7,3},{8,12},{9,13},{10,... | collective-permute-start | bytes 1544 | tf_op jit(solution)/shard_map/ppermute | solution.py:213
  152.6 8.4 %collective-permute-start.14 = (f32[1,128]{1,0:T(1,128)S(1)}, f32[1,128]{1,0:T(1,128)S(1)}, u32[]{:S(2)}, u32[]{:S(2)}) collective-permute-start(f32[1,128]{1,0:T(1,128)S(1)} %add.28), channel_id=1, source_target_pairs={{0,8},{1,9},{2,10},{3,11},{4,12},{5,13},{6,14},{7,15},{8,0},{9,1},... | collective-permute-start | bytes 1544 | tf_op jit(solution)/shard_map/ppermute | solution.py:213
Sparse Core Ops, SparseCore 0:
  84.2 30.8 reduce-scatter.1

commit v3 on v2

v3 whole, which is shorter than its diff:
```python
import jax
import jax.numpy as jnp
from jax import lax
from jax.experimental import pallas as pl
from jax.experimental.pallas import tpu as pltpu
from jax.sharding import Mesh, PartitionSpec as P

beta_one = 0.9
beta_two = 0.999
learn_rate = 0.02
adam_eps = 1e-08
first_fix = 0.9999734386011124
second_fix = 0.09520785288629038

X_SIZE = 4
Z_SIZE = 8
BLOCK = 128
LOW = -1e30
META_ROWS = 16
SLOTS = 16
STAT_ROWS = 8
f32 = jnp.float32
bf16 = jnp.bfloat16


def pack_kernel(
    cols, list_hbm, len_hbm, slot_hbm, row_hbm, m_hbm, t_hbm, m_out, t_out, list_ref, len_ref, slot_ref, row_ref, t_ref, sems
):
    rows, width = m_hbm.shape
    pairs = [
        (list_hbm, list_ref),
        (len_hbm, len_ref),
        (slot_hbm, slot_ref),
        (row_hbm, row_ref),
        (t_hbm, t_ref),
        (m_hbm, m_out.at[pl.ds(0, rows), :]),
    ]
    copies = [pltpu.make_async_copy(src, dst, sems.at[i]) for i, (src, dst) in enumerate(pairs)]
    for copy in copies:
        copy.start()
    for copy in copies[:4]:
        copy.wait()
    owners = lax.div(list_ref[...], cols).astype(f32)
    lens = len_ref[...]
    first = lax.broadcasted_iota(jnp.int32, (1, rows), 1) < BLOCK
    length = jnp.where(first, lens[:, 0:1], lens[:, 1:2])
    slot = slot_ref[...]
    gold = jnp.zeros((1, rows), f32)
    parts = []
    for k in range(SLOTS):
        owner = jnp.where(first, owners[0:1, k : k + 1], owners[1:2, k : k + 1])
        gold = gold + jnp.where(slot == k, owner, 0.0)
        parts.append(jnp.where(length > k, owner, -1.0))
    parts += [gold, row_ref[...].astype(f32)]
    per_row = width // rows
    lines = [
        jnp.concatenate(parts[i : i + per_row], axis=1) for i in range(0, len(parts), per_row)
    ]
    lines.append(jnp.zeros((META_ROWS - len(lines), width), f32))
    m_out[rows : rows + META_ROWS, :] = jnp.concatenate(lines, axis=0).astype(bf16)
    copies[4].wait()
    table = t_ref[...].astype(bf16)
    for z in range(t_out.shape[0]):
        t_out[z] = table
    copies[5].wait()


def read_meta(m_ref, rows):
    meta = m_ref[0, rows : rows + META_ROWS, :].astype(f32)
    per_row = meta.shape[1] // rows
    parts = [
        meta[i // per_row : i // per_row + 1, (i % per_row) * rows : (i % per_row + 1) * rows]
        for i in range(SLOTS + 2)
    ]
    owners = jnp.concatenate(parts[:SLOTS], axis=0)
    return owners, parts[SLOTS], parts[SLOTS + 1].astype(jnp.int32)


def listed_in(owners, owner):
    return jnp.max(jnp.where(owners == owner, 1.0, 0.0), axis=0, keepdims=True) > 0.0


def owner_at(place_ref, line):
    return (line * X_SIZE + place_ref[0]).astype(f32)


def scores_kernel(factor_ref, place_ref, m_ref, t_ref, raw_ref, stat_ref):
    step = pl.program_id(0)
    factor = factor_ref[0]
    rows = m_ref.shape[1] - META_ROWS
    raw_ref[0] = lax.dot_general(
        t_ref[...], m_ref[0, 0:rows, :], (((1,), (1,)), ((), ())), preferred_element_type=f32
    )
    owners, gold_owner, gold_row = read_meta(m_ref, rows)
    ids = lax.broadcasted_iota(jnp.int32, (BLOCK, rows), 0)
    top = jnp.full((1, rows), LOW, f32)
    gold_raw = jnp.zeros((1, rows), f32)
    lives = []
    for c in range(Z_SIZE):
        owner = owner_at(place_ref, c)
        lives.append(listed_in(owners, owner))
        raw = raw_ref[0, c * BLOCK : (c + 1) * BLOCK, :]
        part = jnp.max(factor * raw, axis=0, keepdims=True)
        top = jnp.maximum(top, jnp.where(lives[c], part, LOW))
        gold = jnp.where(gold_owner == owner, gold_row, -1)
        gold_raw = gold_raw + jnp.sum(jnp.where(ids == gold, raw, 0.0), axis=0, keepdims=True)
    total = jnp.zeros((1, rows), f32)
    mass = jnp.zeros((1, rows), f32)
    for c in range(Z_SIZE):
        raw = raw_ref[0, c * BLOCK : (c + 1) * BLOCK, :]
        weights = jnp.where(lives[c], jnp.exp(factor * raw - top), 0.0)
        total = total + jnp.sum(weights, axis=0, keepdims=True)
        mass = mass + jnp.sum(weights * raw, axis=0, keepdims=True)
    stat = jnp.concatenate(
        [top, total, mass, gold_raw, jnp.zeros((STAT_ROWS - 4, rows), f32)], axis=0
    )
    for d in range(stat_ref.shape[0]):
        stat_ref[d, :, pl.ds(pl.multiple_of(step * rows, BLOCK), rows)] = stat


def grads_kernel(
    factor_ref, place_ref, raw_ref, stat_ref, m_ref, t_ref, mention_ref, type_ref, scale_ref, g_ref, acc_ref, sum_ref
):
    step = pl.program_id(0)
    factor = factor_ref[0]
    rows = m_ref.shape[1] - META_ROWS
    tops = stat_ref[:, 0, :]
    top = jnp.max(tops, axis=0, keepdims=True)
    share = jnp.exp(tops - top)
    total = jnp.sum(stat_ref[:, 1, :] * share, axis=0, keepdims=True)
    log_total = top + jnp.log(total)
    mass = jnp.sum(stat_ref[:, 2, :] * share, axis=0, keepdims=True)
    scale = mass / total - jnp.sum(stat_ref[:, 3, :], axis=0, keepdims=True)
    owners, gold_owner, gold_row = read_meta(m_ref, rows)
    ids = lax.broadcasted_iota(jnp.int32, (BLOCK, rows), 0)
    for c in range(Z_SIZE):
        owner = owner_at(place_ref, c)
        live = listed_in(owners, owner)
        raw = raw_ref[0, c * BLOCK : (c + 1) * BLOCK, :]
        weights = jnp.where(live, jnp.exp(factor * raw - log_total), 0.0)
        gold = jnp.where(gold_owner == owner, gold_row, -1)
        grad = weights - jnp.where(ids == gold, 1.0, 0.0)
        g_ref[c * BLOCK : (c + 1) * BLOCK, :] = grad.astype(bf16)
    part = jnp.dot(g_ref[...], m_ref[0, 0:rows, :], preferred_element_type=f32)

    @pl.when(step == 0)
    def _():
        acc_ref[...] = part
        sum_ref[...] = scale

    @pl.when(step > 0)
    def _():
        acc_ref[...] += part
        sum_ref[...] += scale

    mention = lax.dot_general(
        g_ref[...], t_ref[...], (((0,), (0,)), ((), ())), preferred_element_type=f32
    )
    mention_ref[0] = (factor * mention).astype(bf16)

    @pl.when(step == pl.num_programs(0) - 1)
    def _():
        type_ref[...] = (factor * acc_ref[...]).astype(bf16)
        scale_ref[...] = jnp.broadcast_to(
            jnp.sum(sum_ref[...], axis=1, keepdims=True), scale_ref.shape
        )


def adam_kernel(part_ref, table_ref, m_ref, v_ref, table_out, m_out, v_out):
    grad = part_ref[0].astype(f32)
    for z in range(1, part_ref.shape[0]):
        grad = grad + part_ref[z].astype(f32)
    moment_one = beta_one * m_ref[...] + (1.0 - beta_one) * grad
    moment_two = beta_two * v_ref[...] + (1.0 - beta_two) * grad * grad
    table_out[...] = table_ref[...] - learn_rate * (moment_one / first_fix) / (
        jnp.sqrt(moment_two / second_fix) + adam_eps
    )
    m_out[...] = moment_one
    v_out[...] = moment_two


def params(mib=52):
    return pltpu.CompilerParams(vmem_limit_bytes=mib * 1024 * 1024)


def doubled(value, axis, size):
    by = 1
    while by < size:
        value = value + lax.ppermute(value, axis, [(i, i ^ by) for i in range(size)])
        by *= 2
    return value


def per_device(
    mentions,
    type_table,
    adam_m,
    adam_v,
    logit_scale,
    block_lists,
    list_lengths,
    gold_slot,
    gold_row,
):
    cols = lax.axis_size("gy")
    devices = Z_SIZE * X_SIZE * cols
    block_rows, width = type_table.shape
    rows = mentions.shape[0]
    sent_rows = rows + META_ROWS
    types = Z_SIZE * block_rows
    smem = pl.BlockSpec(memory_space=pltpu.SMEM)
    hbm = pl.BlockSpec(memory_space=pltpu.HBM)
    place = lax.axis_index("gx").reshape(1).astype(jnp.int32)

    def tile(*shape):
        return pl.BlockSpec((1,) + shape, lambda j: (j, 0, 0))

    def whole(*shape):
        return pl.BlockSpec(shape, lambda j: (0,) * len(shape))

    packed, copies = pl.pallas_call(
        lambda *refs: pack_kernel(cols, *refs),
        in_specs=[hbm] * 6,
        out_shape=[
            jax.ShapeDtypeStruct((sent_rows, width), bf16),
            jax.ShapeDtypeStruct((Z_SIZE, block_rows, width), bf16),
        ],
        scratch_shapes=[
            pltpu.VMEM((2, SLOTS), jnp.int32),
            pltpu.VMEM((1, 2), jnp.int32),
            pltpu.VMEM((1, rows), jnp.int32),
            pltpu.VMEM((1, rows), jnp.int32),
            pltpu.VMEM((block_rows, width), f32),
            pltpu.SemaphoreType.DMA((6,)),
        ],
        compiler_params=params(60),
        name="pack",
    )(
        block_lists,
        list_lengths.reshape(1, 2),
        gold_slot.reshape(1, rows),
        gold_row.reshape(1, rows),
        mentions,
        type_table,
    )
    table = lax.all_to_all(copies, "gz", 0, 0, tiled=True).reshape(types, width)
    gathered = lax.all_gather(packed, "gx", axis=0, tiled=True)
    gathered = gathered.reshape(X_SIZE, sent_rows, width)

    raw_dot, stats = pl.pallas_call(
        scores_kernel,
        grid=(X_SIZE,),
        in_specs=[smem, smem, tile(sent_rows, width), whole(types, width)],
        out_specs=[tile(types, rows), whole(X_SIZE, STAT_ROWS, X_SIZE * rows)],
        out_shape=[
            jax.ShapeDtypeStruct((X_SIZE, types, rows), f32),
            jax.ShapeDtypeStruct((X_SIZE, STAT_ROWS, X_SIZE * rows), f32),
        ],
        compiler_params=params(),
        name="scores",
    )(logit_scale, place, gathered, table)
    stats = lax.all_to_all(stats, "gx", 0, 0, tiled=True)
    mention_part, type_part, scale_part = pl.pallas_call(
        grads_kernel,
        grid=(X_SIZE,),
        in_specs=[
            smem,
            smem,
            tile(types, rows),
            pl.BlockSpec((X_SIZE, STAT_ROWS, rows), lambda j: (0, 0, j)),
            tile(sent_rows, width),
            whole(types, width),
        ],
        out_specs=[tile(rows, width), whole(types, width), whole(1, 128)],
        out_shape=[
            jax.ShapeDtypeStruct((X_SIZE, rows, width), bf16),
            jax.ShapeDtypeStruct((types, width), bf16),
            jax.ShapeDtypeStruct((1, 128), f32),
        ],
        scratch_shapes=[
            pltpu.VMEM((types, rows), bf16),
            pltpu.VMEM((types, width), f32),
            pltpu.VMEM((1, rows), f32),
        ],
        compiler_params=params(),
        name="grads",
    )(logit_scale, place, raw_dot, stats, gathered, table)
    type_parts = lax.all_to_all(
        type_part.reshape(Z_SIZE, block_rows, width), "gz", 0, 0, tiled=True
    )
    mention_grad = lax.psum_scatter(
        mention_part.reshape(X_SIZE * rows, width), "gx", scatter_dimension=0, tiled=True
    )
    scale_sum = doubled(scale_part, "gy", cols) + 0.0 * type_parts[0, 0:1, 0:128].astype(f32)
    scale_sums = lax.all_to_all(
        jnp.broadcast_to(scale_sum[None], (Z_SIZE, 1, 128)), "gz", 0, 0, tiled=True
    )
    scale_grad = (jnp.sum(scale_sums[:, 0, 0]) / (rows * devices)).reshape(1)
    slab = block_rows // 4
    row_tile = pl.BlockSpec((slab, width), lambda j: (j, 0))
    new_table, new_first, new_second = pl.pallas_call(
        adam_kernel,
        grid=(block_rows // slab,),
        in_specs=[pl.BlockSpec((Z_SIZE, slab, width), lambda j: (0, j, 0))] + [row_tile] * 3,
        out_specs=[row_tile] * 3,
        out_shape=[jax.ShapeDtypeStruct((block_rows, width), f32)] * 3,
        compiler_params=params(16),
        name="adam",
    )(type_parts, type_table, adam_m, adam_v)
    return (new_table, new_first, new_second, mention_grad, scale_grad)


def solution(mesh):
    gx, gy = mesh.devices.shape
    split = Mesh(mesh.devices.reshape(gx // X_SIZE, X_SIZE, gy), ("gz", "gx", "gy"))
    axes = ("gz", "gx", "gy")
    rows = P(axes, None)
    return jax.shard_map(
        per_device,
        mesh=split,
        in_specs=(rows, rows, rows, rows, P(), rows, P(axes), P(axes), P(axes)),
        out_specs=(rows, rows, rows, rows, P()),
        check_vma=False,
    )
```

time: 174 us -> 150 us (0.86); the launches traced: 171 us -> 150 us
  starting transfers between devices: 83.9 us -> 39 us
  waiting for transfers between devices: 38.3 us -> 62.8 us
  local copies, waits for them, and re-layouts: 5.25 us -> 0.62 us
  Pallas kernels: 18.7 us -> 21.5 us
    all_gather x0 -> x1, waiting for transfers between devices: none -> 36 us  [per_device(): gathered = lax.all_gather(packed, 'gx', axis=0, tiled=True)]
    ppermute x8 -> x0, starting transfers between devices: 34 us -> none  [shifted(): lax.ppermute(array, axis, [(i, (i + by) % size) for i in range(size)])]
    ppermute x7 -> x4, waiting for transfers between devices: 31.8 us -> 4.43 us  [doubled(): lax.ppermute(value, axis, [(i, i ^ by) for i in range(size)])]
    all_to_all x2 -> x3, waiting for transfers between devices: 0.01 us -> 21.7 us  [the longest x1 16.3 us: per_device(): lax.all_to_all(type_part.reshape(Z_SIZE, block_rows, width), 'gz', 0, 0,...]
    ppermute x7 -> x4, starting transfers between devices: 41.2 us -> 19.7 us  [doubled(): lax.ppermute(value, axis, [(i, i ^ by) for i in range(size)])]
    all_to_all x2 -> x3, starting transfers between devices: 8.7 us -> 19.2 us  [the longest x1 10.9 us: per_device(): table = lax.all_to_all(copies, 'gz', 0, 0, tiled=True).reshape(types, width)]
    ppermute x8 -> x0, waiting for transfers between devices: 6.53 us -> none  [shifted(): lax.ppermute(array, axis, [(i, (i + by) % size) for i in range(size)])]
    unnamed x20 -> x8, local copies, waits for them, and re-layouts: 5.23 us -> 0.02 us
  transfers between devices with their start and end apart: 18 -> 9, of which waited for: 10 -> 8; matrix products, arithmetic and copies ran while one was open for 0% -> 1% of each run, Pallas kernels for 1% -> 1%
where the time goes in v3:
time: 150 us
  waiting for transfers between devices  62.8 us (42%)
  starting transfers between devices  39 us (26%)
  Pallas kernels  21.5 us (14%)
  between operations  16.6 us (11%)
  blocking collectives  8.63 us (6%)
    all_gather x1, waiting for transfers between devices, per_device(): gathered = lax.all_gather(packed, 'gx', axis=0, tiled=True)  36 us
    ppermute x4, starting transfers between devices, doubled(): lax.ppermute(value, axis, [(i, i ^ by) for i in range(size)])  19.7 us
    all_to_all x1, waiting for transfers between devices, per_device(): lax.all_to_all(type_part.reshape(Z_SIZE, block_rows, width), 'gz', 0, 0,...  16.3 us
    all_to_all x1, starting transfers between devices, per_device(): table = lax.all_to_all(copies, 'gz', 0, 0, tiled=True).reshape(types, width)  10.9 us
    pallas_call x1, Pallas kernels, per_device(): pl.pallas_call(grads_kernel, grid=(X_SIZE,), in_specs=[smem, smem, tile(t...  10.9 us
    all_to_all x1, blocking collectives, per_device(): stats = lax.all_to_all(stats, 'gx', 0, 0, tiled=True)  8.63 us
    pallas_call x1, Pallas kernels, per_device(): pl.pallas_call(scores_kernel, grid=(X_SIZE,), in_specs=[smem, smem, tile(...  6.21 us
    all_to_all x1, starting transfers between devices, per_device(): lax.all_to_all(type_part.reshape(Z_SIZE, block_rows, width), 'gz', 0, 0,...  5.02 us
  transfers between devices with their start and end apart: 9, of which 8 were waited for; matrix products, arithmetic and copies ran while one was open for 1% of the time, Pallas kernels for 1%

profile of v3, /device:TPU:1, one launch (start us, length us, event | category | flops | bytes accessed | tf_op | source)
XLA Modules:
  0.0 149.7 jit_solution(12191898710833790852)
XLA Ops:
  7.2 2.5 %pack.1 = (bf16[272,768]{1,0:T(8,128)(2,1)}, bf16[8,128,768]{2,1,0:T(8,128)(2,1)}) custom-call(s32[2,16]{1,0:T(2,128)} %refs_0_.1, s32[1,2]{1,0:T(1,128)} %bitcast.24, s32[1,256]{1,0:T(1,128)} %bitcast.22, s32[1,256]{1,0:T(1,128)} %bitcast.23, bf16[256,768]{1,0:T(8,128)(2,1)} %refs_4_.1, f32[128,768]{1,0:T(8,128)} %table_ref.1), custom_call_target="tpu_custom_call" | custom-call | tf_op jit(solution)/shard_map/pack/pallas_call | solution.py:221
  9.7 10.9 %all-to-all-start = ((bf16[8,128,768]{2,1,0:T(8,128)(2,1)}), bf16[8,128,768]{2,1,0:T(8,128)(2,1)S(1)}, u32[]{:S(2)}, u32[]{:S(2)}) async-start(bf16[8,128,768]{2,1,0:T(8,128)(2,1)} %get-tuple-element.16), calls=%async_computation | async-start | bytes 3145728 | tf_op jit(solution)/shard_map/all_to_all | solution.py:246
  20.6 0.0 all-gather.2.cloned.1.call-start
  20.6 0.7 all-gather.2.cloned.1.call-update
  21.3 0.0 reduce-scatter.2.cloned.1.call-start
  22.0 36.0 %all-gather.2.cloned.1.call-done = bf16[1088,768]{1,0:T(8,128)(2,1)} async-done(((bf16[272,768]{1,0:T(8,128)(2,1)}), bf16[1088,768]{1,0:T(8,128)(2,1)}) %all-gather.2.cloned.1.call-update) | async-done | bytes 1671184 | tf_op jit(solution)/shard_map/all_gather | solution.py:247
  58.0 0.8 all-to-all-done
  58.9 6.2 %scores.1 = (f32[4,1024,256]{2,1,0:T(8,128)}, f32[4,8,1024]{2,1,0:T(8,128)S(1)}) custom-call(f32[1]{0:T(128)S(6)} %copy.16.factor_ref, s32[1]{0:T(128)} %bitcast.place_ref, bf16[4,272,768]{2,1,0:T(8,128)(2,1)} %bitcast.19, bf16[1024,768]{1,0:T(8,128)(2,1)S(1)} %bitcast.17), custom_call_target="tpu_custom_call" | custom-call | tf_op jit(solution)/shard_map/scores/pallas_call | solution.py:250
  65.1 0.0 copy-done
  65.1 8.6 %all_to_all.20.stat_ref = f32[4,8,1024]{2,1,0:T(8,128)S(1)} all-to-all(f32[4,8,1024]{2,1,0:T(8,128)S(1)} %get-tuple-element.18), channel_id=1, replica_groups=mesh['gz'=8,'gx'=4,'gy'=16] {'gx'}, dimensions={0} | all-to-all | bytes 262144 | tf_op jit(solution)/shard_map/all_to_all | solution.py:262
  73.7 10.9 %grads.1 = (bf16[4,256,768]{2,1,0:T(8,128)(2,1)}, bf16[1024,768]{1,0:T(8,128)(2,1)}, f32[1,128]{1,0:T(1,128)S(1)}) custom-call(f32[1]{0:T(128)S(6)} %copy.16.factor_ref, s32[1]{0:T(128)} %bitcast.place_ref, f32[4,1024,256]{2,1,0:T(8,128)} %get-tuple-element.17.raw_ref, f32[4,8,1024]{2,1,0:T(8,128)S(1)} %all_to_all.20.stat_ref, ...), custom_call_target="tpu_custom_call" | custom-call | tf_op jit(solution)/shard_map/grads/pallas_call | solution.py:263
  84.6 0.0 reduce-scatter.2.cloned.1.call-update
  84.6 0.0 copy-start.1
  84.6 0.0 copy-start.2
  84.6 0.0 copy-start.3
  84.6 5.0 %all-to-all-start.2 = ((bf16[8,128,768]{2,1,0:T(8,128)(2,1)}), bf16[8,128,768]{2,1,0:T(8,128)(2,1)S(1)}, u32[]{:S(2)}, u32[]{:S(2)}) async-start(bf16[8,128,768]{2,1,0:T(8,128)(2,1)} %bitcast.21), calls=%async_computation.2 | async-start | bytes 3145728 | tf_op jit(solution)/shard_map/all_to_all | solution.py:288
  89.7 4.7 %collective-permute-start = (f32[1,128]{1,0:T(1,128)S(1)}, f32[1,128]{1,0:T(1,128)S(1)}, u32[]{:S(2)}, u32[]{:S(2)}) collective-permute-start(f32[1,128]{1,0:T(1,128)S(1)} %get-tuple-element.24), channel_id=1, source_target_pairs={{0,1},{1,0},{2,3},{3,2},{4,5},{5,4},{6,7},{7,6},{8,9},{9,8},{10,11... | collective-permute-start | bytes 1544 | tf_op jit(solution)/shard_map/ppermute | solution.py:189
  94.4 0.8 collective-permute-done
  95.2 3.2 %collective-permute-start.1 = (f32[1,128]{1,0:T(1,128)S(1)}, f32[1,128]{1,0:T(1,128)S(1)}, u32[]{:S(2)}, u32[]{:S(2)}) collective-permute-start(f32[1,128]{1,0:T(1,128)S(1)} %add.17), channel_id=1, source_target_pairs={{0,2},{1,3},{2,0},{3,1},{4,6},{5,7},{6,4},{7,5},{8,10},{9,11},{10,... | collective-permute-start | bytes 1544 | tf_op jit(solution)/shard_map/ppermute | solution.py:189
  98.4 1.4 collective-permute-done.1
  99.7 4.2 %collective-permute-start.2 = (f32[1,128]{1,0:T(1,128)S(1)}, f32[1,128]{1,0:T(1,128)S(1)}, u32[]{:S(2)}, u32[]{:S(2)}) collective-permute-start(f32[1,128]{1,0:T(1,128)S(1)} %add.18), channel_id=1, source_target_pairs={{0,4},{1,5},{2,6},{3,7},{4,0},{5,1},{6,2},{7,3},{8,12},{9,13},{10,... | collective-permute-start | bytes 1544 | tf_op jit(solution)/shard_map/ppermute | solution.py:189
  104.0 1.4 collective-permute-done.2
  105.3 7.6 %collective-permute-start.3 = (f32[1,128]{1,0:T(1,128)S(1)}, f32[1,128]{1,0:T(1,128)S(1)}, u32[]{:S(2)}, u32[]{:S(2)}) collective-permute-start(f32[1,128]{1,0:T(1,128)S(1)} %add.19), channel_id=1, source_target_pairs={{0,8},{1,9},{2,10},{3,11},{4,12},{5,13},{6,14},{7,15},{8,0},{9,1},... | collective-permute-start | bytes 1544 | tf_op jit(solution)/shard_map/ppermute | solution.py:189
  112.9 0.9 collective-permute-done.3
  113.8 16.3 %all-to-all-done.2.part_ref = bf16[8,128,768]{2,1,0:T(8,128)(2,1)S(1)} async-done(((bf16[8,128,768]{2,1,0:T(8,128)(2,1)}), bf16[8,128,768]{2,1,0:T(8,128)(2,1)S(1)}, u32[]{:S(2)}, u32[]{:S(2)}) %all-to-all-start.2) | async-done | bytes 1572896 | tf_op jit(solution)/shard_map/all_to_all | solution.py:288
  130.1 0.6 broadcast_in_dim.9
  130.7 3.3 %all-to-all-start.3 = ((f32[8,1,128]{2,1,0:T(1,128)}), f32[8,1,128]{2,1,0:T(1,128)S(1)}, u32[]{:S(2)}, u32[]{:S(2)}) async-start(f32[8,1,128]{2,1,0:T(1,128)} %broadcast_in_dim.9), calls=%async_computation.4 | async-start | bytes 8192 | tf_op jit(solution)/shard_map/all_to_all | solution.py:295
  134.0 0.0 copy-done.1
  134.1 1.8 %adam.1 = (f32[128,768]{1,0:T(8,128)}, f32[128,768]{1,0:T(8,128)}, f32[128,768]{1,0:T(8,128)}) custom-call(bf16[8,128,768]{2,1,0:T(8,128)(2,1)S(1)} %all-to-all-done.2.part_ref, f32[128,768]{1,0:T(8,128)S(1)} %copy-done.1, f32[128,768]{1,0:T(8,128)S(1)} %copy-done.2, f32[128,768]{1,0:T(8,128)S(1)} %copy-done.3), custom_call_target="tpu_custom_call" | custom-call | tf_op jit(solution)/shard_map/adam/pallas_call | solution.py:301
  135.9 4.6 %all-to-all-done.3 = f32[8,1,128]{2,1,0:T(1,128)S(1)} async-done(((f32[8,1,128]{2,1,0:T(1,128)}), f32[8,1,128]{2,1,0:T(1,128)S(1)}, u32[]{:S(2)}, u32[]{:S(2)}) %all-to-all-start.3) | async-done | bytes 4128 | tf_op jit(solution)/shard_map/all_to_all | solution.py:295
  140.5 0.6 slice_reduce_fusion
  141.7 0.0 reduce-scatter.2.cloned.1.call-done
  (7 shorter events, 0.0 us)
Async XLA Ops:
  9.7 49.1 %all-to-all-start = ((bf16[8,128,768]{2,1,0:T(8,128)(2,1)}), bf16[8,128,768]{2,1,0:T(8,128)(2,1)S(1)}, u32[]{:S(2)}, u32[]{:S(2)}) async-start(bf16[8,128,768]{2,1,0:T(8,128)(2,1)} %get-tuple-element.16), calls=%async_computation | async-start | bytes 3145728 | tf_op jit(solution)/shard_map/all_to_all | solution.py:246
  20.6 37.4 %all-gather.2.cloned.1.call-start = ((), (), s32[]{:S(2)}) async-start(), calls=%async_computation.5 | async-start | bytes 2088960 | tf_op jit(solution)/shard_map/all_gather | solution.py:247
  21.3 120.4 %reduce-scatter.2.cloned.1.call-start = ((), (), s32[]{:S(2)}) async-start(), calls=%async_computation.6 | async-start | bytes 1966080 | tf_op jit(solution)/shard_map/reduce_scatter | solution.py:291
  58.9 6.2 %copy-start = (bf16[8,128,768]{2,1,0:T(8,128)(2,1)}, bf16[8,128,768]{2,1,0:T(8,128)(2,1)S(1)}, u32[]{:S(2)}) copy-start(bf16[8,128,768]{2,1,0:T(8,128)(2,1)S(1)} %all-to-all-done) | copy-start | bytes 4718596
  84.6 49.4 %copy-start.1 = (f32[128,768]{1,0:T(8,128)S(1)}, f32[128,768]{1,0:T(8,128)}, u32[]{:S(2)}) copy-start(f32[128,768]{1,0:T(8,128)} %table_ref.1) | copy-start | bytes 1179652
  84.6 49.4 %copy-start.2 = (f32[128,768]{1,0:T(8,128)S(1)}, f32[128,768]{1,0:T(8,128)}, u32[]{:S(2)}) copy-start(f32[128,768]{1,0:T(8,128)} %m_ref.1) | copy-start | bytes 1179652
  84.6 49.4 %copy-start.3 = (f32[128,768]{1,0:T(8,128)S(1)}, f32[128,768]{1,0:T(8,128)}, u32[]{:S(2)}) copy-start(f32[128,768]{1,0:T(8,128)} %v_ref.1) | copy-start | bytes 1179652
  84.6 45.5 %all-to-all-start.2 = ((bf16[8,128,768]{2,1,0:T(8,128)(2,1)}), bf16[8,128,768]{2,1,0:T(8,128)(2,1)S(1)}, u32[]{:S(2)}, u32[]{:S(2)}) async-start(bf16[8,128,768]{2,1,0:T(8,128)(2,1)} %bitcast.21), calls=%async_computation.2 | async-start | bytes 3145728 | tf_op jit(solution)/shard_map/all_to_all | solution.py:288
  89.7 5.5 %collective-permute-start = (f32[1,128]{1,0:T(1,128)S(1)}, f32[1,128]{1,0:T(1,128)S(1)}, u32[]{:S(2)}, u32[]{:S(2)}) collective-permute-start(f32[1,128]{1,0:T(1,128)S(1)} %get-tuple-element.24), channel_id=1, source_target_pairs={{0,1},{1,0},{2,3},{3,2},{4,5},{5,4},{6,7},{7,6},{8,9},{9,8},{10,11... | collective-permute-start | bytes 1544 | tf_op jit(solution)/shard_map/ppermute | solution.py:189
  95.2 4.6 %collective-permute-start.1 = (f32[1,128]{1,0:T(1,128)S(1)}, f32[1,128]{1,0:T(1,128)S(1)}, u32[]{:S(2)}, u32[]{:S(2)}) collective-permute-start(f32[1,128]{1,0:T(1,128)S(1)} %add.17), channel_id=1, source_target_pairs={{0,2},{1,3},{2,0},{3,1},{4,6},{5,7},{6,4},{7,5},{8,10},{9,11},{10,... | collective-permute-start | bytes 1544 | tf_op jit(solution)/shard_map/ppermute | solution.py:189
  99.7 5.6 %collective-permute-start.2 = (f32[1,128]{1,0:T(1,128)S(1)}, f32[1,128]{1,0:T(1,128)S(1)}, u32[]{:S(2)}, u32[]{:S(2)}) collective-permute-start(f32[1,128]{1,0:T(1,128)S(1)} %add.18), channel_id=1, source_target_pairs={{0,4},{1,5},{2,6},{3,7},{4,0},{5,1},{6,2},{7,3},{8,12},{9,13},{10,... | collective-permute-start | bytes 1544 | tf_op jit(solution)/shard_map/ppermute | solution.py:189
  105.3 8.5 %collective-permute-start.3 = (f32[1,128]{1,0:T(1,128)S(1)}, f32[1,128]{1,0:T(1,128)S(1)}, u32[]{:S(2)}, u32[]{:S(2)}) collective-permute-start(f32[1,128]{1,0:T(1,128)S(1)} %add.19), channel_id=1, source_target_pairs={{0,8},{1,9},{2,10},{3,11},{4,12},{5,13},{6,14},{7,15},{8,0},{9,1},... | collective-permute-start | bytes 1544 | tf_op jit(solution)/shard_map/ppermute | solution.py:189
  130.7 9.8 %all-to-all-start.3 = ((f32[8,1,128]{2,1,0:T(1,128)}), f32[8,1,128]{2,1,0:T(1,128)S(1)}, u32[]{:S(2)}, u32[]{:S(2)}) async-start(f32[8,1,128]{2,1,0:T(1,128)} %broadcast_in_dim.9), calls=%async_computation.4 | async-start | bytes 8192 | tf_op jit(solution)/shard_map/all_to_all | solution.py:295
Sparse Core Ops, SparseCore 0:
  23.5 34.4 all-gather.1
  84.7 28.8 reduce-scatter.1

commit v4 on v3

v4 whole, which is shorter than its diff:
```python
import jax
import jax.numpy as jnp
from jax import lax
from jax.experimental import pallas as pl
from jax.experimental.pallas import tpu as pltpu
from jax.sharding import Mesh, PartitionSpec as P

beta_one = 0.9
beta_two = 0.999
learn_rate = 0.02
adam_eps = 1e-08
first_fix = 0.9999734386011124
second_fix = 0.09520785288629038

X_SIZE = 4
Z_SIZE = 8
BLOCK = 128
LOW = -1e30
META_ROWS = 16
SLOTS = 16
STAT_ROWS = 8
f32 = jnp.float32
bf16 = jnp.bfloat16


def pack_kernel(
    cols, list_hbm, len_hbm, slot_hbm, row_hbm, m_hbm, out_ref, list_ref, len_ref, slot_ref, row_ref, sems
):
    rows, width = m_hbm.shape
    pairs = [(list_hbm, list_ref), (len_hbm, len_ref), (slot_hbm, slot_ref), (row_hbm, row_ref)]
    pairs += [(m_hbm, out_ref.at[x, pl.ds(0, rows), :]) for x in range(X_SIZE)]
    copies = [pltpu.make_async_copy(src, dst, sems.at[i]) for i, (src, dst) in enumerate(pairs)]
    for copy in copies:
        copy.start()
    for copy in copies[:4]:
        copy.wait()
    owners = lax.div(list_ref[...], cols).astype(f32)
    lens = len_ref[...]
    first = lax.broadcasted_iota(jnp.int32, (1, rows), 1) < BLOCK
    length = jnp.where(first, lens[:, 0:1], lens[:, 1:2])
    slot = slot_ref[...]
    gold = jnp.zeros((1, rows), f32)
    parts = []
    for k in range(SLOTS):
        owner = jnp.where(first, owners[0:1, k : k + 1], owners[1:2, k : k + 1])
        gold = gold + jnp.where(slot == k, owner, 0.0)
        parts.append(jnp.where(length > k, owner, -1.0))
    parts += [gold, row_ref[...].astype(f32)]
    per_row = width // rows
    lines = [
        jnp.concatenate(parts[i : i + per_row], axis=1) for i in range(0, len(parts), per_row)
    ]
    lines.append(jnp.zeros((META_ROWS - len(lines), width), f32))
    meta = jnp.concatenate(lines, axis=0).astype(bf16)
    for x in range(X_SIZE):
        out_ref[x, rows : rows + META_ROWS, :] = meta
    for copy in copies[4:]:
        copy.wait()


def read_meta(m_ref, rows):
    meta = m_ref[0, rows : rows + META_ROWS, :].astype(f32)
    per_row = meta.shape[1] // rows
    parts = [
        meta[i // per_row : i // per_row + 1, (i % per_row) * rows : (i % per_row + 1) * rows]
        for i in range(SLOTS + 2)
    ]
    owners = jnp.concatenate(parts[:SLOTS], axis=0)
    return owners, parts[SLOTS], parts[SLOTS + 1].astype(jnp.int32)


def listed_in(owners, owner):
    return jnp.max(jnp.where(owners == owner, 1.0, 0.0), axis=0, keepdims=True) > 0.0


def owner_at(place_ref, line):
    return (line * X_SIZE + place_ref[0]).astype(f32)


def scores_kernel(factor_ref, place_ref, m_ref, t_ref, exp_ref, stat_ref, raw_ref):
    step = pl.program_id(0)
    factor = factor_ref[0]
    rows = m_ref.shape[1] - META_ROWS
    raw_ref[...] = lax.dot_general(
        t_ref[...], m_ref[0, 0:rows, :], (((1,), (1,)), ((), ())), preferred_element_type=f32
    )
    owners, gold_owner, gold_row = read_meta(m_ref, rows)
    ids = lax.broadcasted_iota(jnp.int32, (BLOCK, rows), 0)
    top = jnp.full((1, rows), LOW, f32)
    gold_raw = jnp.zeros((1, rows), f32)
    lives = []
    for c in range(Z_SIZE):
        owner = owner_at(place_ref, c)
        lives.append(listed_in(owners, owner))
        raw = raw_ref[c * BLOCK : (c + 1) * BLOCK, :]
        top = jnp.maximum(top, jnp.where(lives[c], jnp.max(raw, axis=0, keepdims=True), LOW))
        gold = jnp.where(gold_owner == owner, gold_row, -1)
        gold_raw = gold_raw + jnp.sum(jnp.where(ids == gold, raw, 0.0), axis=0, keepdims=True)
    total = jnp.zeros((1, rows), f32)
    mass = jnp.zeros((1, rows), f32)
    for c in range(Z_SIZE):
        below = jnp.where(lives[c], top, -LOW)
        gap = raw_ref[c * BLOCK : (c + 1) * BLOCK, :] - below
        weights = jnp.exp(factor * gap)
        exp_ref[0, c * BLOCK : (c + 1) * BLOCK, :] = weights
        total = total + jnp.sum(weights, axis=0, keepdims=True)
        mass = mass + jnp.sum(weights * gap, axis=0, keepdims=True)
    stat = jnp.concatenate(
        [top, total, mass, gold_raw, jnp.zeros((STAT_ROWS - 4, rows), f32)], axis=0
    )
    for d in range(stat_ref.shape[0]):
        stat_ref[d, :, pl.ds(pl.multiple_of(step * rows, BLOCK), rows)] = stat


def grads_kernel(
    factor_ref, place_ref, exp_ref, stat_ref, m_ref, g_ref, type_ref, scale_ref, acc_ref, sum_ref
):
    step = pl.program_id(0)
    factor = factor_ref[0]
    rows = m_ref.shape[1] - META_ROWS
    tops = stat_ref[:, 0, :]
    sums = stat_ref[:, 1, :]
    top = jnp.max(tops, axis=0, keepdims=True)
    shares = jnp.exp(factor * (tops - top))
    total = jnp.sum(sums * shares, axis=0, keepdims=True)
    masses = stat_ref[:, 2, :] + sums * tops
    mass = jnp.sum(jnp.where(sums > 0.0, masses * shares, 0.0), axis=0, keepdims=True)
    scale = mass / total - jnp.sum(stat_ref[:, 3, :], axis=0, keepdims=True)
    ids = lax.broadcasted_iota(jnp.int32, (X_SIZE, rows), 0)
    own = jnp.max(jnp.where(ids == place_ref[0], tops, LOW), axis=0, keepdims=True)
    share = jnp.exp(factor * (own - top) - jnp.log(total))
    _, gold_owner, gold_row = read_meta(m_ref, rows)
    ids = lax.broadcasted_iota(jnp.int32, (BLOCK, rows), 0)
    for c in range(Z_SIZE):
        gold = jnp.where(gold_owner == owner_at(place_ref, c), gold_row, -1)
        weights = share * exp_ref[0, c * BLOCK : (c + 1) * BLOCK, :]
        grad = weights - jnp.where(ids == gold, 1.0, 0.0)
        g_ref[0, c * BLOCK : (c + 1) * BLOCK, :] = grad.astype(bf16)
    part = jnp.dot(g_ref[0], m_ref[0, 0:rows, :], preferred_element_type=f32)

    @pl.when(step == 0)
    def _():
        acc_ref[...] = part
        sum_ref[...] = scale

    @pl.when(step > 0)
    def _():
        acc_ref[...] += part
        sum_ref[...] += scale

    @pl.when(step == pl.num_programs(0) - 1)
    def _():
        type_ref[...] = (factor * acc_ref[...]).astype(bf16)
        scale_ref[...] = jnp.broadcast_to(
            jnp.sum(sum_ref[...], axis=1, keepdims=True), scale_ref.shape
        )


def mention_kernel(factor_ref, scale_ref, g_ref, t_ref, out_ref, scales_ref):
    part = lax.dot_general(
        g_ref[0], t_ref[...], (((0,), (0,)), ((), ())), preferred_element_type=f32
    )
    out_ref[0] = (factor_ref[0] * part).astype(bf16)

    @pl.when(pl.program_id(0) == 0)
    def _():
        scales_ref[...] = jnp.broadcast_to(scale_ref[...][None], scales_ref.shape)


def adam_rows(type_table, adam_m, adam_v, type_grad):
    moment_one = beta_one * adam_m + (1.0 - beta_one) * type_grad
    moment_two = beta_two * adam_v + (1.0 - beta_two) * type_grad * type_grad
    updated = type_table - learn_rate * (moment_one / first_fix) / (
        jnp.sqrt(moment_two / second_fix) + adam_eps
    )
    return (updated, moment_one, moment_two)


def params():
    return pltpu.CompilerParams(vmem_limit_bytes=60 * 1024 * 1024)


def per_device(
    mentions,
    type_table,
    adam_m,
    adam_v,
    logit_scale,
    block_lists,
    list_lengths,
    gold_slot,
    gold_row,
):
    cols = lax.axis_size("gy")
    devices = Z_SIZE * X_SIZE * cols
    block_rows, width = type_table.shape
    rows = mentions.shape[0]
    sent_rows = rows + META_ROWS
    types = Z_SIZE * block_rows
    smem = pl.BlockSpec(memory_space=pltpu.SMEM)
    hbm = pl.BlockSpec(memory_space=pltpu.HBM)
    place = lax.axis_index("gx").reshape(1).astype(jnp.int32)

    def tile(*shape):
        return pl.BlockSpec((1,) + shape, lambda j: (j, 0, 0))

    def whole(*shape):
        return pl.BlockSpec(shape, lambda j: (0,) * len(shape))

    table = lax.all_gather(type_table.astype(bf16), "gz", axis=0, tiled=True)
    packed = pl.pallas_call(
        lambda *refs: pack_kernel(cols, *refs),
        in_specs=[hbm] * 5,
        out_shape=jax.ShapeDtypeStruct((X_SIZE, sent_rows, width), bf16),
        scratch_shapes=[
            pltpu.VMEM((2, SLOTS), jnp.int32),
            pltpu.VMEM((1, 2), jnp.int32),
            pltpu.VMEM((1, rows), jnp.int32),
            pltpu.VMEM((1, rows), jnp.int32),
            pltpu.SemaphoreType.DMA((4 + X_SIZE,)),
        ],
        compiler_params=params(),
        name="pack",
    )(
        block_lists,
        list_lengths.reshape(1, 2),
        gold_slot.reshape(1, rows),
        gold_row.reshape(1, rows),
        mentions,
    )
    gathered = lax.all_to_all(packed, "gx", 0, 0, tiled=True)

    exps, stats = pl.pallas_call(
        scores_kernel,
        grid=(X_SIZE,),
        in_specs=[smem, smem, tile(sent_rows, width), whole(types, width)],
        out_specs=[tile(types, rows), whole(X_SIZE, STAT_ROWS, X_SIZE * rows)],
        out_shape=[
            jax.ShapeDtypeStruct((X_SIZE, types, rows), f32),
            jax.ShapeDtypeStruct((X_SIZE, STAT_ROWS, X_SIZE * rows), f32),
        ],
        scratch_shapes=[pltpu.VMEM((types, rows), f32)],
        compiler_params=params(),
        name="scores",
    )(logit_scale, place, gathered, table)
    stats = lax.all_to_all(stats, "gx", 0, 0, tiled=True)
    grads, type_part, scale_part = pl.pallas_call(
        grads_kernel,
        grid=(X_SIZE,),
        in_specs=[
            smem,
            smem,
            tile(types, rows),
            pl.BlockSpec((X_SIZE, STAT_ROWS, rows), lambda j: (0, 0, j)),
            tile(sent_rows, width),
        ],
        out_specs=[tile(types, rows), whole(types, width), whole(1, 128)],
        out_shape=[
            jax.ShapeDtypeStruct((X_SIZE, types, rows), bf16),
            jax.ShapeDtypeStruct((types, width), bf16),
            jax.ShapeDtypeStruct((1, 128), f32),
        ],
        scratch_shapes=[pltpu.VMEM((types, width), f32), pltpu.VMEM((1, rows), f32)],
        compiler_params=params(),
        name="grads",
    )(logit_scale, place, exps, stats, gathered)
    type_grad = lax.psum_scatter(type_part, "gz", scatter_dimension=0, tiled=True)
    mention_part, scale_parts = pl.pallas_call(
        mention_kernel,
        grid=(X_SIZE,),
        in_specs=[smem, whole(1, 128), tile(types, rows), whole(types, width)],
        out_specs=[tile(rows, width), whole(Z_SIZE * cols, 1, 128)],
        out_shape=[
            jax.ShapeDtypeStruct((X_SIZE, rows, width), bf16),
            jax.ShapeDtypeStruct((Z_SIZE * cols, 1, 128), f32),
        ],
        compiler_params=params(),
        name="mention_part",
    )(logit_scale, scale_part, grads, table)
    mention_grad = lax.all_to_all(mention_part, "gx", 0, 0, tiled=True)
    mention_grad = jnp.sum(mention_grad, axis=0, dtype=f32).astype(bf16)
    scale_parts = lax.all_to_all(scale_parts, ("gz", "gy"), 0, 0, tiled=True)
    scale_grad = (jnp.sum(scale_parts[:, 0, 0]) / (rows * devices)).reshape(1)
    new_table, new_first, new_second = adam_rows(
        type_table, adam_m, adam_v, type_grad.astype(f32)
    )
    return (new_table, new_first, new_second, mention_grad, scale_grad)


def solution(mesh):
    gx, gy = mesh.devices.shape
    split = Mesh(mesh.devices.reshape(gx // X_SIZE, X_SIZE, gy), ("gz", "gx", "gy"))
    axes = ("gz", "gx", "gy")
    rows = P(axes, None)
    return jax.shard_map(
        per_device,
        mesh=split,
        in_specs=(rows, rows, rows, rows, P(), rows, P(axes), P(axes), P(axes)),
        out_specs=(rows, rows, rows, rows, P()),
        check_vma=False,
    )
```

time: 150 us -> 148 us (0.987)
  starting transfers between devices: 39 us -> 8.46 us
  blocking collectives: 8.63 us -> 37.2 us
  waiting for transfers between devices: 62.8 us -> 56.8 us
  other arithmetic: 0.62 us -> 5.58 us
    all_to_all x0 -> x1, blocking collectives: none -> 28.3 us  [per_device(): scale_parts = lax.all_to_all(scale_parts, ('gz', 'gy'), 0, 0, tiled=True)]
    ppermute x4 -> x0, starting transfers between devices: 19.7 us -> none  [doubled(): lax.ppermute(value, axis, [(i, i ^ by) for i in range(size)])]
    all_gather x1, waiting for transfers between devices: 36 us -> 22.8 us  [per_device(): table = lax.all_gather(type_table.astype(bf16), 'gz', axis=0, tiled=True)]
    all_to_all x3 -> x2, waiting for transfers between devices: 21.7 us -> 34 us  [the longest x1 18.8 us: per_device(): mention_grad = lax.all_to_all(mention_part, 'gx', 0, 0, tiled=True)]
    all_to_all x3 -> x2, starting transfers between devices: 19.2 us -> 8.42 us  [the longest x1 4.85 us: per_device(): gathered = lax.all_to_all(packed, 'gx', 0, 0, tiled=True)]
    ppermute x4 -> x0, waiting for transfers between devices: 4.43 us -> none  [doubled(): lax.ppermute(value, axis, [(i, i ^ by) for i in range(size)])]
    pallas_call x2, Pallas kernels: 4.39 us -> 8.29 us  [the longest x1 5.53 us: per_device(): pl.pallas_call(mention_kernel, grid=(X_SIZE,), in_specs=[smem, whole(1, 1...]
    pallas_call x1, Pallas kernels: 10.9 us -> 7.52 us  [per_device(): pl.pallas_call(grads_kernel, grid=(X_SIZE,), in_specs=[smem, smem, tile(t...]
  transfers between devices with their start and end apart: 9 -> 4, of which waited for: 8 -> 3; matrix products, arithmetic and copies ran while one was open for 1% -> 1% of each run, Pallas kernels for 1% -> 6%
where the time goes in v4:
time: 148 us; the launch traced here: 147 us
  waiting for transfers between devices  56.8 us (38%)
  blocking collectives  37.2 us (25%)
  Pallas kernels  22.5 us (15%)
  between operations  16.5 us (11%)
  starting transfers between devices  8.46 us (6%)
  other arithmetic  5.58 us (4%)
    all_to_all x1, blocking collectives, per_device(): scale_parts = lax.all_to_all(scale_parts, ('gz', 'gy'), 0, 0, tiled=True)  28.3 us
    all_gather x1, waiting for transfers between devices, per_device(): table = lax.all_gather(type_table.astype(bf16), 'gz', axis=0, tiled=True)  22.8 us
    all_to_all x1, waiting for transfers between devices, per_device(): mention_grad = lax.all_to_all(mention_part, 'gx', 0, 0, tiled=True)  18.8 us
    all_to_all x1, waiting for transfers between devices, per_device(): gathered = lax.all_to_all(packed, 'gx', 0, 0, tiled=True)  15.3 us
    all_to_all x1, blocking collectives, per_device(): stats = lax.all_to_all(stats, 'gx', 0, 0, tiled=True)  8.91 us
    pallas_call x1, Pallas kernels, per_device(): pl.pallas_call(grads_kernel, grid=(X_SIZE,), in_specs=[smem, smem, tile(t...  7.52 us
    pallas_call x1, Pallas kernels, per_device(): pl.pallas_call(scores_kernel, grid=(X_SIZE,), in_specs=[smem, smem, tile(...  6.69 us
    pallas_call x1, Pallas kernels, per_device(): pl.pallas_call(mention_kernel, grid=(X_SIZE,), in_specs=[smem, whole(1, 1...  5.53 us
  transfers between devices with their start and end apart: 4, of which 3 were waited for; matrix products, arithmetic and copies ran while one was open for 1% of the time, Pallas kernels for 6%

profile of v4, /device:TPU:1, one launch (start us, length us, event | category | flops | bytes accessed | tf_op | source)
XLA Modules:
  0.0 147.1 jit_solution(1542892312383779875)
XLA Ops:
  7.2 0.0 all-gather.2.cloned.1.call-start
  7.2 1.7 %convert_element_type.8 = bf16[128,768]{1,0:T(8,128)(2,1)} convert(f32[128,768]{1,0:T(8,128)} %param.10) | non-fusion elementwise | flops 98304 | bytes 589824 | tf_op jit(solution)/shard_map/convert_element_type | solution.py:210
  8.9 0.0 all-gather.2.cloned.1.call-update
  8.9 2.8 %pack.1 = bf16[4,272,768]{2,1,0:T(8,128)(2,1)} custom-call(s32[2,16]{1,0:T(2,128)} %refs_0_.1, s32[1,2]{1,0:T(1,128)} %bitcast.7, s32[1,256]{1,0:T(1,128)} %bitcast.5, s32[1,256]{1,0:T(1,128)} %bitcast.6, bf16[256,768]{1,0:T(8,128)(2,1)} %refs_4_.1), custom_call_target="tpu_custom_call" | custom-call | tf_op jit(solution)/shard_map/pack/pallas_call | solution.py:211
  11.7 4.9 %all-to-all-start = ((bf16[4,272,768]{2,1,0:T(8,128)(2,1)}), bf16[4,272,768]{2,1,0:T(8,128)(2,1)S(1)}, u32[]{:S(2)}, u32[]{:S(2)}) async-start(bf16[4,272,768]{2,1,0:T(8,128)(2,1)} %pack.1), calls=%async_computation | async-start | bytes 3342336 | tf_op jit(solution)/shard_map/all_to_all | solution.py:231
  16.5 0.0 reduce-scatter.2.cloned.1.call-start
  17.2 15.3 %all-to-all-done.m_ref = bf16[4,272,768]{2,1,0:T(8,128)(2,1)S(1)} async-done(((bf16[4,272,768]{2,1,0:T(8,128)(2,1)}), bf16[4,272,768]{2,1,0:T(8,128)(2,1)S(1)}, u32[]{:S(2)}, u32[]{:S(2)}) %all-to-all-start) | async-done | bytes 1671200 | tf_op jit(solution)/shard_map/all_to_all | solution.py:231
  32.5 0.0 copy-start
  32.5 22.8 %all-gather.2.cloned.1.call-done.t_ref = bf16[1024,768]{1,0:T(8,128)(2,1)} async-done(((bf16[128,768]{1,0:T(8,128)(2,1)}), bf16[1024,768]{1,0:T(8,128)(2,1)}) %all-gather.2.cloned.1.call-update) | async-done | bytes 1572880 | tf_op jit(solution)/shard_map/all_gather | solution.py:210
  55.2 0.0 copy-done
  55.2 6.7 %scores.1 = (f32[4,1024,256]{2,1,0:T(8,128)}, f32[4,8,1024]{2,1,0:T(8,128)}) custom-call(f32[1]{0:T(128)S(6)} %copy.14.factor_ref, s32[1]{0:T(128)} %bitcast.place_ref, bf16[4,272,768]{2,1,0:T(8,128)(2,1)} %copy-done, bf16[1024,768]{1,0:T(8,128)(2,1)} %all-gather.2.cloned.1.call-done.t_ref), custom_call_target="tpu_custom_call" | custom-call | tf_op jit(solution)/shard_map/scores/pallas_call | solution.py:233
  61.9 8.9 %all_to_all.20.stat_ref = f32[4,8,1024]{2,1,0:T(8,128)} all-to-all(f32[4,8,1024]{2,1,0:T(8,128)} %get-tuple-element.13), channel_id=1, replica_groups=mesh['gz'=8,'gx'=4,'gy'=16] {'gx'}, dimensions={0} | all-to-all | bytes 262144 | tf_op jit(solution)/shard_map/all_to_all | solution.py:246
  70.8 7.5 %grads.1 = (bf16[4,1024,256]{2,1,0:T(8,128)(2,1)}, bf16[1024,768]{1,0:T(8,128)(2,1)}, f32[1,128]{1,0:T(1,128)}) custom-call(f32[1]{0:T(128)S(6)} %copy.14.factor_ref, s32[1]{0:T(128)} %bitcast.place_ref, f32[4,1024,256]{2,1,0:T(8,128)} %get-tuple-element.12.exp_ref, f32[4,8,1024]{2,1,0:T(8,128)} %all_to_all.20.stat_ref, bf16[4,272,768]{2,1,0:T(8,128)(2,1)} %copy-done), custom_call_target="tpu_custom_call" | custom-call | tf_op jit(solution)/shard_map/grads/pallas_call | solution.py:247
  78.4 0.0 reduce-scatter.2.cloned.1.call-update
  78.4 5.5 %mention_part.1 = (bf16[4,256,768]{2,1,0:T(8,128)(2,1)}, f32[128,1,128]{2,1,0:T(1,128)}) custom-call(f32[1]{0:T(128)S(6)} %copy.14.factor_ref, f32[1,128]{1,0:T(1,128)} %get-tuple-element.15.scale_ref, bf16[4,1024,256]{2,1,0:T(8,128)(2,1)} %get-tuple-element.16.g_ref, bf16[1024,768]{1,0:T(8,128)(2,1)} %all-gather.2.cloned.1.call-done.t_ref), custom_call_target="tpu_custom_call" | custom-call | tf_op jit(solution)/shard_map/mention_part/pallas_call | solution.py:268
  83.9 28.3 %all_to_all.21 = f32[128,1,128]{2,1,0:T(1,128)S(1)} all-to-all(f32[128,1,128]{2,1,0:T(1,128)} %get-tuple-element.18), channel_id=1, replica_groups=mesh['gz'=8,'gx'=4,'gy'=16] {'gz','gy'}, dimensions={0} | all-to-all | bytes 131072 | tf_op jit(solution)/shard_map/all_to_all | solution.py:282
  112.2 3.6 %all-to-all-start.2 = ((bf16[4,256,768]{2,1,0:T(8,128)(2,1)}), bf16[4,256,768]{2,1,0:T(8,128)(2,1)S(1)}, u32[]{:S(2)}, u32[]{:S(2)}) async-start(bf16[4,256,768]{2,1,0:T(8,128)(2,1)} %get-tuple-element.17), calls=%async_computation.3 | async-start | bytes 3145728 | tf_op jit(solution)/shard_map/all_to_all | solution.py:280
  115.8 0.0 copy-start.1
  115.8 0.0 copy-start.2
  115.8 0.0 copy-start.3
  115.9 0.7 slice_reduce_fusion
  117.2 18.8 %all-to-all-done.2 = bf16[4,256,768]{2,1,0:T(8,128)(2,1)S(1)} async-done(((bf16[4,256,768]{2,1,0:T(8,128)(2,1)}), bf16[4,256,768]{2,1,0:T(8,128)(2,1)S(1)}, u32[]{:S(2)}, u32[]{:S(2)}) %all-to-all-start.2) | async-done | bytes 1572896 | tf_op jit(solution)/shard_map/all_to_all | solution.py:280
  136.0 1.1 reduce_sum.21
  137.1 0.0 reduce-scatter.2.cloned.1.call-done
  137.1 0.0 copy-done.1
  137.1 0.0 copy-done.2
  137.1 0.0 copy-done.3
  137.1 2.1 %divide_subtract_fusion = (f32[128,768]{1,0:T(8,128)}, f32[128,768]{1,0:T(8,128)}, f32[128,768]{1,0:T(8,128)}) fusion(f32[128,768]{1,0:T(8,128)S(1)} %copy-done.1, bf16[128,768]{1,0:T(8,128)(2,1)} %reduce-scatter.2.cloned.1.call-done, f32[128,768]{1,0:T(8,128)S(1)} %copy-done.2, f32[128,768]{1,0:T(8,128)S(1)} %copy-done.3), kind=kLoop, calls=%fused_computation.4 | loop fusion | flops 1277952 | bytes 2555904 | tf_op jit(solution)/shard_map/sub | solution.py:173
Async XLA Ops:
  7.2 48.1 %all-gather.2.cloned.1.call-start = ((), (), s32[]{:S(2)}) async-start(), calls=%async_computation.5 | async-start | bytes 1769472 | tf_op jit(solution)/shard_map/all_gather | solution.py:210
  11.7 20.8 %all-to-all-start = ((bf16[4,272,768]{2,1,0:T(8,128)(2,1)}), bf16[4,272,768]{2,1,0:T(8,128)(2,1)S(1)}, u32[]{:S(2)}, u32[]{:S(2)}) async-start(bf16[4,272,768]{2,1,0:T(8,128)(2,1)} %pack.1), calls=%async_computation | async-start | bytes 3342336 | tf_op jit(solution)/shard_map/all_to_all | solution.py:231
  16.5 120.5 %reduce-scatter.2.cloned.1.call-start = ((), (), s32[]{:S(2)}) async-start(), calls=%async_computation.6 | async-start | bytes 1769472 | tf_op jit(solution)/shard_map/reduce_scatter | solution.py:267
  32.5 22.8 %copy-start = (bf16[4,272,768]{2,1,0:T(8,128)(2,1)}, bf16[4,272,768]{2,1,0:T(8,128)(2,1)S(1)}, u32[]{:S(2)}) copy-start(bf16[4,272,768]{2,1,0:T(8,128)(2,1)S(1)} %all-to-all-done.m_ref) | copy-start | bytes 5013508
  112.2 23.8 %all-to-all-start.2 = ((bf16[4,256,768]{2,1,0:T(8,128)(2,1)}), bf16[4,256,768]{2,1,0:T(8,128)(2,1)S(1)}, u32[]{:S(2)}, u32[]{:S(2)}) async-start(bf16[4,256,768]{2,1,0:T(8,128)(2,1)} %get-tuple-element.17), calls=%async_computation.3 | async-start | bytes 3145728 | tf_op jit(solution)/shard_map/all_to_all | solution.py:280
  115.8 21.3 %copy-start.1 = (f32[128,768]{1,0:T(8,128)S(1)}, f32[128,768]{1,0:T(8,128)}, u32[]{:S(2)}) copy-start(f32[128,768]{1,0:T(8,128)} %param.10) | copy-start | bytes 1179652
  115.8 21.3 %copy-start.2 = (f32[128,768]{1,0:T(8,128)S(1)}, f32[128,768]{1,0:T(8,128)}, u32[]{:S(2)}) copy-start(f32[128,768]{1,0:T(8,128)} %param.11) | copy-start | bytes 1179652
  115.8 21.2 %copy-start.3 = (f32[128,768]{1,0:T(8,128)S(1)}, f32[128,768]{1,0:T(8,128)}, u32[]{:S(2)}) copy-start(f32[128,768]{1,0:T(8,128)} %param.12) | copy-start | bytes 1179652
Sparse Core Ops, SparseCore 0:
  10.7 44.5 all-gather.1
  78.5 42.5 reduce-scatter.1

commit v5 on v4

v5 whole, which is shorter than its diff:
```python
import jax
import jax.numpy as jnp
from jax import lax
from jax.experimental import pallas as pl
from jax.experimental.pallas import tpu as pltpu
from jax.sharding import Mesh, PartitionSpec as P

beta_one = 0.9
beta_two = 0.999
learn_rate = 0.02
adam_eps = 1e-08
first_fix = 0.9999734386011124
second_fix = 0.09520785288629038

X_SIZE = 4
Z_SIZE = 8
BLOCK = 128
LOW = -1e30
META_ROWS = 32
SLOTS = 16
STAT_ROWS = 8
f32 = jnp.float32
bf16 = jnp.bfloat16


def cast_kernel(t_ref, out_ref):
    block = t_ref[...].astype(bf16)
    for k in range(out_ref.shape[0]):
        out_ref[k] = block


def pack_kernel(
    cols, list_hbm, len_hbm, slot_hbm, row_hbm, m_hbm, out_ref, list_ref, len_ref, slot_ref, row_ref, sems
):
    rows, width = m_hbm.shape
    pairs = [(list_hbm, list_ref), (len_hbm, len_ref), (slot_hbm, slot_ref), (row_hbm, row_ref)]
    pairs.append((m_hbm, out_ref.at[pl.ds(0, rows), :]))
    copies = [pltpu.make_async_copy(src, dst, sems.at[i]) for i, (src, dst) in enumerate(pairs)]
    for copy in copies:
        copy.start()
    for copy in copies[:4]:
        copy.wait()
    owners = lax.div(list_ref[...], cols).astype(f32)
    lens = len_ref[...]
    first = lax.broadcasted_iota(jnp.int32, (1, rows), 1) < BLOCK
    length = jnp.where(first, lens[:, 0:1], lens[:, 1:2])
    slot = slot_ref[...]
    gold = jnp.zeros((1, rows), f32)
    lines = []
    for k in range(SLOTS):
        owner = jnp.where(first, owners[0:1, k : k + 1], owners[1:2, k : k + 1])
        gold = gold + jnp.where(slot == k, owner, 0.0)
        lines.append(jnp.where(length > k, owner, -1.0))
    lines += [gold, row_ref[...].astype(f32)]
    lines.append(jnp.zeros((META_ROWS - len(lines), rows), f32))
    out_ref[rows : rows + META_ROWS, :] = jnp.zeros((META_ROWS, width), bf16)
    out_ref[rows : rows + META_ROWS, 0:rows] = jnp.concatenate(lines, axis=0).astype(bf16)
    copies[4].wait()


def owner_at(place_ref, line):
    return (line * X_SIZE + place_ref[1]).astype(f32)


def tile_from(place_ref, step):
    return lax.rem(place_ref[1] - step + X_SIZE, X_SIZE)


def join_types(place_ref, near_ref, below_ref, above_ref, tile_ref):
    parity = lax.rem(place_ref[0], 2)
    half = Z_SIZE // 4
    for k in range(Z_SIZE // 2):
        other = below_ref[k] if k < half else above_ref[k - half]
        tile_ref[pl.ds(pl.multiple_of((2 * k + parity) * BLOCK, BLOCK), BLOCK), :] = near_ref[k]
        tile_ref[pl.ds(pl.multiple_of((2 * k + 1 - parity) * BLOCK, BLOCK), BLOCK), :] = other


def scores_kernel(
    factor_ref, place_ref, m_ref, near_ref, below_ref, above_ref, exp_ref, stat_ref, tile_ref, raw_ref
):
    step = pl.program_id(0)
    factor = factor_ref[0]
    rows = m_ref.shape[1] - META_ROWS

    @pl.when(step == 0)
    def _():
        join_types(place_ref, near_ref, below_ref, above_ref, tile_ref)

    raw_ref[...] = lax.dot_general(
        tile_ref[...], m_ref[0, 0:rows, :], (((1,), (1,)), ((), ())), preferred_element_type=f32
    )
    meta = m_ref[0, rows : rows + META_ROWS, 0:rows].astype(f32)
    owners = meta[0:SLOTS, :]
    gold_owner = meta[SLOTS : SLOTS + 1, :]
    gold_row = meta[SLOTS + 1 : SLOTS + 2, :].astype(jnp.int32)
    ids = lax.broadcasted_iota(jnp.int32, (BLOCK, rows), 0)
    top = jnp.full((1, rows), LOW, f32)
    gold_raw = jnp.zeros((1, rows), f32)
    lives = []
    for c in range(Z_SIZE):
        owner = owner_at(place_ref, c)
        lives.append(jnp.max(jnp.where(owners == owner, 1.0, 0.0), axis=0, keepdims=True) > 0.0)
        raw = raw_ref[c * BLOCK : (c + 1) * BLOCK, :]
        top = jnp.maximum(top, jnp.where(lives[c], jnp.max(raw, axis=0, keepdims=True), LOW))
        gold = jnp.where(gold_owner == owner, gold_row, -1)
        gold_raw = gold_raw + jnp.sum(jnp.where(ids == gold, raw, 0.0), axis=0, keepdims=True)
    total = jnp.zeros((1, rows), f32)
    mass = jnp.zeros((1, rows), f32)
    for c in range(Z_SIZE):
        below = jnp.where(lives[c], top, -LOW)
        gap = raw_ref[c * BLOCK : (c + 1) * BLOCK, :] - below
        weights = jnp.exp(factor * gap)
        exp_ref[0, c * BLOCK : (c + 1) * BLOCK, :] = weights
        total = total + jnp.sum(weights, axis=0, keepdims=True)
        mass = mass + jnp.sum(weights * gap, axis=0, keepdims=True)
    stat = jnp.concatenate(
        [top, total, mass, gold_raw, jnp.zeros((STAT_ROWS - 4, rows), f32)], axis=0
    )
    at = pl.multiple_of(tile_from(place_ref, step) * rows, BLOCK)
    for d in range(stat_ref.shape[0]):
        stat_ref[d, :, pl.ds(at, rows)] = stat


def merge_stats(factor, place_ref, stat_ref, share_ref, scale_ref):
    tops = stat_ref[:, 0, :]
    sums = stat_ref[:, 1, :]
    top = jnp.max(tops, axis=0, keepdims=True)
    shares = jnp.exp(factor * (tops - top))
    total = jnp.sum(sums * shares, axis=0, keepdims=True)
    masses = stat_ref[:, 2, :] + sums * tops
    mass = jnp.sum(jnp.where(sums > 0.0, masses * shares, 0.0), axis=0, keepdims=True)
    scale = mass / total - jnp.sum(stat_ref[:, 3, :], axis=0, keepdims=True)
    scale_ref[...] = jnp.broadcast_to(jnp.sum(scale, axis=1, keepdims=True), scale_ref.shape)
    ids = lax.broadcasted_iota(jnp.int32, tops.shape, 0)
    own = jnp.max(jnp.where(ids == place_ref[1], tops, LOW), axis=0, keepdims=True)
    share_ref[...] = jnp.exp(factor * (own - top) - jnp.log(total))


def grads_kernel(
    factor_ref, place_ref, exp_ref, stat_ref, m_ref, g_ref, type_ref, scale_ref, share_ref, rows_ref, grad_ref
):
    step = pl.program_id(0)
    factor = factor_ref[0]
    rows = m_ref.shape[1] - META_ROWS
    chunk = exp_ref.shape[1]

    @pl.when(step == 0)
    def _():
        merge_stats(factor, place_ref, stat_ref, share_ref, scale_ref)
        for s in range(X_SIZE):
            rows_ref[s * rows : (s + 1) * rows, :] = m_ref[s, 0:rows, :]

    ids = lax.broadcasted_iota(jnp.int32, (BLOCK, rows), 0)
    for s in range(X_SIZE):
        at = pl.multiple_of(tile_from(place_ref, s) * rows, BLOCK)
        share = share_ref[:, pl.ds(at, rows)]
        gold_owner = m_ref[s, rows + SLOTS : rows + META_ROWS, 0:rows].astype(f32)[0:1, :]
        gold_row = m_ref[s, rows + SLOTS : rows + META_ROWS, 0:rows].astype(f32)[1:2, :]
        for c in range(chunk // BLOCK):
            owner = owner_at(place_ref, step * (chunk // BLOCK) + c)
            gold = jnp.where(gold_owner == owner, gold_row, -1.0).astype(jnp.int32)
            weights = share * exp_ref[s, c * BLOCK : (c + 1) * BLOCK, :]
            grad = (weights - jnp.where(ids == gold, 1.0, 0.0)).astype(bf16)
            g_ref[s, c * BLOCK : (c + 1) * BLOCK, :] = grad
            grad_ref[c * BLOCK : (c + 1) * BLOCK, s * rows : (s + 1) * rows] = grad
    part = jnp.dot(grad_ref[...], rows_ref[...], preferred_element_type=f32)
    type_ref[...] = (factor * part).astype(bf16)


def mention_kernel(
    factor_ref, place_ref, scale_ref, g_ref, near_ref, below_ref, above_ref, *refs
):
    out_refs, (scales_ref, tile_ref) = refs[:X_SIZE], refs[X_SIZE:]
    step = pl.program_id(0)

    @pl.when(step == 0)
    def _():
        join_types(place_ref, near_ref, below_ref, above_ref, tile_ref)
        scales_ref[...] = jnp.broadcast_to(scale_ref[...][None], scales_ref.shape)

    part = lax.dot_general(
        g_ref[0], tile_ref[...], (((0,), (0,)), ((), ())), preferred_element_type=f32
    )
    part = (factor_ref[0] * part).astype(bf16)
    for s, out_ref in enumerate(out_refs):

        @pl.when(step == s)
        def _(out_ref=out_ref):
            out_ref[...] = part


def adam_rows(type_table, adam_m, adam_v, type_grad):
    moment_one = beta_one * adam_m + (1.0 - beta_one) * type_grad
    moment_two = beta_two * adam_v + (1.0 - beta_two) * type_grad * type_grad
    updated = type_table - learn_rate * (moment_one / first_fix) / (
        jnp.sqrt(moment_two / second_fix) + adam_eps
    )
    return (updated, moment_one, moment_two)


def params(mib=60):
    return pltpu.CompilerParams(vmem_limit_bytes=mib * 1024 * 1024)


def shifted(array, axis, by):
    size = lax.axis_size(axis)
    return lax.ppermute(array, axis, [(i, (i + by) % size) for i in range(size)])


def per_device(
    mentions,
    type_table,
    adam_m,
    adam_v,
    logit_scale,
    block_lists,
    list_lengths,
    gold_slot,
    gold_row,
):
    cols = lax.axis_size("gy")
    devices = Z_SIZE * X_SIZE * cols
    block_rows, width = type_table.shape
    rows = mentions.shape[0]
    sent_rows = rows + META_ROWS
    types = Z_SIZE * block_rows
    smem = pl.BlockSpec(memory_space=pltpu.SMEM)
    hbm = pl.BlockSpec(memory_space=pltpu.HBM)
    place = jnp.stack([lax.axis_index("gz"), lax.axis_index("gx")]).astype(jnp.int32)
    half = Z_SIZE // 2

    def tile(*shape):
        return pl.BlockSpec((1,) + shape, lambda j: (j, 0, 0))

    def whole(*shape):
        return pl.BlockSpec(shape, lambda j: (0,) * len(shape))

    copies = pl.pallas_call(
        cast_kernel,
        out_shape=jax.ShapeDtypeStruct((half, block_rows, width), bf16),
        compiler_params=params(),
        name="cast",
    )(type_table)
    parities = [list(range(p, Z_SIZE, 2)) for p in range(2)]
    near = lax.all_to_all(copies, "gz", 0, 0, tiled=True, axis_index_groups=parities)
    lower = shifted(near[: half // 2], "gz", 1)
    upper = shifted(near[half // 2 :], "gz", -1)
    table = (near, lower, upper)
    table_specs = [whole(t.shape[0], block_rows, width) for t in table]
    packed = pl.pallas_call(
        lambda *refs: pack_kernel(cols, *refs),
        in_specs=[hbm] * 5,
        out_shape=jax.ShapeDtypeStruct((sent_rows, width), bf16),
        scratch_shapes=[
            pltpu.VMEM((2, SLOTS), jnp.int32),
            pltpu.VMEM((1, 2), jnp.int32),
            pltpu.VMEM((1, rows), jnp.int32),
            pltpu.VMEM((1, rows), jnp.int32),
            pltpu.SemaphoreType.DMA((5,)),
        ],
        compiler_params=params(),
        name="pack",
    )(
        block_lists,
        list_lengths.reshape(1, 2),
        gold_slot.reshape(1, rows),
        gold_row.reshape(1, rows),
        mentions,
    )
    gathered = jnp.stack([packed] + [shifted(packed, "gx", s) for s in range(1, X_SIZE)])

    exps, stats = pl.pallas_call(
        scores_kernel,
        grid=(X_SIZE,),
        in_specs=[smem, smem, tile(sent_rows, width)] + table_specs,
        out_specs=[tile(types, rows), whole(X_SIZE, STAT_ROWS, X_SIZE * rows)],
        out_shape=[
            jax.ShapeDtypeStruct((X_SIZE, types, rows), f32),
            jax.ShapeDtypeStruct((X_SIZE, STAT_ROWS, X_SIZE * rows), f32),
        ],
        scratch_shapes=[pltpu.VMEM((types, width), bf16), pltpu.VMEM((types, rows), f32)],
        compiler_params=params(50),
        name="scores",
    )(logit_scale, place, gathered, *table)
    stats = lax.all_to_all(stats, "gx", 0, 0, tiled=True)
    chunk = 2 * block_rows
    chunk_spec = pl.BlockSpec((X_SIZE, chunk, rows), lambda i: (0, i, 0))
    grads, type_part, scale_part = pl.pallas_call(
        grads_kernel,
        grid=(types // chunk,),
        in_specs=[
            smem,
            smem,
            chunk_spec,
            whole(X_SIZE, STAT_ROWS, X_SIZE * rows),
            whole(X_SIZE, sent_rows, width),
        ],
        out_specs=[chunk_spec, pl.BlockSpec((chunk, width), lambda i: (i, 0)), whole(1, 128)],
        out_shape=[
            jax.ShapeDtypeStruct((X_SIZE, types, rows), bf16),
            jax.ShapeDtypeStruct((types, width), bf16),
            jax.ShapeDtypeStruct((1, 128), f32),
        ],
        scratch_shapes=[
            pltpu.VMEM((1, X_SIZE * rows), f32),
            pltpu.VMEM((X_SIZE * rows, width), bf16),
            pltpu.VMEM((chunk, X_SIZE * rows), bf16),
        ],
        compiler_params=params(50),
        name="grads",
    )(logit_scale, place, exps, stats, gathered)
    type_grad = lax.psum_scatter(type_part, "gz", scatter_dimension=0, tiled=True)
    *parts, scale_parts = pl.pallas_call(
        mention_kernel,
        grid=(X_SIZE,),
        in_specs=[smem, smem, whole(1, 128), tile(types, rows)] + table_specs,
        out_specs=[whole(rows, width)] * X_SIZE + [whole(Z_SIZE * cols, 1, 128)],
        out_shape=[jax.ShapeDtypeStruct((rows, width), bf16)] * X_SIZE
        + [jax.ShapeDtypeStruct((Z_SIZE * cols, 1, 128), f32)],
        scratch_shapes=[pltpu.VMEM((types, width), bf16)],
        compiler_params=params(50),
        name="mention_part",
    )(logit_scale, place, scale_part, grads, *table)
    mention_grad = parts[0].astype(f32)
    for s in range(1, X_SIZE):
        mention_grad = mention_grad + shifted(parts[s], "gx", -s).astype(f32)
    mention_grad = mention_grad.astype(bf16)
    scale_parts = lax.all_to_all(scale_parts, ("gz", "gy"), 0, 0, tiled=True)
    scale_grad = (jnp.sum(scale_parts[:, 0, 0]) / (rows * devices)).reshape(1)
    new_table, new_first, new_second = adam_rows(
        type_table, adam_m, adam_v, type_grad.astype(f32)
    )
    return (new_table, new_first, new_second, mention_grad, scale_grad)


def solution(mesh):
    gx, gy = mesh.devices.shape
    split = Mesh(mesh.devices.reshape(gx // X_SIZE, X_SIZE, gy), ("gz", "gx", "gy"))
    axes = ("gz", "gx", "gy")
    rows = P(axes, None)
    return jax.shard_map(
        per_device,
        mesh=split,
        in_specs=(rows, rows, rows, rows, P(), rows, P(axes), P(axes), P(axes)),
        out_specs=(rows, rows, rows, rows, P()),
        check_vma=False,
    )
```

time: 148 us -> 132 us (0.89); the launches traced: 147 us -> 129 us
  waiting for transfers between devices: 56.8 us -> 13.6 us
  starting transfers between devices: 8.46 us -> 40.3 us
  blocking collectives: 37.2 us -> 32.9 us
  Pallas kernels: 22.5 us -> 19.5 us
    all_to_all x2 -> x1, waiting for transfers between devices: 34 us -> 3.78 us  [per_device(): lax.all_to_all(copies, 'gz', 0, 0, tiled=True, axis_index_groups=parities)]
    ppermute x0 -> x8, starting transfers between devices: none -> 29.5 us  [shifted(): lax.ppermute(array, axis, [(i, (i + by) % size) for i in range(size)])]
    all_gather x1 -> x0, waiting for transfers between devices: 22.8 us -> none  [per_device(): table = lax.all_gather(type_table.astype(bf16), 'gz', axis=0, tiled=True)]
    ppermute x0 -> x8, waiting for transfers between devices: none -> 9.83 us  [shifted(): lax.ppermute(array, axis, [(i, (i + by) % size) for i in range(size)])]
    all_to_all x1, blocking collectives: 28.3 us -> 24.2 us  [per_device(): scale_parts = lax.all_to_all(scale_parts, ('gz', 'gy'), 0, 0, tiled=True)]
    all_to_all x2 -> x1, starting transfers between devices: 8.42 us -> 10.8 us  [per_device(): lax.all_to_all(copies, 'gz', 0, 0, tiled=True, axis_index_groups=parities)]
    pallas_call x2 -> x3, Pallas kernels: 13.1 us -> 12.3 us  [the longest x1 5.96 us: per_device(): pl.pallas_call(grads_kernel, grid=(types // chunk,), in_specs=[smem, smem...]
  transfers between devices with their start and end apart: 4 -> 10, of which waited for: 3 -> 4; matrix products, arithmetic and copies ran while one was open for 1% -> 3% of each run, Pallas kernels for 6% -> 5%
where the time goes in v5:
time: 132 us; the launch traced here: 129 us
  starting transfers between devices  40.3 us (31%)
  blocking collectives  32.9 us (25%)
  Pallas kernels  19.5 us (15%)
  between operations  16.6 us (13%)
  waiting for transfers between devices  13.6 us (10%)
  other arithmetic  5.08 us (4%)
    ppermute x8, starting transfers between devices, shifted(): lax.ppermute(array, axis, [(i, (i + by) % size) for i in range(size)])  29.5 us
    all_to_all x1, blocking collectives, per_device(): scale_parts = lax.all_to_all(scale_parts, ('gz', 'gy'), 0, 0, tiled=True)  24.2 us
    all_to_all x1, starting transfers between devices, per_device(): lax.all_to_all(copies, 'gz', 0, 0, tiled=True, axis_index_groups=parities)  10.8 us
    ppermute x8, waiting for transfers between devices, shifted(): lax.ppermute(array, axis, [(i, (i + by) % size) for i in range(size)])  9.83 us
    all_to_all x1, blocking collectives, per_device(): stats = lax.all_to_all(stats, 'gx', 0, 0, tiled=True)  8.63 us
    pallas_call x1, Pallas kernels, per_device(): pl.pallas_call(grads_kernel, grid=(types // chunk,), in_specs=[smem, smem...  5.96 us
    pallas_call x1, Pallas kernels, per_device(): pl.pallas_call(scores_kernel, grid=(X_SIZE,), in_specs=[smem, smem, tile(...  5.41 us
    pallas_call x1, Pallas kernels, per_device(): pl.pallas_call(mention_kernel, grid=(X_SIZE,), in_specs=[smem, smem, whol...  4.35 us
  transfers between devices with their start and end apart: 10, of which 4 were waited for; matrix products, arithmetic and copies ran while one was open for 3% of the time, Pallas kernels for 5%

profile of v5, /device:TPU:1, one launch (start us, length us, event | category | flops | bytes accessed | tf_op | source)
XLA Modules:
  0.0 129.0 jit_solution(2377651789139612333)
XLA Ops:
  7.2 2.0 %cast.1 = bf16[4,128,768]{2,1,0:T(8,128)(2,1)} custom-call(f32[128,768]{1,0:T(8,128)} %t_ref.1), custom_call_target="tpu_custom_call" | custom-call | tf_op jit(solution)/shard_map/cast/pallas_call | solution.py:238
  9.1 10.8 %all-to-all-start = ((bf16[4,128,768]{2,1,0:T(8,128)(2,1)}), bf16[4,128,768]{2,1,0:T(8,128)(2,1)S(1)}, u32[]{:S(2)}, u32[]{:S(2)}) async-start(bf16[4,128,768]{2,1,0:T(8,128)(2,1)} %cast.1), calls=%async_computation | async-start | bytes 1572864 | tf_op jit(solution)/shard_map/all_to_all | solution.py:245
  20.0 1.9 %pack.1 = bf16[288,768]{1,0:T(8,128)(2,1)} custom-call(s32[2,16]{1,0:T(2,128)} %refs_0_.1, s32[1,2]{1,0:T(1,128)} %bitcast.16, s32[1,256]{1,0:T(1,128)} %bitcast.14, s32[1,256]{1,0:T(1,128)} %bitcast.15, bf16[256,768]{1,0:T(8,128)(2,1)} %refs_4_.1), custom_call_target="tpu_custom_call" | custom-call | tf_op jit(solution)/shard_map/pack/pallas_call | solution.py:250
  21.9 4.5 %collective-permute-start.2 = (bf16[288,768]{1,0:T(8,128)(2,1)}, bf16[288,768]{1,0:T(8,128)(2,1)S(1)}, u32[]{:S(2)}, u32[]{:S(2)}) collective-permute-start(bf16[288,768]{1,0:T(8,128)(2,1)} %pack.1), channel_id=1, source_target_pairs={{0,48},{16,0},{32,16},{48,32},{1,49},{17,1},{33,17},{49,33},{2,50}... | collective-permute-start | bytes 1327112 | tf_op jit(solution)/shard_map/ppermute | solution.py:207
  26.4 2.4 %collective-permute-start.1 = (bf16[288,768]{1,0:T(8,128)(2,1)}, bf16[288,768]{1,0:T(8,128)(2,1)S(1)}, u32[]{:S(2)}, u32[]{:S(2)}) collective-permute-start(bf16[288,768]{1,0:T(8,128)(2,1)} %pack.1), channel_id=1, source_target_pairs={{0,32},{16,48},{32,0},{48,16},{1,33},{17,49},{33,1},{49,17},{2,34}... | collective-permute-start | bytes 1327112 | tf_op jit(solution)/shard_map/ppermute | solution.py:207
  28.8 2.5 %collective-permute-start = (bf16[288,768]{1,0:T(8,128)(2,1)}, bf16[288,768]{1,0:T(8,128)(2,1)S(1)}, u32[]{:S(2)}, u32[]{:S(2)}) collective-permute-start(bf16[288,768]{1,0:T(8,128)(2,1)} %pack.1), channel_id=1, source_target_pairs={{0,16},{16,32},{32,48},{48,0},{1,17},{17,33},{33,49},{49,1},{2,18}... | collective-permute-start | bytes 1327112 | tf_op jit(solution)/shard_map/ppermute | solution.py:207
  31.3 3.8 %all-to-all-done.near_ref = bf16[4,128,768]{2,1,0:T(8,128)(2,1)S(1)} async-done(((bf16[4,128,768]{2,1,0:T(8,128)(2,1)}), bf16[4,128,768]{2,1,0:T(8,128)(2,1)S(1)}, u32[]{:S(2)}, u32[]{:S(2)}) %all-to-all-start) | async-done | bytes 786464 | tf_op jit(solution)/shard_map/all_to_all | solution.py:245
  35.1 0.9 fusion.4
  36.1 10.2 %collective-permute-start.4 = (bf16[2,128,768]{2,1,0:T(8,128)(2,1)}, bf16[2,128,768]{2,1,0:T(8,128)(2,1)S(1)}, u32[]{:S(2)}, u32[]{:S(2)}) collective-permute-start(bf16[2,128,768]{2,1,0:T(8,128)(2,1)} %get-tuple-element.28), channel_id=1, source_target_pairs={{0,448},{64,0},{128,64},{192,128},{256,192},{320,256},{384,320},{4... | collective-permute-start | bytes 1179656 | tf_op jit(solution)/shard_map/ppermute | solution.py:207
  46.2 1.9 %collective-permute-start.3 = (bf16[2,128,768]{2,1,0:T(8,128)(2,1)}, bf16[2,128,768]{2,1,0:T(8,128)(2,1)S(1)}, u32[]{:S(2)}, u32[]{:S(2)}) collective-permute-start(bf16[2,128,768]{2,1,0:T(8,128)(2,1)} %get-tuple-element.29), channel_id=1, source_target_pairs={{0,64},{64,128},{128,192},{192,256},{256,320},{320,384},{384,448},... | collective-permute-start | bytes 1179656 | tf_op jit(solution)/shard_map/ppermute | solution.py:207
  48.8 0.1 pad_add_fusion.place_ref
  48.9 2.7 %collective-permute-done = bf16[288,768]{1,0:T(8,128)(2,1)S(1)} collective-permute-done((bf16[288,768]{1,0:T(8,128)(2,1)}, bf16[288,768]{1,0:T(8,128)(2,1)S(1)}, u32[]{:S(2)}, u32[]{:S(2)}) %collective-permute-start) | collective-permute-done | bytes 442400 | tf_op jit(solution)/shard_map/ppermute | solution.py:207
  51.6 0.2 pad_maximum_fusion.m_ref
  51.8 2.2 %collective-permute-done.4.above_ref = bf16[2,128,768]{2,1,0:T(8,128)(2,1)S(1)} collective-permute-done((bf16[2,128,768]{2,1,0:T(8,128)(2,1)}, bf16[2,128,768]{2,1,0:T(8,128)(2,1)S(1)}, u32[]{:S(2)}, u32[]{:S(2)}) %collective-permute-start.4) | collective-permute-done | bytes 393248 | tf_op jit(solution)/shard_map/ppermute | solution.py:207
  54.0 4.9 %collective-permute-done.3.below_ref = bf16[2,128,768]{2,1,0:T(8,128)(2,1)S(1)} collective-permute-done((bf16[2,128,768]{2,1,0:T(8,128)(2,1)}, bf16[2,128,768]{2,1,0:T(8,128)(2,1)S(1)}, u32[]{:S(2)}, u32[]{:S(2)}) %collective-permute-start.3) | collective-permute-done | bytes 393248 | tf_op jit(solution)/shard_map/ppermute | solution.py:207
  58.9 5.4 %scores.1 = (f32[4,1024,256]{2,1,0:T(8,128)}, f32[4,8,1024]{2,1,0:T(8,128)S(1)}) custom-call(f32[1]{0:T(128)S(6)} %copy.14.factor_ref, s32[2]{0:T(128)S(1)} %pad_add_fusion.place_ref, bf16[4,288,768]{2,1,0:T(8,128)(2,1)S(1)} %pad_maximum_fusion.m_ref, bf16[4,128,768]{2,1,0:T(8,128)(2,1)S(1)} %all-to-all-done.near_ref, ...), custom_call_target="tpu_custom_call" | custom-call | tf_op jit(solution)/shard_map/scores/pallas_call | solution.py:272
  64.3 8.6 %all_to_all.15.stat_ref = f32[4,8,1024]{2,1,0:T(8,128)S(1)} all-to-all(f32[4,8,1024]{2,1,0:T(8,128)S(1)} %get-tuple-element.16), channel_id=1, replica_groups=mesh['gz'=8,'gx'=4,'gy'=16] {'gx'}, dimensions={0} | all-to-all | bytes 262144 | tf_op jit(solution)/shard_map/all_to_all | solution.py:285
  73.0 6.0 %grads.1 = (bf16[4,1024,256]{2,1,0:T(8,128)(2,1)}, bf16[1024,768]{1,0:T(8,128)(2,1)}, f32[1,128]{1,0:T(1,128)S(1)}) custom-call(f32[1]{0:T(128)S(6)} %copy.14.factor_ref, s32[2]{0:T(128)S(1)} %pad_add_fusion.place_ref, f32[4,1024,256]{2,1,0:T(8,128)} %get-tuple-element.15.exp_ref, f32[4,8,1024]{2,1,0:T(8,128)S(1)} %all_to_all.15.stat_ref, ...), custom_call_target="tpu_custom_call" | custom-call | tf_op jit(solution)/shard_map/grads/pallas_call | solution.py:288
  78.9 0.0 reduce-scatter.2.cloned.1.call-update
  78.9 4.3 %mention_part.1 = (bf16[256,768]{1,0:T(8,128)(2,1)S(1)}, bf16[256,768]{1,0:T(8,128)(2,1)S(1)}, bf16[256,768]{1,0:T(8,128)(2,1)S(1)}, bf16[256,768]{1,0:T(8,128)(2,1)S(1)}, f32[128,1,128]{2,1,0:T(1,128)S(1)}) custom-call(f32[1]{0:T(128)S(6)} %copy.14.factor_ref, s32[2]{0:T(128)S(1)} %pad_add_fusion.place_ref, f32[1,128]{1,0:T(1,128)S(1)} %get-tuple-element.18.scale_ref, ...), custom_call_target="tpu_custom_call" | custom-call | tf_op jit(solution)/shard_map/mention_part/pallas_call | solution.py:313
  83.3 0.0 copy-start.1
  83.3 0.0 copy-start.2
  83.3 0.0 copy-start.3
  83.3 2.9 %collective-permute-start.5 = (bf16[256,768]{1,0:T(8,128)(2,1)S(1)}, bf16[256,768]{1,0:T(8,128)(2,1)S(1)}, u32[]{:S(2)}, u32[]{:S(2)}) collective-permute-start(bf16[256,768]{1,0:T(8,128)(2,1)S(1)} %get-tuple-element.21), channel_id=1, source_target_pairs={{0,48},{16,0},{32,16},{48,32},{1,49},{17,1},{33,17},{49,33},{2,50}... | collective-permute-start | bytes 1179656 | tf_op jit(solution)/shard_map/ppermute | solution.py:207
  86.3 3.1 %collective-permute-start.6 = (bf16[256,768]{1,0:T(8,128)(2,1)S(1)}, bf16[256,768]{1,0:T(8,128)(2,1)S(1)}, u32[]{:S(2)}, u32[]{:S(2)}) collective-permute-start(bf16[256,768]{1,0:T(8,128)(2,1)S(1)} %get-tuple-element.22), channel_id=1, source_target_pairs={{0,32},{16,48},{32,0},{48,16},{1,33},{17,49},{33,1},{49,17},{2,34}... | collective-permute-start | bytes 1179656 | tf_op jit(solution)/shard_map/ppermute | solution.py:207
  89.4 1.9 %collective-permute-start.7 = (bf16[256,768]{1,0:T(8,128)(2,1)S(1)}, bf16[256,768]{1,0:T(8,128)(2,1)}, u32[]{:S(2)}, u32[]{:S(2)}) collective-permute-start(bf16[256,768]{1,0:T(8,128)(2,1)S(1)} %get-tuple-element.23), channel_id=1, source_target_pairs={{0,16},{16,32},{32,48},{48,0},{1,17},{17,33},{33,49},{49,1},{2,18}... | collective-permute-start | bytes 1179656 | tf_op jit(solution)/shard_map/ppermute | solution.py:207
  91.3 24.2 %all_to_all.16 = f32[128,1,128]{2,1,0:T(1,128)S(1)} all-to-all(f32[128,1,128]{2,1,0:T(1,128)S(1)} %get-tuple-element.24), channel_id=1, replica_groups=mesh['gz'=8,'gx'=4,'gy'=16] {'gz','gy'}, dimensions={0} | all-to-all | bytes 131072 | tf_op jit(solution)/shard_map/all_to_all | solution.py:328
  115.5 0.7 slice_reduce_fusion
  116.9 0.0 collective-permute-done.5
  116.9 0.0 collective-permute-done.6
  117.0 2.0 %add_convert_fusion = bf16[256,768]{1,0:T(8,128)(2,1)} fusion(bf16[256,768]{1,0:T(8,128)(2,1)} %collective-permute-done.7, bf16[256,768]{1,0:T(8,128)(2,1)S(1)} %collective-permute-done.6, bf16[256,768]{1,0:T(8,128)(2,1)S(1)} %collective-permute-done.5, bf16[256,768]{1,0:T(8,128)(2,1)S(1)} %get-tuple-element.20), kind=kLoop, calls=%fused_computation.1 | loop fusion | flops 1572864 | bytes 1966080 | tf_op jit(solution)/shard_map/convert_element_type | solution.py:327
  118.9 2.1 %divide_subtract_fusion = (f32[128,768]{1,0:T(8,128)}, f32[128,768]{1,0:T(8,128)}, f32[128,768]{1,0:T(8,128)}) fusion(f32[128,768]{1,0:T(8,128)S(1)} %copy-done.1, bf16[128,768]{1,0:T(8,128)(2,1)} %reduce-scatter.2.cloned.1.call-done, f32[128,768]{1,0:T(8,128)S(1)} %copy-done.2, f32[128,768]{1,0:T(8,128)S(1)} %copy-done.3), kind=kLoop, calls=%fused_computation.6 | loop fusion | flops 1277952 | bytes 2555904 | tf_op jit(solution)/shard_map/sub | solution.py:195
  (10 shorter events, 0.0 us)
Async XLA Ops:
  9.1 26.0 %all-to-all-start = ((bf16[4,128,768]{2,1,0:T(8,128)(2,1)}), bf16[4,128,768]{2,1,0:T(8,128)(2,1)S(1)}, u32[]{:S(2)}, u32[]{:S(2)}) async-start(bf16[4,128,768]{2,1,0:T(8,128)(2,1)} %cast.1), calls=%async_computation | async-start | bytes 1572864 | tf_op jit(solution)/shard_map/all_to_all | solution.py:245
  20.0 99.0 %reduce-scatter.2.cloned.1.call-start = ((), (), s32[]{:S(2)}) async-start(), calls=%async_computation.4 | async-start | bytes 1769472 | tf_op jit(solution)/shard_map/reduce_scatter | solution.py:312
  21.9 29.7 %copy-start = (bf16[288,768]{1,0:T(8,128)(2,1)S(1)}, bf16[288,768]{1,0:T(8,128)(2,1)}, u32[]{:S(2)}) copy-start(bf16[288,768]{1,0:T(8,128)(2,1)} %pack.1) | copy-start | bytes 1327108
  21.9 27.0 %collective-permute-start.2 = (bf16[288,768]{1,0:T(8,128)(2,1)}, bf16[288,768]{1,0:T(8,128)(2,1)S(1)}, u32[]{:S(2)}, u32[]{:S(2)}) collective-permute-start(bf16[288,768]{1,0:T(8,128)(2,1)} %pack.1), channel_id=1, source_target_pairs={{0,48},{16,0},{32,16},{48,32},{1,49},{17,1},{33,17},{49,33},{2,50}... | collective-permute-start | bytes 1327112 | tf_op jit(solution)/shard_map/ppermute | solution.py:207
  26.4 22.5 %collective-permute-start.1 = (bf16[288,768]{1,0:T(8,128)(2,1)}, bf16[288,768]{1,0:T(8,128)(2,1)S(1)}, u32[]{:S(2)}, u32[]{:S(2)}) collective-permute-start(bf16[288,768]{1,0:T(8,128)(2,1)} %pack.1), channel_id=1, source_target_pairs={{0,32},{16,48},{32,0},{48,16},{1,33},{17,49},{33,1},{49,17},{2,34}... | collective-permute-start | bytes 1327112 | tf_op jit(solution)/shard_map/ppermute | solution.py:207
  28.8 22.7 %collective-permute-start = (bf16[288,768]{1,0:T(8,128)(2,1)}, bf16[288,768]{1,0:T(8,128)(2,1)S(1)}, u32[]{:S(2)}, u32[]{:S(2)}) collective-permute-start(bf16[288,768]{1,0:T(8,128)(2,1)} %pack.1), channel_id=1, source_target_pairs={{0,16},{16,32},{32,48},{48,0},{1,17},{17,33},{33,49},{49,1},{2,18}... | collective-permute-start | bytes 1327112 | tf_op jit(solution)/shard_map/ppermute | solution.py:207
  36.1 17.9 %collective-permute-start.4 = (bf16[2,128,768]{2,1,0:T(8,128)(2,1)}, bf16[2,128,768]{2,1,0:T(8,128)(2,1)S(1)}, u32[]{:S(2)}, u32[]{:S(2)}) collective-permute-start(bf16[2,128,768]{2,1,0:T(8,128)(2,1)} %get-tuple-element.28), channel_id=1, source_target_pairs={{0,448},{64,0},{128,64},{192,128},{256,192},{320,256},{384,320},{4... | collective-permute-start | bytes 1179656 | tf_op jit(solution)/shard_map/ppermute | solution.py:207
  46.2 12.7 %collective-permute-start.3 = (bf16[2,128,768]{2,1,0:T(8,128)(2,1)}, bf16[2,128,768]{2,1,0:T(8,128)(2,1)S(1)}, u32[]{:S(2)}, u32[]{:S(2)}) collective-permute-start(bf16[2,128,768]{2,1,0:T(8,128)(2,1)} %get-tuple-element.29), channel_id=1, source_target_pairs={{0,64},{64,128},{128,192},{192,256},{256,320},{320,384},{384,448},... | collective-permute-start | bytes 1179656 | tf_op jit(solution)/shard_map/ppermute | solution.py:207
  83.3 35.6 %copy-start.1 = (f32[128,768]{1,0:T(8,128)S(1)}, f32[128,768]{1,0:T(8,128)}, u32[]{:S(2)}) copy-start(f32[128,768]{1,0:T(8,128)} %t_ref.1) | copy-start | bytes 1179652
  83.3 35.6 %copy-start.2 = (f32[128,768]{1,0:T(8,128)S(1)}, f32[128,768]{1,0:T(8,128)}, u32[]{:S(2)}) copy-start(f32[128,768]{1,0:T(8,128)} %param.11) | copy-start | bytes 1179652
  83.3 35.6 %copy-start.3 = (f32[128,768]{1,0:T(8,128)S(1)}, f32[128,768]{1,0:T(8,128)}, u32[]{:S(2)}) copy-start(f32[128,768]{1,0:T(8,128)} %param.12) | copy-start | bytes 1179652
  83.3 33.6 %collective-permute-start.5 = (bf16[256,768]{1,0:T(8,128)(2,1)S(1)}, bf16[256,768]{1,0:T(8,128)(2,1)S(1)}, u32[]{:S(2)}, u32[]{:S(2)}) collective-permute-start(bf16[256,768]{1,0:T(8,128)(2,1)S(1)} %get-tuple-element.21), channel_id=1, source_target_pairs={{0,48},{16,0},{32,16},{48,32},{1,49},{17,1},{33,17},{49,33},{2,50}... | collective-permute-start | bytes 1179656 | tf_op jit(solution)/shard_map/ppermute | solution.py:207
  86.3 30.7 %collective-permute-start.6 = (bf16[256,768]{1,0:T(8,128)(2,1)S(1)}, bf16[256,768]{1,0:T(8,128)(2,1)S(1)}, u32[]{:S(2)}, u32[]{:S(2)}) collective-permute-start(bf16[256,768]{1,0:T(8,128)(2,1)S(1)} %get-tuple-element.22), channel_id=1, source_target_pairs={{0,32},{16,48},{32,0},{48,16},{1,33},{17,49},{33,1},{49,17},{2,34}... | collective-permute-start | bytes 1179656 | tf_op jit(solution)/shard_map/ppermute | solution.py:207
  89.4 27.6 %collective-permute-start.7 = (bf16[256,768]{1,0:T(8,128)(2,1)S(1)}, bf16[256,768]{1,0:T(8,128)(2,1)}, u32[]{:S(2)}, u32[]{:S(2)}) collective-permute-start(bf16[256,768]{1,0:T(8,128)(2,1)S(1)} %get-tuple-element.23), channel_id=1, source_target_pairs={{0,16},{16,32},{32,48},{48,0},{1,17},{17,33},{33,49},{49,1},{2,18}... | collective-permute-start | bytes 1179656 | tf_op jit(solution)/shard_map/ppermute | solution.py:207
Sparse Core Ops, SparseCore 0:
  79.1 37.9 reduce-scatter.1

commit v6 on v5

--- a/solution.py
+++ b/solution.py
@@ -63,29 +63,20 @@
 
 
 def tile_from(place_ref, step):
-    return lax.rem(place_ref[1] - step + X_SIZE, X_SIZE)
-
-
-def join_types(place_ref, near_ref, below_ref, above_ref, tile_ref):
+    return jnp.bitwise_xor(place_ref[1], step)
+
+
+def join_types(place_ref, near_ref, low_ref, high_ref, tile_ref):
     parity = lax.rem(place_ref[0], 2)
     half = Z_SIZE // 4
     for k in range(Z_SIZE // 2):
-        other = below_ref[k] if k < half else above_ref[k - half]
+        other = low_ref[k] if k < half else high_ref[k - half]
         tile_ref[pl.ds(pl.multiple_of((2 * k + parity) * BLOCK, BLOCK), BLOCK), :] = near_ref[k]
         tile_ref[pl.ds(pl.multiple_of((2 * k + 1 - parity) * BLOCK, BLOCK), BLOCK), :] = other
 
 
-def scores_kernel(
-    factor_ref, place_ref, m_ref, near_ref, below_ref, above_ref, exp_ref, stat_ref, tile_ref, raw_ref
-):
-    step = pl.program_id(0)
-    factor = factor_ref[0]
+def score_half(factor, place_ref, shift, m_ref, tile_ref, raw_ref, exp_ref):
     rows = m_ref.shape[1] - META_ROWS
-
-    @pl.when(step == 0)
-    def _():
-        join_types(place_ref, near_ref, below_ref, above_ref, tile_ref)
-
     raw_ref[...] = lax.dot_general(
         tile_ref[...], m_ref[0, 0:rows, :], (((1,), (1,)), ((), ())), preferred_element_type=f32
     )
@@ -97,52 +88,90 @@
     top = jnp.full((1, rows), LOW, f32)
     gold_raw = jnp.zeros((1, rows), f32)
     lives = []
-    for c in range(Z_SIZE):
-        owner = owner_at(place_ref, c)
+    for k in range(Z_SIZE // 2):
+        owner = owner_at(place_ref, 2 * k + shift)
         lives.append(jnp.max(jnp.where(owners == owner, 1.0, 0.0), axis=0, keepdims=True) > 0.0)
-        raw = raw_ref[c * BLOCK : (c + 1) * BLOCK, :]
-        top = jnp.maximum(top, jnp.where(lives[c], jnp.max(raw, axis=0, keepdims=True), LOW))
+        raw = raw_ref[k * BLOCK : (k + 1) * BLOCK, :]
+        top = jnp.maximum(top, jnp.where(lives[k], jnp.max(raw, axis=0, keepdims=True), LOW))
         gold = jnp.where(gold_owner == owner, gold_row, -1)
         gold_raw = gold_raw + jnp.sum(jnp.where(ids == gold, raw, 0.0), axis=0, keepdims=True)
     total = jnp.zeros((1, rows), f32)
     mass = jnp.zeros((1, rows), f32)
-    for c in range(Z_SIZE):
-        below = jnp.where(lives[c], top, -LOW)
-        gap = raw_ref[c * BLOCK : (c + 1) * BLOCK, :] - below
+    for k in range(Z_SIZE // 2):
+        below = jnp.where(lives[k], top, -LOW)
+        gap = raw_ref[k * BLOCK : (k + 1) * BLOCK, :] - below
         weights = jnp.exp(factor * gap)
-        exp_ref[0, c * BLOCK : (c + 1) * BLOCK, :] = weights
+        exp_ref[0, k * BLOCK : (k + 1) * BLOCK, :] = weights
         total = total + jnp.sum(weights, axis=0, keepdims=True)
         mass = mass + jnp.sum(weights * gap, axis=0, keepdims=True)
-    stat = jnp.concatenate(
-        [top, total, mass, gold_raw, jnp.zeros((STAT_ROWS - 4, rows), f32)], axis=0
-    )
+    return top, total, mass, gold_raw
+
+
+def near_kernel(factor_ref, place_ref, m_ref, near_ref, exp_ref, stat_ref, tile_ref, raw_ref):
+    step = pl.program_id(0)
+
+    @pl.when(step == 0)
+    def _():
+        for k in range(near_ref.shape[0]):
+            tile_ref[k * BLOCK : (k + 1) * BLOCK, :] = near_ref[k]
+
+    shift = lax.rem(place_ref[0], 2)
+    stats = score_half(factor_ref[0], place_ref, shift, m_ref, tile_ref, raw_ref, exp_ref)
+    rows = stats[0].shape[1]
+    rest = jnp.zeros((STAT_ROWS - len(stats), rows), f32)
+    stat_ref[0] = jnp.concatenate(list(stats) + [rest], axis=0)
+
+
+def far_kernel(
+    factor_ref, place_ref, m_ref, low_ref, high_ref, part_ref, exp_ref, stat_ref, tile_ref, raw_ref
+):
+    step = pl.program_id(0)
+
+    @pl.when(step == 0)
+    def _():
+        half = low_ref.shape[0]
+        for k in range(2 * half):
+            other = low_ref[k] if k < half else high_ref[k - half]
+            tile_ref[k * BLOCK : (k + 1) * BLOCK, :] = other
+
+    shift = 1 - lax.rem(place_ref[0], 2)
+    top, total, mass, gold_raw = score_half(
+        factor_ref[0], place_ref, shift, m_ref, tile_ref, raw_ref, exp_ref
+    )
+    rows = top.shape[1]
+    near = part_ref[0]
+    lines = [near[0:3, :], top, total, mass, gold_raw + near[3:4, :]]
+    lines.append(jnp.zeros((STAT_ROWS - 7, rows), f32))
+    stat = jnp.concatenate(lines, axis=0)
     at = pl.multiple_of(tile_from(place_ref, step) * rows, BLOCK)
     for d in range(stat_ref.shape[0]):
         stat_ref[d, :, pl.ds(at, rows)] = stat
 
 
 def merge_stats(factor, place_ref, stat_ref, share_ref, scale_ref):
-    tops = stat_ref[:, 0, :]
-    sums = stat_ref[:, 1, :]
+    tops, sums, masses = [
+        jnp.concatenate([stat_ref[:, r, :], stat_ref[:, r + 3, :]], axis=0) for r in range(3)
+    ]
     top = jnp.max(tops, axis=0, keepdims=True)
     shares = jnp.exp(factor * (tops - top))
     total = jnp.sum(sums * shares, axis=0, keepdims=True)
-    masses = stat_ref[:, 2, :] + sums * tops
+    masses = masses + sums * tops
     mass = jnp.sum(jnp.where(sums > 0.0, masses * shares, 0.0), axis=0, keepdims=True)
-    scale = mass / total - jnp.sum(stat_ref[:, 3, :], axis=0, keepdims=True)
+    scale = mass / total - jnp.sum(stat_ref[:, 6, :], axis=0, keepdims=True)
     scale_ref[...] = jnp.broadcast_to(jnp.sum(scale, axis=1, keepdims=True), scale_ref.shape)
     ids = lax.broadcasted_iota(jnp.int32, tops.shape, 0)
-    own = jnp.max(jnp.where(ids == place_ref[1], tops, LOW), axis=0, keepdims=True)
-    share_ref[...] = jnp.exp(factor * (own - top) - jnp.log(total))
+    for h in range(2):
+        mine = ids == place_ref[1] + h * X_SIZE
+        own = jnp.max(jnp.where(mine, tops, LOW), axis=0, keepdims=True)
+        share_ref[h : h + 1, :] = jnp.exp(factor * (own - top) - jnp.log(total))
 
 
 def grads_kernel(
-    factor_ref, place_ref, exp_ref, stat_ref, m_ref, g_ref, type_ref, scale_ref, share_ref, rows_ref, grad_ref
+    factor_ref, place_ref, near_ref, far_ref, stat_ref, m_ref, g_ref, type_ref, scale_ref, share_ref, rows_ref, grad_ref
 ):
     step = pl.program_id(0)
     factor = factor_ref[0]
     rows = m_ref.shape[1] - META_ROWS
-    chunk = exp_ref.shape[1]
 
     @pl.when(step == 0)
     def _():
@@ -151,31 +180,34 @@
             rows_ref[s * rows : (s + 1) * rows, :] = m_ref[s, 0:rows, :]
 
     ids = lax.broadcasted_iota(jnp.int32, (BLOCK, rows), 0)
+    parity = lax.rem(place_ref[0], 2)
     for s in range(X_SIZE):
         at = pl.multiple_of(tile_from(place_ref, s) * rows, BLOCK)
-        share = share_ref[:, pl.ds(at, rows)]
-        gold_owner = m_ref[s, rows + SLOTS : rows + META_ROWS, 0:rows].astype(f32)[0:1, :]
-        gold_row = m_ref[s, rows + SLOTS : rows + META_ROWS, 0:rows].astype(f32)[1:2, :]
-        for c in range(chunk // BLOCK):
-            owner = owner_at(place_ref, step * (chunk // BLOCK) + c)
+        meta = m_ref[s, rows + SLOTS : rows + META_ROWS, 0:rows].astype(f32)
+        gold_owner = meta[0:1, :]
+        gold_row = meta[1:2, :]
+        for h, exp_ref in enumerate((near_ref, far_ref)):
+            place = parity if h == 0 else 1 - parity
+            owner = owner_at(place_ref, 2 * step + place)
             gold = jnp.where(gold_owner == owner, gold_row, -1.0).astype(jnp.int32)
-            weights = share * exp_ref[s, c * BLOCK : (c + 1) * BLOCK, :]
+            weights = share_ref[h : h + 1, pl.ds(at, rows)] * exp_ref[s]
             grad = (weights - jnp.where(ids == gold, 1.0, 0.0)).astype(bf16)
-            g_ref[s, c * BLOCK : (c + 1) * BLOCK, :] = grad
-            grad_ref[c * BLOCK : (c + 1) * BLOCK, s * rows : (s + 1) * rows] = grad
+            line = pl.ds(pl.multiple_of(place * BLOCK, BLOCK), BLOCK)
+            g_ref[s, line, :] = grad
+            grad_ref[line, s * rows : (s + 1) * rows] = grad
     part = jnp.dot(grad_ref[...], rows_ref[...], preferred_element_type=f32)
     type_ref[...] = (factor * part).astype(bf16)
 
 
 def mention_kernel(
-    factor_ref, place_ref, scale_ref, g_ref, near_ref, below_ref, above_ref, *refs
+    factor_ref, place_ref, scale_ref, g_ref, near_ref, low_ref, high_ref, *refs
 ):
     out_refs, (scales_ref, tile_ref) = refs[:X_SIZE], refs[X_SIZE:]
     step = pl.program_id(0)
 
     @pl.when(step == 0)
     def _():
-        join_types(place_ref, near_ref, below_ref, above_ref, tile_ref)
+        join_types(place_ref, near_ref, low_ref, high_ref, tile_ref)
         scales_ref[...] = jnp.broadcast_to(scale_ref[...][None], scales_ref.shape)
 
     part = lax.dot_general(
@@ -202,9 +234,8 @@
     return pltpu.CompilerParams(vmem_limit_bytes=mib * 1024 * 1024)
 
 
-def shifted(array, axis, by):
-    size = lax.axis_size(axis)
-    return lax.ppermute(array, axis, [(i, (i + by) % size) for i in range(size)])
+def paired(array, axis, partner):
+    return lax.ppermute(array, axis, [(i, partner(i)) for i in range(lax.axis_size(axis))])
 
 
 def per_device(
@@ -243,9 +274,9 @@
     )(type_table)
     parities = [list(range(p, Z_SIZE, 2)) for p in range(2)]
     near = lax.all_to_all(copies, "gz", 0, 0, tiled=True, axis_index_groups=parities)
-    lower = shifted(near[: half // 2], "gz", 1)
-    upper = shifted(near[half // 2 :], "gz", -1)
-    table = (near, lower, upper)
+    low = paired(near[: half // 2], "gz", lambda z: z ^ 1)
+    high = paired(near[half // 2 :], "gz", lambda z: ((z + 1) ^ 1) - 1 & Z_SIZE - 1)
+    table = (near, low, high)
     table_specs = [whole(t.shape[0], block_rows, width) for t in table]
     packed = pl.pallas_call(
         lambda *refs: pack_kernel(cols, *refs),
@@ -267,21 +298,33 @@
         gold_row.reshape(1, rows),
         mentions,
     )
-    gathered = jnp.stack([packed] + [shifted(packed, "gx", s) for s in range(1, X_SIZE)])
-
-    exps, stats = pl.pallas_call(
-        scores_kernel,
+    gathered = jnp.stack(
+        [packed] + [paired(packed, "gx", lambda x, s=s: x ^ s) for s in range(1, X_SIZE)]
+    )
+
+    half_types = half * block_rows
+    scratch = [pltpu.VMEM((half_types, width), bf16), pltpu.VMEM((half_types, rows), f32)]
+    exps_shape = jax.ShapeDtypeStruct((X_SIZE, half_types, rows), f32)
+    near_exps, near_stats = pl.pallas_call(
+        near_kernel,
         grid=(X_SIZE,),
-        in_specs=[smem, smem, tile(sent_rows, width)] + table_specs,
-        out_specs=[tile(types, rows), whole(X_SIZE, STAT_ROWS, X_SIZE * rows)],
-        out_shape=[
-            jax.ShapeDtypeStruct((X_SIZE, types, rows), f32),
-            jax.ShapeDtypeStruct((X_SIZE, STAT_ROWS, X_SIZE * rows), f32),
-        ],
-        scratch_shapes=[pltpu.VMEM((types, width), bf16), pltpu.VMEM((types, rows), f32)],
-        compiler_params=params(50),
-        name="scores",
-    )(logit_scale, place, gathered, *table)
+        in_specs=[smem, smem, tile(sent_rows, width)] + table_specs[:1],
+        out_specs=[tile(half_types, rows), tile(STAT_ROWS, rows)],
+        out_shape=[exps_shape, jax.ShapeDtypeStruct((X_SIZE, STAT_ROWS, rows), f32)],
+        scratch_shapes=scratch,
+        compiler_params=params(16),
+        name="near_scores",
+    )(logit_scale, place, gathered, near)
+    far_exps, stats = pl.pallas_call(
+        far_kernel,
+        grid=(X_SIZE,),
+        in_specs=[smem, smem, tile(sent_rows, width)] + table_specs[1:] + [tile(STAT_ROWS, rows)],
+        out_specs=[tile(half_types, rows), whole(X_SIZE, STAT_ROWS, X_SIZE * rows)],
+        out_shape=[exps_shape, jax.ShapeDtypeStruct((X_SIZE, STAT_ROWS, X_SIZE * rows), f32)],
+        scratch_shapes=scratch,
+        compiler_params=params(16),
+        name="far_scores",
+    )(logit_scale, place, gathered, low, high, near_stats)
     stats = lax.all_to_all(stats, "gx", 0, 0, tiled=True)
     chunk = 2 * block_rows
     chunk_spec = pl.BlockSpec((X_SIZE, chunk, rows), lambda i: (0, i, 0))
@@ -291,7 +334,8 @@
         in_specs=[
             smem,
             smem,
-            chunk_spec,
+            pl.BlockSpec((X_SIZE, block_rows, rows), lambda i: (0, i, 0)),
+            pl.BlockSpec((X_SIZE, block_rows, rows), lambda i: (0, i, 0)),
             whole(X_SIZE, STAT_ROWS, X_SIZE * rows),
             whole(X_SIZE, sent_rows, width),
         ],
@@ -302,13 +346,13 @@
             jax.ShapeDtypeStruct((1, 128), f32),
         ],
         scratch_shapes=[
-            pltpu.VMEM((1, X_SIZE * rows), f32),
+            pltpu.VMEM((2, X_SIZE * rows), f32),
             pltpu.VMEM((X_SIZE * rows, width), bf16),
             pltpu.VMEM((chunk, X_SIZE * rows), bf16),
         ],
-        compiler_params=params(50),
+        compiler_params=params(16),
         name="grads",
-    )(logit_scale, place, exps, stats, gathered)
+    )(logit_scale, place, near_exps, far_exps, stats, gathered)
     type_grad = lax.psum_scatter(type_part, "gz", scatter_dimension=0, tiled=True)
     *parts, scale_parts = pl.pallas_call(
         mention_kernel,
@@ -318,12 +362,14 @@
         out_shape=[jax.ShapeDtypeStruct((rows, width), bf16)] * X_SIZE
         + [jax.ShapeDtypeStruct((Z_SIZE * cols, 1, 128), f32)],
         scratch_shapes=[pltpu.VMEM((types, width), bf16)],
-        compiler_params=params(50),
+        compiler_params=params(16),
         name="mention_part",
     )(logit_scale, place, scale_part, grads, *table)
     mention_grad = parts[0].astype(f32)
     for s in range(1, X_SIZE):
-        mention_grad = mention_grad + shifted(parts[s], "gx", -s).astype(f32)
+        mention_grad = mention_grad + paired(
+            parts[s], "gx", lambda x, s=s: x ^ s
+        ).astype(f32)
     mention_grad = mention_grad.astype(bf16)
     scale_parts = lax.all_to_all(scale_parts, ("gz", "gy"), 0, 0, tiled=True)
     scale_grad = (jnp.sum(scale_parts[:, 0, 0]) / (rows * devices)).reshape(1)

time: 132 us -> 129 us (0.977); the launches traced: 129 us -> 128 us
  waiting for transfers between devices: 13.6 us -> 9.79 us
  local copies, waits for them, and re-layouts: 0.95 us -> 3.84 us
  starting transfers between devices: 40.3 us -> 41.7 us
    ppermute x8, waiting for transfers between devices: 9.83 us -> 5.64 us  [paired(): lax.ppermute(array, axis, [(i, partner(i)) for i in range(lax.axis_size(a...]
    unnamed x8 -> x16, local copies, waits for them, and re-layouts: 0.02 us -> 2.92 us
    pallas_call x1, Pallas kernels: 5.96 us -> 4.09 us  [per_device(): pl.pallas_call(grads_kernel, grid=(types // chunk,), in_specs=[smem, smem...]
    ppermute x8, starting transfers between devices: 29.5 us -> 30.9 us  [paired(): lax.ppermute(array, axis, [(i, partner(i)) for i in range(lax.axis_size(a...]
    pallas_call x1 -> x2, Pallas kernels: 5.41 us -> 5.9 us  [the longest x1 2.95 us: per_device(): pl.pallas_call(near_kernel, grid=(X_SIZE,), in_specs=[smem, smem, tile(se...]
  transfers between devices with their start and end apart: 10 -> 10, of which waited for: 4 -> 3; matrix products, arithmetic and copies ran while one was open for 3% -> 3% of each run, Pallas kernels for 5% -> 7%
where the time goes in v6:
time: 129 us; the launch traced here: 128 us
  starting transfers between devices  41.7 us (32%)
  blocking collectives  33.2 us (26%)
  Pallas kernels  18.2 us (14%)
  between operations  16.6 us (13%)
  waiting for transfers between devices  9.79 us (8%)
  other arithmetic  5.05 us (4%)
  local copies, waits for them, and re-layouts  3.84 us (3%)
    ppermute x8, starting transfers between devices, paired(): lax.ppermute(array, axis, [(i, partner(i)) for i in range(lax.axis_size(a...  30.9 us
    all_to_all x1, blocking collectives, per_device(): scale_parts = lax.all_to_all(scale_parts, ('gz', 'gy'), 0, 0, tiled=True)  24.5 us
    all_to_all x1, starting transfers between devices, per_device(): lax.all_to_all(copies, 'gz', 0, 0, tiled=True, axis_index_groups=parities)  10.8 us
    all_to_all x1, blocking collectives, per_device(): stats = lax.all_to_all(stats, 'gx', 0, 0, tiled=True)  8.64 us
    ppermute x8, waiting for transfers between devices, paired(): lax.ppermute(array, axis, [(i, partner(i)) for i in range(lax.axis_size(a...  5.64 us
    pallas_call x1, Pallas kernels, per_device(): pl.pallas_call(mention_kernel, grid=(X_SIZE,), in_specs=[smem, smem, whol...  4.42 us
    all_to_all x1, waiting for transfers between devices, per_device(): lax.all_to_all(copies, 'gz', 0, 0, tiled=True, axis_index_groups=parities)  4.13 us
    pallas_call x1, Pallas kernels, per_device(): pl.pallas_call(grads_kernel, grid=(types // chunk,), in_specs=[smem, smem...  4.09 us
  transfers between devices with their start and end apart: 10, of which 3 were waited for; matrix products, arithmetic and copies ran while one was open for 3% of the time, Pallas kernels for 7%

profile of v6, /device:TPU:1, one launch (start us, length us, event | category | flops | bytes accessed | tf_op | source)
XLA Modules:
  0.0 128.4 jit_solution(9815926351641235164)
XLA Ops:
  7.2 1.9 %cast.1 = bf16[4,128,768]{2,1,0:T(8,128)(2,1)} custom-call(f32[128,768]{1,0:T(8,128)} %t_ref.1), custom_call_target="tpu_custom_call" | custom-call | tf_op jit(solution)/shard_map/cast/pallas_call | solution.py:269
  9.1 10.8 %all-to-all-start = ((bf16[4,128,768]{2,1,0:T(8,128)(2,1)}), bf16[4,128,768]{2,1,0:T(8,128)(2,1)S(1)}, u32[]{:S(2)}, u32[]{:S(2)}) async-start(bf16[4,128,768]{2,1,0:T(8,128)(2,1)} %cast.1), calls=%async_computation | async-start | bytes 1572864 | tf_op jit(solution)/shard_map/all_to_all | solution.py:276
  19.9 1.9 %pack.1 = bf16[288,768]{1,0:T(8,128)(2,1)} custom-call(s32[2,16]{1,0:T(2,128)} %refs_0_.1, s32[1,2]{1,0:T(1,128)} %bitcast.16, s32[1,256]{1,0:T(1,128)} %bitcast.14, s32[1,256]{1,0:T(1,128)} %bitcast.15, bf16[256,768]{1,0:T(8,128)(2,1)} %refs_4_.1), custom_call_target="tpu_custom_call" | custom-call | tf_op jit(solution)/shard_map/pack/pallas_call | solution.py:281
  21.8 4.5 %collective-permute-start.2 = (bf16[288,768]{1,0:T(8,128)(2,1)}, bf16[288,768]{1,0:T(8,128)(2,1)S(1)}, u32[]{:S(2)}, u32[]{:S(2)}) collective-permute-start(bf16[288,768]{1,0:T(8,128)(2,1)} %pack.1), channel_id=1, source_target_pairs={{0,48},{16,32},{32,16},{48,0},{1,49},{17,33},{33,17},{49,1},{2,50}... | collective-permute-start | bytes 1327112 | tf_op jit(solution)/shard_map/ppermute | solution.py:238
  26.4 2.4 %collective-permute-start.1 = (bf16[288,768]{1,0:T(8,128)(2,1)}, bf16[288,768]{1,0:T(8,128)(2,1)S(1)}, u32[]{:S(2)}, u32[]{:S(2)}) collective-permute-start(bf16[288,768]{1,0:T(8,128)(2,1)} %pack.1), channel_id=1, source_target_pairs={{0,32},{16,48},{32,0},{48,16},{1,33},{17,49},{33,1},{49,17},{2,34}... | collective-permute-start | bytes 1327112 | tf_op jit(solution)/shard_map/ppermute | solution.py:238
  28.8 2.2 %collective-permute-start = (bf16[288,768]{1,0:T(8,128)(2,1)}, bf16[288,768]{1,0:T(8,128)(2,1)S(1)}, u32[]{:S(2)}, u32[]{:S(2)}) collective-permute-start(bf16[288,768]{1,0:T(8,128)(2,1)} %pack.1), channel_id=1, source_target_pairs={{0,16},{16,0},{32,48},{48,32},{1,17},{17,1},{33,49},{49,33},{2,18}... | collective-permute-start | bytes 1327112 | tf_op jit(solution)/shard_map/ppermute | solution.py:238
  31.0 4.1 %all-to-all-done.near_ref = bf16[4,128,768]{2,1,0:T(8,128)(2,1)S(1)} async-done(((bf16[4,128,768]{2,1,0:T(8,128)(2,1)}), bf16[4,128,768]{2,1,0:T(8,128)(2,1)S(1)}, u32[]{:S(2)}, u32[]{:S(2)}) %all-to-all-start) | async-done | bytes 786464 | tf_op jit(solution)/shard_map/all_to_all | solution.py:276
  35.1 0.9 fusion.4
  36.0 10.2 %collective-permute-start.4 = (bf16[2,128,768]{2,1,0:T(8,128)(2,1)}, bf16[2,128,768]{2,1,0:T(8,128)(2,1)S(1)}, u32[]{:S(2)}, u32[]{:S(2)}) collective-permute-start(bf16[2,128,768]{2,1,0:T(8,128)(2,1)} %get-tuple-element.32), channel_id=1, source_target_pairs={{0,448},{64,128},{128,64},{192,256},{256,192},{320,384},{384,320},... | collective-permute-start | bytes 1179656 | tf_op jit(solution)/shard_map/ppermute | solution.py:238
  46.2 1.9 %collective-permute-start.3 = (bf16[2,128,768]{2,1,0:T(8,128)(2,1)}, bf16[2,128,768]{2,1,0:T(8,128)(2,1)S(1)}, u32[]{:S(2)}, u32[]{:S(2)}) collective-permute-start(bf16[2,128,768]{2,1,0:T(8,128)(2,1)} %get-tuple-element.33), channel_id=1, source_target_pairs={{0,64},{64,0},{128,192},{192,128},{256,320},{320,256},{384,448},{4... | collective-permute-start | bytes 1179656 | tf_op jit(solution)/shard_map/ppermute | solution.py:238
  48.8 0.1 pad_add_fusion.place_ref
  48.8 0.0 collective-permute-done.2
  48.9 0.2 pad_maximum_fusion.m_ref
  49.1 3.0 %near_scores.1 = (f32[4,512,256]{2,1,0:T(8,128)S(1)}, f32[4,8,256]{2,1,0:T(8,128)S(1)}) custom-call(f32[1]{0:T(128)S(6)} %copy.14.factor_ref, s32[2]{0:T(128)S(1)} %pad_add_fusion.place_ref, bf16[4,288,768]{2,1,0:T(8,128)(2,1)S(1)} %pad_maximum_fusion.m_ref, bf16[4,128,768]{2,1,0:T(8,128)(2,1)S(1)} %all-to-all-done.near_ref), custom_call_target="tpu_custom_call" | custom-call | tf_op jit(solution)/shard_map/near_scores/pallas_call | solution.py:308
  52.1 2.9 %collective-permute-done.4.high_ref = bf16[2,128,768]{2,1,0:T(8,128)(2,1)S(1)} collective-permute-done((bf16[2,128,768]{2,1,0:T(8,128)(2,1)}, bf16[2,128,768]{2,1,0:T(8,128)(2,1)S(1)}, u32[]{:S(2)}, u32[]{:S(2)}) %collective-permute-start.4) | collective-permute-done | bytes 393248 | tf_op jit(solution)/shard_map/ppermute | solution.py:238
  54.9 2.8 %collective-permute-done.3.low_ref = bf16[2,128,768]{2,1,0:T(8,128)(2,1)S(1)} collective-permute-done((bf16[2,128,768]{2,1,0:T(8,128)(2,1)}, bf16[2,128,768]{2,1,0:T(8,128)(2,1)S(1)}, u32[]{:S(2)}, u32[]{:S(2)}) %collective-permute-start.3) | collective-permute-done | bytes 393248 | tf_op jit(solution)/shard_map/ppermute | solution.py:238
  57.7 2.9 %far_scores.1 = (f32[4,512,256]{2,1,0:T(8,128)S(1)}, f32[4,8,1024]{2,1,0:T(8,128)S(1)}) custom-call(f32[1]{0:T(128)S(6)} %copy.14.factor_ref, s32[2]{0:T(128)S(1)} %pad_add_fusion.place_ref, bf16[4,288,768]{2,1,0:T(8,128)(2,1)S(1)} %pad_maximum_fusion.m_ref, bf16[2,128,768]{2,1,0:T(8,128)(2,1)S(1)} %collective-permute-done.3.low_ref, ...), custom_call_target="tpu_custom_call" | custom-call | tf_op jit(solution)/shard_map/far_scores/pallas_call | solution.py:318
  60.6 8.6 %all_to_all.15.stat_ref = f32[4,8,1024]{2,1,0:T(8,128)S(1)} all-to-all(f32[4,8,1024]{2,1,0:T(8,128)S(1)} %get-tuple-element.20), channel_id=1, replica_groups=mesh['gz'=8,'gx'=4,'gy'=16] {'gx'}, dimensions={0} | all-to-all | bytes 262144 | tf_op jit(solution)/shard_map/all_to_all | solution.py:328
  69.3 4.1 %grads.1 = (bf16[4,1024,256]{2,1,0:T(8,128)(2,1)S(1)}, bf16[1024,768]{1,0:T(8,128)(2,1)S(1)}, f32[1,128]{1,0:T(1,128)S(1)}) custom-call(f32[1]{0:T(128)S(6)} %copy.14.factor_ref, s32[2]{0:T(128)S(1)} %pad_add_fusion.place_ref, f32[4,512,256]{2,1,0:T(8,128)S(1)} %get-tuple-element.17.near_ref, f32[4,512,256]{2,1,0:T(8,128)S(1)} %get-tuple-element.19.far_ref, ...), custom_call_target="tpu_custom_call" | custom-call | tf_op jit(solution)/shard_map/grads/pallas_call | solution.py:331
  73.4 1.2 copy-done
  74.6 0.0 reduce-scatter.2.cloned.1.call-update
  74.6 0.0 copy-start.2
  74.6 1.0 copy-done.2
  75.6 4.4 %mention_part.1 = (bf16[256,768]{1,0:T(8,128)(2,1)S(1)}, bf16[256,768]{1,0:T(8,128)(2,1)}, bf16[256,768]{1,0:T(8,128)(2,1)}, bf16[256,768]{1,0:T(8,128)(2,1)}, f32[128,1,128]{2,1,0:T(1,128)S(1)}) custom-call(f32[1]{0:T(128)S(6)} %copy.14.factor_ref, s32[2]{0:T(128)S(1)} %pad_add_fusion.place_ref, f32[1,128]{1,0:T(1,128)S(1)} %get-tuple-element.22.scale_ref, ...), custom_call_target="tpu_custom_call" | custom-call | tf_op jit(solution)/shard_map/mention_part/pallas_call | solution.py:357
  80.0 0.7 copy-done.3
  80.8 2.3 %collective-permute-start.5 = (bf16[256,768]{1,0:T(8,128)(2,1)}, bf16[256,768]{1,0:T(8,128)(2,1)S(1)}, u32[]{:S(2)}, u32[]{:S(2)}) collective-permute-start(bf16[256,768]{1,0:T(8,128)(2,1)} %get-tuple-element.25), channel_id=1, source_target_pairs={{0,16},{16,0},{32,48},{48,32},{1,17},{17,1},{33,49},{49,33},{2,18}... | collective-permute-start | bytes 1179656 | tf_op jit(solution)/shard_map/ppermute | solution.py:238
  83.1 3.7 %collective-permute-start.6 = (bf16[256,768]{1,0:T(8,128)(2,1)}, bf16[256,768]{1,0:T(8,128)(2,1)S(1)}, u32[]{:S(2)}, u32[]{:S(2)}) collective-permute-start(bf16[256,768]{1,0:T(8,128)(2,1)} %get-tuple-element.26), channel_id=1, source_target_pairs={{0,32},{16,48},{32,0},{48,16},{1,33},{17,49},{33,1},{49,17},{2,34}... | collective-permute-start | bytes 1179656 | tf_op jit(solution)/shard_map/ppermute | solution.py:238
  86.8 3.7 %collective-permute-start.7 = (bf16[256,768]{1,0:T(8,128)(2,1)}, bf16[256,768]{1,0:T(8,128)(2,1)S(1)}, u32[]{:S(2)}, u32[]{:S(2)}) collective-permute-start(bf16[256,768]{1,0:T(8,128)(2,1)} %get-tuple-element.27), channel_id=1, source_target_pairs={{0,48},{16,32},{32,16},{48,0},{1,49},{17,33},{33,17},{49,1},{2,50}... | collective-permute-start | bytes 1179656 | tf_op jit(solution)/shard_map/ppermute | solution.py:238
  90.5 24.5 %all_to_all.16 = f32[128,1,128]{2,1,0:T(1,128)S(1)} all-to-all(f32[128,1,128]{2,1,0:T(1,128)S(1)} %get-tuple-element.28), channel_id=1, replica_groups=mesh['gz'=8,'gx'=4,'gy'=16] {'gz','gy'}, dimensions={0} | all-to-all | bytes 131072 | tf_op jit(solution)/shard_map/all_to_all | solution.py:374
  115.0 0.7 slice_reduce_fusion
  116.4 1.9 %add_convert_fusion = bf16[256,768]{1,0:T(8,128)(2,1)} fusion(bf16[256,768]{1,0:T(8,128)(2,1)S(1)} %collective-permute-done.7, bf16[256,768]{1,0:T(8,128)(2,1)S(1)} %collective-permute-done.6, bf16[256,768]{1,0:T(8,128)(2,1)S(1)} %collective-permute-done.5, bf16[256,768]{1,0:T(8,128)(2,1)} %copy-done.3), kind=kLoop, calls=%fused_computation.1 | loop fusion | flops 1572864 | bytes 1966080 | tf_op jit(solution)/shard_map/convert_element_type | solution.py:373
  118.4 2.1 %divide_subtract_fusion = (f32[128,768]{1,0:T(8,128)}, f32[128,768]{1,0:T(8,128)}, f32[128,768]{1,0:T(8,128)}) fusion(f32[128,768]{1,0:T(8,128)S(1)} %copy-done.5, bf16[128,768]{1,0:T(8,128)(2,1)} %reduce-scatter.2.cloned.1.call-done, f32[128,768]{1,0:T(8,128)S(1)} %copy-done.6, f32[128,768]{1,0:T(8,128)S(1)} %copy-done.7), kind=kLoop, calls=%fused_computation.6 | loop fusion | flops 1277952 | bytes 2555904 | tf_op jit(solution)/shard_map/sub | solution.py:227
  (19 shorter events, 0.0 us)
Async XLA Ops:
  9.1 26.0 %all-to-all-start = ((bf16[4,128,768]{2,1,0:T(8,128)(2,1)}), bf16[4,128,768]{2,1,0:T(8,128)(2,1)S(1)}, u32[]{:S(2)}, u32[]{:S(2)}) async-start(bf16[4,128,768]{2,1,0:T(8,128)(2,1)} %cast.1), calls=%async_computation | async-start | bytes 1572864 | tf_op jit(solution)/shard_map/all_to_all | solution.py:276
  19.9 98.4 %reduce-scatter.2.cloned.1.call-start = ((), (), s32[]{:S(2)}) async-start(), calls=%async_computation.4 | async-start | bytes 1769472 | tf_op jit(solution)/shard_map/reduce_scatter | solution.py:356
  21.8 27.0 %copy-start.4 = (bf16[288,768]{1,0:T(8,128)(2,1)S(1)}, bf16[288,768]{1,0:T(8,128)(2,1)}, u32[]{:S(2)}) copy-start(bf16[288,768]{1,0:T(8,128)(2,1)} %pack.1) | copy-start | bytes 1327108
  21.8 27.0 %collective-permute-start.2 = (bf16[288,768]{1,0:T(8,128)(2,1)}, bf16[288,768]{1,0:T(8,128)(2,1)S(1)}, u32[]{:S(2)}, u32[]{:S(2)}) collective-permute-start(bf16[288,768]{1,0:T(8,128)(2,1)} %pack.1), channel_id=1, source_target_pairs={{0,48},{16,32},{32,16},{48,0},{1,49},{17,33},{33,17},{49,1},{2,50}... | collective-permute-start | bytes 1327112 | tf_op jit(solution)/shard_map/ppermute | solution.py:238
  26.4 22.5 %collective-permute-start.1 = (bf16[288,768]{1,0:T(8,128)(2,1)}, bf16[288,768]{1,0:T(8,128)(2,1)S(1)}, u32[]{:S(2)}, u32[]{:S(2)}) collective-permute-start(bf16[288,768]{1,0:T(8,128)(2,1)} %pack.1), channel_id=1, source_target_pairs={{0,32},{16,48},{32,0},{48,16},{1,33},{17,49},{33,1},{49,17},{2,34}... | collective-permute-start | bytes 1327112 | tf_op jit(solution)/shard_map/ppermute | solution.py:238
  28.8 20.1 %collective-permute-start = (bf16[288,768]{1,0:T(8,128)(2,1)}, bf16[288,768]{1,0:T(8,128)(2,1)S(1)}, u32[]{:S(2)}, u32[]{:S(2)}) collective-permute-start(bf16[288,768]{1,0:T(8,128)(2,1)} %pack.1), channel_id=1, source_target_pairs={{0,16},{16,0},{32,48},{48,32},{1,17},{17,1},{33,49},{49,33},{2,18}... | collective-permute-start | bytes 1327112 | tf_op jit(solution)/shard_map/ppermute | solution.py:238
  36.0 18.9 %collective-permute-start.4 = (bf16[2,128,768]{2,1,0:T(8,128)(2,1)}, bf16[2,128,768]{2,1,0:T(8,128)(2,1)S(1)}, u32[]{:S(2)}, u32[]{:S(2)}) collective-permute-start(bf16[2,128,768]{2,1,0:T(8,128)(2,1)} %get-tuple-element.32), channel_id=1, source_target_pairs={{0,448},{64,128},{128,64},{192,256},{256,192},{320,384},{384,320},... | collective-permute-start | bytes 1179656 | tf_op jit(solution)/shard_map/ppermute | solution.py:238
  46.2 11.5 %collective-permute-start.3 = (bf16[2,128,768]{2,1,0:T(8,128)(2,1)}, bf16[2,128,768]{2,1,0:T(8,128)(2,1)S(1)}, u32[]{:S(2)}, u32[]{:S(2)}) collective-permute-start(bf16[2,128,768]{2,1,0:T(8,128)(2,1)} %get-tuple-element.33), channel_id=1, source_target_pairs={{0,64},{64,0},{128,192},{192,128},{256,320},{320,256},{384,448},{4... | collective-permute-start | bytes 1179656 | tf_op jit(solution)/shard_map/ppermute | solution.py:238
  57.7 11.6 %copy-start.1 = (bf16[2,128,768]{2,1,0:T(8,128)(2,1)}, bf16[2,128,768]{2,1,0:T(8,128)(2,1)S(1)}, u32[]{:S(2)}) copy-start(bf16[2,128,768]{2,1,0:T(8,128)(2,1)S(1)} %collective-permute-done.3.low_ref) | copy-start | bytes 1179652
  73.4 1.2 copy-start
  74.6 1.0 copy-start.2
  80.0 0.7 copy-start.3
  80.7 37.6 %copy-start.5 = (f32[128,768]{1,0:T(8,128)S(1)}, f32[128,768]{1,0:T(8,128)}, u32[]{:S(2)}) copy-start(f32[128,768]{1,0:T(8,128)} %t_ref.1) | copy-start | bytes 1179652
  80.7 37.6 %copy-start.6 = (f32[128,768]{1,0:T(8,128)S(1)}, f32[128,768]{1,0:T(8,128)}, u32[]{:S(2)}) copy-start(f32[128,768]{1,0:T(8,128)} %param.11) | copy-start | bytes 1179652
  80.7 37.6 %copy-start.7 = (f32[128,768]{1,0:T(8,128)S(1)}, f32[128,768]{1,0:T(8,128)}, u32[]{:S(2)}) copy-start(f32[128,768]{1,0:T(8,128)} %param.12) | copy-start | bytes 1179652
  80.8 35.7 %collective-permute-start.5 = (bf16[256,768]{1,0:T(8,128)(2,1)}, bf16[256,768]{1,0:T(8,128)(2,1)S(1)}, u32[]{:S(2)}, u32[]{:S(2)}) collective-permute-start(bf16[256,768]{1,0:T(8,128)(2,1)} %get-tuple-element.25), channel_id=1, source_target_pairs={{0,16},{16,0},{32,48},{48,32},{1,17},{17,1},{33,49},{49,33},{2,18}... | collective-permute-start | bytes 1179656 | tf_op jit(solution)/shard_map/ppermute | solution.py:238
  83.1 33.3 %collective-permute-start.6 = (bf16[256,768]{1,0:T(8,128)(2,1)}, bf16[256,768]{1,0:T(8,128)(2,1)S(1)}, u32[]{:S(2)}, u32[]{:S(2)}) collective-permute-start(bf16[256,768]{1,0:T(8,128)(2,1)} %get-tuple-element.26), channel_id=1, source_target_pairs={{0,32},{16,48},{32,0},{48,16},{1,33},{17,49},{33,1},{49,17},{2,34}... | collective-permute-start | bytes 1179656 | tf_op jit(solution)/shard_map/ppermute | solution.py:238
  86.8 29.7 %collective-permute-start.7 = (bf16[256,768]{1,0:T(8,128)(2,1)}, bf16[256,768]{1,0:T(8,128)(2,1)S(1)}, u32[]{:S(2)}, u32[]{:S(2)}) collective-permute-start(bf16[256,768]{1,0:T(8,128)(2,1)} %get-tuple-element.27), channel_id=1, source_target_pairs={{0,48},{16,32},{32,16},{48,0},{1,49},{17,33},{33,17},{49,1},{2,50}... | collective-permute-start | bytes 1179656 | tf_op jit(solution)/shard_map/ppermute | solution.py:238
Sparse Core Ops, SparseCore 0:
  74.7 38.1 reduce-scatter.1

commit v7 on v6

--- a/solution.py
+++ b/solution.py
@@ -23,8 +23,9 @@
 bf16 = jnp.bfloat16
 
 
-def cast_kernel(t_ref, out_ref):
+def cast_kernel(t_ref, own_ref, out_ref):
     block = t_ref[...].astype(bf16)
+    own_ref[...] = block
     for k in range(out_ref.shape[0]):
         out_ref[k] = block
 
@@ -66,16 +67,24 @@
     return jnp.bitwise_xor(place_ref[1], step)
 
 
-def join_types(place_ref, near_ref, low_ref, high_ref, tile_ref):
-    parity = lax.rem(place_ref[0], 2)
-    half = Z_SIZE // 4
-    for k in range(Z_SIZE // 2):
-        other = low_ref[k] if k < half else high_ref[k - half]
-        tile_ref[pl.ds(pl.multiple_of((2 * k + parity) * BLOCK, BLOCK), BLOCK), :] = near_ref[k]
-        tile_ref[pl.ds(pl.multiple_of((2 * k + 1 - parity) * BLOCK, BLOCK), BLOCK), :] = other
-
-
-def score_half(factor, place_ref, shift, m_ref, tile_ref, raw_ref, exp_ref):
+def other_blocks(place):
+    parity = lax.rem(place[0], 2)
+    index = lax.div(place[0], 2)
+    half = Z_SIZE // 2
+    sign = 2 * parity - 1
+    order = (index, index + sign + half, index - sign + half, index + half // 2)
+    return parity, [lax.rem(k, half) for k in order]
+
+
+def join_types(place_ref, near_ref, other_refs, tile_ref):
+    parity, order = other_blocks(place_ref)
+    lines = [2 * k + parity for k in range(Z_SIZE // 2)] + [2 * k + 1 - parity for k in order]
+    blocks = [near_ref[k] for k in range(Z_SIZE // 2)] + [ref[...] for ref in other_refs]
+    for line, block in zip(lines, blocks):
+        tile_ref[pl.ds(pl.multiple_of(line * BLOCK, BLOCK), BLOCK), :] = block
+
+
+def score_blocks(factor, place_ref, lines, m_ref, tile_ref, raw_ref, store):
     rows = m_ref.shape[1] - META_ROWS
     raw_ref[...] = lax.dot_general(
         tile_ref[...], m_ref[0, 0:rows, :], (((1,), (1,)), ((), ())), preferred_element_type=f32
@@ -88,8 +97,8 @@
     top = jnp.full((1, rows), LOW, f32)
     gold_raw = jnp.zeros((1, rows), f32)
     lives = []
-    for k in range(Z_SIZE // 2):
-        owner = owner_at(place_ref, 2 * k + shift)
+    for k, line in enumerate(lines):
+        owner = owner_at(place_ref, line)
         lives.append(jnp.max(jnp.where(owners == owner, 1.0, 0.0), axis=0, keepdims=True) > 0.0)
         raw = raw_ref[k * BLOCK : (k + 1) * BLOCK, :]
         top = jnp.maximum(top, jnp.where(lives[k], jnp.max(raw, axis=0, keepdims=True), LOW))
@@ -97,46 +106,68 @@
         gold_raw = gold_raw + jnp.sum(jnp.where(ids == gold, raw, 0.0), axis=0, keepdims=True)
     total = jnp.zeros((1, rows), f32)
     mass = jnp.zeros((1, rows), f32)
-    for k in range(Z_SIZE // 2):
+    for k in range(len(lines)):
         below = jnp.where(lives[k], top, -LOW)
         gap = raw_ref[k * BLOCK : (k + 1) * BLOCK, :] - below
         weights = jnp.exp(factor * gap)
-        exp_ref[0, k * BLOCK : (k + 1) * BLOCK, :] = weights
+        store(k, weights)
         total = total + jnp.sum(weights, axis=0, keepdims=True)
         mass = mass + jnp.sum(weights * gap, axis=0, keepdims=True)
     return top, total, mass, gold_raw
 
 
-def near_kernel(factor_ref, place_ref, m_ref, near_ref, exp_ref, stat_ref, tile_ref, raw_ref):
-    step = pl.program_id(0)
-
-    @pl.when(step == 0)
+def near_kernel(
+    factor_ref, place_ref, m_ref, near_ref, one_ref, two_ref, exp_ref, mid_ref, stat_ref, tile_ref, raw_ref
+):
+    half = Z_SIZE // 2
+
+    @pl.when(pl.program_id(0) == 0)
     def _():
-        for k in range(near_ref.shape[0]):
+        for k in range(half):
             tile_ref[k * BLOCK : (k + 1) * BLOCK, :] = near_ref[k]
-
-    shift = lax.rem(place_ref[0], 2)
-    stats = score_half(factor_ref[0], place_ref, shift, m_ref, tile_ref, raw_ref, exp_ref)
+        for k, ref in enumerate((one_ref, two_ref)):
+            tile_ref[(half + k) * BLOCK : (half + k + 1) * BLOCK, :] = ref[...]
+
+    def store(k, weights):
+        if k < half:
+            exp_ref[0, k * BLOCK : (k + 1) * BLOCK, :] = weights
+        else:
+            mid_ref[0, (k - half) * BLOCK : (k - half + 1) * BLOCK, :] = weights
+
+    parity, order = other_blocks(place_ref)
+    lines = [2 * k + parity for k in range(half)] + [2 * k + 1 - parity for k in order[:2]]
+    stats = score_blocks(factor_ref[0], place_ref, lines, m_ref, tile_ref, raw_ref, store)
     rows = stats[0].shape[1]
     rest = jnp.zeros((STAT_ROWS - len(stats), rows), f32)
     stat_ref[0] = jnp.concatenate(list(stats) + [rest], axis=0)
 
 
 def far_kernel(
-    factor_ref, place_ref, m_ref, low_ref, high_ref, part_ref, exp_ref, stat_ref, tile_ref, raw_ref
+    factor_ref, place_ref, m_ref, low_ref, high_ref, mid_ref, part_ref, exp_ref, stat_ref, tile_ref, raw_ref
 ):
     step = pl.program_id(0)
 
     @pl.when(step == 0)
     def _():
-        half = low_ref.shape[0]
-        for k in range(2 * half):
-            other = low_ref[k] if k < half else high_ref[k - half]
-            tile_ref[k * BLOCK : (k + 1) * BLOCK, :] = other
-
-    shift = 1 - lax.rem(place_ref[0], 2)
-    top, total, mass, gold_raw = score_half(
-        factor_ref[0], place_ref, shift, m_ref, tile_ref, raw_ref, exp_ref
+        for k, ref in enumerate((low_ref, high_ref)):
+            tile_ref[k * BLOCK : (k + 1) * BLOCK, :] = ref[...]
+
+    parity, order = other_blocks(place_ref)
+
+    def put(index, weights):
+        exp_ref[0, pl.ds(pl.multiple_of(index * BLOCK, BLOCK), BLOCK), :] = weights
+
+    for k in range(2):
+        put(order[k], mid_ref[0, k * BLOCK : (k + 1) * BLOCK, :])
+    lines = [2 * k + 1 - parity for k in order[2:]]
+    top, total, mass, gold_raw = score_blocks(
+        factor_ref[0],
+        place_ref,
+        lines,
+        m_ref,
+        tile_ref,
+        raw_ref,
+        lambda k, weights: put(order[2 + k], weights),
     )
     rows = top.shape[1]
     near = part_ref[0]
@@ -158,7 +189,8 @@
     masses = masses + sums * tops
     mass = jnp.sum(jnp.where(sums > 0.0, masses * shares, 0.0), axis=0, keepdims=True)
     scale = mass / total - jnp.sum(stat_ref[:, 6, :], axis=0, keepdims=True)
-    scale_ref[...] = jnp.broadcast_to(jnp.sum(scale, axis=1, keepdims=True), scale_ref.shape)
+    scale = jnp.sum(scale, axis=1, keepdims=True)
+    scale_ref[...] = jnp.broadcast_to(scale[None], scale_ref.shape)
     ids = lax.broadcasted_iota(jnp.int32, tops.shape, 0)
     for h in range(2):
         mine = ids == place_ref[1] + h * X_SIZE
@@ -180,7 +212,8 @@
             rows_ref[s * rows : (s + 1) * rows, :] = m_ref[s, 0:rows, :]
 
     ids = lax.broadcasted_iota(jnp.int32, (BLOCK, rows), 0)
-    parity = lax.rem(place_ref[0], 2)
+    parity, order = other_blocks(place_ref)
+    early = (step == order[0]) | (step == order[1])
     for s in range(X_SIZE):
         at = pl.multiple_of(tile_from(place_ref, s) * rows, BLOCK)
         meta = m_ref[s, rows + SLOTS : rows + META_ROWS, 0:rows].astype(f32)
@@ -190,7 +223,10 @@
             place = parity if h == 0 else 1 - parity
             owner = owner_at(place_ref, 2 * step + place)
             gold = jnp.where(gold_owner == owner, gold_row, -1.0).astype(jnp.int32)
-            weights = share_ref[h : h + 1, pl.ds(at, rows)] * exp_ref[s]
+            share = share_ref[0:1, pl.ds(at, rows)]
+            if h == 1:
+                share = jnp.where(early, share, share_ref[1:2, pl.ds(at, rows)])
+            weights = share * exp_ref[s]
             grad = (weights - jnp.where(ids == gold, 1.0, 0.0)).astype(bf16)
             line = pl.ds(pl.multiple_of(place * BLOCK, BLOCK), BLOCK)
             g_ref[s, line, :] = grad
@@ -199,16 +235,13 @@
     type_ref[...] = (factor * part).astype(bf16)
 
 
-def mention_kernel(
-    factor_ref, place_ref, scale_ref, g_ref, near_ref, low_ref, high_ref, *refs
-):
-    out_refs, (scales_ref, tile_ref) = refs[:X_SIZE], refs[X_SIZE:]
+def mention_kernel(factor_ref, place_ref, g_ref, near_ref, *refs):
+    other_refs, out_refs, tile_ref = refs[:4], refs[4 : 4 + X_SIZE], refs[-1]
     step = pl.program_id(0)
 
     @pl.when(step == 0)
     def _():
-        join_types(place_ref, near_ref, low_ref, high_ref, tile_ref)
-        scales_ref[...] = jnp.broadcast_to(scale_ref[...][None], scales_ref.shape)
+        join_types(place_ref, near_ref, other_refs, tile_ref)
 
     part = lax.dot_general(
         g_ref[0], tile_ref[...], (((0,), (0,)), ((), ())), preferred_element_type=f32
@@ -266,18 +299,29 @@
     def whole(*shape):
         return pl.BlockSpec(shape, lambda j: (0,) * len(shape))
 
-    copies = pl.pallas_call(
+    own, copies = pl.pallas_call(
         cast_kernel,
-        out_shape=jax.ShapeDtypeStruct((half, block_rows, width), bf16),
+        out_shape=[
+            jax.ShapeDtypeStruct((block_rows, width), bf16),
+            jax.ShapeDtypeStruct((half, block_rows, width), bf16),
+        ],
         compiler_params=params(),
         name="cast",
     )(type_table)
     parities = [list(range(p, Z_SIZE, 2)) for p in range(2)]
     near = lax.all_to_all(copies, "gz", 0, 0, tiled=True, axis_index_groups=parities)
-    low = paired(near[: half // 2], "gz", lambda z: z ^ 1)
-    high = paired(near[half // 2 :], "gz", lambda z: ((z + 1) ^ 1) - 1 & Z_SIZE - 1)
-    table = (near, low, high)
-    table_specs = [whole(t.shape[0], block_rows, width) for t in table]
+    pairings = [lambda z: z ^ 1, lambda z: ((z + 1) ^ 1) - 1 & Z_SIZE - 1]
+    one, two = [paired(own, "gz", pairing) for pairing in pairings]
+    _, order = other_blocks(place)
+    index = lax.div(place[0], 2)
+    sent = [lax.rem(2 * index - k + half, half) for k in order[2:0:-1]]
+    low, high = [
+        paired(lax.dynamic_index_in_dim(near, k, 0, keepdims=False), "gz", pairing)
+        for k, pairing in zip(sent, pairings)
+    ]
+    others = (one, two, low, high)
+    near_spec = whole(half, block_rows, width)
+    block_spec = whole(block_rows, width)
     packed = pl.pallas_call(
         lambda *refs: pack_kernel(cols, *refs),
         in_specs=[hbm] * 5,
@@ -303,32 +347,42 @@
     )
 
     half_types = half * block_rows
-    scratch = [pltpu.VMEM((half_types, width), bf16), pltpu.VMEM((half_types, rows), f32)]
+    mid_types = 2 * block_rows
     exps_shape = jax.ShapeDtypeStruct((X_SIZE, half_types, rows), f32)
-    near_exps, near_stats = pl.pallas_call(
+
+    def scratch(types):
+        return [pltpu.VMEM((types, width), bf16), pltpu.VMEM((types, rows), f32)]
+
+    near_exps, mid_exps, near_stats = pl.pallas_call(
         near_kernel,
         grid=(X_SIZE,),
-        in_specs=[smem, smem, tile(sent_rows, width)] + table_specs[:1],
-        out_specs=[tile(half_types, rows), tile(STAT_ROWS, rows)],
-        out_shape=[exps_shape, jax.ShapeDtypeStruct((X_SIZE, STAT_ROWS, rows), f32)],
-        scratch_shapes=scratch,
+        in_specs=[smem, smem, tile(sent_rows, width), near_spec] + [block_spec] * 2,
+        out_specs=[tile(half_types, rows), tile(mid_types, rows), tile(STAT_ROWS, rows)],
+        out_shape=[
+            exps_shape,
+            jax.ShapeDtypeStruct((X_SIZE, mid_types, rows), f32),
+            jax.ShapeDtypeStruct((X_SIZE, STAT_ROWS, rows), f32),
+        ],
+        scratch_shapes=scratch(half_types + mid_types),
         compiler_params=params(16),
         name="near_scores",
-    )(logit_scale, place, gathered, near)
+    )(logit_scale, place, gathered, near, one, two)
     far_exps, stats = pl.pallas_call(
         far_kernel,
         grid=(X_SIZE,),
-        in_specs=[smem, smem, tile(sent_rows, width)] + table_specs[1:] + [tile(STAT_ROWS, rows)],
+        in_specs=[smem, smem, tile(sent_rows, width)]
+        + [block_spec] * 2
+        + [tile(mid_types, rows), tile(STAT_ROWS, rows)],
         out_specs=[tile(half_types, rows), whole(X_SIZE, STAT_ROWS, X_SIZE * rows)],
         out_shape=[exps_shape, jax.ShapeDtypeStruct((X_SIZE, STAT_ROWS, X_SIZE * rows), f32)],
-        scratch_shapes=scratch,
+        scratch_shapes=scratch(mid_types),
         compiler_params=params(16),
         name="far_scores",
-    )(logit_scale, place, gathered, low, high, near_stats)
+    )(logit_scale, place, gathered, low, high, mid_exps, near_stats)
     stats = lax.all_to_all(stats, "gx", 0, 0, tiled=True)
     chunk = 2 * block_rows
     chunk_spec = pl.BlockSpec((X_SIZE, chunk, rows), lambda i: (0, i, 0))
-    grads, type_part, scale_part = pl.pallas_call(
+    grads, type_part, scale_parts = pl.pallas_call(
         grads_kernel,
         grid=(types // chunk,),
         in_specs=[
@@ -339,11 +393,11 @@
             whole(X_SIZE, STAT_ROWS, X_SIZE * rows),
             whole(X_SIZE, sent_rows, width),
         ],
-        out_specs=[chunk_spec, pl.BlockSpec((chunk, width), lambda i: (i, 0)), whole(1, 128)],
+        out_specs=[chunk_spec, pl.BlockSpec((chunk, width), lambda i: (i, 0)), whole(Z_SIZE * cols, 1, 128)],
         out_shape=[
             jax.ShapeDtypeStruct((X_SIZE, types, rows), bf16),
             jax.ShapeDtypeStruct((types, width), bf16),
-            jax.ShapeDtypeStruct((1, 128), f32),
+            jax.ShapeDtypeStruct((Z_SIZE * cols, 1, 128), f32),
         ],
         scratch_shapes=[
             pltpu.VMEM((2, X_SIZE * rows), f32),
@@ -354,17 +408,16 @@
         name="grads",
     )(logit_scale, place, near_exps, far_exps, stats, gathered)
     type_grad = lax.psum_scatter(type_part, "gz", scatter_dimension=0, tiled=True)
-    *parts, scale_parts = pl.pallas_call(
+    parts = pl.pallas_call(
         mention_kernel,
         grid=(X_SIZE,),
-        in_specs=[smem, smem, whole(1, 128), tile(types, rows)] + table_specs,
-        out_specs=[whole(rows, width)] * X_SIZE + [whole(Z_SIZE * cols, 1, 128)],
-        out_shape=[jax.ShapeDtypeStruct((rows, width), bf16)] * X_SIZE
-        + [jax.ShapeDtypeStruct((Z_SIZE * cols, 1, 128), f32)],
+        in_specs=[smem, smem, tile(types, rows), near_spec] + [block_spec] * 4,
+        out_specs=[whole(rows, width)] * X_SIZE,
+        out_shape=[jax.ShapeDtypeStruct((rows, width), bf16)] * X_SIZE,
         scratch_shapes=[pltpu.VMEM((types, width), bf16)],
         compiler_params=params(16),
         name="mention_part",
-    )(logit_scale, place, scale_part, grads, *table)
+    )(logit_scale, place, grads, near, *others)
     mention_grad = parts[0].astype(f32)
     for s in range(1, X_SIZE):
         mention_grad = mention_grad + paired(

time: 129 us -> 131 us (1.016)
  waiting for transfers between devices: 9.79 us -> 7.02 us
  blocking collectives: 33.2 us -> 35.5 us
  starting transfers between devices: 41.7 us -> 44 us
    all_to_all x1, waiting for transfers between devices: 4.13 us -> 0.01 us  [per_device(): lax.all_to_all(copies, 'gz', 0, 0, tiled=True, axis_index_groups=parities)]
    all_to_all x1, blocking collectives: 24.5 us -> 27.1 us  [per_device(): scale_parts = lax.all_to_all(scale_parts, ('gz', 'gy'), 0, 0, tiled=True)]
    ppermute x8 -> x10, starting transfers between devices: 30.9 us -> 33.2 us  [paired(): lax.ppermute(array, axis, [(i, partner(i)) for i in range(lax.axis_size(a...]
    ppermute x8 -> x10, waiting for transfers between devices: 5.64 us -> 7 us  [paired(): lax.ppermute(array, axis, [(i, partner(i)) for i in range(lax.axis_size(a...]
    unnamed x16 -> x14, local copies, waits for them, and re-layouts: 2.92 us -> 2.84 us
  transfers between devices with their start and end apart: 10 -> 12, of which waited for: 3 -> 1; matrix products, arithmetic and copies ran while one was open for 3% -> 3% of each run, Pallas kernels for 7% -> 8%
where the time goes in v7:
time: 131 us
  starting transfers between devices  44 us (34%)
  blocking collectives  35.5 us (27%)
  Pallas kernels  18.3 us (14%)
  between operations  16.7 us (13%)
  waiting for transfers between devices  7.02 us (5%)
  other arithmetic  6.06 us (5%)
  local copies, waits for them, and re-layouts  2.87 us (2%)
    ppermute x10, starting transfers between devices, paired(): lax.ppermute(array, axis, [(i, partner(i)) for i in range(lax.axis_size(a...  33.2 us
    all_to_all x1, blocking collectives, per_device(): scale_parts = lax.all_to_all(scale_parts, ('gz', 'gy'), 0, 0, tiled=True)  27.1 us
    all_to_all x1, starting transfers between devices, per_device(): lax.all_to_all(copies, 'gz', 0, 0, tiled=True, axis_index_groups=parities)  10.8 us
    all_to_all x1, blocking collectives, per_device(): stats = lax.all_to_all(stats, 'gx', 0, 0, tiled=True)  8.37 us
    ppermute x10, waiting for transfers between devices, paired(): lax.ppermute(array, axis, [(i, partner(i)) for i in range(lax.axis_size(a...  7 us
    pallas_call x1, Pallas kernels, per_device(): pl.pallas_call(mention_kernel, grid=(X_SIZE,), in_specs=[smem, smem, tile...  4.4 us
    pallas_call x1, Pallas kernels, per_device(): pl.pallas_call(grads_kernel, grid=(types // chunk,), in_specs=[smem, smem...  4.12 us
    pallas_call x1, Pallas kernels, per_device(): pl.pallas_call(near_kernel, grid=(X_SIZE,), in_specs=[smem, smem, tile(se...  3.67 us
  transfers between devices with their start and end apart: 12, of which 1 were waited for; matrix products, arithmetic and copies ran while one was open for 3% of the time, Pallas kernels for 8%

profile of v7, /device:TPU:1, one launch (start us, length us, event | category | flops | bytes accessed | tf_op | source)
XLA Modules:
  0.0 130.6 jit_solution(1734094276014712806)
XLA Ops:
  7.2 2.0 %cast.1 = (bf16[128,768]{1,0:T(8,128)(2,1)}, bf16[4,128,768]{2,1,0:T(8,128)(2,1)}) custom-call(f32[128,768]{1,0:T(8,128)} %t_ref.1), custom_call_target="tpu_custom_call" | custom-call | tf_op jit(solution)/shard_map/cast/pallas_call | solution.py:302
  9.2 10.8 %all-to-all-start = ((bf16[4,128,768]{2,1,0:T(8,128)(2,1)}), bf16[4,128,768]{2,1,0:T(8,128)(2,1)S(1)}, u32[]{:S(2)}, u32[]{:S(2)}) async-start(bf16[4,128,768]{2,1,0:T(8,128)(2,1)} %get-tuple-element.19), calls=%async_computation | async-start | bytes 1572864 | tf_op jit(solution)/shard_map/all_to_all | solution.py:312
  20.0 1.9 %pack.1 = bf16[288,768]{1,0:T(8,128)(2,1)} custom-call(s32[2,16]{1,0:T(2,128)} %refs_0_.1, s32[1,2]{1,0:T(1,128)} %bitcast.20, s32[1,256]{1,0:T(1,128)} %bitcast.18, s32[1,256]{1,0:T(1,128)} %bitcast.19, bf16[256,768]{1,0:T(8,128)(2,1)} %refs_4_.1), custom_call_target="tpu_custom_call" | custom-call | tf_op jit(solution)/shard_map/pack/pallas_call | solution.py:325
  21.9 4.4 %collective-permute-start.2 = (bf16[288,768]{1,0:T(8,128)(2,1)}, bf16[288,768]{1,0:T(8,128)(2,1)S(1)}, u32[]{:S(2)}, u32[]{:S(2)}) collective-permute-start(bf16[288,768]{1,0:T(8,128)(2,1)} %pack.1), channel_id=1, source_target_pairs={{0,48},{16,32},{32,16},{48,0},{1,49},{17,33},{33,17},{49,1},{2,50}... | collective-permute-start | bytes 1327112 | tf_op jit(solution)/shard_map/ppermute | solution.py:271
  26.3 2.4 %collective-permute-start.1 = (bf16[288,768]{1,0:T(8,128)(2,1)}, bf16[288,768]{1,0:T(8,128)(2,1)S(1)}, u32[]{:S(2)}, u32[]{:S(2)}) collective-permute-start(bf16[288,768]{1,0:T(8,128)(2,1)} %pack.1), channel_id=1, source_target_pairs={{0,32},{16,48},{32,0},{48,16},{1,33},{17,49},{33,1},{49,17},{2,34}... | collective-permute-start | bytes 1327112 | tf_op jit(solution)/shard_map/ppermute | solution.py:271
  28.7 2.2 %collective-permute-start = (bf16[288,768]{1,0:T(8,128)(2,1)}, bf16[288,768]{1,0:T(8,128)(2,1)S(1)}, u32[]{:S(2)}, u32[]{:S(2)}) collective-permute-start(bf16[288,768]{1,0:T(8,128)(2,1)} %pack.1), channel_id=1, source_target_pairs={{0,16},{16,0},{32,48},{48,32},{1,17},{17,1},{33,49},{49,33},{2,18}... | collective-permute-start | bytes 1327112 | tf_op jit(solution)/shard_map/ppermute | solution.py:271
  30.9 5.5 %collective-permute-start.4 = (bf16[128,768]{1,0:T(8,128)(2,1)}, bf16[128,768]{1,0:T(8,128)(2,1)S(1)}, u32[]{:S(2)}, u32[]{:S(2)}) collective-permute-start(bf16[128,768]{1,0:T(8,128)(2,1)} %get-tuple-element.20), channel_id=1, source_target_pairs={{0,448},{64,128},{128,64},{192,256},{256,192},{320,384},{384,320},... | collective-permute-start | bytes 589832 | tf_op jit(solution)/shard_map/ppermute | solution.py:271
  36.4 1.9 %collective-permute-start.3 = (bf16[128,768]{1,0:T(8,128)(2,1)}, bf16[128,768]{1,0:T(8,128)(2,1)S(1)}, u32[]{:S(2)}, u32[]{:S(2)}) collective-permute-start(bf16[128,768]{1,0:T(8,128)(2,1)} %get-tuple-element.20), channel_id=1, source_target_pairs={{0,64},{64,0},{128,192},{192,128},{256,320},{320,256},{384,448},{4... | collective-permute-start | bytes 589832 | tf_op jit(solution)/shard_map/ppermute | solution.py:271
  38.4 0.0 all-to-all-done.near_ref
  38.4 7.0 %collective-permute-done.2 = bf16[288,768]{1,0:T(8,128)(2,1)S(1)} collective-permute-done((bf16[288,768]{1,0:T(8,128)(2,1)}, bf16[288,768]{1,0:T(8,128)(2,1)S(1)}, u32[]{:S(2)}, u32[]{:S(2)}) %collective-permute-start.2) | collective-permute-done | bytes 442400 | tf_op jit(solution)/shard_map/ppermute | solution.py:271
  45.4 5.2 %collective-permute-start.6 = (bf16[128,768]{1,0:T(8,128)(2,1)S(1)}, bf16[128,768]{1,0:T(8,128)(2,1)S(1)}, u32[]{:S(2)}, u32[]{:S(2)}) collective-permute-start(bf16[128,768]{1,0:T(8,128)(2,1)S(1)} %get-tuple-element.36), channel_id=1, source_target_pairs={{0,448},{64,128},{128,64},{192,256},{256,192},{320,384},{384,320},... | collective-permute-start | bytes 589832 | tf_op jit(solution)/shard_map/ppermute | solution.py:271
  50.6 1.9 %collective-permute-start.5 = (bf16[128,768]{1,0:T(8,128)(2,1)S(1)}, bf16[128,768]{1,0:T(8,128)(2,1)S(1)}, u32[]{:S(2)}, u32[]{:S(2)}) collective-permute-start(bf16[128,768]{1,0:T(8,128)(2,1)S(1)} %get-tuple-element.37), channel_id=1, source_target_pairs={{0,64},{64,0},{128,192},{192,128},{256,320},{320,256},{384,448},{4... | collective-permute-start | bytes 589832 | tf_op jit(solution)/shard_map/ppermute | solution.py:271
  52.6 0.1 pad_add_fusion.place_ref
  53.3 1.2 pad_maximum_fusion.m_ref
  54.6 0.0 copy-start.1
  54.6 3.7 %near_scores.1 = (f32[4,512,256]{2,1,0:T(8,128)S(1)}, f32[4,256,256]{2,1,0:T(8,128)S(1)}, f32[4,8,256]{2,1,0:T(8,128)S(1)}) custom-call(f32[1]{0:T(128)S(6)} %copy.14.factor_ref, s32[2]{0:T(128)S(1)} %pad_add_fusion.place_ref, bf16[4,288,768]{2,1,0:T(8,128)(2,1)S(1)} %pad_maximum_fusion.m_ref, bf16[4,128,768]{2,1,0:T(8,128)(2,1)S(1)} %all-to-all-done.near_ref, ...), custom_call_target="tpu_custom_call" | custom-call | tf_op jit(solution)/shard_map/near_scores/pallas_call | solution.py:356
  58.3 2.3 %far_scores.1 = (f32[4,512,256]{2,1,0:T(8,128)S(1)}, f32[4,8,1024]{2,1,0:T(8,128)S(1)}) custom-call(f32[1]{0:T(128)S(6)} %copy.14.factor_ref, s32[2]{0:T(128)S(1)} %pad_add_fusion.place_ref, bf16[4,288,768]{2,1,0:T(8,128)(2,1)S(1)} %pad_maximum_fusion.m_ref, bf16[128,768]{1,0:T(8,128)(2,1)S(1)} %collective-permute-done.5.low_ref.refs_2_, ...), custom_call_target="tpu_custom_call" | custom-call | tf_op jit(solution)/shard_map/far_scores/pallas_call | solution.py:370
  60.5 8.4 %all_to_all.15.stat_ref = f32[4,8,1024]{2,1,0:T(8,128)S(1)} all-to-all(f32[4,8,1024]{2,1,0:T(8,128)S(1)} %get-tuple-element.25), channel_id=1, replica_groups=mesh['gz'=8,'gx'=4,'gy'=16] {'gx'}, dimensions={0} | all-to-all | bytes 262144 | tf_op jit(solution)/shard_map/all_to_all | solution.py:382
  68.9 4.1 %grads.1 = (bf16[4,1024,256]{2,1,0:T(8,128)(2,1)S(1)}, bf16[1024,768]{1,0:T(8,128)(2,1)S(1)}, f32[128,1,128]{2,1,0:T(1,128)S(1)}) custom-call(f32[1]{0:T(128)S(6)} %copy.14.factor_ref, s32[2]{0:T(128)S(1)} %pad_add_fusion.place_ref, f32[4,512,256]{2,1,0:T(8,128)S(1)} %get-tuple-element.21.near_ref, f32[4,512,256]{2,1,0:T(8,128)S(1)} %get-tuple-element.24.far_ref, ...), custom_call_target="tpu_custom_call" | custom-call | tf_op jit(solution)/shard_map/grads/pallas_call | solution.py:385
  73.1 1.2 copy-done
  74.2 0.0 reduce-scatter.2.cloned.1.call-update
  74.2 0.0 copy-start.2
  74.2 0.9 copy-done.2
  75.2 4.4 %mention_part.1 = (bf16[256,768]{1,0:T(8,128)(2,1)S(1)}, bf16[256,768]{1,0:T(8,128)(2,1)}, bf16[256,768]{1,0:T(8,128)(2,1)}, bf16[256,768]{1,0:T(8,128)(2,1)}) custom-call(f32[1]{0:T(128)S(6)} %copy.14.factor_ref, s32[2]{0:T(128)S(1)} %pad_add_fusion.place_ref, bf16[4,1024,256]{2,1,0:T(8,128)(2,1)S(1)} %get-tuple-element.27.g_ref, ...), custom_call_target="tpu_custom_call" | custom-call | tf_op jit(solution)/shard_map/mention_part/pallas_call | solution.py:411
  79.6 0.7 copy-done.3
  80.3 2.3 %collective-permute-start.7 = (bf16[256,768]{1,0:T(8,128)(2,1)}, bf16[256,768]{1,0:T(8,128)(2,1)S(1)}, u32[]{:S(2)}, u32[]{:S(2)}) collective-permute-start(bf16[256,768]{1,0:T(8,128)(2,1)} %get-tuple-element.29), channel_id=1, source_target_pairs={{0,16},{16,0},{32,48},{48,32},{1,17},{17,1},{33,49},{49,33},{2,18}... | collective-permute-start | bytes 1179656 | tf_op jit(solution)/shard_map/ppermute | solution.py:271
  82.6 3.7 %collective-permute-start.8 = (bf16[256,768]{1,0:T(8,128)(2,1)}, bf16[256,768]{1,0:T(8,128)(2,1)S(1)}, u32[]{:S(2)}, u32[]{:S(2)}) collective-permute-start(bf16[256,768]{1,0:T(8,128)(2,1)} %get-tuple-element.30), channel_id=1, source_target_pairs={{0,32},{16,48},{32,0},{48,16},{1,33},{17,49},{33,1},{49,17},{2,34}... | collective-permute-start | bytes 1179656 | tf_op jit(solution)/shard_map/ppermute | solution.py:271
  86.4 3.7 %collective-permute-start.9 = (bf16[256,768]{1,0:T(8,128)(2,1)}, bf16[256,768]{1,0:T(8,128)(2,1)S(1)}, u32[]{:S(2)}, u32[]{:S(2)}) collective-permute-start(bf16[256,768]{1,0:T(8,128)(2,1)} %get-tuple-element.31), channel_id=1, source_target_pairs={{0,48},{16,32},{32,16},{48,0},{1,49},{17,33},{33,17},{49,1},{2,50}... | collective-permute-start | bytes 1179656 | tf_op jit(solution)/shard_map/ppermute | solution.py:271
  90.0 27.1 %all_to_all.16 = f32[128,1,128]{2,1,0:T(1,128)S(1)} all-to-all(f32[128,1,128]{2,1,0:T(1,128)S(1)} %get-tuple-element.32), channel_id=1, replica_groups=mesh['gz'=8,'gx'=4,'gy'=16] {'gz','gy'}, dimensions={0} | all-to-all | bytes 131072 | tf_op jit(solution)/shard_map/all_to_all | solution.py:427
  117.2 0.7 slice_reduce_fusion
  118.6 1.9 %add_convert_fusion = bf16[256,768]{1,0:T(8,128)(2,1)} fusion(bf16[256,768]{1,0:T(8,128)(2,1)S(1)} %collective-permute-done.9, bf16[256,768]{1,0:T(8,128)(2,1)S(1)} %collective-permute-done.8, bf16[256,768]{1,0:T(8,128)(2,1)S(1)} %collective-permute-done.7, bf16[256,768]{1,0:T(8,128)(2,1)} %copy-done.3), kind=kLoop, calls=%fused_computation.1 | loop fusion | flops 1572864 | bytes 1966080 | tf_op jit(solution)/shard_map/convert_element_type | solution.py:426
  120.5 2.1 %divide_subtract_fusion = (f32[128,768]{1,0:T(8,128)}, f32[128,768]{1,0:T(8,128)}, f32[128,768]{1,0:T(8,128)}) fusion(f32[128,768]{1,0:T(8,128)S(1)} %copy-done.4, bf16[128,768]{1,0:T(8,128)(2,1)} %reduce-scatter.2.cloned.1.call-done, f32[128,768]{1,0:T(8,128)S(1)} %copy-done.5, f32[128,768]{1,0:T(8,128)S(1)} %copy-done.6), kind=kLoop, calls=%fused_computation.6 | loop fusion | flops 1277952 | bytes 2555904 | tf_op jit(solution)/shard_map/sub | solution.py:260
  (21 shorter events, 0.1 us)
Async XLA Ops:
  9.2 29.2 %all-to-all-start = ((bf16[4,128,768]{2,1,0:T(8,128)(2,1)}), bf16[4,128,768]{2,1,0:T(8,128)(2,1)S(1)}, u32[]{:S(2)}, u32[]{:S(2)}) async-start(bf16[4,128,768]{2,1,0:T(8,128)(2,1)} %get-tuple-element.19), calls=%async_computation | async-start | bytes 1572864 | tf_op jit(solution)/shard_map/all_to_all | solution.py:312
  20.0 100.5 %reduce-scatter.2.cloned.1.call-start = ((), (), s32[]{:S(2)}) async-start(), calls=%async_computation.4 | async-start | bytes 1769472 | tf_op jit(solution)/shard_map/reduce_scatter | solution.py:410
  21.9 23.5 %collective-permute-start.2 = (bf16[288,768]{1,0:T(8,128)(2,1)}, bf16[288,768]{1,0:T(8,128)(2,1)S(1)}, u32[]{:S(2)}, u32[]{:S(2)}) collective-permute-start(bf16[288,768]{1,0:T(8,128)(2,1)} %pack.1), channel_id=1, source_target_pairs={{0,48},{16,32},{32,16},{48,0},{1,49},{17,33},{33,17},{49,1},{2,50}... | collective-permute-start | bytes 1327112 | tf_op jit(solution)/shard_map/ppermute | solution.py:271
  26.3 24.3 %collective-permute-start.1 = (bf16[288,768]{1,0:T(8,128)(2,1)}, bf16[288,768]{1,0:T(8,128)(2,1)S(1)}, u32[]{:S(2)}, u32[]{:S(2)}) collective-permute-start(bf16[288,768]{1,0:T(8,128)(2,1)} %pack.1), channel_id=1, source_target_pairs={{0,32},{16,48},{32,0},{48,16},{1,33},{17,49},{33,1},{49,17},{2,34}... | collective-permute-start | bytes 1327112 | tf_op jit(solution)/shard_map/ppermute | solution.py:271
  28.7 24.5 %collective-permute-start = (bf16[288,768]{1,0:T(8,128)(2,1)}, bf16[288,768]{1,0:T(8,128)(2,1)S(1)}, u32[]{:S(2)}, u32[]{:S(2)}) collective-permute-start(bf16[288,768]{1,0:T(8,128)(2,1)} %pack.1), channel_id=1, source_target_pairs={{0,16},{16,0},{32,48},{48,32},{1,17},{17,1},{33,49},{49,33},{2,18}... | collective-permute-start | bytes 1327112 | tf_op jit(solution)/shard_map/ppermute | solution.py:271
  30.9 23.6 %collective-permute-start.4 = (bf16[128,768]{1,0:T(8,128)(2,1)}, bf16[128,768]{1,0:T(8,128)(2,1)S(1)}, u32[]{:S(2)}, u32[]{:S(2)}) collective-permute-start(bf16[128,768]{1,0:T(8,128)(2,1)} %get-tuple-element.20), channel_id=1, source_target_pairs={{0,448},{64,128},{128,64},{192,256},{256,192},{320,384},{384,320},... | collective-permute-start | bytes 589832 | tf_op jit(solution)/shard_map/ppermute | solution.py:271
  36.4 18.1 %collective-permute-start.3 = (bf16[128,768]{1,0:T(8,128)(2,1)}, bf16[128,768]{1,0:T(8,128)(2,1)S(1)}, u32[]{:S(2)}, u32[]{:S(2)}) collective-permute-start(bf16[128,768]{1,0:T(8,128)(2,1)} %get-tuple-element.20), channel_id=1, source_target_pairs={{0,64},{64,0},{128,192},{192,128},{256,320},{320,256},{384,448},{4... | collective-permute-start | bytes 589832 | tf_op jit(solution)/shard_map/ppermute | solution.py:271
  45.4 12.8 %collective-permute-start.6 = (bf16[128,768]{1,0:T(8,128)(2,1)S(1)}, bf16[128,768]{1,0:T(8,128)(2,1)S(1)}, u32[]{:S(2)}, u32[]{:S(2)}) collective-permute-start(bf16[128,768]{1,0:T(8,128)(2,1)S(1)} %get-tuple-element.36), channel_id=1, source_target_pairs={{0,448},{64,128},{128,64},{192,256},{256,192},{320,384},{384,320},... | collective-permute-start | bytes 589832 | tf_op jit(solution)/shard_map/ppermute | solution.py:271
  50.6 7.6 %collective-permute-start.5 = (bf16[128,768]{1,0:T(8,128)(2,1)S(1)}, bf16[128,768]{1,0:T(8,128)(2,1)S(1)}, u32[]{:S(2)}, u32[]{:S(2)}) collective-permute-start(bf16[128,768]{1,0:T(8,128)(2,1)S(1)} %get-tuple-element.37), channel_id=1, source_target_pairs={{0,64},{64,0},{128,192},{192,128},{256,320},{320,256},{384,448},{4... | collective-permute-start | bytes 589832 | tf_op jit(solution)/shard_map/ppermute | solution.py:271
  54.6 6.0 %copy-start.1 = (bf16[128,768]{1,0:T(8,128)(2,1)}, bf16[128,768]{1,0:T(8,128)(2,1)S(1)}, u32[]{:S(2)}) copy-start(bf16[128,768]{1,0:T(8,128)(2,1)S(1)} %collective-permute-done.3.one_ref.refs_0_) | copy-start | bytes 589828
  73.0 1.2 copy-start
  74.2 0.9 copy-start.2
  79.6 0.7 copy-start.3
  80.3 40.2 %copy-start.4 = (f32[128,768]{1,0:T(8,128)S(1)}, f32[128,768]{1,0:T(8,128)}, u32[]{:S(2)}) copy-start(f32[128,768]{1,0:T(8,128)} %t_ref.1) | copy-start | bytes 1179652
  80.3 40.2 %copy-start.5 = (f32[128,768]{1,0:T(8,128)S(1)}, f32[128,768]{1,0:T(8,128)}, u32[]{:S(2)}) copy-start(f32[128,768]{1,0:T(8,128)} %param.11) | copy-start | bytes 1179652
  80.3 40.2 %copy-start.6 = (f32[128,768]{1,0:T(8,128)S(1)}, f32[128,768]{1,0:T(8,128)}, u32[]{:S(2)}) copy-start(f32[128,768]{1,0:T(8,128)} %param.12) | copy-start | bytes 1179652
  80.3 38.2 %collective-permute-start.7 = (bf16[256,768]{1,0:T(8,128)(2,1)}, bf16[256,768]{1,0:T(8,128)(2,1)S(1)}, u32[]{:S(2)}, u32[]{:S(2)}) collective-permute-start(bf16[256,768]{1,0:T(8,128)(2,1)} %get-tuple-element.29), channel_id=1, source_target_pairs={{0,16},{16,0},{32,48},{48,32},{1,17},{17,1},{33,49},{49,33},{2,18}... | collective-permute-start | bytes 1179656 | tf_op jit(solution)/shard_map/ppermute | solution.py:271
  82.6 35.9 %collective-permute-start.8 = (bf16[256,768]{1,0:T(8,128)(2,1)}, bf16[256,768]{1,0:T(8,128)(2,1)S(1)}, u32[]{:S(2)}, u32[]{:S(2)}) collective-permute-start(bf16[256,768]{1,0:T(8,128)(2,1)} %get-tuple-element.30), channel_id=1, source_target_pairs={{0,32},{16,48},{32,0},{48,16},{1,33},{17,49},{33,1},{49,17},{2,34}... | collective-permute-start | bytes 1179656 | tf_op jit(solution)/shard_map/ppermute | solution.py:271
  86.4 32.2 %collective-permute-start.9 = (bf16[256,768]{1,0:T(8,128)(2,1)}, bf16[256,768]{1,0:T(8,128)(2,1)S(1)}, u32[]{:S(2)}, u32[]{:S(2)}) collective-permute-start(bf16[256,768]{1,0:T(8,128)(2,1)} %get-tuple-element.31), channel_id=1, source_target_pairs={{0,48},{16,32},{32,16},{48,0},{1,49},{17,33},{33,17},{49,1},{2,50}... | collective-permute-start | bytes 1179656 | tf_op jit(solution)/shard_map/ppermute | solution.py:271
Sparse Core Ops, SparseCore 0:
  74.4 40.6 reduce-scatter.1

commit v8 on v6

--- a/solution.py
+++ b/solution.py
@@ -19,6 +19,7 @@
 META_ROWS = 32
 SLOTS = 16
 STAT_ROWS = 8
+SCALE_LANES = 768
 f32 = jnp.float32
 bf16 = jnp.bfloat16
 
@@ -158,7 +159,8 @@
     masses = masses + sums * tops
     mass = jnp.sum(jnp.where(sums > 0.0, masses * shares, 0.0), axis=0, keepdims=True)
     scale = mass / total - jnp.sum(stat_ref[:, 6, :], axis=0, keepdims=True)
-    scale_ref[...] = jnp.broadcast_to(jnp.sum(scale, axis=1, keepdims=True), scale_ref.shape)
+    scale = jnp.sum(scale, axis=1, keepdims=True)
+    scale_ref[...] = jnp.broadcast_to(scale[None], scale_ref.shape)
     ids = lax.broadcasted_iota(jnp.int32, tops.shape, 0)
     for h in range(2):
         mine = ids == place_ref[1] + h * X_SIZE
@@ -199,16 +201,13 @@
     type_ref[...] = (factor * part).astype(bf16)
 
 
-def mention_kernel(
-    factor_ref, place_ref, scale_ref, g_ref, near_ref, low_ref, high_ref, *refs
-):
-    out_refs, (scales_ref, tile_ref) = refs[:X_SIZE], refs[X_SIZE:]
+def mention_kernel(factor_ref, place_ref, g_ref, near_ref, low_ref, high_ref, *refs):
+    out_refs, tile_ref = refs[:X_SIZE], refs[-1]
     step = pl.program_id(0)
 
     @pl.when(step == 0)
     def _():
         join_types(place_ref, near_ref, low_ref, high_ref, tile_ref)
-        scales_ref[...] = jnp.broadcast_to(scale_ref[...][None], scales_ref.shape)
 
     part = lax.dot_general(
         g_ref[0], tile_ref[...], (((0,), (0,)), ((), ())), preferred_element_type=f32
@@ -327,8 +326,9 @@
     )(logit_scale, place, gathered, low, high, near_stats)
     stats = lax.all_to_all(stats, "gx", 0, 0, tiled=True)
     chunk = 2 * block_rows
+    scale_shape = (Z_SIZE * cols, 1, SCALE_LANES)
     chunk_spec = pl.BlockSpec((X_SIZE, chunk, rows), lambda i: (0, i, 0))
-    grads, type_part, scale_part = pl.pallas_call(
+    grads, type_part, scale_parts = pl.pallas_call(
         grads_kernel,
         grid=(types // chunk,),
         in_specs=[
@@ -339,11 +339,11 @@
             whole(X_SIZE, STAT_ROWS, X_SIZE * rows),
             whole(X_SIZE, sent_rows, width),
         ],
-        out_specs=[chunk_spec, pl.BlockSpec((chunk, width), lambda i: (i, 0)), whole(1, 128)],
+        out_specs=[chunk_spec, pl.BlockSpec((chunk, width), lambda i: (i, 0)), whole(*scale_shape)],
         out_shape=[
             jax.ShapeDtypeStruct((X_SIZE, types, rows), bf16),
             jax.ShapeDtypeStruct((types, width), bf16),
-            jax.ShapeDtypeStruct((1, 128), f32),
+            jax.ShapeDtypeStruct(scale_shape, f32),
         ],
         scratch_shapes=[
             pltpu.VMEM((2, X_SIZE * rows), f32),
@@ -354,17 +354,16 @@
         name="grads",
     )(logit_scale, place, near_exps, far_exps, stats, gathered)
     type_grad = lax.psum_scatter(type_part, "gz", scatter_dimension=0, tiled=True)
-    *parts, scale_parts = pl.pallas_call(
+    parts = pl.pallas_call(
         mention_kernel,
         grid=(X_SIZE,),
-        in_specs=[smem, smem, whole(1, 128), tile(types, rows)] + table_specs,
-        out_specs=[whole(rows, width)] * X_SIZE + [whole(Z_SIZE * cols, 1, 128)],
-        out_shape=[jax.ShapeDtypeStruct((rows, width), bf16)] * X_SIZE
-        + [jax.ShapeDtypeStruct((Z_SIZE * cols, 1, 128), f32)],
+        in_specs=[smem, smem, tile(types, rows)] + table_specs,
+        out_specs=[whole(rows, width)] * X_SIZE,
+        out_shape=[jax.ShapeDtypeStruct((rows, width), bf16)] * X_SIZE,
         scratch_shapes=[pltpu.VMEM((types, width), bf16)],
         compiler_params=params(16),
         name="mention_part",
-    )(logit_scale, place, scale_part, grads, *table)
+    )(logit_scale, place, grads, *table)
     mention_grad = parts[0].astype(f32)
     for s in range(1, X_SIZE):
         mention_grad = mention_grad + paired(

time: 129 us -> 135 us (1.047)
  blocking collectives: 33.2 us -> 8.64 us
  waiting for transfers between devices: 9.79 us -> 27.5 us
  starting transfers between devices: 41.7 us -> 54.6 us
    all_to_all x1 -> x0, blocking collectives: 24.5 us -> none  [per_device(): scale_parts = lax.all_to_all(scale_parts, ('gz', 'gy'), 0, 0, tiled=True)]
    ppermute x8, waiting for transfers between devices: 5.64 us -> 23.3 us  [paired(): lax.ppermute(array, axis, [(i, partner(i)) for i in range(lax.axis_size(a...]
    all_to_all x0 -> x1, starting transfers between devices: none -> 12.9 us  [per_device(): scale_parts = lax.all_to_all(scale_parts, ('gz', 'gy'), 0, 0, tiled=True)]
  transfers between devices with their start and end apart: 10 -> 11, of which waited for: 3 -> 6; matrix products, arithmetic and copies ran while one was open for 3% -> 3% of each run, Pallas kernels for 7% -> 6%
where the time goes in v8:
time: 135 us; the launch traced here: 133 us
  starting transfers between devices  54.6 us (40%)
  waiting for transfers between devices  27.5 us (20%)
  Pallas kernels  17.2 us (13%)
  between operations  16.7 us (12%)
  blocking collectives  8.64 us (6%)
  other arithmetic  4.9 us (4%)
  local copies, waits for them, and re-layouts  3.84 us (3%)
    ppermute x8, starting transfers between devices, paired(): lax.ppermute(array, axis, [(i, partner(i)) for i in range(lax.axis_size(a...  30.9 us
    ppermute x8, waiting for transfers between devices, paired(): lax.ppermute(array, axis, [(i, partner(i)) for i in range(lax.axis_size(a...  23.3 us
    all_to_all x1, starting transfers between devices, per_device(): scale_parts = lax.all_to_all(scale_parts, ('gz', 'gy'), 0, 0, tiled=True)  12.9 us
    all_to_all x1, starting transfers between devices, per_device(): lax.all_to_all(copies, 'gz', 0, 0, tiled=True, axis_index_groups=parities)  10.8 us
    all_to_all x1, blocking collectives, per_device(): stats = lax.all_to_all(stats, 'gx', 0, 0, tiled=True)  8.64 us
    all_to_all x1, waiting for transfers between devices, per_device(): lax.all_to_all(copies, 'gz', 0, 0, tiled=True, axis_index_groups=parities)  4.14 us
    pallas_call x1, Pallas kernels, per_device(): pl.pallas_call(grads_kernel, grid=(types // chunk,), in_specs=[smem, smem...  4.12 us
    pallas_call x1, Pallas kernels, per_device(): pl.pallas_call(mention_kernel, grid=(X_SIZE,), in_specs=[smem, smem, tile...  3.37 us
  transfers between devices with their start and end apart: 11, of which 6 were waited for; matrix products, arithmetic and copies ran while one was open for 3% of the time, Pallas kernels for 6%

profile of v8, /device:TPU:1, one launch (start us, length us, event | category | flops | bytes accessed | tf_op | source)
XLA Modules:
  0.0 133.4 jit_solution(17852392779568636891)
XLA Ops:
  7.2 1.9 %cast.1 = bf16[4,128,768]{2,1,0:T(8,128)(2,1)} custom-call(f32[128,768]{1,0:T(8,128)} %t_ref.1), custom_call_target="tpu_custom_call" | custom-call | tf_op jit(solution)/shard_map/cast/pallas_call | solution.py:268
  9.1 10.8 %all-to-all-start = ((bf16[4,128,768]{2,1,0:T(8,128)(2,1)}), bf16[4,128,768]{2,1,0:T(8,128)(2,1)S(1)}, u32[]{:S(2)}, u32[]{:S(2)}) async-start(bf16[4,128,768]{2,1,0:T(8,128)(2,1)} %cast.1), calls=%async_computation | async-start | bytes 1572864 | tf_op jit(solution)/shard_map/all_to_all | solution.py:275
  20.0 1.9 %pack.1 = bf16[288,768]{1,0:T(8,128)(2,1)} custom-call(s32[2,16]{1,0:T(2,128)} %refs_0_.1, s32[1,2]{1,0:T(1,128)} %bitcast.16, s32[1,256]{1,0:T(1,128)} %bitcast.14, s32[1,256]{1,0:T(1,128)} %bitcast.15, bf16[256,768]{1,0:T(8,128)(2,1)} %refs_4_.1), custom_call_target="tpu_custom_call" | custom-call | tf_op jit(solution)/shard_map/pack/pallas_call | solution.py:280
  21.8 4.5 %collective-permute-start.2 = (bf16[288,768]{1,0:T(8,128)(2,1)}, bf16[288,768]{1,0:T(8,128)(2,1)S(1)}, u32[]{:S(2)}, u32[]{:S(2)}) collective-permute-start(bf16[288,768]{1,0:T(8,128)(2,1)} %pack.1), channel_id=1, source_target_pairs={{0,48},{16,32},{32,16},{48,0},{1,49},{17,33},{33,17},{49,1},{2,50}... | collective-permute-start | bytes 1327112 | tf_op jit(solution)/shard_map/ppermute | solution.py:237
  26.4 2.4 %collective-permute-start.1 = (bf16[288,768]{1,0:T(8,128)(2,1)}, bf16[288,768]{1,0:T(8,128)(2,1)S(1)}, u32[]{:S(2)}, u32[]{:S(2)}) collective-permute-start(bf16[288,768]{1,0:T(8,128)(2,1)} %pack.1), channel_id=1, source_target_pairs={{0,32},{16,48},{32,0},{48,16},{1,33},{17,49},{33,1},{49,17},{2,34}... | collective-permute-start | bytes 1327112 | tf_op jit(solution)/shard_map/ppermute | solution.py:237
  28.8 2.2 %collective-permute-start = (bf16[288,768]{1,0:T(8,128)(2,1)}, bf16[288,768]{1,0:T(8,128)(2,1)S(1)}, u32[]{:S(2)}, u32[]{:S(2)}) collective-permute-start(bf16[288,768]{1,0:T(8,128)(2,1)} %pack.1), channel_id=1, source_target_pairs={{0,16},{16,0},{32,48},{48,32},{1,17},{17,1},{33,49},{49,33},{2,18}... | collective-permute-start | bytes 1327112 | tf_op jit(solution)/shard_map/ppermute | solution.py:237
  31.0 4.1 %all-to-all-done.near_ref = bf16[4,128,768]{2,1,0:T(8,128)(2,1)S(1)} async-done(((bf16[4,128,768]{2,1,0:T(8,128)(2,1)}), bf16[4,128,768]{2,1,0:T(8,128)(2,1)S(1)}, u32[]{:S(2)}, u32[]{:S(2)}) %all-to-all-start) | async-done | bytes 786464 | tf_op jit(solution)/shard_map/all_to_all | solution.py:275
  35.1 0.9 fusion.4
  36.0 10.2 %collective-permute-start.4 = (bf16[2,128,768]{2,1,0:T(8,128)(2,1)}, bf16[2,128,768]{2,1,0:T(8,128)(2,1)S(1)}, u32[]{:S(2)}, u32[]{:S(2)}) collective-permute-start(bf16[2,128,768]{2,1,0:T(8,128)(2,1)} %get-tuple-element.30), channel_id=1, source_target_pairs={{0,448},{64,128},{128,64},{192,256},{256,192},{320,384},{384,320},... | collective-permute-start | bytes 1179656 | tf_op jit(solution)/shard_map/ppermute | solution.py:237
  46.2 1.9 %collective-permute-start.3 = (bf16[2,128,768]{2,1,0:T(8,128)(2,1)}, bf16[2,128,768]{2,1,0:T(8,128)(2,1)S(1)}, u32[]{:S(2)}, u32[]{:S(2)}) collective-permute-start(bf16[2,128,768]{2,1,0:T(8,128)(2,1)} %get-tuple-element.31), channel_id=1, source_target_pairs={{0,64},{64,0},{128,192},{192,128},{256,320},{320,256},{384,448},{4... | collective-permute-start | bytes 1179656 | tf_op jit(solution)/shard_map/ppermute | solution.py:237
  48.8 0.1 pad_add_fusion.place_ref
  48.9 0.2 pad_maximum_fusion.m_ref
  49.1 3.0 %near_scores.1 = (f32[4,512,256]{2,1,0:T(8,128)S(1)}, f32[4,8,256]{2,1,0:T(8,128)S(1)}) custom-call(f32[1]{0:T(128)S(6)} %copy.14.factor_ref, s32[2]{0:T(128)S(1)} %pad_add_fusion.place_ref, bf16[4,288,768]{2,1,0:T(8,128)(2,1)S(1)} %pad_maximum_fusion.m_ref, bf16[4,128,768]{2,1,0:T(8,128)(2,1)S(1)} %all-to-all-done.near_ref), custom_call_target="tpu_custom_call" | custom-call | tf_op jit(solution)/shard_map/near_scores/pallas_call | solution.py:307
  52.1 2.9 %collective-permute-done.4.high_ref = bf16[2,128,768]{2,1,0:T(8,128)(2,1)S(1)} collective-permute-done((bf16[2,128,768]{2,1,0:T(8,128)(2,1)}, bf16[2,128,768]{2,1,0:T(8,128)(2,1)S(1)}, u32[]{:S(2)}, u32[]{:S(2)}) %collective-permute-start.4) | collective-permute-done | bytes 393248 | tf_op jit(solution)/shard_map/ppermute | solution.py:237
  54.9 2.8 %collective-permute-done.3.low_ref = bf16[2,128,768]{2,1,0:T(8,128)(2,1)S(1)} collective-permute-done((bf16[2,128,768]{2,1,0:T(8,128)(2,1)}, bf16[2,128,768]{2,1,0:T(8,128)(2,1)S(1)}, u32[]{:S(2)}, u32[]{:S(2)}) %collective-permute-start.3) | collective-permute-done | bytes 393248 | tf_op jit(solution)/shard_map/ppermute | solution.py:237
  57.7 2.9 %far_scores.1 = (f32[4,512,256]{2,1,0:T(8,128)S(1)}, f32[4,8,1024]{2,1,0:T(8,128)S(1)}) custom-call(f32[1]{0:T(128)S(6)} %copy.14.factor_ref, s32[2]{0:T(128)S(1)} %pad_add_fusion.place_ref, bf16[4,288,768]{2,1,0:T(8,128)(2,1)S(1)} %pad_maximum_fusion.m_ref, bf16[2,128,768]{2,1,0:T(8,128)(2,1)S(1)} %collective-permute-done.3.low_ref, ...), custom_call_target="tpu_custom_call" | custom-call | tf_op jit(solution)/shard_map/far_scores/pallas_call | solution.py:317
  60.7 8.6 %all_to_all.15.stat_ref = f32[4,8,1024]{2,1,0:T(8,128)S(1)} all-to-all(f32[4,8,1024]{2,1,0:T(8,128)S(1)} %get-tuple-element.19), channel_id=1, replica_groups=mesh['gz'=8,'gx'=4,'gy'=16] {'gx'}, dimensions={0} | all-to-all | bytes 262144 | tf_op jit(solution)/shard_map/all_to_all | solution.py:327
  69.3 4.1 %grads.1 = (bf16[4,1024,256]{2,1,0:T(8,128)(2,1)S(1)}, bf16[1024,768]{1,0:T(8,128)(2,1)S(1)}, f32[128,1,768]{2,1,0:T(1,128)S(1)}) custom-call(f32[1]{0:T(128)S(6)} %copy.14.factor_ref, s32[2]{0:T(128)S(1)} %pad_add_fusion.place_ref, f32[4,512,256]{2,1,0:T(8,128)S(1)} %get-tuple-element.16.near_ref, f32[4,512,256]{2,1,0:T(8,128)S(1)} %get-tuple-element.18.far_ref, ...), custom_call_target="tpu_custom_call" | custom-call | tf_op jit(solution)/shard_map/grads/pallas_call | solution.py:331
  73.4 1.2 copy-done
  74.6 0.7 copy-done.3
  75.4 12.9 %all-to-all-start.2 = ((f32[128,1,768]{2,1,0:T(1,128)}), f32[128,1,768]{2,1,0:T(1,128)}, u32[]{:S(2)}, u32[]{:S(2)}) async-start(f32[128,1,768]{2,1,0:T(1,128)} %copy-done.3), calls=%async_computation.3 | async-start | bytes 786432 | tf_op jit(solution)/shard_map/all_to_all | solution.py:373
  88.2 1.0 copy-done.2
  89.2 3.4 %mention_part.1 = (bf16[256,768]{1,0:T(8,128)(2,1)S(1)}, bf16[256,768]{1,0:T(8,128)(2,1)S(1)}, bf16[256,768]{1,0:T(8,128)(2,1)S(1)}, bf16[256,768]{1,0:T(8,128)(2,1)S(1)}) custom-call(f32[1]{0:T(128)S(6)} %copy.14.factor_ref, s32[2]{0:T(128)S(1)} %pad_add_fusion.place_ref, bf16[4,1024,256]{2,1,0:T(8,128)(2,1)S(1)} %get-tuple-element.21.g_ref, ...), custom_call_target="tpu_custom_call" | custom-call | tf_op jit(solution)/shard_map/mention_part/pallas_call | solution.py:357
  92.6 2.3 %collective-permute-start.5 = (bf16[256,768]{1,0:T(8,128)(2,1)S(1)}, bf16[256,768]{1,0:T(8,128)(2,1)S(1)}, u32[]{:S(2)}, u32[]{:S(2)}) collective-permute-start(bf16[256,768]{1,0:T(8,128)(2,1)S(1)} %get-tuple-element.23), channel_id=1, source_target_pairs={{0,16},{16,0},{32,48},{48,32},{1,17},{17,1},{33,49},{49,33},{2,18}... | collective-permute-start | bytes 1179656 | tf_op jit(solution)/shard_map/ppermute | solution.py:237
  95.0 3.7 %collective-permute-start.6 = (bf16[256,768]{1,0:T(8,128)(2,1)S(1)}, bf16[256,768]{1,0:T(8,128)(2,1)S(1)}, u32[]{:S(2)}, u32[]{:S(2)}) collective-permute-start(bf16[256,768]{1,0:T(8,128)(2,1)S(1)} %get-tuple-element.24), channel_id=1, source_target_pairs={{0,32},{16,48},{32,0},{48,16},{1,33},{17,49},{33,1},{49,17},{2,34}... | collective-permute-start | bytes 1179656 | tf_op jit(solution)/shard_map/ppermute | solution.py:237
  98.7 3.7 %collective-permute-start.7 = (bf16[256,768]{1,0:T(8,128)(2,1)S(1)}, bf16[256,768]{1,0:T(8,128)(2,1)S(1)}, u32[]{:S(2)}, u32[]{:S(2)}) collective-permute-start(bf16[256,768]{1,0:T(8,128)(2,1)S(1)} %get-tuple-element.25), channel_id=1, source_target_pairs={{0,48},{16,32},{32,16},{48,0},{1,49},{17,33},{33,17},{49,1},{2,50}... | collective-permute-start | bytes 1179656 | tf_op jit(solution)/shard_map/ppermute | solution.py:237
  102.4 2.1 %collective-permute-done.5 = bf16[256,768]{1,0:T(8,128)(2,1)S(1)} collective-permute-done((bf16[256,768]{1,0:T(8,128)(2,1)S(1)}, bf16[256,768]{1,0:T(8,128)(2,1)S(1)}, u32[]{:S(2)}, u32[]{:S(2)}) %collective-permute-start.5) | collective-permute-done | bytes 393248 | tf_op jit(solution)/shard_map/ppermute | solution.py:237
  104.4 9.0 %collective-permute-done.6 = bf16[256,768]{1,0:T(8,128)(2,1)S(1)} collective-permute-done((bf16[256,768]{1,0:T(8,128)(2,1)S(1)}, bf16[256,768]{1,0:T(8,128)(2,1)S(1)}, u32[]{:S(2)}, u32[]{:S(2)}) %collective-permute-start.6) | collective-permute-done | bytes 393248 | tf_op jit(solution)/shard_map/ppermute | solution.py:237
  113.4 6.7 %collective-permute-done.7 = bf16[256,768]{1,0:T(8,128)(2,1)S(1)} collective-permute-done((bf16[256,768]{1,0:T(8,128)(2,1)S(1)}, bf16[256,768]{1,0:T(8,128)(2,1)S(1)}, u32[]{:S(2)}, u32[]{:S(2)}) %collective-permute-start.7) | collective-permute-done | bytes 393248 | tf_op jit(solution)/shard_map/ppermute | solution.py:237
  120.1 0.9 add_convert_fusion
  121.0 1.6 %slice_reduce_fusion = f32[]{:T(128)} fusion(f32[128,1,768]{2,1,0:T(1,128)} %all-to-all-done.2), kind=kLoop, calls=%fused_computation.7 | loop fusion | flops 127 | bytes 516 | tf_op jit(solution)/shard_map/reduce_sum | solution.py:374
  123.3 2.1 %divide_subtract_fusion = (f32[128,768]{1,0:T(8,128)}, f32[128,768]{1,0:T(8,128)}, f32[128,768]{1,0:T(8,128)}) fusion(f32[128,768]{1,0:T(8,128)S(1)} %copy-done.5, bf16[128,768]{1,0:T(8,128)(2,1)} %reduce-scatter.2.cloned.1.call-done, f32[128,768]{1,0:T(8,128)S(1)} %copy-done.6, f32[128,768]{1,0:T(8,128)S(1)} %copy-done.7), kind=kLoop, calls=%fused_computation.6 | loop fusion | flops 1277952 | bytes 2555904 | tf_op jit(solution)/shard_map/sub | solution.py:226
  (20 shorter events, 0.1 us)
Async XLA Ops:
  9.1 26.0 %all-to-all-start = ((bf16[4,128,768]{2,1,0:T(8,128)(2,1)}), bf16[4,128,768]{2,1,0:T(8,128)(2,1)S(1)}, u32[]{:S(2)}, u32[]{:S(2)}) async-start(bf16[4,128,768]{2,1,0:T(8,128)(2,1)} %cast.1), calls=%async_computation | async-start | bytes 1572864 | tf_op jit(solution)/shard_map/all_to_all | solution.py:275
  19.9 103.3 %reduce-scatter.2.cloned.1.call-start = ((), (), s32[]{:S(2)}) async-start(), calls=%async_computation.4 | async-start | bytes 1769472 | tf_op jit(solution)/shard_map/reduce_scatter | solution.py:356
  21.8 27.0 %copy-start.4 = (bf16[288,768]{1,0:T(8,128)(2,1)S(1)}, bf16[288,768]{1,0:T(8,128)(2,1)}, u32[]{:S(2)}) copy-start(bf16[288,768]{1,0:T(8,128)(2,1)} %pack.1) | copy-start | bytes 1327108
  21.8 27.0 %collective-permute-start.2 = (bf16[288,768]{1,0:T(8,128)(2,1)}, bf16[288,768]{1,0:T(8,128)(2,1)S(1)}, u32[]{:S(2)}, u32[]{:S(2)}) collective-permute-start(bf16[288,768]{1,0:T(8,128)(2,1)} %pack.1), channel_id=1, source_target_pairs={{0,48},{16,32},{32,16},{48,0},{1,49},{17,33},{33,17},{49,1},{2,50}... | collective-permute-start | bytes 1327112 | tf_op jit(solution)/shard_map/ppermute | solution.py:237
  26.4 22.5 %collective-permute-start.1 = (bf16[288,768]{1,0:T(8,128)(2,1)}, bf16[288,768]{1,0:T(8,128)(2,1)S(1)}, u32[]{:S(2)}, u32[]{:S(2)}) collective-permute-start(bf16[288,768]{1,0:T(8,128)(2,1)} %pack.1), channel_id=1, source_target_pairs={{0,32},{16,48},{32,0},{48,16},{1,33},{17,49},{33,1},{49,17},{2,34}... | collective-permute-start | bytes 1327112 | tf_op jit(solution)/shard_map/ppermute | solution.py:237
  28.8 20.1 %collective-permute-start = (bf16[288,768]{1,0:T(8,128)(2,1)}, bf16[288,768]{1,0:T(8,128)(2,1)S(1)}, u32[]{:S(2)}, u32[]{:S(2)}) collective-permute-start(bf16[288,768]{1,0:T(8,128)(2,1)} %pack.1), channel_id=1, source_target_pairs={{0,16},{16,0},{32,48},{48,32},{1,17},{17,1},{33,49},{49,33},{2,18}... | collective-permute-start | bytes 1327112 | tf_op jit(solution)/shard_map/ppermute | solution.py:237
  36.0 18.9 %collective-permute-start.4 = (bf16[2,128,768]{2,1,0:T(8,128)(2,1)}, bf16[2,128,768]{2,1,0:T(8,128)(2,1)S(1)}, u32[]{:S(2)}, u32[]{:S(2)}) collective-permute-start(bf16[2,128,768]{2,1,0:T(8,128)(2,1)} %get-tuple-element.30), channel_id=1, source_target_pairs={{0,448},{64,128},{128,64},{192,256},{256,192},{320,384},{384,320},... | collective-permute-start | bytes 1179656 | tf_op jit(solution)/shard_map/ppermute | solution.py:237
  46.2 11.5 %collective-permute-start.3 = (bf16[2,128,768]{2,1,0:T(8,128)(2,1)}, bf16[2,128,768]{2,1,0:T(8,128)(2,1)S(1)}, u32[]{:S(2)}, u32[]{:S(2)}) collective-permute-start(bf16[2,128,768]{2,1,0:T(8,128)(2,1)} %get-tuple-element.31), channel_id=1, source_target_pairs={{0,64},{64,0},{128,192},{192,128},{256,320},{320,256},{384,448},{4... | collective-permute-start | bytes 1179656 | tf_op jit(solution)/shard_map/ppermute | solution.py:237
  57.7 11.6 %copy-start.1 = (bf16[2,128,768]{2,1,0:T(8,128)(2,1)}, bf16[2,128,768]{2,1,0:T(8,128)(2,1)S(1)}, u32[]{:S(2)}) copy-start(bf16[2,128,768]{2,1,0:T(8,128)(2,1)S(1)} %collective-permute-done.3.low_ref) | copy-start | bytes 1179652
  73.4 1.2 copy-start
  74.6 0.7 copy-start.3
  75.4 45.6 %all-to-all-start.2 = ((f32[128,1,768]{2,1,0:T(1,128)}), f32[128,1,768]{2,1,0:T(1,128)}, u32[]{:S(2)}, u32[]{:S(2)}) async-start(f32[128,1,768]{2,1,0:T(1,128)} %copy-done.3), calls=%async_computation.3 | async-start | bytes 786432 | tf_op jit(solution)/shard_map/all_to_all | solution.py:373
  88.2 1.0 copy-start.2
  92.6 30.7 %copy-start.5 = (f32[128,768]{1,0:T(8,128)S(1)}, f32[128,768]{1,0:T(8,128)}, u32[]{:S(2)}) copy-start(f32[128,768]{1,0:T(8,128)} %t_ref.1) | copy-start | bytes 1179652
  92.6 30.7 %copy-start.6 = (f32[128,768]{1,0:T(8,128)S(1)}, f32[128,768]{1,0:T(8,128)}, u32[]{:S(2)}) copy-start(f32[128,768]{1,0:T(8,128)} %param.11) | copy-start | bytes 1179652
  92.6 30.7 %copy-start.7 = (f32[128,768]{1,0:T(8,128)S(1)}, f32[128,768]{1,0:T(8,128)}, u32[]{:S(2)}) copy-start(f32[128,768]{1,0:T(8,128)} %param.12) | copy-start | bytes 1179652
  92.6 11.8 %collective-permute-start.5 = (bf16[256,768]{1,0:T(8,128)(2,1)S(1)}, bf16[256,768]{1,0:T(8,128)(2,1)S(1)}, u32[]{:S(2)}, u32[]{:S(2)}) collective-permute-start(bf16[256,768]{1,0:T(8,128)(2,1)S(1)} %get-tuple-element.23), channel_id=1, source_target_pairs={{0,16},{16,0},{32,48},{48,32},{1,17},{17,1},{33,49},{49,33},{2,18}... | collective-permute-start | bytes 1179656 | tf_op jit(solution)/shard_map/ppermute | solution.py:237
  95.0 18.4 %collective-permute-start.6 = (bf16[256,768]{1,0:T(8,128)(2,1)S(1)}, bf16[256,768]{1,0:T(8,128)(2,1)S(1)}, u32[]{:S(2)}, u32[]{:S(2)}) collective-permute-start(bf16[256,768]{1,0:T(8,128)(2,1)S(1)} %get-tuple-element.24), channel_id=1, source_target_pairs={{0,32},{16,48},{32,0},{48,16},{1,33},{17,49},{33,1},{49,17},{2,34}... | collective-permute-start | bytes 1179656 | tf_op jit(solution)/shard_map/ppermute | solution.py:237
  98.7 21.4 %collective-permute-start.7 = (bf16[256,768]{1,0:T(8,128)(2,1)S(1)}, bf16[256,768]{1,0:T(8,128)(2,1)S(1)}, u32[]{:S(2)}, u32[]{:S(2)}) collective-permute-start(bf16[256,768]{1,0:T(8,128)(2,1)S(1)} %get-tuple-element.25), channel_id=1, source_target_pairs={{0,48},{16,32},{32,16},{48,0},{1,49},{17,33},{33,17},{49,1},{2,50}... | collective-permute-start | bytes 1179656 | tf_op jit(solution)/shard_map/ppermute | solution.py:237
Sparse Core Ops, SparseCore 0:
  75.5 44.2 reduce-scatter.1

commit v9 on v8

--- a/solution.py
+++ b/solution.py
@@ -19,7 +19,6 @@
 META_ROWS = 32
 SLOTS = 16
 STAT_ROWS = 8
-SCALE_LANES = 768
 f32 = jnp.float32
 bf16 = jnp.bfloat16
 
@@ -159,8 +158,7 @@
     masses = masses + sums * tops
     mass = jnp.sum(jnp.where(sums > 0.0, masses * shares, 0.0), axis=0, keepdims=True)
     scale = mass / total - jnp.sum(stat_ref[:, 6, :], axis=0, keepdims=True)
-    scale = jnp.sum(scale, axis=1, keepdims=True)
-    scale_ref[...] = jnp.broadcast_to(scale[None], scale_ref.shape)
+    scale_ref[...] = jnp.broadcast_to(jnp.sum(scale, axis=1, keepdims=True), scale_ref.shape)
     ids = lax.broadcasted_iota(jnp.int32, tops.shape, 0)
     for h in range(2):
         mine = ids == place_ref[1] + h * X_SIZE
@@ -326,9 +324,8 @@
     )(logit_scale, place, gathered, low, high, near_stats)
     stats = lax.all_to_all(stats, "gx", 0, 0, tiled=True)
     chunk = 2 * block_rows
-    scale_shape = (Z_SIZE * cols, 1, SCALE_LANES)
     chunk_spec = pl.BlockSpec((X_SIZE, chunk, rows), lambda i: (0, i, 0))
-    grads, type_part, scale_parts = pl.pallas_call(
+    grads, type_part, scale_part = pl.pallas_call(
         grads_kernel,
         grid=(types // chunk,),
         in_specs=[
@@ -339,11 +336,11 @@
             whole(X_SIZE, STAT_ROWS, X_SIZE * rows),
             whole(X_SIZE, sent_rows, width),
         ],
-        out_specs=[chunk_spec, pl.BlockSpec((chunk, width), lambda i: (i, 0)), whole(*scale_shape)],
+        out_specs=[chunk_spec, pl.BlockSpec((chunk, width), lambda i: (i, 0)), whole(1, 128)],
         out_shape=[
             jax.ShapeDtypeStruct((X_SIZE, types, rows), bf16),
             jax.ShapeDtypeStruct((types, width), bf16),
-            jax.ShapeDtypeStruct(scale_shape, f32),
+            jax.ShapeDtypeStruct((1, 128), f32),
         ],
         scratch_shapes=[
             pltpu.VMEM((2, X_SIZE * rows), f32),
@@ -353,7 +350,9 @@
         compiler_params=params(16),
         name="grads",
     )(logit_scale, place, near_exps, far_exps, stats, gathered)
-    type_grad = lax.psum_scatter(type_part, "gz", scatter_dimension=0, tiled=True)
+    type_parts = lax.all_to_all(
+        type_part.reshape(Z_SIZE, block_rows, width), "gz", 0, 0, tiled=True
+    )
     parts = pl.pallas_call(
         mention_kernel,
         grid=(X_SIZE,),
@@ -370,11 +369,18 @@
             parts[s], "gx", lambda x, s=s: x ^ s
         ).astype(f32)
     mention_grad = mention_grad.astype(bf16)
-    scale_parts = lax.all_to_all(scale_parts, ("gz", "gy"), 0, 0, tiled=True)
-    scale_grad = (jnp.sum(scale_parts[:, 0, 0]) / (rows * devices)).reshape(1)
-    new_table, new_first, new_second = adam_rows(
-        type_table, adam_m, adam_v, type_grad.astype(f32)
-    )
+    scale_sum = scale_part
+    by = 1
+    while by < cols:
+        scale_sum = scale_sum + paired(scale_sum, "gy", lambda y, by=by: y ^ by)
+        by *= 2
+    scale_sum = scale_sum + 0.0 * type_parts[0, 0:1, 0:128].astype(f32)
+    scale_sums = lax.all_to_all(
+        jnp.broadcast_to(scale_sum[None], (Z_SIZE, 1, 128)), "gz", 0, 0, tiled=True
+    )
+    scale_grad = (jnp.sum(scale_sums[:, 0, 0]) / (rows * devices)).reshape(1)
+    type_grad = jnp.sum(type_parts, axis=0, dtype=f32)
+    new_table, new_first, new_second = adam_rows(type_table, adam_m, adam_v, type_grad)
     return (new_table, new_first, new_second, mention_grad, scale_grad)
 
 

time: 135 us -> 133 us (0.985)
  the two profiles are of different devices: /device:TPU:1 before, /device:TPU:56 now
where the time goes in v9:
time: 133 us; the launch traced here: 132 us
  starting transfers between devices  66.9 us (50%)
  waiting for transfers between devices  24.2 us (18%)
  Pallas kernels  17.2 us (13%)
  blocking collectives  10.1 us (8%)
  other arithmetic  6.37 us (5%)
  local copies, waits for them, and re-layouts  3.67 us (3%)
  between operations  3.33 us (3%)
    ppermute x12, starting transfers between devices, paired(): lax.ppermute(array, axis, [(i, partner(i)) for i in range(lax.axis_size(a...  45.2 us
    ppermute x12, waiting for transfers between devices, paired(): lax.ppermute(array, axis, [(i, partner(i)) for i in range(lax.axis_size(a...  14.7 us
    all_to_all x1, starting transfers between devices, per_device(): lax.all_to_all(copies, 'gz', 0, 0, tiled=True, axis_index_groups=parities)  10.3 us
    all_to_all x1, blocking collectives, per_device(): stats = lax.all_to_all(stats, 'gx', 0, 0, tiled=True)  10.1 us
    all_to_all x1, starting transfers between devices, per_device(): lax.all_to_all(jnp.broadcast_to(scale_sum[None], (Z_SIZE, 1, 128)), 'gz',...  7.09 us
    all_to_all x1, waiting for transfers between devices, per_device(): lax.all_to_all(jnp.broadcast_to(scale_sum[None], (Z_SIZE, 1, 128)), 'gz',...  4.82 us
    all_to_all x1, waiting for transfers between devices, per_device(): lax.all_to_all(copies, 'gz', 0, 0, tiled=True, axis_index_groups=parities)  4.69 us
    all_to_all x1, starting transfers between devices, per_device(): lax.all_to_all(type_part.reshape(Z_SIZE, block_rows, width), 'gz', 0, 0,...  4.29 us
  transfers between devices with their start and end apart: 15, of which 8 were waited for; matrix products, arithmetic and copies ran while one was open for 5% of the time, Pallas kernels for 6%

profile of v9, /device:TPU:56, one launch (start us, length us, event | category | flops | bytes accessed | tf_op | source)
XLA Modules:
  0.0 131.7 jit_solution(9476227797637702339)
XLA Ops:
  0.6 1.9 %cast.1 = bf16[4,128,768]{2,1,0:T(8,128)(2,1)} custom-call(f32[128,768]{1,0:T(8,128)} %t_ref.1), custom_call_target="tpu_custom_call" | custom-call | tf_op jit(solution)/shard_map/cast/pallas_call | solution.py:266
  2.6 10.3 %all-to-all-start = ((bf16[4,128,768]{2,1,0:T(8,128)(2,1)}), bf16[4,128,768]{2,1,0:T(8,128)(2,1)S(1)}, u32[]{:S(2)}, u32[]{:S(2)}) async-start(bf16[4,128,768]{2,1,0:T(8,128)(2,1)} %cast.1), calls=%async_computation | async-start | bytes 1572864 | tf_op jit(solution)/shard_map/all_to_all | solution.py:273
  12.9 1.9 %pack.1 = bf16[288,768]{1,0:T(8,128)(2,1)} custom-call(s32[2,16]{1,0:T(2,128)} %refs_0_.1, s32[1,2]{1,0:T(1,128)} %bitcast.25, s32[1,256]{1,0:T(1,128)} %bitcast.23, s32[1,256]{1,0:T(1,128)} %bitcast.24, bf16[256,768]{1,0:T(8,128)(2,1)} %refs_4_.1), custom_call_target="tpu_custom_call" | custom-call | tf_op jit(solution)/shard_map/pack/pallas_call | solution.py:278
  14.8 4.8 %collective-permute-start.2 = (bf16[288,768]{1,0:T(8,128)(2,1)}, bf16[288,768]{1,0:T(8,128)(2,1)S(1)}, u32[]{:S(2)}, u32[]{:S(2)}) collective-permute-start(bf16[288,768]{1,0:T(8,128)(2,1)} %pack.1), channel_id=1, source_target_pairs={{0,48},{16,32},{32,16},{48,0},{1,49},{17,33},{33,17},{49,1},{2,50}... | collective-permute-start | bytes 1327112 | tf_op jit(solution)/shard_map/ppermute | solution.py:235
  19.6 2.7 %collective-permute-start.1 = (bf16[288,768]{1,0:T(8,128)(2,1)}, bf16[288,768]{1,0:T(8,128)(2,1)S(1)}, u32[]{:S(2)}, u32[]{:S(2)}) collective-permute-start(bf16[288,768]{1,0:T(8,128)(2,1)} %pack.1), channel_id=1, source_target_pairs={{0,32},{16,48},{32,0},{48,16},{1,33},{17,49},{33,1},{49,17},{2,34}... | collective-permute-start | bytes 1327112 | tf_op jit(solution)/shard_map/ppermute | solution.py:235
  22.3 2.4 %collective-permute-start = (bf16[288,768]{1,0:T(8,128)(2,1)}, bf16[288,768]{1,0:T(8,128)(2,1)}, u32[]{:S(2)}, u32[]{:S(2)}) collective-permute-start(bf16[288,768]{1,0:T(8,128)(2,1)} %pack.1), channel_id=1, source_target_pairs={{0,16},{16,0},{32,48},{48,32},{1,17},{17,1},{33,49},{49,33},{2,18}... | collective-permute-start | bytes 1327112 | tf_op jit(solution)/shard_map/ppermute | solution.py:235
  24.7 4.7 %all-to-all-done.near_ref = bf16[4,128,768]{2,1,0:T(8,128)(2,1)S(1)} async-done(((bf16[4,128,768]{2,1,0:T(8,128)(2,1)}), bf16[4,128,768]{2,1,0:T(8,128)(2,1)S(1)}, u32[]{:S(2)}, u32[]{:S(2)}) %all-to-all-start) | async-done | bytes 786464 | tf_op jit(solution)/shard_map/all_to_all | solution.py:273
  30.4 9.0 %collective-permute-start.4 = (bf16[2,128,768]{2,1,0:T(8,128)(2,1)}, bf16[2,128,768]{2,1,0:T(8,128)(2,1)S(1)}, u32[]{:S(2)}, u32[]{:S(2)}) collective-permute-start(bf16[2,128,768]{2,1,0:T(8,128)(2,1)} %get-tuple-element.30), channel_id=1, source_target_pairs={{0,448},{64,128},{128,64},{192,256},{256,192},{320,384},{384,320},... | collective-permute-start | bytes 1179656 | tf_op jit(solution)/shard_map/ppermute | solution.py:235
  39.4 1.9 %collective-permute-start.3 = (bf16[2,128,768]{2,1,0:T(8,128)(2,1)}, bf16[2,128,768]{2,1,0:T(8,128)(2,1)S(1)}, u32[]{:S(2)}, u32[]{:S(2)}) collective-permute-start(bf16[2,128,768]{2,1,0:T(8,128)(2,1)} %get-tuple-element.31), channel_id=1, source_target_pairs={{0,64},{64,0},{128,192},{192,128},{256,320},{320,256},{384,448},{4... | collective-permute-start | bytes 1179656 | tf_op jit(solution)/shard_map/ppermute | solution.py:235
  42.0 1.2 pad_maximum_fusion.m_ref
  43.3 3.0 %near_scores.1 = (f32[4,512,256]{2,1,0:T(8,128)S(1)}, f32[4,8,256]{2,1,0:T(8,128)S(1)}) custom-call(f32[1]{0:T(128)S(6)} %copy.16.factor_ref, s32[2]{0:T(128)S(1)} %pad_add_fusion.place_ref, bf16[4,288,768]{2,1,0:T(8,128)(2,1)S(1)} %pad_maximum_fusion.m_ref, bf16[4,128,768]{2,1,0:T(8,128)(2,1)S(1)} %all-to-all-done.near_ref), custom_call_target="tpu_custom_call" | custom-call | tf_op jit(solution)/shard_map/near_scores/pallas_call | solution.py:305
  46.2 2.2 %collective-permute-done.4.high_ref = bf16[2,128,768]{2,1,0:T(8,128)(2,1)S(1)} collective-permute-done((bf16[2,128,768]{2,1,0:T(8,128)(2,1)}, bf16[2,128,768]{2,1,0:T(8,128)(2,1)S(1)}, u32[]{:S(2)}, u32[]{:S(2)}) %collective-permute-start.4) | collective-permute-done | bytes 393248 | tf_op jit(solution)/shard_map/ppermute | solution.py:235
  48.4 3.4 %collective-permute-done.3.low_ref = bf16[2,128,768]{2,1,0:T(8,128)(2,1)S(1)} collective-permute-done((bf16[2,128,768]{2,1,0:T(8,128)(2,1)}, bf16[2,128,768]{2,1,0:T(8,128)(2,1)S(1)}, u32[]{:S(2)}, u32[]{:S(2)}) %collective-permute-start.3) | collective-permute-done | bytes 393248 | tf_op jit(solution)/shard_map/ppermute | solution.py:235
  51.8 2.9 %far_scores.1 = (f32[4,512,256]{2,1,0:T(8,128)S(1)}, f32[4,8,1024]{2,1,0:T(8,128)S(1)}) custom-call(f32[1]{0:T(128)S(6)} %copy.16.factor_ref, s32[2]{0:T(128)S(1)} %pad_add_fusion.place_ref, bf16[4,288,768]{2,1,0:T(8,128)(2,1)S(1)} %pad_maximum_fusion.m_ref, bf16[2,128,768]{2,1,0:T(8,128)(2,1)S(1)} %collective-permute-done.3.low_ref, ...), custom_call_target="tpu_custom_call" | custom-call | tf_op jit(solution)/shard_map/far_scores/pallas_call | solution.py:315
  54.7 10.1 %all_to_all.20.stat_ref = f32[4,8,1024]{2,1,0:T(8,128)S(1)} all-to-all(f32[4,8,1024]{2,1,0:T(8,128)S(1)} %get-tuple-element.19), channel_id=1, replica_groups=mesh['gz'=8,'gx'=4,'gy'=16] {'gx'}, dimensions={0} | all-to-all | bytes 262144 | tf_op jit(solution)/shard_map/all_to_all | solution.py:325
  64.8 4.1 %grads.1 = (bf16[4,1024,256]{2,1,0:T(8,128)(2,1)S(1)}, bf16[1024,768]{1,0:T(8,128)(2,1)S(1)}, f32[1,128]{1,0:T(1,128)S(1)}) custom-call(f32[1]{0:T(128)S(6)} %copy.16.factor_ref, s32[2]{0:T(128)S(1)} %pad_add_fusion.place_ref, f32[4,512,256]{2,1,0:T(8,128)S(1)} %get-tuple-element.16.near_ref, f32[4,512,256]{2,1,0:T(8,128)S(1)} %get-tuple-element.18.far_ref, ...), custom_call_target="tpu_custom_call" | custom-call | tf_op jit(solution)/shard_map/grads/pallas_call | solution.py:328
  70.1 4.3 %all-to-all-start.2 = ((bf16[8,128,768]{2,1,0:T(8,128)(2,1)}), bf16[8,128,768]{2,1,0:T(8,128)(2,1)}, u32[]{:S(2)}, u32[]{:S(2)}) async-start(bf16[8,128,768]{2,1,0:T(8,128)(2,1)} %bitcast.19), calls=%async_computation.2 | async-start | bytes 3145728 | tf_op jit(solution)/shard_map/all_to_all | solution.py:353
  75.4 3.4 %mention_part.1 = (bf16[256,768]{1,0:T(8,128)(2,1)S(1)}, bf16[256,768]{1,0:T(8,128)(2,1)S(1)}, bf16[256,768]{1,0:T(8,128)(2,1)S(1)}, bf16[256,768]{1,0:T(8,128)(2,1)S(1)}) custom-call(f32[1]{0:T(128)S(6)} %copy.16.factor_ref, s32[2]{0:T(128)S(1)} %pad_add_fusion.place_ref, bf16[4,1024,256]{2,1,0:T(8,128)(2,1)S(1)} %get-tuple-element.21.g_ref, ...), custom_call_target="tpu_custom_call" | custom-call | tf_op jit(solution)/shard_map/mention_part/pallas_call | solution.py:356
  78.7 2.5 %collective-permute-start.5 = (bf16[256,768]{1,0:T(8,128)(2,1)S(1)}, bf16[256,768]{1,0:T(8,128)(2,1)S(1)}, u32[]{:S(2)}, u32[]{:S(2)}) collective-permute-start(bf16[256,768]{1,0:T(8,128)(2,1)S(1)} %get-tuple-element.23), channel_id=1, source_target_pairs={{0,16},{16,0},{32,48},{48,32},{1,17},{17,1},{33,49},{49,33},{2,18}... | collective-permute-start | bytes 1179656 | tf_op jit(solution)/shard_map/ppermute | solution.py:235
  81.2 4.0 %collective-permute-start.6 = (bf16[256,768]{1,0:T(8,128)(2,1)S(1)}, bf16[256,768]{1,0:T(8,128)(2,1)S(1)}, u32[]{:S(2)}, u32[]{:S(2)}) collective-permute-start(bf16[256,768]{1,0:T(8,128)(2,1)S(1)} %get-tuple-element.24), channel_id=1, source_target_pairs={{0,32},{16,48},{32,0},{48,16},{1,33},{17,49},{33,1},{49,17},{2,34}... | collective-permute-start | bytes 1179656 | tf_op jit(solution)/shard_map/ppermute | solution.py:235
  85.2 4.0 %collective-permute-start.7 = (bf16[256,768]{1,0:T(8,128)(2,1)S(1)}, bf16[256,768]{1,0:T(8,128)(2,1)S(1)}, u32[]{:S(2)}, u32[]{:S(2)}) collective-permute-start(bf16[256,768]{1,0:T(8,128)(2,1)S(1)} %get-tuple-element.25), channel_id=1, source_target_pairs={{0,48},{16,32},{32,16},{48,0},{1,49},{17,33},{33,17},{49,1},{2,50}... | collective-permute-start | bytes 1179656 | tf_op jit(solution)/shard_map/ppermute | solution.py:235
  89.2 1.9 %collective-permute-start.8 = (f32[1,128]{1,0:T(1,128)S(1)}, f32[1,128]{1,0:T(1,128)S(1)}, u32[]{:S(2)}, u32[]{:S(2)}) collective-permute-start(f32[1,128]{1,0:T(1,128)S(1)} %get-tuple-element.26), channel_id=1, source_target_pairs={{0,1},{1,0},{2,3},{3,2},{4,5},{5,4},{6,7},{7,6},{8,9},{9,8},{10,11... | collective-permute-start | bytes 1544 | tf_op jit(solution)/shard_map/ppermute | solution.py:235
  92.2 3.2 %collective-permute-start.9 = (f32[1,128]{1,0:T(1,128)S(1)}, f32[1,128]{1,0:T(1,128)S(1)}, u32[]{:S(2)}, u32[]{:S(2)}) collective-permute-start(f32[1,128]{1,0:T(1,128)S(1)} %add.43), channel_id=1, source_target_pairs={{0,2},{1,3},{2,0},{3,1},{4,6},{5,7},{6,4},{7,5},{8,10},{9,11},{10,... | collective-permute-start | bytes 1544 | tf_op jit(solution)/shard_map/ppermute | solution.py:235
  95.4 2.2 %collective-permute-done.9 = f32[1,128]{1,0:T(1,128)S(1)} collective-permute-done((f32[1,128]{1,0:T(1,128)S(1)}, f32[1,128]{1,0:T(1,128)S(1)}, u32[]{:S(2)}, u32[]{:S(2)}) %collective-permute-start.9) | collective-permute-done | bytes 544 | tf_op jit(solution)/shard_map/ppermute | solution.py:235
  97.6 4.0 %collective-permute-start.10 = (f32[1,128]{1,0:T(1,128)S(1)}, f32[1,128]{1,0:T(1,128)S(1)}, u32[]{:S(2)}, u32[]{:S(2)}) collective-permute-start(f32[1,128]{1,0:T(1,128)S(1)} %add.44), channel_id=1, source_target_pairs={{0,4},{1,5},{2,6},{3,7},{4,0},{5,1},{6,2},{7,3},{8,12},{9,13},{10,... | collective-permute-start | bytes 1544 | tf_op jit(solution)/shard_map/ppermute | solution.py:235
  101.7 2.3 %collective-permute-done.10 = f32[1,128]{1,0:T(1,128)S(1)} collective-permute-done((f32[1,128]{1,0:T(1,128)S(1)}, f32[1,128]{1,0:T(1,128)S(1)}, u32[]{:S(2)}, u32[]{:S(2)}) %collective-permute-start.10) | collective-permute-done | bytes 544 | tf_op jit(solution)/shard_map/ppermute | solution.py:235
  104.0 4.7 %collective-permute-start.11 = (f32[1,128]{1,0:T(1,128)S(1)}, f32[1,128]{1,0:T(1,128)S(1)}, u32[]{:S(2)}, u32[]{:S(2)}) collective-permute-start(f32[1,128]{1,0:T(1,128)S(1)} %add.45), channel_id=1, source_target_pairs={{0,8},{1,9},{2,10},{3,11},{4,12},{5,13},{6,14},{7,15},{8,0},{9,1},... | collective-permute-start | bytes 1544 | tf_op jit(solution)/shard_map/ppermute | solution.py:235
  109.7 3.6 %collective-permute-done.11 = f32[1,128]{1,0:T(1,128)S(1)} collective-permute-done((f32[1,128]{1,0:T(1,128)S(1)}, f32[1,128]{1,0:T(1,128)S(1)}, u32[]{:S(2)}, u32[]{:S(2)}) %collective-permute-start.11) | collective-permute-done | bytes 544 | tf_op jit(solution)/shard_map/ppermute | solution.py:235
  114.6 7.1 %all-to-all-start.3 = ((f32[8,1,128]{2,1,0:T(1,128)}), f32[8,1,128]{2,1,0:T(1,128)S(1)}, u32[]{:S(2)}, u32[]{:S(2)}) async-start(f32[8,1,128]{2,1,0:T(1,128)} %broadcast_in_dim.9), calls=%async_computation.3 | async-start | bytes 8192 | tf_op jit(solution)/shard_map/all_to_all | solution.py:378
  121.7 1.7 %convert_reduce_fusion = f32[128,768]{1,0:T(8,128)S(1)} fusion(bf16[8,128,768]{2,1,0:T(8,128)(2,1)} %all-to-all-done.2), kind=kLoop, calls=%fused_computation | loop fusion | flops 1474560 | bytes 1966080 | tf_op jit(solution)/shard_map/reduce_sum | solution.py:382
  123.4 1.2 divide_subtract_fusion
  124.5 4.8 %all-to-all-done.3 = f32[8,1,128]{2,1,0:T(1,128)S(1)} async-done(((f32[8,1,128]{2,1,0:T(1,128)}), f32[8,1,128]{2,1,0:T(1,128)S(1)}, u32[]{:S(2)}, u32[]{:S(2)}) %all-to-all-start.3) | async-done | bytes 4128 | tf_op jit(solution)/shard_map/all_to_all | solution.py:378
  (31 shorter events, 7.1 us)
Async XLA Ops:
  2.6 26.9 %all-to-all-start = ((bf16[4,128,768]{2,1,0:T(8,128)(2,1)}), bf16[4,128,768]{2,1,0:T(8,128)(2,1)S(1)}, u32[]{:S(2)}, u32[]{:S(2)}) async-start(bf16[4,128,768]{2,1,0:T(8,128)(2,1)} %cast.1), calls=%async_computation | async-start | bytes 1572864 | tf_op jit(solution)/shard_map/all_to_all | solution.py:273
  14.7 27.3 %copy-start.3 = (bf16[288,768]{1,0:T(8,128)(2,1)S(1)}, bf16[288,768]{1,0:T(8,128)(2,1)}, u32[]{:S(2)}) copy-start(bf16[288,768]{1,0:T(8,128)(2,1)} %pack.1) | copy-start | bytes 1327108
  14.8 27.3 %collective-permute-start.2 = (bf16[288,768]{1,0:T(8,128)(2,1)}, bf16[288,768]{1,0:T(8,128)(2,1)S(1)}, u32[]{:S(2)}, u32[]{:S(2)}) collective-permute-start(bf16[288,768]{1,0:T(8,128)(2,1)} %pack.1), channel_id=1, source_target_pairs={{0,48},{16,32},{32,16},{48,0},{1,49},{17,33},{33,17},{49,1},{2,50}... | collective-permute-start | bytes 1327112 | tf_op jit(solution)/shard_map/ppermute | solution.py:235
  19.6 22.5 %collective-permute-start.1 = (bf16[288,768]{1,0:T(8,128)(2,1)}, bf16[288,768]{1,0:T(8,128)(2,1)S(1)}, u32[]{:S(2)}, u32[]{:S(2)}) collective-permute-start(bf16[288,768]{1,0:T(8,128)(2,1)} %pack.1), channel_id=1, source_target_pairs={{0,32},{16,48},{32,0},{48,16},{1,33},{17,49},{33,1},{49,17},{2,34}... | collective-permute-start | bytes 1327112 | tf_op jit(solution)/shard_map/ppermute | solution.py:235
  22.3 19.8 %collective-permute-start = (bf16[288,768]{1,0:T(8,128)(2,1)}, bf16[288,768]{1,0:T(8,128)(2,1)}, u32[]{:S(2)}, u32[]{:S(2)}) collective-permute-start(bf16[288,768]{1,0:T(8,128)(2,1)} %pack.1), channel_id=1, source_target_pairs={{0,16},{16,0},{32,48},{48,32},{1,17},{17,1},{33,49},{49,33},{2,18}... | collective-permute-start | bytes 1327112 | tf_op jit(solution)/shard_map/ppermute | solution.py:235
  30.4 18.1 %collective-permute-start.4 = (bf16[2,128,768]{2,1,0:T(8,128)(2,1)}, bf16[2,128,768]{2,1,0:T(8,128)(2,1)S(1)}, u32[]{:S(2)}, u32[]{:S(2)}) collective-permute-start(bf16[2,128,768]{2,1,0:T(8,128)(2,1)} %get-tuple-element.30), channel_id=1, source_target_pairs={{0,448},{64,128},{128,64},{192,256},{256,192},{320,384},{384,320},... | collective-permute-start | bytes 1179656 | tf_op jit(solution)/shard_map/ppermute | solution.py:235
  39.4 12.4 %collective-permute-start.3 = (bf16[2,128,768]{2,1,0:T(8,128)(2,1)}, bf16[2,128,768]{2,1,0:T(8,128)(2,1)S(1)}, u32[]{:S(2)}, u32[]{:S(2)}) collective-permute-start(bf16[2,128,768]{2,1,0:T(8,128)(2,1)} %get-tuple-element.31), channel_id=1, source_target_pairs={{0,64},{64,0},{128,192},{192,128},{256,320},{320,256},{384,448},{4... | collective-permute-start | bytes 1179656 | tf_op jit(solution)/shard_map/ppermute | solution.py:235
  51.8 13.0 %copy-start.1 = (bf16[2,128,768]{2,1,0:T(8,128)(2,1)}, bf16[2,128,768]{2,1,0:T(8,128)(2,1)S(1)}, u32[]{:S(2)}) copy-start(bf16[2,128,768]{2,1,0:T(8,128)(2,1)S(1)} %collective-permute-done.3.low_ref) | copy-start | bytes 1179652
  68.9 1.1 copy-start
  70.1 43.2 %all-to-all-start.2 = ((bf16[8,128,768]{2,1,0:T(8,128)(2,1)}), bf16[8,128,768]{2,1,0:T(8,128)(2,1)}, u32[]{:S(2)}, u32[]{:S(2)}) async-start(bf16[8,128,768]{2,1,0:T(8,128)(2,1)} %bitcast.19), calls=%async_computation.2 | async-start | bytes 3145728 | tf_op jit(solution)/shard_map/all_to_all | solution.py:353
  74.4 1.0 copy-start.2
  78.7 29.9 %collective-permute-start.5 = (bf16[256,768]{1,0:T(8,128)(2,1)S(1)}, bf16[256,768]{1,0:T(8,128)(2,1)S(1)}, u32[]{:S(2)}, u32[]{:S(2)}) collective-permute-start(bf16[256,768]{1,0:T(8,128)(2,1)S(1)} %get-tuple-element.23), channel_id=1, source_target_pairs={{0,16},{16,0},{32,48},{48,32},{1,17},{17,1},{33,49},{49,33},{2,18}... | collective-permute-start | bytes 1179656 | tf_op jit(solution)/shard_map/ppermute | solution.py:235
  81.2 27.5 %collective-permute-start.6 = (bf16[256,768]{1,0:T(8,128)(2,1)S(1)}, bf16[256,768]{1,0:T(8,128)(2,1)S(1)}, u32[]{:S(2)}, u32[]{:S(2)}) collective-permute-start(bf16[256,768]{1,0:T(8,128)(2,1)S(1)} %get-tuple-element.24), channel_id=1, source_target_pairs={{0,32},{16,48},{32,0},{48,16},{1,33},{17,49},{33,1},{49,17},{2,34}... | collective-permute-start | bytes 1179656 | tf_op jit(solution)/shard_map/ppermute | solution.py:235
  85.2 23.5 %collective-permute-start.7 = (bf16[256,768]{1,0:T(8,128)(2,1)S(1)}, bf16[256,768]{1,0:T(8,128)(2,1)S(1)}, u32[]{:S(2)}, u32[]{:S(2)}) collective-permute-start(bf16[256,768]{1,0:T(8,128)(2,1)S(1)} %get-tuple-element.25), channel_id=1, source_target_pairs={{0,48},{16,32},{32,16},{48,0},{1,49},{17,33},{33,17},{49,1},{2,50}... | collective-permute-start | bytes 1179656 | tf_op jit(solution)/shard_map/ppermute | solution.py:235
  89.2 3.0 %collective-permute-start.8 = (f32[1,128]{1,0:T(1,128)S(1)}, f32[1,128]{1,0:T(1,128)S(1)}, u32[]{:S(2)}, u32[]{:S(2)}) collective-permute-start(f32[1,128]{1,0:T(1,128)S(1)} %get-tuple-element.26), channel_id=1, source_target_pairs={{0,1},{1,0},{2,3},{3,2},{4,5},{5,4},{6,7},{7,6},{8,9},{9,8},{10,11... | collective-permute-start | bytes 1544 | tf_op jit(solution)/shard_map/ppermute | solution.py:235
  92.2 5.4 %collective-permute-start.9 = (f32[1,128]{1,0:T(1,128)S(1)}, f32[1,128]{1,0:T(1,128)S(1)}, u32[]{:S(2)}, u32[]{:S(2)}) collective-permute-start(f32[1,128]{1,0:T(1,128)S(1)} %add.43), channel_id=1, source_target_pairs={{0,2},{1,3},{2,0},{3,1},{4,6},{5,7},{6,4},{7,5},{8,10},{9,11},{10,... | collective-permute-start | bytes 1544 | tf_op jit(solution)/shard_map/ppermute | solution.py:235
  97.6 6.3 %collective-permute-start.10 = (f32[1,128]{1,0:T(1,128)S(1)}, f32[1,128]{1,0:T(1,128)S(1)}, u32[]{:S(2)}, u32[]{:S(2)}) collective-permute-start(f32[1,128]{1,0:T(1,128)S(1)} %add.44), channel_id=1, source_target_pairs={{0,4},{1,5},{2,6},{3,7},{4,0},{5,1},{6,2},{7,3},{8,12},{9,13},{10,... | collective-permute-start | bytes 1544 | tf_op jit(solution)/shard_map/ppermute | solution.py:235
  104.0 9.3 %collective-permute-start.11 = (f32[1,128]{1,0:T(1,128)S(1)}, f32[1,128]{1,0:T(1,128)S(1)}, u32[]{:S(2)}, u32[]{:S(2)}) collective-permute-start(f32[1,128]{1,0:T(1,128)S(1)} %add.45), channel_id=1, source_target_pairs={{0,8},{1,9},{2,10},{3,11},{4,12},{5,13},{6,14},{7,15},{8,0},{9,1},... | collective-permute-start | bytes 1544 | tf_op jit(solution)/shard_map/ppermute | solution.py:235
  108.7 14.6 %copy-start.4 = (f32[128,768]{1,0:T(8,128)S(1)}, f32[128,768]{1,0:T(8,128)}, u32[]{:S(2)}) copy-start(f32[128,768]{1,0:T(8,128)} %t_ref.1) | copy-start | bytes 1179652
  108.7 14.6 %copy-start.5 = (f32[128,768]{1,0:T(8,128)S(1)}, f32[128,768]{1,0:T(8,128)}, u32[]{:S(2)}) copy-start(f32[128,768]{1,0:T(8,128)} %param.11) | copy-start | bytes 1179652
  108.7 14.6 %copy-start.6 = (f32[128,768]{1,0:T(8,128)S(1)}, f32[128,768]{1,0:T(8,128)}, u32[]{:S(2)}) copy-start(f32[128,768]{1,0:T(8,128)} %param.12) | copy-start | bytes 1179652
  114.6 14.8 %all-to-all-start.3 = ((f32[8,1,128]{2,1,0:T(1,128)}), f32[8,1,128]{2,1,0:T(1,128)S(1)}, u32[]{:S(2)}, u32[]{:S(2)}) async-start(f32[8,1,128]{2,1,0:T(1,128)} %broadcast_in_dim.9), calls=%async_computation.3 | async-start | bytes 8192 | tf_op jit(solution)/shard_map/all_to_all | solution.py:378

commit v10 on v9

--- a/solution.py
+++ b/solution.py
@@ -19,6 +19,8 @@
 META_ROWS = 32
 SLOTS = 16
 STAT_ROWS = 8
+FIRST_ROWS = 96
+SCALE_ROWS = 16
 f32 = jnp.float32
 bf16 = jnp.bfloat16
 
@@ -167,11 +169,12 @@
 
 
 def grads_kernel(
-    factor_ref, place_ref, near_ref, far_ref, stat_ref, m_ref, g_ref, type_ref, scale_ref, share_ref, rows_ref, grad_ref
+    factor_ref, place_ref, near_ref, far_ref, stat_ref, m_ref, g_ref, first_ref, second_ref, scale_ref, share_ref, rows_ref, grad_ref
 ):
     step = pl.program_id(0)
     factor = factor_ref[0]
     rows = m_ref.shape[1] - META_ROWS
+    chunk = grad_ref.shape[0]
 
     @pl.when(step == 0)
     def _():
@@ -196,10 +199,15 @@
             g_ref[s, line, :] = grad
             grad_ref[line, s * rows : (s + 1) * rows] = grad
     part = jnp.dot(grad_ref[...], rows_ref[...], preferred_element_type=f32)
-    type_ref[...] = (factor * part).astype(bf16)
-
-
-def mention_kernel(factor_ref, place_ref, g_ref, near_ref, low_ref, high_ref, *refs):
+    part = (factor * part).astype(bf16)
+    for c in range(chunk // BLOCK):
+        at = c * BLOCK
+        first_ref[c] = part[at : at + FIRST_ROWS, :]
+        second_ref[c, 0 : BLOCK - FIRST_ROWS, :] = part[at + FIRST_ROWS : at + BLOCK, :]
+        second_ref[c, BLOCK - FIRST_ROWS :, :] = jnp.zeros((SCALE_ROWS, part.shape[1]), bf16)
+
+
+def mention_kernel(factor_ref, place_ref, scale_ref, g_ref, near_ref, low_ref, high_ref, *refs):
     out_refs, tile_ref = refs[:X_SIZE], refs[-1]
     step = pl.program_id(0)
 
@@ -324,8 +332,10 @@
     )(logit_scale, place, gathered, low, high, near_stats)
     stats = lax.all_to_all(stats, "gx", 0, 0, tiled=True)
     chunk = 2 * block_rows
+    last_rows = block_rows - FIRST_ROWS
+    second_rows = last_rows + SCALE_ROWS
     chunk_spec = pl.BlockSpec((X_SIZE, chunk, rows), lambda i: (0, i, 0))
-    grads, type_part, scale_part = pl.pallas_call(
+    grads, first_part, second_part, scale_sum = pl.pallas_call(
         grads_kernel,
         grid=(types // chunk,),
         in_specs=[
@@ -336,10 +346,16 @@
             whole(X_SIZE, STAT_ROWS, X_SIZE * rows),
             whole(X_SIZE, sent_rows, width),
         ],
-        out_specs=[chunk_spec, pl.BlockSpec((chunk, width), lambda i: (i, 0)), whole(1, 128)],
+        out_specs=[
+            chunk_spec,
+            pl.BlockSpec((2, FIRST_ROWS, width), lambda i: (i, 0, 0)),
+            pl.BlockSpec((2, second_rows, width), lambda i: (i, 0, 0)),
+            whole(1, 128),
+        ],
         out_shape=[
             jax.ShapeDtypeStruct((X_SIZE, types, rows), bf16),
-            jax.ShapeDtypeStruct((types, width), bf16),
+            jax.ShapeDtypeStruct((Z_SIZE, FIRST_ROWS, width), bf16),
+            jax.ShapeDtypeStruct((Z_SIZE, second_rows, width), bf16),
             jax.ShapeDtypeStruct((1, 128), f32),
         ],
         scratch_shapes=[
@@ -350,36 +366,42 @@
         compiler_params=params(16),
         name="grads",
     )(logit_scale, place, near_exps, far_exps, stats, gathered)
-    type_parts = lax.all_to_all(
-        type_part.reshape(Z_SIZE, block_rows, width), "gz", 0, 0, tiled=True
-    )
+    first = lax.all_to_all(first_part, "gz", 0, 0, tiled=True)
+    by = 1
+    while by < cols:
+        scale_sum = scale_sum + paired(scale_sum, "gy", lambda y, by=by: y ^ by)
+        by *= 2
+    scale_sum = scale_sum + 0.0 * first[0, 0:1, 0:128].astype(f32)
+    hi = lax.reduce_precision(scale_sum, 8, 7)
+    mid = lax.reduce_precision(scale_sum - hi, 8, 7)
+    pieces = jnp.concatenate([hi, mid, scale_sum - hi - mid], axis=1).astype(bf16)
+    pieces = jnp.broadcast_to(pieces[None], (Z_SIZE, SCALE_ROWS, pieces.shape[1]))
+    second_part = lax.dynamic_update_slice(second_part, pieces, (0, last_rows, 0))
+    second = lax.all_to_all(second_part, "gz", 0, 0, tiled=True)
     parts = pl.pallas_call(
         mention_kernel,
         grid=(X_SIZE,),
-        in_specs=[smem, smem, tile(types, rows)] + table_specs,
+        in_specs=[smem, smem, whole(1, 128), tile(types, rows)] + table_specs,
         out_specs=[whole(rows, width)] * X_SIZE,
         out_shape=[jax.ShapeDtypeStruct((rows, width), bf16)] * X_SIZE,
         scratch_shapes=[pltpu.VMEM((types, width), bf16)],
         compiler_params=params(16),
         name="mention_part",
-    )(logit_scale, place, grads, *table)
+    )(logit_scale, place, scale_sum, grads, *table)
     mention_grad = parts[0].astype(f32)
     for s in range(1, X_SIZE):
         mention_grad = mention_grad + paired(
             parts[s], "gx", lambda x, s=s: x ^ s
         ).astype(f32)
     mention_grad = mention_grad.astype(bf16)
-    scale_sum = scale_part
-    by = 1
-    while by < cols:
-        scale_sum = scale_sum + paired(scale_sum, "gy", lambda y, by=by: y ^ by)
-        by *= 2
-    scale_sum = scale_sum + 0.0 * type_parts[0, 0:1, 0:128].astype(f32)
-    scale_sums = lax.all_to_all(
-        jnp.broadcast_to(scale_sum[None], (Z_SIZE, 1, 128)), "gz", 0, 0, tiled=True
-    )
-    scale_grad = (jnp.sum(scale_sums[:, 0, 0]) / (rows * devices)).reshape(1)
-    type_grad = jnp.sum(type_parts, axis=0, dtype=f32)
+    pieces = second[:, last_rows, 0 : 3 * 128 : 128].astype(f32)
+    scale_grad = (jnp.sum(pieces) / (rows * devices)).reshape(1)
+    type_grad = jnp.concatenate(
+        [
+            jnp.sum(first, axis=0, dtype=f32),
+            jnp.sum(second[:, 0:last_rows], axis=0, dtype=f32),
+        ]
+    )
     new_table, new_first, new_second = adam_rows(type_table, adam_m, adam_v, type_grad)
     return (new_table, new_first, new_second, mention_grad, scale_grad)
 

time: 133 us -> 146 us (1.098)
  the two profiles are of different devices: /device:TPU:56 before, /device:TPU:1 now
where the time goes in v10:
time: 146 us; the launch traced here: 145 us
  starting transfers between devices  70.5 us (48%)
  waiting for transfers between devices  33.3 us (23%)
  Pallas kernels  17.2 us (12%)
  blocking collectives  8.65 us (6%)
  other arithmetic  6.24 us (4%)
  local copies, waits for them, and re-layouts  5.36 us (4%)
  between operations  3.34 us (2%)
    ppermute x12, starting transfers between devices, paired(): lax.ppermute(array, axis, [(i, partner(i)) for i in range(lax.axis_size(a...  51.2 us
    ppermute x12, waiting for transfers between devices, paired(): lax.ppermute(array, axis, [(i, partner(i)) for i in range(lax.axis_size(a...  24.6 us
    all_to_all x1, starting transfers between devices, per_device(): lax.all_to_all(copies, 'gz', 0, 0, tiled=True, axis_index_groups=parities)  10.8 us
    all_to_all x1, blocking collectives, per_device(): stats = lax.all_to_all(stats, 'gx', 0, 0, tiled=True)  8.65 us
    all_to_all x1, waiting for transfers between devices, per_device(): first = lax.all_to_all(first_part, 'gz', 0, 0, tiled=True)  4.54 us
    all_to_all x1, starting transfers between devices, per_device(): first = lax.all_to_all(first_part, 'gz', 0, 0, tiled=True)  4.25 us
    all_to_all x1, starting transfers between devices, per_device(): second = lax.all_to_all(second_part, 'gz', 0, 0, tiled=True)  4.19 us
    all_to_all x1, waiting for transfers between devices, per_device(): lax.all_to_all(copies, 'gz', 0, 0, tiled=True, axis_index_groups=parities)  4.13 us
  transfers between devices with their start and end apart: 15, of which 10 were waited for; matrix products, arithmetic and copies ran while one was open for 3% of the time, Pallas kernels for 6%

profile of v10, /device:TPU:1, one launch (start us, length us, event | category | flops | bytes accessed | tf_op | source)
XLA Modules:
  0.0 144.5 jit_solution(480285577878504945)
XLA Ops:
  0.6 1.9 %cast.1 = bf16[4,128,768]{2,1,0:T(8,128)(2,1)} custom-call(f32[128,768]{1,0:T(8,128)} %t_ref.1), custom_call_target="tpu_custom_call" | custom-call | tf_op jit(solution)/shard_map/cast/pallas_call | solution.py:274
  2.6 10.8 %all-to-all-start = ((bf16[4,128,768]{2,1,0:T(8,128)(2,1)}), bf16[4,128,768]{2,1,0:T(8,128)(2,1)S(1)}, u32[]{:S(2)}, u32[]{:S(2)}) async-start(bf16[4,128,768]{2,1,0:T(8,128)(2,1)} %cast.1), calls=%async_computation | async-start | bytes 1572864 | tf_op jit(solution)/shard_map/all_to_all | solution.py:281
  13.4 1.9 %pack.1 = bf16[288,768]{1,0:T(8,128)(2,1)} custom-call(s32[2,16]{1,0:T(2,128)} %refs_0_.1, s32[1,2]{1,0:T(1,128)} %bitcast.27, s32[1,256]{1,0:T(1,128)} %bitcast.25, s32[1,256]{1,0:T(1,128)} %bitcast.26, bf16[256,768]{1,0:T(8,128)(2,1)} %refs_4_.1), custom_call_target="tpu_custom_call" | custom-call | tf_op jit(solution)/shard_map/pack/pallas_call | solution.py:286
  15.3 4.5 %collective-permute-start.2 = (bf16[288,768]{1,0:T(8,128)(2,1)}, bf16[288,768]{1,0:T(8,128)(2,1)S(1)}, u32[]{:S(2)}, u32[]{:S(2)}) collective-permute-start(bf16[288,768]{1,0:T(8,128)(2,1)} %pack.1), channel_id=1, source_target_pairs={{0,48},{16,32},{32,16},{48,0},{1,49},{17,33},{33,17},{49,1},{2,50}... | collective-permute-start | bytes 1327112 | tf_op jit(solution)/shard_map/ppermute | solution.py:243
  19.8 2.4 %collective-permute-start.1 = (bf16[288,768]{1,0:T(8,128)(2,1)}, bf16[288,768]{1,0:T(8,128)(2,1)S(1)}, u32[]{:S(2)}, u32[]{:S(2)}) collective-permute-start(bf16[288,768]{1,0:T(8,128)(2,1)} %pack.1), channel_id=1, source_target_pairs={{0,32},{16,48},{32,0},{48,16},{1,33},{17,49},{33,1},{49,17},{2,34}... | collective-permute-start | bytes 1327112 | tf_op jit(solution)/shard_map/ppermute | solution.py:243
  22.3 2.2 %collective-permute-start = (bf16[288,768]{1,0:T(8,128)(2,1)}, bf16[288,768]{1,0:T(8,128)(2,1)S(1)}, u32[]{:S(2)}, u32[]{:S(2)}) collective-permute-start(bf16[288,768]{1,0:T(8,128)(2,1)} %pack.1), channel_id=1, source_target_pairs={{0,16},{16,0},{32,48},{48,32},{1,17},{17,1},{33,49},{49,33},{2,18}... | collective-permute-start | bytes 1327112 | tf_op jit(solution)/shard_map/ppermute | solution.py:243
  24.4 4.1 %all-to-all-done.near_ref = bf16[4,128,768]{2,1,0:T(8,128)(2,1)S(1)} async-done(((bf16[4,128,768]{2,1,0:T(8,128)(2,1)}), bf16[4,128,768]{2,1,0:T(8,128)(2,1)S(1)}, u32[]{:S(2)}, u32[]{:S(2)}) %all-to-all-start) | async-done | bytes 786464 | tf_op jit(solution)/shard_map/all_to_all | solution.py:281
  29.5 10.2 %collective-permute-start.4 = (bf16[2,128,768]{2,1,0:T(8,128)(2,1)}, bf16[2,128,768]{2,1,0:T(8,128)(2,1)S(1)}, u32[]{:S(2)}, u32[]{:S(2)}) collective-permute-start(bf16[2,128,768]{2,1,0:T(8,128)(2,1)} %get-tuple-element.34), channel_id=1, source_target_pairs={{0,448},{64,128},{128,64},{192,256},{256,192},{320,384},{384,320},... | collective-permute-start | bytes 1179656 | tf_op jit(solution)/shard_map/ppermute | solution.py:243
  39.7 1.9 %collective-permute-start.3 = (bf16[2,128,768]{2,1,0:T(8,128)(2,1)}, bf16[2,128,768]{2,1,0:T(8,128)(2,1)S(1)}, u32[]{:S(2)}, u32[]{:S(2)}) collective-permute-start(bf16[2,128,768]{2,1,0:T(8,128)(2,1)} %get-tuple-element.35), channel_id=1, source_target_pairs={{0,64},{64,0},{128,192},{192,128},{256,320},{320,256},{384,448},{4... | collective-permute-start | bytes 1179656 | tf_op jit(solution)/shard_map/ppermute | solution.py:243
  42.6 3.0 %near_scores.1 = (f32[4,512,256]{2,1,0:T(8,128)S(1)}, f32[4,8,256]{2,1,0:T(8,128)S(1)}) custom-call(f32[1]{0:T(128)S(6)} %copy.15.factor_ref, s32[2]{0:T(128)S(1)} %pad_add_fusion.place_ref, bf16[4,288,768]{2,1,0:T(8,128)(2,1)S(1)} %pad_maximum_fusion.m_ref, bf16[4,128,768]{2,1,0:T(8,128)(2,1)S(1)} %all-to-all-done.near_ref), custom_call_target="tpu_custom_call" | custom-call | tf_op jit(solution)/shard_map/near_scores/pallas_call | solution.py:313
  45.5 2.9 %collective-permute-done.4.high_ref = bf16[2,128,768]{2,1,0:T(8,128)(2,1)S(1)} collective-permute-done((bf16[2,128,768]{2,1,0:T(8,128)(2,1)}, bf16[2,128,768]{2,1,0:T(8,128)(2,1)S(1)}, u32[]{:S(2)}, u32[]{:S(2)}) %collective-permute-start.4) | collective-permute-done | bytes 393248 | tf_op jit(solution)/shard_map/ppermute | solution.py:243
  48.4 2.8 %collective-permute-done.3.low_ref = bf16[2,128,768]{2,1,0:T(8,128)(2,1)S(1)} collective-permute-done((bf16[2,128,768]{2,1,0:T(8,128)(2,1)}, bf16[2,128,768]{2,1,0:T(8,128)(2,1)S(1)}, u32[]{:S(2)}, u32[]{:S(2)}) %collective-permute-start.3) | collective-permute-done | bytes 393248 | tf_op jit(solution)/shard_map/ppermute | solution.py:243
  51.2 2.9 %far_scores.1 = (f32[4,512,256]{2,1,0:T(8,128)S(1)}, f32[4,8,1024]{2,1,0:T(8,128)S(1)}) custom-call(f32[1]{0:T(128)S(6)} %copy.15.factor_ref, s32[2]{0:T(128)S(1)} %pad_add_fusion.place_ref, bf16[4,288,768]{2,1,0:T(8,128)(2,1)S(1)} %pad_maximum_fusion.m_ref, bf16[2,128,768]{2,1,0:T(8,128)(2,1)S(1)} %collective-permute-done.3.low_ref, ...), custom_call_target="tpu_custom_call" | custom-call | tf_op jit(solution)/shard_map/far_scores/pallas_call | solution.py:323
  54.1 8.6 %all_to_all.20.stat_ref = f32[4,8,1024]{2,1,0:T(8,128)S(1)} all-to-all(f32[4,8,1024]{2,1,0:T(8,128)S(1)} %get-tuple-element.20), channel_id=1, replica_groups=mesh['gz'=8,'gx'=4,'gy'=16] {'gx'}, dimensions={0} | all-to-all | bytes 262144 | tf_op jit(solution)/shard_map/all_to_all | solution.py:333
  62.8 4.1 %grads.1 = (bf16[4,1024,256]{2,1,0:T(8,128)(2,1)S(1)}, bf16[8,96,768]{2,1,0:T(8,128)(2,1)S(1)}, bf16[8,48,768]{2,1,0:T(8,128)(2,1)S(1)}, f32[1,128]{1,0:T(1,128)S(1)}) custom-call(f32[1]{0:T(128)S(6)} %copy.15.factor_ref, s32[2]{0:T(128)S(1)} %pad_add_fusion.place_ref, f32[4,512,256]{2,1,0:T(8,128)S(1)} %get-tuple-element.17.near_ref, ...), custom_call_target="tpu_custom_call" | custom-call | tf_op jit(solution)/shard_map/grads/pallas_call | solution.py:338
  68.7 4.3 %all-to-all-start.2 = ((bf16[8,96,768]{2,1,0:T(8,128)(2,1)}), bf16[8,96,768]{2,1,0:T(8,128)(2,1)}, u32[]{:S(2)}, u32[]{:S(2)}) async-start(bf16[8,96,768]{2,1,0:T(8,128)(2,1)} %copy-done.2), calls=%async_computation.2 | async-start | bytes 2359296 | tf_op jit(solution)/shard_map/all_to_all | solution.py:369
  72.9 5.5 %collective-permute-start.5 = (f32[1,128]{1,0:T(1,128)S(1)}, f32[1,128]{1,0:T(1,128)S(1)}, u32[]{:S(2)}, u32[]{:S(2)}) collective-permute-start(f32[1,128]{1,0:T(1,128)S(1)} %get-tuple-element.23), channel_id=1, source_target_pairs={{0,1},{1,0},{2,3},{3,2},{4,5},{5,4},{6,7},{7,6},{8,9},{9,8},{10,11... | collective-permute-start | bytes 1544 | tf_op jit(solution)/shard_map/ppermute | solution.py:243
  79.2 3.2 %collective-permute-start.6 = (f32[1,128]{1,0:T(1,128)S(1)}, f32[1,128]{1,0:T(1,128)S(1)}, u32[]{:S(2)}, u32[]{:S(2)}) collective-permute-start(f32[1,128]{1,0:T(1,128)S(1)} %add.36), channel_id=1, source_target_pairs={{0,2},{1,3},{2,0},{3,1},{4,6},{5,7},{6,4},{7,5},{8,10},{9,11},{10,... | collective-permute-start | bytes 1544 | tf_op jit(solution)/shard_map/ppermute | solution.py:243
  82.4 1.5 %collective-permute-done.6 = f32[1,128]{1,0:T(1,128)S(1)} collective-permute-done((f32[1,128]{1,0:T(1,128)S(1)}, f32[1,128]{1,0:T(1,128)S(1)}, u32[]{:S(2)}, u32[]{:S(2)}) %collective-permute-start.6) | collective-permute-done | bytes 544 | tf_op jit(solution)/shard_map/ppermute | solution.py:243
  83.9 4.2 %collective-permute-start.7 = (f32[1,128]{1,0:T(1,128)S(1)}, f32[1,128]{1,0:T(1,128)S(1)}, u32[]{:S(2)}, u32[]{:S(2)}) collective-permute-start(f32[1,128]{1,0:T(1,128)S(1)} %add.37), channel_id=1, source_target_pairs={{0,4},{1,5},{2,6},{3,7},{4,0},{5,1},{6,2},{7,3},{8,12},{9,13},{10,... | collective-permute-start | bytes 1544 | tf_op jit(solution)/shard_map/ppermute | solution.py:243
  88.1 1.4 collective-permute-done.7
  89.5 7.4 %collective-permute-start.8 = (f32[1,128]{1,0:T(1,128)S(1)}, f32[1,128]{1,0:T(1,128)S(1)}, u32[]{:S(2)}, u32[]{:S(2)}) collective-permute-start(f32[1,128]{1,0:T(1,128)S(1)} %add.38), channel_id=1, source_target_pairs={{0,8},{1,9},{2,10},{3,11},{4,12},{5,13},{6,14},{7,15},{8,0},{9,1},... | collective-permute-start | bytes 1544 | tf_op jit(solution)/shard_map/ppermute | solution.py:243
  97.8 4.5 %all-to-all-done.2 = bf16[8,96,768]{2,1,0:T(8,128)(2,1)} async-done(((bf16[8,96,768]{2,1,0:T(8,128)(2,1)}), bf16[8,96,768]{2,1,0:T(8,128)(2,1)}, u32[]{:S(2)}, u32[]{:S(2)}) %all-to-all-start.2) | async-done | bytes 1179680 | tf_op jit(solution)/shard_map/all_to_all | solution.py:369
  103.7 4.2 %all-to-all-start.3 = ((bf16[8,48,768]{2,1,0:T(8,128)(2,1)}), bf16[8,48,768]{2,1,0:T(8,128)(2,1)}, u32[]{:S(2)}, u32[]{:S(2)}) async-start(bf16[8,48,768]{2,1,0:T(8,128)(2,1)} %broadcast_dynamic-update-slice_fusion), calls=%async_computation.3 | async-start | bytes 1179648 | tf_op jit(solution)/shard_map/all_to_all | solution.py:380
  108.9 3.4 %mention_part.1 = (bf16[256,768]{1,0:T(8,128)(2,1)S(1)}, bf16[256,768]{1,0:T(8,128)(2,1)S(1)}, bf16[256,768]{1,0:T(8,128)(2,1)S(1)}, bf16[256,768]{1,0:T(8,128)(2,1)S(1)}) custom-call(f32[1]{0:T(128)S(6)} %copy.15.factor_ref, s32[2]{0:T(128)S(1)} %pad_add_fusion.place_ref, f32[1,128]{1,0:T(1,128)S(1)} %get-tuple-element.33.scale_ref, ...), custom_call_target="tpu_custom_call" | custom-call | tf_op jit(solution)/shard_map/mention_part/pallas_call | solution.py:381
  112.3 2.2 %collective-permute-start.9 = (bf16[256,768]{1,0:T(8,128)(2,1)S(1)}, bf16[256,768]{1,0:T(8,128)(2,1)S(1)}, u32[]{:S(2)}, u32[]{:S(2)}) collective-permute-start(bf16[256,768]{1,0:T(8,128)(2,1)S(1)} %get-tuple-element.26), channel_id=1, source_target_pairs={{0,16},{16,0},{32,48},{48,32},{1,17},{17,1},{33,49},{49,33},{2,18}... | collective-permute-start | bytes 1179656 | tf_op jit(solution)/shard_map/ppermute | solution.py:243
  114.5 3.7 %collective-permute-start.10 = (bf16[256,768]{1,0:T(8,128)(2,1)S(1)}, bf16[256,768]{1,0:T(8,128)(2,1)S(1)}, u32[]{:S(2)}, u32[]{:S(2)}) collective-permute-start(bf16[256,768]{1,0:T(8,128)(2,1)S(1)} %get-tuple-element.27), channel_id=1, source_target_pairs={{0,32},{16,48},{32,0},{48,16},{1,33},{17,49},{33,1},{49,17},{2,34}... | collective-permute-start | bytes 1179656 | tf_op jit(solution)/shard_map/ppermute | solution.py:243
  118.2 3.8 %collective-permute-start.11 = (bf16[256,768]{1,0:T(8,128)(2,1)S(1)}, bf16[256,768]{1,0:T(8,128)(2,1)S(1)}, u32[]{:S(2)}, u32[]{:S(2)}) collective-permute-start(bf16[256,768]{1,0:T(8,128)(2,1)S(1)} %get-tuple-element.28), channel_id=1, source_target_pairs={{0,48},{16,32},{32,16},{48,0},{1,49},{17,33},{33,17},{49,1},{2,50}... | collective-permute-start | bytes 1179656 | tf_op jit(solution)/shard_map/ppermute | solution.py:243
  122.1 1.5 %convert_reduce_fusion = f32[96,768]{1,0:T(8,128)S(1)} fusion(bf16[8,96,768]{2,1,0:T(8,128)(2,1)} %all-to-all-done.2), kind=kLoop, calls=%fused_computation | loop fusion | flops 1105920 | bytes 1474560 | tf_op jit(solution)/shard_map/reduce_sum | solution.py:401
  123.6 7.2 %collective-permute-done.10 = bf16[256,768]{1,0:T(8,128)(2,1)S(1)} collective-permute-done((bf16[256,768]{1,0:T(8,128)(2,1)S(1)}, bf16[256,768]{1,0:T(8,128)(2,1)S(1)}, u32[]{:S(2)}, u32[]{:S(2)}) %collective-permute-start.10) | collective-permute-done | bytes 393248 | tf_op jit(solution)/shard_map/ppermute | solution.py:243
  130.8 7.2 %collective-permute-done.11 = bf16[256,768]{1,0:T(8,128)(2,1)S(1)} collective-permute-done((bf16[256,768]{1,0:T(8,128)(2,1)S(1)}, bf16[256,768]{1,0:T(8,128)(2,1)S(1)}, u32[]{:S(2)}, u32[]{:S(2)}) %collective-permute-start.11) | collective-permute-done | bytes 393248 | tf_op jit(solution)/shard_map/ppermute | solution.py:243
  142.2 1.2 divide_subtract_fusion
  (37 shorter events, 10.7 us)
Async XLA Ops:
  2.6 26.0 %all-to-all-start = ((bf16[4,128,768]{2,1,0:T(8,128)(2,1)}), bf16[4,128,768]{2,1,0:T(8,128)(2,1)S(1)}, u32[]{:S(2)}, u32[]{:S(2)}) async-start(bf16[4,128,768]{2,1,0:T(8,128)(2,1)} %cast.1), calls=%async_computation | async-start | bytes 1572864 | tf_op jit(solution)/shard_map/all_to_all | solution.py:281
  15.3 27.0 %copy-start.4 = (bf16[288,768]{1,0:T(8,128)(2,1)S(1)}, bf16[288,768]{1,0:T(8,128)(2,1)}, u32[]{:S(2)}) copy-start(bf16[288,768]{1,0:T(8,128)(2,1)} %pack.1) | copy-start | bytes 1327108
  15.3 27.0 %collective-permute-start.2 = (bf16[288,768]{1,0:T(8,128)(2,1)}, bf16[288,768]{1,0:T(8,128)(2,1)S(1)}, u32[]{:S(2)}, u32[]{:S(2)}) collective-permute-start(bf16[288,768]{1,0:T(8,128)(2,1)} %pack.1), channel_id=1, source_target_pairs={{0,48},{16,32},{32,16},{48,0},{1,49},{17,33},{33,17},{49,1},{2,50}... | collective-permute-start | bytes 1327112 | tf_op jit(solution)/shard_map/ppermute | solution.py:243
  19.8 22.5 %collective-permute-start.1 = (bf16[288,768]{1,0:T(8,128)(2,1)}, bf16[288,768]{1,0:T(8,128)(2,1)S(1)}, u32[]{:S(2)}, u32[]{:S(2)}) collective-permute-start(bf16[288,768]{1,0:T(8,128)(2,1)} %pack.1), channel_id=1, source_target_pairs={{0,32},{16,48},{32,0},{48,16},{1,33},{17,49},{33,1},{49,17},{2,34}... | collective-permute-start | bytes 1327112 | tf_op jit(solution)/shard_map/ppermute | solution.py:243
  22.3 20.1 %collective-permute-start = (bf16[288,768]{1,0:T(8,128)(2,1)}, bf16[288,768]{1,0:T(8,128)(2,1)S(1)}, u32[]{:S(2)}, u32[]{:S(2)}) collective-permute-start(bf16[288,768]{1,0:T(8,128)(2,1)} %pack.1), channel_id=1, source_target_pairs={{0,16},{16,0},{32,48},{48,32},{1,17},{17,1},{33,49},{49,33},{2,18}... | collective-permute-start | bytes 1327112 | tf_op jit(solution)/shard_map/ppermute | solution.py:243
  29.5 18.9 %collective-permute-start.4 = (bf16[2,128,768]{2,1,0:T(8,128)(2,1)}, bf16[2,128,768]{2,1,0:T(8,128)(2,1)S(1)}, u32[]{:S(2)}, u32[]{:S(2)}) collective-permute-start(bf16[2,128,768]{2,1,0:T(8,128)(2,1)} %get-tuple-element.34), channel_id=1, source_target_pairs={{0,448},{64,128},{128,64},{192,256},{256,192},{320,384},{384,320},... | collective-permute-start | bytes 1179656 | tf_op jit(solution)/shard_map/ppermute | solution.py:243
  39.7 11.5 %collective-permute-start.3 = (bf16[2,128,768]{2,1,0:T(8,128)(2,1)}, bf16[2,128,768]{2,1,0:T(8,128)(2,1)S(1)}, u32[]{:S(2)}, u32[]{:S(2)}) collective-permute-start(bf16[2,128,768]{2,1,0:T(8,128)(2,1)} %get-tuple-element.35), channel_id=1, source_target_pairs={{0,64},{64,0},{128,192},{192,128},{256,320},{320,256},{384,448},{4... | collective-permute-start | bytes 1179656 | tf_op jit(solution)/shard_map/ppermute | solution.py:243
  51.2 11.6 %copy-start = (bf16[2,128,768]{2,1,0:T(8,128)(2,1)}, bf16[2,128,768]{2,1,0:T(8,128)(2,1)S(1)}, u32[]{:S(2)}) copy-start(bf16[2,128,768]{2,1,0:T(8,128)(2,1)S(1)} %collective-permute-done.3.low_ref) | copy-start | bytes 1179652
  66.8 1.0 copy-start.2
  67.9 0.8 copy-start.3
  68.7 33.7 %all-to-all-start.2 = ((bf16[8,96,768]{2,1,0:T(8,128)(2,1)}), bf16[8,96,768]{2,1,0:T(8,128)(2,1)}, u32[]{:S(2)}, u32[]{:S(2)}) async-start(bf16[8,96,768]{2,1,0:T(8,128)(2,1)} %copy-done.2), calls=%async_computation.2 | async-start | bytes 2359296 | tf_op jit(solution)/shard_map/all_to_all | solution.py:369
  72.9 6.3 %collective-permute-start.5 = (f32[1,128]{1,0:T(1,128)S(1)}, f32[1,128]{1,0:T(1,128)S(1)}, u32[]{:S(2)}, u32[]{:S(2)}) collective-permute-start(f32[1,128]{1,0:T(1,128)S(1)} %get-tuple-element.23), channel_id=1, source_target_pairs={{0,1},{1,0},{2,3},{3,2},{4,5},{5,4},{6,7},{7,6},{8,9},{9,8},{10,11... | collective-permute-start | bytes 1544 | tf_op jit(solution)/shard_map/ppermute | solution.py:243
  79.2 4.7 %collective-permute-start.6 = (f32[1,128]{1,0:T(1,128)S(1)}, f32[1,128]{1,0:T(1,128)S(1)}, u32[]{:S(2)}, u32[]{:S(2)}) collective-permute-start(f32[1,128]{1,0:T(1,128)S(1)} %add.36), channel_id=1, source_target_pairs={{0,2},{1,3},{2,0},{3,1},{4,6},{5,7},{6,4},{7,5},{8,10},{9,11},{10,... | collective-permute-start | bytes 1544 | tf_op jit(solution)/shard_map/ppermute | solution.py:243
  83.9 5.6 %collective-permute-start.7 = (f32[1,128]{1,0:T(1,128)S(1)}, f32[1,128]{1,0:T(1,128)S(1)}, u32[]{:S(2)}, u32[]{:S(2)}) collective-permute-start(f32[1,128]{1,0:T(1,128)S(1)} %add.37), channel_id=1, source_target_pairs={{0,4},{1,5},{2,6},{3,7},{4,0},{5,1},{6,2},{7,3},{8,12},{9,13},{10,... | collective-permute-start | bytes 1544 | tf_op jit(solution)/shard_map/ppermute | solution.py:243
  89.5 8.4 %collective-permute-start.8 = (f32[1,128]{1,0:T(1,128)S(1)}, f32[1,128]{1,0:T(1,128)S(1)}, u32[]{:S(2)}, u32[]{:S(2)}) collective-permute-start(f32[1,128]{1,0:T(1,128)S(1)} %add.38), channel_id=1, source_target_pairs={{0,8},{1,9},{2,10},{3,11},{4,12},{5,13},{6,14},{7,15},{8,0},{9,1},... | collective-permute-start | bytes 1544 | tf_op jit(solution)/shard_map/ppermute | solution.py:243
  103.7 35.2 %all-to-all-start.3 = ((bf16[8,48,768]{2,1,0:T(8,128)(2,1)}), bf16[8,48,768]{2,1,0:T(8,128)(2,1)}, u32[]{:S(2)}, u32[]{:S(2)}) async-start(bf16[8,48,768]{2,1,0:T(8,128)(2,1)} %broadcast_dynamic-update-slice_fusion), calls=%async_computation.3 | async-start | bytes 1179648 | tf_op jit(solution)/shard_map/all_to_all | solution.py:380
  107.9 1.0 copy-start.1
  112.3 11.2 %collective-permute-start.9 = (bf16[256,768]{1,0:T(8,128)(2,1)S(1)}, bf16[256,768]{1,0:T(8,128)(2,1)S(1)}, u32[]{:S(2)}, u32[]{:S(2)}) collective-permute-start(bf16[256,768]{1,0:T(8,128)(2,1)S(1)} %get-tuple-element.26), channel_id=1, source_target_pairs={{0,16},{16,0},{32,48},{48,32},{1,17},{17,1},{33,49},{49,33},{2,18}... | collective-permute-start | bytes 1179656 | tf_op jit(solution)/shard_map/ppermute | solution.py:243
  114.5 16.3 %collective-permute-start.10 = (bf16[256,768]{1,0:T(8,128)(2,1)S(1)}, bf16[256,768]{1,0:T(8,128)(2,1)S(1)}, u32[]{:S(2)}, u32[]{:S(2)}) collective-permute-start(bf16[256,768]{1,0:T(8,128)(2,1)S(1)} %get-tuple-element.27), channel_id=1, source_target_pairs={{0,32},{16,48},{32,0},{48,16},{1,33},{17,49},{33,1},{49,17},{2,34}... | collective-permute-start | bytes 1179656 | tf_op jit(solution)/shard_map/ppermute | solution.py:243
  118.2 24.0 %copy-start.5 = (f32[128,768]{1,0:T(8,128)S(1)}, f32[128,768]{1,0:T(8,128)}, u32[]{:S(2)}) copy-start(f32[128,768]{1,0:T(8,128)} %t_ref.1) | copy-start | bytes 1179652
  118.2 24.0 %copy-start.6 = (f32[128,768]{1,0:T(8,128)S(1)}, f32[128,768]{1,0:T(8,128)}, u32[]{:S(2)}) copy-start(f32[128,768]{1,0:T(8,128)} %param.11) | copy-start | bytes 1179652
  118.2 24.0 %copy-start.7 = (f32[128,768]{1,0:T(8,128)S(1)}, f32[128,768]{1,0:T(8,128)}, u32[]{:S(2)}) copy-start(f32[128,768]{1,0:T(8,128)} %param.12) | copy-start | bytes 1179652
  118.2 19.7 %collective-permute-start.11 = (bf16[256,768]{1,0:T(8,128)(2,1)S(1)}, bf16[256,768]{1,0:T(8,128)(2,1)S(1)}, u32[]{:S(2)}, u32[]{:S(2)}) collective-permute-start(bf16[256,768]{1,0:T(8,128)(2,1)S(1)} %get-tuple-element.28), channel_id=1, source_target_pairs={{0,48},{16,32},{32,16},{48,0},{1,49},{17,33},{33,17},{49,1},{2,50}... | collective-permute-start | bytes 1179656 | tf_op jit(solution)/shard_map/ppermute | solution.py:243

commit v11 on v8

--- a/solution.py
+++ b/solution.py
@@ -19,7 +19,6 @@
 META_ROWS = 32
 SLOTS = 16
 STAT_ROWS = 8
-SCALE_LANES = 768
 f32 = jnp.float32
 bf16 = jnp.bfloat16
 
@@ -169,7 +168,7 @@
 
 
 def grads_kernel(
-    factor_ref, place_ref, near_ref, far_ref, stat_ref, m_ref, g_ref, type_ref, scale_ref, share_ref, rows_ref, grad_ref
+    factor_ref, place_ref, near_ref, far_ref, stat_ref, m_ref, g_ref, own_ref, low_ref, high_ref, scale_ref, share_ref, rows_ref, grad_ref
 ):
     step = pl.program_id(0)
     factor = factor_ref[0]
@@ -196,12 +195,20 @@
             grad = (weights - jnp.where(ids == gold, 1.0, 0.0)).astype(bf16)
             line = pl.ds(pl.multiple_of(place * BLOCK, BLOCK), BLOCK)
             g_ref[s, line, :] = grad
-            grad_ref[line, s * rows : (s + 1) * rows] = grad
+            grad_ref[h * BLOCK : (h + 1) * BLOCK, s * rows : (s + 1) * rows] = grad
     part = jnp.dot(grad_ref[...], rows_ref[...], preferred_element_type=f32)
-    type_ref[...] = (factor * part).astype(bf16)
-
-
-def mention_kernel(factor_ref, place_ref, g_ref, near_ref, low_ref, high_ref, *refs):
+    part = (factor * part).astype(bf16)
+    own_ref[0] = part[0:BLOCK, :]
+    half = low_ref.shape[0]
+    for k in range(2 * half):
+
+        @pl.when(step == k)
+        def _(k=k):
+            out_ref = low_ref if k < half else high_ref
+            out_ref[k % half] = part[BLOCK:, :]
+
+
+def mention_kernel(factor_ref, place_ref, scale_ref, g_ref, near_ref, low_ref, high_ref, *refs):
     out_refs, tile_ref = refs[:X_SIZE], refs[-1]
     step = pl.program_id(0)
 
@@ -326,9 +333,8 @@
     )(logit_scale, place, gathered, low, high, near_stats)
     stats = lax.all_to_all(stats, "gx", 0, 0, tiled=True)
     chunk = 2 * block_rows
-    scale_shape = (Z_SIZE * cols, 1, SCALE_LANES)
     chunk_spec = pl.BlockSpec((X_SIZE, chunk, rows), lambda i: (0, i, 0))
-    grads, type_part, scale_parts = pl.pallas_call(
+    grads, own_part, low_part, high_part, scale_parts = pl.pallas_call(
         grads_kernel,
         grid=(types // chunk,),
         in_specs=[
@@ -339,11 +345,19 @@
             whole(X_SIZE, STAT_ROWS, X_SIZE * rows),
             whole(X_SIZE, sent_rows, width),
         ],
-        out_specs=[chunk_spec, pl.BlockSpec((chunk, width), lambda i: (i, 0)), whole(*scale_shape)],
+        out_specs=[
+            chunk_spec,
+            tile(block_rows, width),
+            whole(half // 2, block_rows, width),
+            whole(half // 2, block_rows, width),
+            whole(Z_SIZE * cols, 1, 128),
+        ],
         out_shape=[
             jax.ShapeDtypeStruct((X_SIZE, types, rows), bf16),
-            jax.ShapeDtypeStruct((types, width), bf16),
-            jax.ShapeDtypeStruct(scale_shape, f32),
+            jax.ShapeDtypeStruct((half, block_rows, width), bf16),
+            jax.ShapeDtypeStruct((half // 2, block_rows, width), bf16),
+            jax.ShapeDtypeStruct((half // 2, block_rows, width), bf16),
+            jax.ShapeDtypeStruct((Z_SIZE * cols, 1, 128), f32),
         ],
         scratch_shapes=[
             pltpu.VMEM((2, X_SIZE * rows), f32),
@@ -353,28 +367,32 @@
         compiler_params=params(16),
         name="grads",
     )(logit_scale, place, near_exps, far_exps, stats, gathered)
-    type_grad = lax.psum_scatter(type_part, "gz", scatter_dimension=0, tiled=True)
+    from_low = paired(low_part, "gz", lambda z: z ^ 1)
+    from_high = paired(high_part, "gz", lambda z: ((z + 1) ^ 1) - 1 & Z_SIZE - 1)
+    scale_parts = lax.all_to_all(scale_parts, ("gz", "gy"), 0, 0, tiled=True)
+    scale_sum = jnp.sum(scale_parts[:, 0, 0])
+    scale_grad = (scale_sum / (rows * devices)).reshape(1)
+    received = jnp.concatenate([from_low, from_high]).astype(f32)
+    own_part = (own_part.astype(f32) + received + 0.0 * scale_sum).astype(bf16)
+    type_parts = lax.all_to_all(own_part, "gz", 0, 0, tiled=True, axis_index_groups=parities)
     parts = pl.pallas_call(
         mention_kernel,
         grid=(X_SIZE,),
-        in_specs=[smem, smem, tile(types, rows)] + table_specs,
+        in_specs=[smem, smem, smem, tile(types, rows)] + table_specs,
         out_specs=[whole(rows, width)] * X_SIZE,
         out_shape=[jax.ShapeDtypeStruct((rows, width), bf16)] * X_SIZE,
         scratch_shapes=[pltpu.VMEM((types, width), bf16)],
         compiler_params=params(16),
         name="mention_part",
-    )(logit_scale, place, grads, *table)
+    )(logit_scale, place, scale_grad, grads, *table)
     mention_grad = parts[0].astype(f32)
     for s in range(1, X_SIZE):
         mention_grad = mention_grad + paired(
             parts[s], "gx", lambda x, s=s: x ^ s
         ).astype(f32)
     mention_grad = mention_grad.astype(bf16)
-    scale_parts = lax.all_to_all(scale_parts, ("gz", "gy"), 0, 0, tiled=True)
-    scale_grad = (jnp.sum(scale_parts[:, 0, 0]) / (rows * devices)).reshape(1)
-    new_table, new_first, new_second = adam_rows(
-        type_table, adam_m, adam_v, type_grad.astype(f32)
-    )
+    type_grad = jnp.sum(type_parts, axis=0, dtype=f32)
+    new_table, new_first, new_second = adam_rows(type_table, adam_m, adam_v, type_grad)
     return (new_table, new_first, new_second, mention_grad, scale_grad)
 
 

time: 135 us -> 146 us (1.081)
  blocking collectives: 8.64 us -> 35.9 us
  between operations: 16.7 us -> 3.95 us
  starting transfers between devices: 54.6 us -> 50.3 us
  other arithmetic: 4.9 us -> 6.87 us
    all_to_all x0 -> x1, blocking collectives: none -> 27.3 us  [per_device(): scale_parts = lax.all_to_all(scale_parts, ('gz', 'gy'), 0, 0, tiled=True)]
    all_to_all x1, starting transfers between devices: 12.9 us -> 4.19 us  [per_device(): lax.all_to_all(own_part, 'gz', 0, 0, tiled=True, axis_index_groups=parities)]
    ppermute x8 -> x10, starting transfers between devices: 30.9 us -> 35.3 us  [paired(): lax.ppermute(array, axis, [(i, partner(i)) for i in range(lax.axis_size(a...]
    convert_element_type x0 -> x1, other arithmetic: none -> 2.46 us  [per_device(): own_part = (own_part.astype(f32) + received + 0.0 * scale_sum).astype(bf16)]
    ppermute x8 -> x10, waiting for transfers between devices: 23.3 us -> 23.3 us  [paired(): lax.ppermute(array, axis, [(i, partner(i)) for i in range(lax.axis_size(a...]
  transfers between devices with their start and end apart: 11 -> 12, of which waited for: 6 -> 6; matrix products, arithmetic and copies ran while one was open for 3% -> 2% of each run, Pallas kernels for 6% -> 6%
where the time goes in v11:
time: 146 us; the launch traced here: 145 us
  starting transfers between devices  50.3 us (34%)
  blocking collectives  35.9 us (25%)
  waiting for transfers between devices  27.4 us (19%)
  Pallas kernels  17.9 us (12%)
  other arithmetic  6.87 us (5%)
  between operations  3.95 us (3%)
  local copies, waits for them, and re-layouts  2.86 us (2%)
    ppermute x10, starting transfers between devices, paired(): lax.ppermute(array, axis, [(i, partner(i)) for i in range(lax.axis_size(a...  35.3 us
    all_to_all x1, blocking collectives, per_device(): scale_parts = lax.all_to_all(scale_parts, ('gz', 'gy'), 0, 0, tiled=True)  27.3 us
    ppermute x10, waiting for transfers between devices, paired(): lax.ppermute(array, axis, [(i, partner(i)) for i in range(lax.axis_size(a...  23.3 us
    all_to_all x1, starting transfers between devices, per_device(): lax.all_to_all(copies, 'gz', 0, 0, tiled=True, axis_index_groups=parities)  10.8 us
    all_to_all x1, blocking collectives, per_device(): stats = lax.all_to_all(stats, 'gx', 0, 0, tiled=True)  8.64 us
    pallas_call x1, Pallas kernels, per_device(): pl.pallas_call(grads_kernel, grid=(types // chunk,), in_specs=[smem, smem...  4.79 us
    all_to_all x1, starting transfers between devices, per_device(): lax.all_to_all(own_part, 'gz', 0, 0, tiled=True, axis_index_groups=parities)  4.19 us
    all_to_all x1, waiting for transfers between devices, per_device(): lax.all_to_all(copies, 'gz', 0, 0, tiled=True, axis_index_groups=parities)  4.13 us
  transfers between devices with their start and end apart: 12, of which 6 were waited for; matrix products, arithmetic and copies ran while one was open for 2% of the time, Pallas kernels for 6%

profile of v11, /device:TPU:1, one launch (start us, length us, event | category | flops | bytes accessed | tf_op | source)
XLA Modules:
  0.0 145.2 jit_solution(4460811734906958597)
XLA Ops:
  0.6 1.9 %cast.1 = bf16[4,128,768]{2,1,0:T(8,128)(2,1)} custom-call(f32[128,768]{1,0:T(8,128)} %t_ref.1), custom_call_target="tpu_custom_call" | custom-call | tf_op jit(solution)/shard_map/cast/pallas_call | solution.py:275
  2.6 10.8 %all-to-all-start = ((bf16[4,128,768]{2,1,0:T(8,128)(2,1)}), bf16[4,128,768]{2,1,0:T(8,128)(2,1)S(1)}, u32[]{:S(2)}, u32[]{:S(2)}) async-start(bf16[4,128,768]{2,1,0:T(8,128)(2,1)} %cast.1), calls=%async_computation | async-start | bytes 1572864 | tf_op jit(solution)/shard_map/all_to_all | solution.py:282
  13.4 1.9 %pack.1 = bf16[288,768]{1,0:T(8,128)(2,1)} custom-call(s32[2,16]{1,0:T(2,128)} %refs_0_.1, s32[1,2]{1,0:T(1,128)} %bitcast.16, s32[1,256]{1,0:T(1,128)} %bitcast.14, s32[1,256]{1,0:T(1,128)} %bitcast.15, bf16[256,768]{1,0:T(8,128)(2,1)} %refs_4_.1), custom_call_target="tpu_custom_call" | custom-call | tf_op jit(solution)/shard_map/pack/pallas_call | solution.py:287
  15.3 4.5 %collective-permute-start.2 = (bf16[288,768]{1,0:T(8,128)(2,1)}, bf16[288,768]{1,0:T(8,128)(2,1)S(1)}, u32[]{:S(2)}, u32[]{:S(2)}) collective-permute-start(bf16[288,768]{1,0:T(8,128)(2,1)} %pack.1), channel_id=1, source_target_pairs={{0,48},{16,32},{32,16},{48,0},{1,49},{17,33},{33,17},{49,1},{2,50}... | collective-permute-start | bytes 1327112 | tf_op jit(solution)/shard_map/ppermute | solution.py:244
  19.8 2.4 %collective-permute-start.1 = (bf16[288,768]{1,0:T(8,128)(2,1)}, bf16[288,768]{1,0:T(8,128)(2,1)S(1)}, u32[]{:S(2)}, u32[]{:S(2)}) collective-permute-start(bf16[288,768]{1,0:T(8,128)(2,1)} %pack.1), channel_id=1, source_target_pairs={{0,32},{16,48},{32,0},{48,16},{1,33},{17,49},{33,1},{49,17},{2,34}... | collective-permute-start | bytes 1327112 | tf_op jit(solution)/shard_map/ppermute | solution.py:244
  22.3 2.2 %collective-permute-start = (bf16[288,768]{1,0:T(8,128)(2,1)}, bf16[288,768]{1,0:T(8,128)(2,1)S(1)}, u32[]{:S(2)}, u32[]{:S(2)}) collective-permute-start(bf16[288,768]{1,0:T(8,128)(2,1)} %pack.1), channel_id=1, source_target_pairs={{0,16},{16,0},{32,48},{48,32},{1,17},{17,1},{33,49},{49,33},{2,18}... | collective-permute-start | bytes 1327112 | tf_op jit(solution)/shard_map/ppermute | solution.py:244
  24.4 4.1 %all-to-all-done.near_ref = bf16[4,128,768]{2,1,0:T(8,128)(2,1)S(1)} async-done(((bf16[4,128,768]{2,1,0:T(8,128)(2,1)}), bf16[4,128,768]{2,1,0:T(8,128)(2,1)S(1)}, u32[]{:S(2)}, u32[]{:S(2)}) %all-to-all-start) | async-done | bytes 786464 | tf_op jit(solution)/shard_map/all_to_all | solution.py:282
  28.6 0.9 fusion.2
  29.5 10.2 %collective-permute-start.4 = (bf16[2,128,768]{2,1,0:T(8,128)(2,1)}, bf16[2,128,768]{2,1,0:T(8,128)(2,1)S(1)}, u32[]{:S(2)}, u32[]{:S(2)}) collective-permute-start(bf16[2,128,768]{2,1,0:T(8,128)(2,1)} %get-tuple-element.34), channel_id=1, source_target_pairs={{0,448},{64,128},{128,64},{192,256},{256,192},{320,384},{384,320},... | collective-permute-start | bytes 1179656 | tf_op jit(solution)/shard_map/ppermute | solution.py:244
  39.7 1.9 %collective-permute-start.3 = (bf16[2,128,768]{2,1,0:T(8,128)(2,1)}, bf16[2,128,768]{2,1,0:T(8,128)(2,1)S(1)}, u32[]{:S(2)}, u32[]{:S(2)}) collective-permute-start(bf16[2,128,768]{2,1,0:T(8,128)(2,1)} %get-tuple-element.35), channel_id=1, source_target_pairs={{0,64},{64,0},{128,192},{192,128},{256,320},{320,256},{384,448},{4... | collective-permute-start | bytes 1179656 | tf_op jit(solution)/shard_map/ppermute | solution.py:244
  42.6 3.0 %near_scores.1 = (f32[4,512,256]{2,1,0:T(8,128)S(1)}, f32[4,8,256]{2,1,0:T(8,128)S(1)}) custom-call(f32[1]{0:T(128)S(6)} %copy.14.factor_ref, s32[2]{0:T(128)S(1)} %pad_add_fusion.place_ref, bf16[4,288,768]{2,1,0:T(8,128)(2,1)S(1)} %pad_maximum_fusion.m_ref, bf16[4,128,768]{2,1,0:T(8,128)(2,1)S(1)} %all-to-all-done.near_ref), custom_call_target="tpu_custom_call" | custom-call | tf_op jit(solution)/shard_map/near_scores/pallas_call | solution.py:314
  45.5 2.9 %collective-permute-done.4.high_ref = bf16[2,128,768]{2,1,0:T(8,128)(2,1)S(1)} collective-permute-done((bf16[2,128,768]{2,1,0:T(8,128)(2,1)}, bf16[2,128,768]{2,1,0:T(8,128)(2,1)S(1)}, u32[]{:S(2)}, u32[]{:S(2)}) %collective-permute-start.4) | collective-permute-done | bytes 393248 | tf_op jit(solution)/shard_map/ppermute | solution.py:244
  48.4 2.8 %collective-permute-done.3.low_ref = bf16[2,128,768]{2,1,0:T(8,128)(2,1)S(1)} collective-permute-done((bf16[2,128,768]{2,1,0:T(8,128)(2,1)}, bf16[2,128,768]{2,1,0:T(8,128)(2,1)S(1)}, u32[]{:S(2)}, u32[]{:S(2)}) %collective-permute-start.3) | collective-permute-done | bytes 393248 | tf_op jit(solution)/shard_map/ppermute | solution.py:244
  51.2 2.9 %far_scores.1 = (f32[4,512,256]{2,1,0:T(8,128)S(1)}, f32[4,8,1024]{2,1,0:T(8,128)S(1)}) custom-call(f32[1]{0:T(128)S(6)} %copy.14.factor_ref, s32[2]{0:T(128)S(1)} %pad_add_fusion.place_ref, bf16[4,288,768]{2,1,0:T(8,128)(2,1)S(1)} %pad_maximum_fusion.m_ref, bf16[2,128,768]{2,1,0:T(8,128)(2,1)S(1)} %collective-permute-done.3.low_ref, ...), custom_call_target="tpu_custom_call" | custom-call | tf_op jit(solution)/shard_map/far_scores/pallas_call | solution.py:324
  54.1 8.6 %all_to_all.20.stat_ref = f32[4,8,1024]{2,1,0:T(8,128)S(1)} all-to-all(f32[4,8,1024]{2,1,0:T(8,128)S(1)} %get-tuple-element.21), channel_id=1, replica_groups=mesh['gz'=8,'gx'=4,'gy'=16] {'gx'}, dimensions={0} | all-to-all | bytes 262144 | tf_op jit(solution)/shard_map/all_to_all | solution.py:334
  62.8 4.8 %grads.1 = (bf16[4,1024,256]{2,1,0:T(8,128)(2,1)S(1)}, bf16[4,128,768]{2,1,0:T(8,128)(2,1)S(1)}, bf16[2,128,768]{2,1,0:T(8,128)(2,1)}, bf16[2,128,768]{2,1,0:T(8,128)(2,1)}, f32[128,1,128]{2,1,0:T(1,128)S(1)}) custom-call(f32[1]{0:T(128)S(6)} %copy.14.factor_ref, s32[2]{0:T(128)S(1)} %pad_add_fusion.place_ref, ...), custom_call_target="tpu_custom_call" | custom-call | tf_op jit(solution)/shard_map/grads/pallas_call | solution.py:337
  68.5 2.2 %collective-permute-start.5 = (bf16[2,128,768]{2,1,0:T(8,128)(2,1)}, bf16[2,128,768]{2,1,0:T(8,128)(2,1)}, u32[]{:S(2)}, u32[]{:S(2)}) collective-permute-start(bf16[2,128,768]{2,1,0:T(8,128)(2,1)} %get-tuple-element.23), channel_id=1, source_target_pairs={{0,64},{64,0},{128,192},{192,128},{256,320},{320,256},{384,448},{4... | collective-permute-start | bytes 1179656 | tf_op jit(solution)/shard_map/ppermute | solution.py:244
  70.7 2.2 %collective-permute-start.6 = (bf16[2,128,768]{2,1,0:T(8,128)(2,1)}, bf16[2,128,768]{2,1,0:T(8,128)(2,1)}, u32[]{:S(2)}, u32[]{:S(2)}) collective-permute-start(bf16[2,128,768]{2,1,0:T(8,128)(2,1)} %get-tuple-element.24), channel_id=1, source_target_pairs={{0,448},{64,128},{128,64},{192,256},{256,192},{320,384},{384,320},... | collective-permute-start | bytes 1179656 | tf_op jit(solution)/shard_map/ppermute | solution.py:244
  72.9 27.3 %all_to_all.21 = f32[128,1,128]{2,1,0:T(1,128)S(1)} all-to-all(f32[128,1,128]{2,1,0:T(1,128)S(1)} %get-tuple-element.25), channel_id=1, replica_groups=mesh['gz'=8,'gx'=4,'gy'=16] {'gz','gy'}, dimensions={0} | all-to-all | bytes 131072 | tf_op jit(solution)/shard_map/all_to_all | solution.py:372
  101.5 2.5 %add_convert_fusion = bf16[4,128,768]{2,1,0:T(8,128)(2,1)} fusion(bf16[4,128,768]{2,1,0:T(8,128)(2,1)} %copy-done.2, bf16[2,128,768]{2,1,0:T(8,128)(2,1)} %collective-permute-done.6, bf16[2,128,768]{2,1,0:T(8,128)(2,1)} %collective-permute-done.5, f32[]{:T(128)S(6)} %mul.38), kind=kLoop, calls=%fused_computation.2 | loop fusion | flops 2359296 | bytes 2359300 | tf_op jit(solution)/shard_map/convert_element_type | solution.py:376
  104.0 4.2 %all-to-all-start.3 = ((bf16[4,128,768]{2,1,0:T(8,128)(2,1)}), bf16[4,128,768]{2,1,0:T(8,128)(2,1)}, u32[]{:S(2)}, u32[]{:S(2)}) async-start(bf16[4,128,768]{2,1,0:T(8,128)(2,1)} %add_convert_fusion), calls=%async_computation.3 | async-start | bytes 1572864 | tf_op jit(solution)/shard_map/all_to_all | solution.py:377
  108.9 1.0 copy-done.1
  109.8 3.4 %mention_part.1 = (bf16[256,768]{1,0:T(8,128)(2,1)S(1)}, bf16[256,768]{1,0:T(8,128)(2,1)S(1)}, bf16[256,768]{1,0:T(8,128)(2,1)S(1)}, bf16[256,768]{1,0:T(8,128)(2,1)S(1)}) custom-call(f32[1]{0:T(128)S(6)} %copy.14.factor_ref, s32[2]{0:T(128)S(1)} %pad_add_fusion.place_ref, f32[1]{0:T(128)} %bitcast.9.scale_ref, ...), custom_call_target="tpu_custom_call" | custom-call | tf_op jit(solution)/shard_map/mention_part/pallas_call | solution.py:378
  113.3 2.3 %collective-permute-start.7 = (bf16[256,768]{1,0:T(8,128)(2,1)S(1)}, bf16[256,768]{1,0:T(8,128)(2,1)S(1)}, u32[]{:S(2)}, u32[]{:S(2)}) collective-permute-start(bf16[256,768]{1,0:T(8,128)(2,1)S(1)} %get-tuple-element.28), channel_id=1, source_target_pairs={{0,16},{16,0},{32,48},{48,32},{1,17},{17,1},{33,49},{49,33},{2,18}... | collective-permute-start | bytes 1179656 | tf_op jit(solution)/shard_map/ppermute | solution.py:244
  115.6 3.7 %collective-permute-start.8 = (bf16[256,768]{1,0:T(8,128)(2,1)S(1)}, bf16[256,768]{1,0:T(8,128)(2,1)S(1)}, u32[]{:S(2)}, u32[]{:S(2)}) collective-permute-start(bf16[256,768]{1,0:T(8,128)(2,1)S(1)} %get-tuple-element.29), channel_id=1, source_target_pairs={{0,32},{16,48},{32,0},{48,16},{1,33},{17,49},{33,1},{49,17},{2,34}... | collective-permute-start | bytes 1179656 | tf_op jit(solution)/shard_map/ppermute | solution.py:244
  119.3 3.7 %collective-permute-start.9 = (bf16[256,768]{1,0:T(8,128)(2,1)S(1)}, bf16[256,768]{1,0:T(8,128)(2,1)S(1)}, u32[]{:S(2)}, u32[]{:S(2)}) collective-permute-start(bf16[256,768]{1,0:T(8,128)(2,1)S(1)} %get-tuple-element.30), channel_id=1, source_target_pairs={{0,48},{16,32},{32,16},{48,0},{1,49},{17,33},{33,17},{49,1},{2,50}... | collective-permute-start | bytes 1179656 | tf_op jit(solution)/shard_map/ppermute | solution.py:244
  123.0 2.5 %collective-permute-done.7 = bf16[256,768]{1,0:T(8,128)(2,1)S(1)} collective-permute-done((bf16[256,768]{1,0:T(8,128)(2,1)S(1)}, bf16[256,768]{1,0:T(8,128)(2,1)S(1)}, u32[]{:S(2)}, u32[]{:S(2)}) %collective-permute-start.7) | collective-permute-done | bytes 393248 | tf_op jit(solution)/shard_map/ppermute | solution.py:244
  125.5 9.0 %collective-permute-done.8 = bf16[256,768]{1,0:T(8,128)(2,1)S(1)} collective-permute-done((bf16[256,768]{1,0:T(8,128)(2,1)S(1)}, bf16[256,768]{1,0:T(8,128)(2,1)S(1)}, u32[]{:S(2)}, u32[]{:S(2)}) %collective-permute-start.8) | collective-permute-done | bytes 393248 | tf_op jit(solution)/shard_map/ppermute | solution.py:244
  134.4 6.2 %collective-permute-done.9 = bf16[256,768]{1,0:T(8,128)(2,1)S(1)} collective-permute-done((bf16[256,768]{1,0:T(8,128)(2,1)S(1)}, bf16[256,768]{1,0:T(8,128)(2,1)S(1)}, u32[]{:S(2)}, u32[]{:S(2)}) %collective-permute-start.9) | collective-permute-done | bytes 393248 | tf_op jit(solution)/shard_map/ppermute | solution.py:244
  140.6 0.9 add_convert_fusion.1
  141.6 1.3 convert_reduce_fusion
  142.9 1.2 divide_subtract_fusion
  (22 shorter events, 2.0 us)
Async XLA Ops:
  2.6 26.0 %all-to-all-start = ((bf16[4,128,768]{2,1,0:T(8,128)(2,1)}), bf16[4,128,768]{2,1,0:T(8,128)(2,1)S(1)}, u32[]{:S(2)}, u32[]{:S(2)}) async-start(bf16[4,128,768]{2,1,0:T(8,128)(2,1)} %cast.1), calls=%async_computation | async-start | bytes 1572864 | tf_op jit(solution)/shard_map/all_to_all | solution.py:282
  15.3 27.0 %copy-start.3 = (bf16[288,768]{1,0:T(8,128)(2,1)S(1)}, bf16[288,768]{1,0:T(8,128)(2,1)}, u32[]{:S(2)}) copy-start(bf16[288,768]{1,0:T(8,128)(2,1)} %pack.1) | copy-start | bytes 1327108
  15.3 27.0 %collective-permute-start.2 = (bf16[288,768]{1,0:T(8,128)(2,1)}, bf16[288,768]{1,0:T(8,128)(2,1)S(1)}, u32[]{:S(2)}, u32[]{:S(2)}) collective-permute-start(bf16[288,768]{1,0:T(8,128)(2,1)} %pack.1), channel_id=1, source_target_pairs={{0,48},{16,32},{32,16},{48,0},{1,49},{17,33},{33,17},{49,1},{2,50}... | collective-permute-start | bytes 1327112 | tf_op jit(solution)/shard_map/ppermute | solution.py:244
  19.8 22.5 %collective-permute-start.1 = (bf16[288,768]{1,0:T(8,128)(2,1)}, bf16[288,768]{1,0:T(8,128)(2,1)S(1)}, u32[]{:S(2)}, u32[]{:S(2)}) collective-permute-start(bf16[288,768]{1,0:T(8,128)(2,1)} %pack.1), channel_id=1, source_target_pairs={{0,32},{16,48},{32,0},{48,16},{1,33},{17,49},{33,1},{49,17},{2,34}... | collective-permute-start | bytes 1327112 | tf_op jit(solution)/shard_map/ppermute | solution.py:244
  22.3 20.1 %collective-permute-start = (bf16[288,768]{1,0:T(8,128)(2,1)}, bf16[288,768]{1,0:T(8,128)(2,1)S(1)}, u32[]{:S(2)}, u32[]{:S(2)}) collective-permute-start(bf16[288,768]{1,0:T(8,128)(2,1)} %pack.1), channel_id=1, source_target_pairs={{0,16},{16,0},{32,48},{48,32},{1,17},{17,1},{33,49},{49,33},{2,18}... | collective-permute-start | bytes 1327112 | tf_op jit(solution)/shard_map/ppermute | solution.py:244
  29.5 18.9 %collective-permute-start.4 = (bf16[2,128,768]{2,1,0:T(8,128)(2,1)}, bf16[2,128,768]{2,1,0:T(8,128)(2,1)S(1)}, u32[]{:S(2)}, u32[]{:S(2)}) collective-permute-start(bf16[2,128,768]{2,1,0:T(8,128)(2,1)} %get-tuple-element.34), channel_id=1, source_target_pairs={{0,448},{64,128},{128,64},{192,256},{256,192},{320,384},{384,320},... | collective-permute-start | bytes 1179656 | tf_op jit(solution)/shard_map/ppermute | solution.py:244
  39.7 11.5 %collective-permute-start.3 = (bf16[2,128,768]{2,1,0:T(8,128)(2,1)}, bf16[2,128,768]{2,1,0:T(8,128)(2,1)S(1)}, u32[]{:S(2)}, u32[]{:S(2)}) collective-permute-start(bf16[2,128,768]{2,1,0:T(8,128)(2,1)} %get-tuple-element.35), channel_id=1, source_target_pairs={{0,64},{64,0},{128,192},{192,128},{256,320},{320,256},{384,448},{4... | collective-permute-start | bytes 1179656 | tf_op jit(solution)/shard_map/ppermute | solution.py:244
  51.2 11.6 %copy-start = (bf16[2,128,768]{2,1,0:T(8,128)(2,1)}, bf16[2,128,768]{2,1,0:T(8,128)(2,1)S(1)}, u32[]{:S(2)}) copy-start(bf16[2,128,768]{2,1,0:T(8,128)(2,1)S(1)} %collective-permute-done.3.low_ref) | copy-start | bytes 1179652
  67.5 0.9 copy-start.2
  68.5 33.0 %collective-permute-start.5 = (bf16[2,128,768]{2,1,0:T(8,128)(2,1)}, bf16[2,128,768]{2,1,0:T(8,128)(2,1)}, u32[]{:S(2)}, u32[]{:S(2)}) collective-permute-start(bf16[2,128,768]{2,1,0:T(8,128)(2,1)} %get-tuple-element.23), channel_id=1, source_target_pairs={{0,64},{64,0},{128,192},{192,128},{256,320},{320,256},{384,448},{4... | collective-permute-start | bytes 1179656 | tf_op jit(solution)/shard_map/ppermute | solution.py:244
  70.7 30.9 %collective-permute-start.6 = (bf16[2,128,768]{2,1,0:T(8,128)(2,1)}, bf16[2,128,768]{2,1,0:T(8,128)(2,1)}, u32[]{:S(2)}, u32[]{:S(2)}) collective-permute-start(bf16[2,128,768]{2,1,0:T(8,128)(2,1)} %get-tuple-element.24), channel_id=1, source_target_pairs={{0,448},{64,128},{128,64},{192,256},{256,192},{320,384},{384,320},... | collective-permute-start | bytes 1179656 | tf_op jit(solution)/shard_map/ppermute | solution.py:244
  104.0 37.6 %all-to-all-start.3 = ((bf16[4,128,768]{2,1,0:T(8,128)(2,1)}), bf16[4,128,768]{2,1,0:T(8,128)(2,1)}, u32[]{:S(2)}, u32[]{:S(2)}) async-start(bf16[4,128,768]{2,1,0:T(8,128)(2,1)} %add_convert_fusion), calls=%async_computation.3 | async-start | bytes 1572864 | tf_op jit(solution)/shard_map/all_to_all | solution.py:377
  108.8 1.0 copy-start.1
  113.2 29.7 %copy-start.4 = (f32[128,768]{1,0:T(8,128)S(1)}, f32[128,768]{1,0:T(8,128)}, u32[]{:S(2)}) copy-start(f32[128,768]{1,0:T(8,128)} %t_ref.1) | copy-start | bytes 1179652
  113.2 29.7 %copy-start.5 = (f32[128,768]{1,0:T(8,128)S(1)}, f32[128,768]{1,0:T(8,128)}, u32[]{:S(2)}) copy-start(f32[128,768]{1,0:T(8,128)} %param.11) | copy-start | bytes 1179652
  113.2 29.6 %copy-start.6 = (f32[128,768]{1,0:T(8,128)S(1)}, f32[128,768]{1,0:T(8,128)}, u32[]{:S(2)}) copy-start(f32[128,768]{1,0:T(8,128)} %param.12) | copy-start | bytes 1179652
  113.3 12.2 %collective-permute-start.7 = (bf16[256,768]{1,0:T(8,128)(2,1)S(1)}, bf16[256,768]{1,0:T(8,128)(2,1)S(1)}, u32[]{:S(2)}, u32[]{:S(2)}) collective-permute-start(bf16[256,768]{1,0:T(8,128)(2,1)S(1)} %get-tuple-element.28), channel_id=1, source_target_pairs={{0,16},{16,0},{32,48},{48,32},{1,17},{17,1},{33,49},{49,33},{2,18}... | collective-permute-start | bytes 1179656 | tf_op jit(solution)/shard_map/ppermute | solution.py:244
  115.6 18.8 %collective-permute-start.8 = (bf16[256,768]{1,0:T(8,128)(2,1)S(1)}, bf16[256,768]{1,0:T(8,128)(2,1)S(1)}, u32[]{:S(2)}, u32[]{:S(2)}) collective-permute-start(bf16[256,768]{1,0:T(8,128)(2,1)S(1)} %get-tuple-element.29), channel_id=1, source_target_pairs={{0,32},{16,48},{32,0},{48,16},{1,33},{17,49},{33,1},{49,17},{2,34}... | collective-permute-start | bytes 1179656 | tf_op jit(solution)/shard_map/ppermute | solution.py:244
  119.3 21.4 %collective-permute-start.9 = (bf16[256,768]{1,0:T(8,128)(2,1)S(1)}, bf16[256,768]{1,0:T(8,128)(2,1)S(1)}, u32[]{:S(2)}, u32[]{:S(2)}) collective-permute-start(bf16[256,768]{1,0:T(8,128)(2,1)S(1)} %get-tuple-element.30), channel_id=1, source_target_pairs={{0,48},{16,32},{32,16},{48,0},{1,49},{17,33},{33,17},{49,1},{2,50}... | collective-permute-start | bytes 1179656 | tf_op jit(solution)/shard_map/ppermute | solution.py:244
